TPU v7x, 128 devices: a whole 4x4x4 slice. The times are simulated.
128 devices in a mesh: tm: 16 (over y, z), fsdp: 8 (over x, core).
Axes of the slice: x: 4, y: 4, z: 4, core: 2. Of those that a mesh axis runs over, the one named last changes fastest.
Arguments:
- clip: bfloat16 [8, 32, 16, 64, 256], P('fsdp', 'tm'), may hold values from -12 to 12
- cotangent: bfloat16 [8, 32, 16, 64, 256], P('fsdp', 'tm'), may hold values from -5 to 5
- weights: bfloat16 [6912, 256], P('fsdp'), may hold values from -0.1 to 0.1
Outputs:
- grad_input: bfloat16 [8, 32, 16, 64, 256], P('fsdp', 'tm')
- grad_weight: float32 [6912, 256], P('fsdp')
All inputs are finite; a program needn't handle non-finite values.
Results may differ from a plain program's by a relative error of at most 0.015.
Values may be sent and summed in bfloat16 or wider, within the bound.
No kernel may reach another device: no remote copies, remote signals or barrier semaphores. Data moves between devices by JAX's collectives and lax.ppermute only.
A program may use at most 128 MiB of HBM per device.

v0:
```python
import math

import jax
import jax.numpy as jnp
from jax import lax
from jax.sharding import PartitionSpec as P

GROUPS = 32


epsilon = 1e-06


def passed_along(block, axis, distance):
    devices = range(lax.axis_size(axis))
    route = [(i - distance, i) for i in devices if i - distance in devices]
    return lax.ppermute(block, axis, route)


def group_sums(values):
    shaped = values.reshape(values.shape[:4] + (GROUPS, values.shape[4] // GROUPS))
    return shaped.sum(axis=(1, 2, 3, 5))


def expand(stat, channels):
    return jnp.repeat(stat, channels // GROUPS, axis=1)[:, None, None, None, :]


def per_device(clip, cotangent, weights):
    batch_dev, frames, height, tile_width, channels = clip.shape
    time_shards = lax.axis_size("tm")
    weight_shards = lax.axis_size("fsdp")
    group_count = frames * time_shards * height * tile_width * (channels // GROUPS)
    values = clip.astype(jnp.float32)
    first_sum, square_sum = lax.psum((group_sums(values), group_sums(values * values)), "tm")
    center = first_sum / group_count
    spread = square_sum / group_count - center * center
    inverse = lax.rsqrt(spread + epsilon)
    normed = (values - expand(center, channels)) * expand(inverse, channels)
    activation = jax.nn.silu(normed).astype(jnp.bfloat16)
    carried = passed_along(activation, "tm", 1)
    act_pad = jnp.pad(
        jnp.concatenate([carried, activation], axis=1), ((0, 0), (0, 0), (1, 1), (1, 1), (0, 0))
    )
    next_frames = passed_along(cotangent, "tm", -1)
    cot_pad = jnp.pad(
        jnp.concatenate([cotangent, next_frames], axis=1), ((0, 0), (0, 0), (1, 1), (1, 1), (0, 0))
    )
    full_weights = lax.all_gather(weights, "fsdp", axis=0, tiled=True)
    row_count = batch_dev * frames * height * tile_width
    flat_cot = cotangent.reshape(row_count, channels)
    blocks = []
    input_grad = jnp.zeros((row_count, channels), jnp.float32)
    for depth_tap in range(3):
        for level_tap in range(3):
            stacked = jnp.concatenate(
                [
                    act_pad[
                        :,
                        depth_tap : depth_tap + frames,
                        level_tap : level_tap + height,
                        width_tap : width_tap + tile_width,
                        :,
                    ]
                    for width_tap in range(3)
                ],
                axis=-1,
            ).reshape(row_count, 3 * channels)
            blocks.append(
                lax.dot_general(
                    stacked, flat_cot, (((0,), (0,)), ((), ())), preferred_element_type=jnp.float32
                )
            )
            row_start = (depth_tap * 9 + level_tap * 3) * channels
            kernel = (
                full_weights[row_start : row_start + 3 * channels]
                .reshape(3, channels, channels)
                .transpose(0, 2, 1)
                .reshape(3 * channels, channels)
            )
            shifted = jnp.concatenate(
                [
                    cot_pad[
                        :,
                        2 - depth_tap : 2 - depth_tap + frames,
                        2 - level_tap : 2 - level_tap + height,
                        2 - width_tap : 2 - width_tap + tile_width,
                        :,
                    ]
                    for width_tap in range(3)
                ],
                axis=-1,
            ).reshape(row_count, 3 * channels)
            input_grad = input_grad + jnp.dot(shifted, kernel, preferred_element_type=jnp.float32)
    grad_scale = 1.0 / math.sqrt(row_count * time_shards * weight_shards)
    grad_local = jnp.concatenate(blocks, axis=0) * grad_scale
    grad_part = lax.psum_scatter(
        grad_local.astype(jnp.bfloat16), "fsdp", scatter_dimension=0, tiled=True
    )
    grad_weight = lax.psum(grad_part, "tm").astype(jnp.float32)
    sigmoid_val = jax.nn.sigmoid(normed)
    derivative = sigmoid_val * (1.0 + normed * (1.0 - sigmoid_val))
    norm_grad = input_grad.reshape(clip.shape) * derivative
    grad_total, grad_cross = lax.psum((group_sums(norm_grad), group_sums(norm_grad * normed)), "tm")
    grad_input = cotangent.astype(jnp.float32) + expand(inverse, channels) * (
        norm_grad
        - expand(grad_total / group_count, channels)
        - normed * expand(grad_cross / group_count, channels)
    )
    return (grad_input.astype(jnp.bfloat16), grad_weight)


def solution(mesh):
    in_specs = (
        P("fsdp", "tm", None, None, None),
        P("fsdp", "tm", None, None, None),
        P("fsdp", None),
    )
    out_specs = (P("fsdp", "tm", None, None, None), P("fsdp", None))
    return jax.shard_map(
        per_device, mesh=mesh, in_specs=in_specs, out_specs=out_specs, check_vma=False
    )
```

profile of v0, /device:TPU:6, one launch (start us, length us, event | category | flops | bytes accessed | tf_op | source)
XLA Modules:
  0.0 310.8 jit_solution(10717905325942856755)
XLA Ops:
  11.2 53.8 %all-reduce.3 = (f32[1,32]{1,0:T(1,128)S(1)}, f32[1,32]{1,0:T(1,128)S(1)}) all-reduce(f32[1,32]{1,0:T(1,128)S(1)} %bitcast.241, f32[1,32]{1,0:T(1,128)S(1)} %bitcast.243), channel_id=1, replica_groups=mesh['tm'=16,'fsdp'=8] {'tm'}, use_global_device_ids=true, to_apply=%region_5.6 | all-reduce | flops 64 | bytes 512 | tf_op jit(solution)/shard_map/psum | solution.py:35
  66.8 2.6 pad_slice_fusion.27
  69.8 7.5 %pad_slice_fusion.28 = (bf16[1,2,16,64,256]{4,3,2,1,0:T(8,128)(2,1)}, bf16[1,2,16,64,256]{4,3,2,1,0:T(8,128)(2,1)S(1)}, bf16[1,2,16,64,256]{4,3,2,1,0:T(8,128)(2...) fusion(bf16[1,4,16,64,256]{4,3,2,1,0:T(8,128)(2,1)S(1)} %consta, ...), kind=kLoop, calls=%fused_computation.123 | loop fusion | bytes 22020096 | tf_op jit(solution)/shard_map/slice | solution.py:83
  77.3 5.4 %pad_maximum_fusion.2 = (bf16[1,2,16,64,768]{4,3,2,1,0:T(8,128)(2,1)}, bf16[1,2,16,64,768]{4,3,2,1,0:T(8,128)(2,1)}) fusion(bf16[1,2,16,64,256]{4,3,2,1,0:T(8,128)(2,1)} %get-tuple-element.51, bf16[1,2,16,64,256]{4,3,2,1,0:T(8,128)(2,1)} %get-tuple-element.50, bf16[1,2,16,64,256]{4,3,2,1,0:T(8,128)(2,1)} %get-tuple-element.49, ...), kind=kLoop, calls=%fused_computation.3 | loop fusion | flops 18874368 | bytes 12582912 | tf_op jit(solution)/shard_map/concatenate | solution.py:81
  83.9 3.4 %pad_maximum_fusion.4 = (bf16[1,2,16,64,768]{4,3,2,1,0:T(8,128)(2,1)}, bf16[1,2,16,64,768]{4,3,2,1,0:T(8,128)(2,1)}) fusion(bf16[1,2,16,64,256]{4,3,2,1,0:T(8,128)(2,1)S(1)} %copy-done.19, bf16[1,2,16,64,256]{4,3,2,1,0:T(8,128)(2,1)S(1)} %get-tuple-element.67, bf16[1,2,16,64,256]{4,3,2,1,0:T(8,128)(2,1)S(1)} %copy-done.18, ...), kind=kLoop, calls=%fused_computation.5 | loop fusion | flops 18874368 | bytes 12582912 | tf_op jit(solution)/shard_map/concatenate | solution.py:81
  88.3 2.8 pad_maximum_fusion.6
  91.1 2.9 pad_maximum_fusion
  94.1 3.6 %fusion.103 = (bf16[768,256]{1,0:T(8,128)(2,1)}, bf16[768,256]{1,0:T(8,128)(2,1)S(1)}, bf16[768,256]{1,0:T(8,128)(2,1)}, bf16[768,256]{1,0:T(8,128)(2,1)}, bf16[...) fusion(bf16[6912,256]{1,0:T(8,128)(2,1)} %all-gather.2.cloned.1, ...), kind=kLoop, calls=%fused_computation.189 | loop fusion | bytes 7077888 | tf_op jit(solution)/shard_map/slice | solution.py:76
  97.7 1.9 copy.5
  99.6 1.9 copy.6
  101.5 1.9 copy.7
  103.5 1.9 copy.8
  105.4 1.9 copy.9
  113.3 3.1 fusion.104
  130.2 2.5 fusion.101
  132.7 2.8 collective-permute-start.1
  135.5 16.0 %collective-permute-done.1 = bf16[1,2,16,64,256]{4,3,2,1,0:T(8,128)(2,1)S(1)} collective-permute-done((bf16[1,2,16,64,256]{4,3,2,1,0:T(8,128)(2,1)S(1)}, bf16[1,2,16,64,256]{4,3,2,1,0:T(8,128)(2,1)S(1)}, u32[]{:S(2)}, u32[]{:S(2)}) %collective-permute-start.1) | collective-permute-done | bytes 1048608 | tf_op jit(solution)/shard_map/ppermute | solution.py:17
  151.7 7.2 %pad_slice_fusion.4 = (bf16[1,2,16,64,256]{4,3,2,1,0:T(8,128)(2,1)S(1)}, bf16[1,2,16,64,256]{4,3,2,1,0:T(8,128)(2,1)}, bf16[1,2,16,64,256]{4,3,2,1,0:T(8,128)(2,...) fusion(bf16[1,4,16,64,256]{4,3,2,1,0:T(8,128)(2,1)S(1)} %pad_ma, ...), kind=kLoop, calls=%fused_computation.99 | loop fusion | bytes 22020096 | tf_op jit(solution)/shard_map/slice | solution.py:58
  159.0 2.0 pad_slice_fusion.3
  174.0 2.5 multiply_convert_fusion
  177.0 38.4 %all-reduce.2 = (f32[1,32]{1,0:T(1,128)S(1)}, f32[1,32]{1,0:T(1,128)S(1)}) all-reduce(f32[1,32]{1,0:T(1,128)S(1)} %bitcast.240, f32[1,32]{1,0:T(1,128)S(1)} %bitcast.242), channel_id=1, replica_groups=mesh['tm'=16,'fsdp'=8] {'tm'}, use_global_device_ids=true, to_apply=%region_11.12 | all-reduce | flops 64 | bytes 512 | tf_op jit(solution)/shard_map/psum | solution.py:104
  215.7 3.2 %fusion.62 = bf16[1,2,16,64,256]{4,3,2,1,0:T(8,128)(2,1)} fusion(bf16[1,2,16,64,256]{4,3,2,1,0:T(8,128)(2,1)S(1)} %copy-done.8, f32[1,2,16,64,256]{4,3,2,1,0:T(8,128)} %get-tuple-element.10, bf16[1,2,16,64,256]{4,3,2,1,0:T(8,128)(2,1)S(1)} %copy-done.11, f32[256]{0:T(256)S(1)} %broadcast_in_dim.28, f32[256]{0:T(256)S(1)} %broadcast_in_dim.26, ...), kind=kLoop, calls=%fused_computation.95 | loop fusion | flops 5242880 | bytes 5246976 | tf_op jit(solution)/shard_map/convert_element_type | solution.py:110
  219.0 83.4 %all-reduce.6.cloned.1.call-done = bf16[864,256]{1,0:T(8,128)(2,1)} async-done(((bf16[864,256]{1,0:T(8,128)(2,1)}), bf16[864,256]{1,0:T(8,128)(2,1)}) %all-reduce.6.cloned.1.call-update) | async-done | bytes 442384 | tf_op jit(solution)/shard_map/psum | solution.py:100
  302.3 2.0 convert_element_type.26
  (140 shorter events, 41.7 us)
Async XLA Ops:
  7.2 86.9 %all-gather.2.cloned.1.call-start = ((), (), s32[]{:S(2)}) async-start(), calls=%async_computation.1 | async-start | bytes 3981312 | tf_op jit(solution)/shard_map/all_gather | solution.py:49
  7.9 207.5 %reduce-scatter.2.cloned.1.call-start = ((), (), s32[]{:S(2)}) async-start(), calls=%async_computation.2 | async-start | bytes 3981312 | tf_op jit(solution)/shard_map/reduce_scatter | solution.py:97
  7.9 58.7 %collective-permute-start = (bf16[1,2,16,64,256]{4,3,2,1,0:T(8,128)(2,1)}, bf16[1,2,16,64,256]{4,3,2,1,0:T(8,128)(2,1)S(1)}, u32[]{:S(2)}, u32[]{:S(2)}) collective-permute-start(bf16[1,2,16,64,256]{4,3,2,1,0:T(8,128)(2,1)} %param.4), channel_id=1, source_target_pairs={{8,0},{16,8},{24,16},{32,24},{40,32},{48,40},{56,48},{64,56},{72,6... | collective-permute-start | bytes 3145736 | tf_op jit(solution)/shard_map/ppermute | solution.py:17
  66.7 2.7 copy-start.12
  66.8 2.6 copy-start.9
  77.3 5.5 %copy-start.18 = (bf16[1,2,16,64,256]{4,3,2,1,0:T(8,128)(2,1)S(1)}, bf16[1,2,16,64,256]{4,3,2,1,0:T(8,128)(2,1)}, u32[]{:S(2)}) copy-start(bf16[1,2,16,64,256]{4,3,2,1,0:T(8,128)(2,1)} %get-tuple-element.55) | copy-start | bytes 3145732
  77.3 5.5 %copy-start.19 = (bf16[1,2,16,64,256]{4,3,2,1,0:T(8,128)(2,1)S(1)}, bf16[1,2,16,64,256]{4,3,2,1,0:T(8,128)(2,1)}, u32[]{:S(2)}) copy-start(bf16[1,2,16,64,256]{4,3,2,1,0:T(8,128)(2,1)} %get-tuple-element.56) | copy-start | bytes 3145732
  77.3 5.5 %copy-start.20 = (bf16[1,2,16,64,256]{4,3,2,1,0:T(8,128)(2,1)S(1)}, bf16[1,2,16,64,256]{4,3,2,1,0:T(8,128)(2,1)}, u32[]{:S(2)}) copy-start(bf16[1,2,16,64,256]{4,3,2,1,0:T(8,128)(2,1)} %get-tuple-element.57) | copy-start | bytes 3145732
  77.3 6.0 %copy-start.21 = (bf16[1,2,16,64,256]{4,3,2,1,0:T(8,128)(2,1)S(1)}, bf16[1,2,16,64,256]{4,3,2,1,0:T(8,128)(2,1)}, u32[]{:S(2)}) copy-start(bf16[1,2,16,64,256]{4,3,2,1,0:T(8,128)(2,1)} %get-tuple-element.58) | copy-start | bytes 3145732
  77.3 6.6 %copy-start.22 = (bf16[1,2,16,64,256]{4,3,2,1,0:T(8,128)(2,1)S(1)}, bf16[1,2,16,64,256]{4,3,2,1,0:T(8,128)(2,1)}, u32[]{:S(2)}) copy-start(bf16[1,2,16,64,256]{4,3,2,1,0:T(8,128)(2,1)} %get-tuple-element.59) | copy-start | bytes 3145732
  83.9 3.5 %copy-start.14 = (bf16[1,2,16,64,256]{4,3,2,1,0:T(8,128)(2,1)S(1)}, bf16[1,2,16,64,256]{4,3,2,1,0:T(8,128)(2,1)}, u32[]{:S(2)}) copy-start(bf16[1,2,16,64,256]{4,3,2,1,0:T(8,128)(2,1)} %get-tuple-element.44) | copy-start | bytes 3145732
  83.9 3.5 %copy-start.15 = (bf16[1,2,16,64,256]{4,3,2,1,0:T(8,128)(2,1)S(1)}, bf16[1,2,16,64,256]{4,3,2,1,0:T(8,128)(2,1)}, u32[]{:S(2)}) copy-start(bf16[1,2,16,64,256]{4,3,2,1,0:T(8,128)(2,1)} %get-tuple-element.60) | copy-start | bytes 3145732
  83.9 3.5 %copy-start.16 = (bf16[1,2,16,64,256]{4,3,2,1,0:T(8,128)(2,1)S(1)}, bf16[1,2,16,64,256]{4,3,2,1,0:T(8,128)(2,1)}, u32[]{:S(2)}) copy-start(bf16[1,2,16,64,256]{4,3,2,1,0:T(8,128)(2,1)} %get-tuple-element.61) | copy-start | bytes 3145732
  83.9 4.4 %copy-start.17 = (bf16[1,2,16,64,256]{4,3,2,1,0:T(8,128)(2,1)S(1)}, bf16[1,2,16,64,256]{4,3,2,1,0:T(8,128)(2,1)}, u32[]{:S(2)}) copy-start(bf16[1,2,16,64,256]{4,3,2,1,0:T(8,128)(2,1)} %get-tuple-element.62) | copy-start | bytes 3145732
  88.3 2.8 copy-start.13
  113.2 3.1 %copy-start.6 = (bf16[1,2,16,64,768]{4,3,2,1,0:T(8,128)(2,1)S(1)}, bf16[1,2,16,64,768]{4,3,2,1,0:T(8,128)(2,1)}, u32[]{:S(2)}) copy-start(bf16[1,2,16,64,768]{4,3,2,1,0:T(8,128)(2,1)} %get-tuple-element.73) | copy-start | bytes 9437188
  113.2 3.1 %copy-start.29 = (bf16[3,256,256]{2,1,0:T(8,128)(2,1)S(1)}, bf16[3,256,256]{2,1,0:T(8,128)(2,1)}, u32[]{:S(2)}) copy-start(bf16[3,256,256]{2,1,0:T(8,128)(2,1)} %copy.6) | copy-start | bytes 1179652
  132.7 18.8 %collective-permute-start.1 = (bf16[1,2,16,64,256]{4,3,2,1,0:T(8,128)(2,1)S(1)}, bf16[1,2,16,64,256]{4,3,2,1,0:T(8,128)(2,1)S(1)}, u32[]{:S(2)}, u32[]{:S(2)}) collective-permute-start(bf16[1,2,16,64,256]{4,3,2,1,0:T(8,128)(2,1)S(1)} %get-tuple-element.69), channel_id=1, source_target_pairs={{0,8},{8,16},{16,24},{24,32},{32,40},{40,48},{48,56},{56,64},{64,7... | collective-permute-start | bytes 3145736 | tf_op jit(solution)/shard_map/ppermute | solution.py:17
  158.9 2.0 copy-start.10
  159.0 2.0 copy-start.40
  159.0 2.0 copy-start.41
  176.5 39.2 %copy-start.8 = (bf16[1,2,16,64,256]{4,3,2,1,0:T(8,128)(2,1)S(1)}, bf16[1,2,16,64,256]{4,3,2,1,0:T(8,128)(2,1)}, u32[]{:S(2)}) copy-start(bf16[1,2,16,64,256]{4,3,2,1,0:T(8,128)(2,1)} %param.3) | copy-start | bytes 3145732
  176.5 39.2 %copy-start.11 = (bf16[1,2,16,64,256]{4,3,2,1,0:T(8,128)(2,1)S(1)}, bf16[1,2,16,64,256]{4,3,2,1,0:T(8,128)(2,1)}, u32[]{:S(2)}) copy-start(bf16[1,2,16,64,256]{4,3,2,1,0:T(8,128)(2,1)} %param.4) | copy-start | bytes 3145732
  176.5 125.8 %all-reduce.6.cloned.1.call-start = ((), (), s32[]{:S(2)}) async-start(), calls=%async_computation.3 | async-start | bytes 884736 | tf_op jit(solution)/shard_map/psum | solution.py:100
  (23 other events, 38.0 us)
Sparse Core Ops, SparseCore 0:
  9.7 30.0 all-gather.1
  176.6 35.2 reduce-scatter.1
  215.6 86.7 all-reduce.5
where the time goes:
time: 312 us; the launch traced here: 311 us
  waiting for transfers between devices  100 us (32%)
  blocking collectives  92.2 us (30%)
  local copies, waits for them, and re-layouts  52.2 us (17%)
  other arithmetic  27.5 us (9%)
  matrix products  20.3 us (7%)
  between operations  14.3 us (5%)
  starting transfers between devices  4.2 us (1%)
    psum x1, waiting for transfers between devices, per_device(): grad_weight = lax.psum(grad_part, 'tm').astype(jnp.float32)  83.4 us
    psum x1, blocking collectives, per_device(): lax.psum((group_sums(values), group_sums(values * values)), 'tm')  53.8 us
    psum x1, blocking collectives, per_device(): lax.psum((group_sums(norm_grad), group_sums(norm_grad * normed)), 'tm')  38.4 us
    ppermute x2, waiting for transfers between devices, passed_along(): return lax.ppermute(block, axis, route)  16 us
    transpose x9, local copies, waits for them, and re-layouts, per_device(): kernel = full_weights[row_start:row_start + 3 * channels].reshape(3, chan...  15.5 us
    concatenate x5, other arithmetic, per_device(): jnp.concatenate([cot_pad[:, 2 - depth_tap:2 - depth_tap + frames, 2 - lev...  15 us
    unnamed x85, local copies, waits for them, and re-layouts  12.7 us
    dot_general x9, matrix products, per_device(): jnp.dot(shifted, kernel, preferred_element_type=jnp.float32)  11.1 us
  transfers between devices with their start and end apart: 5, of which 2 were waited for; matrix products, arithmetic and copies ran while one was open for 11% of the time, Pallas kernels for 0%

commit v1 on v0

v1 whole, which is shorter than its diff:
```python
import functools
import math

import jax
import jax.numpy as jnp
from jax import lax
from jax.experimental import pallas as pl
from jax.experimental.pallas import tpu as pltpu
from jax.sharding import PartitionSpec as P

GROUPS = 32
C = 256
H = 16
W = 64
ROWS = H * W
PADDED = ROWS + 2 * W
SHARD = 864
SHARD_PAD = 896
QUARTER = 112
UNIT = 32
VMEM = 56 * 1024 * 1024
epsilon = 1e-06
f32 = jnp.float32
bf16 = jnp.bfloat16


def group_total(rows):
    lane = lax.broadcasted_iota(jnp.int32, rows.shape, 1)
    for s in (1, 2, 4):
        up = pltpu.roll(rows, s, 1)
        down = pltpu.roll(rows, C - s, 1)
        rows = rows + jnp.where((lane & s) != 0, up, down)
    return rows


def center_inverse(stats, count):
    sums = group_total(stats) / count
    center = sums[0:1]
    spread = sums[1:2] - center * center
    return center, lax.rsqrt(spread + epsilon)


def sigmoid(v):
    return 1.0 / (1.0 + jnp.exp(-v))


def widths(target, cot, slot):
    zero = jnp.zeros((W, C), bf16)
    for kw in range(3):
        target[kw, slot, 0:W] = zero
        target[kw, slot, W + ROWS : PADDED] = zero
    column = lax.broadcasted_iota(jnp.int32, (W, C), 0)

    @pl.loop(0, H)
    def _(h):
        row = cot(pl.multiple_of(h * W, W))
        at = pl.ds(pl.multiple_of(h * W + W, W), W)
        wide = row.astype(f32)
        target[1, slot, at] = row
        target[0, slot, at] = jnp.where(column == W - 1, 0.0, pltpu.roll(wide, W - 1, 0)).astype(bf16)
        target[2, slot, at] = jnp.where(column == 0, 0.0, pltpu.roll(wide, 1, 0)).astype(bf16)


def stats_kernel(clip, out):
    def step(i, carry):
        a, b = carry
        v = clip[pl.ds(pl.multiple_of(i * 128, 128), 128)].astype(f32)
        v = v.reshape(16, 8, C)
        return a + v.sum(0), b + (v * v).sum(0)

    zero = jnp.zeros((8, C), f32)
    a, b = lax.fori_loop(0, clip.shape[0] // 128, step, (zero, zero))
    out[0:1] = a.sum(0, keepdims=True)
    out[1:2] = b.sum(0, keepdims=True)


def weight_grad_kernel(count, scale, where, stats, clip, before, cot, after, keep, send, act, wide):
    center, inverse = center_inverse(stats[...], count)
    first = where[0]
    core = where[1]

    def activate(frame, slot, gain):
        @pl.loop(0, ROWS // 256)
        def _(i):
            at = pl.ds(pl.multiple_of(i * 256, 256), 256)
            v = (frame(at).astype(f32) - center) * inverse
            v = v * sigmoid(v)
            if gain is not None:
                v = v * gain
            act[slot, :, at] = v.T.astype(bf16)

    activate(lambda at: before[at], 0, jnp.where(first == 1, 0.0, 1.0))
    activate(lambda at: clip[0, at], 1, None)
    activate(lambda at: clip[1, at], 2, None)
    for t in range(2):
        widths(wide, lambda r, t=t: cot[t, pl.ds(r, W)], t)
    widths(wide, lambda r: after[pl.ds(r, W)], 2)

    @pl.loop(0, 9)
    def _(tap):
        kt = tap // 3
        kh = tap % 3
        frame = jnp.where(kt == 0, 0, 1)
        slot = jnp.where(kt == 2, 0, 1)
        rows = pl.ds(pl.multiple_of((2 - kh) * W, W), ROWS)
        for kw in range(3):
            total = jnp.dot(act[frame], wide[kw, slot, rows], preferred_element_type=f32)
            total += jnp.dot(act[frame + 1], wide[kw, slot + 1, rows], preferred_element_type=f32)
            total = total * scale
            for u in range(C // UNIT):
                unit = (tap * 3 + kw) * (C // UNIT) + u
                shard = unit // (SHARD // UNIT)
                x = shard // 2
                place = jnp.where(x == 0, 0, jnp.where(x == 3, 1, x + 1))
                dest = place * SHARD_PAD + (unit - shard * (SHARD // UNIT)) * UNIT
                mine = (shard % 2) == core
                spare = 4 * SHARD_PAD
                piece = total[u * UNIT : (u + 1) * UNIT]
                keep[pl.ds(pl.multiple_of(jnp.where(mine, dest, spare), UNIT), UNIT)] = piece
                send[pl.ds(pl.multiple_of(jnp.where(mine, spare, dest), UNIT), UNIT)] = piece.astype(bf16)

    for place in range(4):
        tail = slice(place * SHARD_PAD + SHARD, (place + 1) * SHARD_PAD)
        keep[tail] = jnp.zeros((SHARD_PAD - SHARD, C), f32)
        send[tail] = jnp.zeros((SHARD_PAD - SHARD, C), bf16)


def input_grad_kernel(count, stats, clip, cot, after, later, weights, grad, sums, wide):
    center, inverse = center_inverse(stats[...], count)
    for t in range(2):
        widths(wide, lambda r, t=t: cot[t, pl.ds(r, W)], t)
    widths(wide, lambda r: after[pl.ds(r, W)], 2)
    widths(wide, lambda r: later[pl.ds(r, W)], 3)
    contract = (((1,), (1,)), ((), ()))
    grad[...] = jnp.zeros_like(grad)

    @pl.loop(0, 18)
    def _(step):
        tap = step // 2
        frame = step % 2
        kt = tap // 3
        kh = tap % 3
        slot = frame + 2 - kt
        rows = pl.ds(pl.multiple_of((2 - kh) * W, W), ROWS)
        total = None
        for kw in range(3):
            w = weights[pl.ds(pl.multiple_of((tap * 3 + kw) * C, C), C)]
            part = lax.dot_general(wide[kw, slot, rows], w, contract, preferred_element_type=f32)
            total = part if total is None else total + part
        grad[frame] += total

    zero = jnp.zeros((8, C), f32)

    def finish(i, carry):
        a, b = carry
        at = pl.ds(pl.multiple_of((i % 16) * 64, 64), 64)
        frame = i // 16
        v = (clip[frame, at].astype(f32) - center) * inverse
        s = sigmoid(v)
        g = grad[frame, at] * (s * (1.0 + v * (1.0 - s)))
        grad[frame, at] = g
        return a + g.reshape(8, 8, C).sum(0), b + (g * v).reshape(8, 8, C).sum(0)

    a, b = lax.fori_loop(0, 32, finish, (zero, zero))
    sums[0:1] = a.sum(0, keepdims=True)
    sums[1:2] = b.sum(0, keepdims=True)


def final_kernel(count, stats, sums, clip, cot, grad, out):
    center, inverse = center_inverse(stats[...], count)
    means = group_total(sums[...]) / count
    total, cross = means[0:1], means[1:2]

    @pl.loop(0, 32)
    def _(i):
        at = pl.ds(pl.multiple_of((i % 16) * 64, 64), 64)
        frame = i // 16
        v = (clip[frame, at].astype(f32) - center) * inverse
        g = cot[frame, at].astype(f32) + inverse * (grad[frame, at] - total - v * cross)
        out[frame, at] = g.astype(bf16)


def call(kernel, out_shape, args, scratch=(), flops=0, bytes_accessed=4_000_000, scalars=0):
    specs = [pl.BlockSpec(memory_space=pltpu.SMEM)] * scalars
    specs += [pl.BlockSpec(memory_space=pltpu.VMEM)] * (len(args) - scalars)
    return pl.pallas_call(
        kernel,
        out_shape=out_shape,
        in_specs=specs,
        out_specs=jax.tree.map(lambda _: pl.BlockSpec(memory_space=pltpu.VMEM), out_shape),
        scratch_shapes=list(scratch),
        compiler_params=pltpu.CompilerParams(vmem_limit_bytes=VMEM),
        cost_estimate=pl.CostEstimate(flops=flops, bytes_accessed=bytes_accessed, transcendentals=0),
    )(*args)


FLIP = {"a": (1, 0, 3, 2), "b": (3, 2, 1, 0)}
AXES = {"z": ("tm", 16, 1), "y": ("tm", 16, 4), "x": ("fsdp", 8, 2)}


def swap(block, axis, step):
    name, size, stride = AXES[axis]
    route = []
    for i in range(size):
        place = (i // stride) % 4
        route.append((i, i + (FLIP[step][place] - place) * stride))
    return lax.ppermute(block, name, route)


def bit(axis, step):
    name, _, stride = AXES[axis]
    place = (lax.axis_index(name) // stride) % 4
    high, low = place // 2, place % 2
    return high ^ low if step == "a" else high


def pick(block, index, dim):
    return lax.dynamic_index_in_dim(block, index, dim, keepdims=False)


def halve(block, axis, step, dim):
    mine = bit(axis, step)
    arrived = swap(pick(block, 1 - mine, dim).astype(bf16), axis, step)
    return pick(block, mine, dim) + arrived.astype(f32)


def both(block, axis, step):
    sent = block.astype(bf16)
    return sent.astype(f32) + swap(sent, axis, step).astype(f32)


def double(block, axis, step, dim):
    other = swap(block, axis, step)
    mine = bit(axis, step)
    pair = jnp.stack([block, other], dim)
    flipped = jnp.stack([other, block], dim)
    return jnp.where(mine == 0, pair, flipped)


def all_sum(values):
    for axis, step in (("z", "a"), ("z", "b"), ("y", "a"), ("y", "b")):
        values = values + swap(values, axis, step)
    return values


def reduce_weight_grad(keep, send):
    arrived = lax.ppermute(send, "fsdp", [(i, i ^ 1) for i in range(8)])
    local = keep[: 4 * SHARD_PAD] + arrived[: 4 * SHARD_PAD].astype(f32)
    local = local.reshape(2, 2, 2, 2, 2, QUARTER, C)
    halves = []
    for half, axis in ((0, "z"), (1, "y")):
        left = local[:, :, half, :, :, :, : C // 2]
        right = local[:, :, half, :, :, :, C // 2 :]
        left = halve(left, axis, "a", 2)
        right = halve(right, axis, "b", 3)
        left = halve(left, axis, "b", 2)
        right = halve(right, axis, "a", 2)
        halves.append(jnp.concatenate([left, right], axis=-1))
    zs, ys = halves
    zs = halve(zs, "x", "a", 0)
    ys = halve(ys, "x", "b", 1)
    zs = halve(zs, "x", "b", 0)
    ys = halve(ys, "x", "a", 0)
    zs = both(both(zs, "y", "a"), "y", "b").astype(bf16)
    ys = both(both(ys, "z", "a"), "z", "b").astype(bf16)
    zs = double(double(zs, "z", "b", 0), "z", "a", 0)
    ys = double(double(ys, "y", "b", 0), "y", "a", 0)
    full = jnp.stack([zs, ys], 0).reshape(SHARD_PAD, C)
    return full[:SHARD].astype(f32)


def passed(block, distance):
    route = [(i - distance, i) for i in range(16) if 0 <= i - distance < 16]
    return lax.ppermute(block, "tm", route)


def per_device(clip, cotangent, weights):
    shape = clip.shape
    clip = clip.reshape(2, ROWS, C)
    cot = cotangent.reshape(2, ROWS, C)
    count = 32 * ROWS * (C // GROUPS)
    scale = 1.0 / math.sqrt(8 * 32 * ROWS)
    after = passed(cot[0], -1)
    before = passed(clip[1], 1)
    later = passed(cot[1], -1)
    full_weights = lax.all_gather(weights, "fsdp", axis=0, tiled=True)
    S = jax.ShapeDtypeStruct
    stats = call(stats_kernel, S((2, C), f32), (clip.reshape(2 * ROWS, C),))
    stats = all_sum(stats)
    where = jnp.stack([(lax.axis_index("tm") == 0).astype(jnp.int32), (lax.axis_index("fsdp") % 2).astype(jnp.int32)])


    keep, send = call(
        functools.partial(weight_grad_kernel, count, scale),
        (S((4 * SHARD_PAD + UNIT, C), f32), S((4 * SHARD_PAD + UNIT, C), bf16)),
        (where, stats, clip, before, cot, after),
        [pltpu.VMEM((3, C, ROWS), bf16), pltpu.VMEM((3, 3, PADDED, C), bf16)],
        flops=2 * 27 * C * C * 2 * ROWS,
        scalars=1,
    )
    grad_weight = reduce_weight_grad(keep, send)
    grad, sums = call(
        functools.partial(input_grad_kernel, count),
        (S((2, ROWS, C), f32), S((2, C), f32)),
        (stats, clip, cot, after, later, full_weights),
        [pltpu.VMEM((3, 4, PADDED, C), bf16)],
        flops=2 * 27 * C * C * 2 * ROWS,
    )
    sums = all_sum(sums)
    grad_input = call(
        functools.partial(final_kernel, count),
        S((2, ROWS, C), bf16),
        (stats, sums, clip, cot, grad),
    )
    return grad_input.reshape(shape), grad_weight


def solution(mesh):
    in_specs = (
        P("fsdp", "tm", None, None, None),
        P("fsdp", "tm", None, None, None),
        P("fsdp", None),
    )
    out_specs = (P("fsdp", "tm", None, None, None), P("fsdp", None))
    return jax.shard_map(
        per_device, mesh=mesh, in_specs=in_specs, out_specs=out_specs, check_vma=False
    )
```

time: 312 us -> 170 us (0.54)
  blocking collectives: 92.2 us -> 0 us
  local copies, waits for them, and re-layouts: 52.2 us -> 4.86 us
  waiting for transfers between devices: 100 us -> 56 us
  Pallas kernels: 0 us -> 42.6 us
  starting transfers between devices: 4.2 us -> 43.2 us
  other arithmetic: 27.5 us -> 7.14 us
  matrix products: 20.3 us -> 0 us
    psum x2 -> x0, blocking collectives: 92.2 us -> none  [the longest x1 53.8 us: per_device(): lax.psum((group_sums(values), group_sums(values * values)), 'tm')]
    psum x1 -> x0, waiting for transfers between devices: 83.4 us -> none  [per_device(): grad_weight = lax.psum(grad_part, 'tm').astype(jnp.float32)]
    pallas_call x0 -> x4, Pallas kernels: none -> 42.6 us  [call(): pl.pallas_call(kernel, out_shape=out_shape, in_specs=specs, out_specs=jax...]
    ppermute x2 -> x32, waiting for transfers between devices: 16 us -> 56 us  [the longest x28 53.5 us: swap(): return lax.ppermute(block, name, route)]
    ppermute x2 -> x32, starting transfers between devices: 4.08 us -> 43.2 us  [the longest x28 36 us: swap(): return lax.ppermute(block, name, route)]
    dot_general x18 -> x0, matrix products: 20.3 us -> none  [the longest x9 11.1 us: per_device(): jnp.dot(shifted, kernel, preferred_element_type=jnp.float32)]
    slice x5 -> x3, local copies, waits for them, and re-layouts: 22.9 us -> 2.82 us  [the longest x1 1.29 us: per_device(): later = passed(cot[1], -1)]
    transpose x9 -> x0, local copies, waits for them, and re-layouts: 15.5 us -> none  [per_device(): kernel = full_weights[row_start:row_start + 3 * channels].reshape(3, chan...]
  transfers between devices with their start and end apart: 5 -> 33, of which waited for: 2 -> 22; matrix products, arithmetic and copies ran while one was open for 11% -> 5% of each run, Pallas kernels for 0% -> 13%
where the time goes in v1:
time: 170 us; the launch traced here: 168 us
  waiting for transfers between devices  56 us (33%)
  starting transfers between devices  43.2 us (25%)
  Pallas kernels  42.6 us (25%)
  between operations  14.6 us (9%)
  other arithmetic  7.14 us (4%)
  local copies, waits for them, and re-layouts  4.86 us (3%)
    ppermute x28, waiting for transfers between devices, swap(): return lax.ppermute(block, name, route)  53.5 us
    pallas_call x4, Pallas kernels, call(): pl.pallas_call(kernel, out_shape=out_shape, in_specs=specs, out_specs=jax...  42.6 us
    ppermute x28, starting transfers between devices, swap(): return lax.ppermute(block, name, route)  36 us
    ppermute x3, starting transfers between devices, passed(): return lax.ppermute(block, 'tm', route)  7.15 us
  transfers between devices with their start and end apart: 33, of which 22 were waited for; matrix products, arithmetic and copies ran while one was open for 5% of the time, Pallas kernels for 13%

profile of v1, /device:TPU:6, one launch (start us, length us, event | category | flops | bytes accessed | tf_op | source)
XLA Modules:
  0.0 168.5 jit_solution(3091656907616520874)
XLA Ops:
  10.9 4.6 %collective-permute-start.10 = (bf16[1024,256]{1,0:T(8,128)(2,1)S(1)}, bf16[1024,256]{1,0:T(8,128)(2,1)S(1)}, u32[]{:S(2)}, u32[]{:S(2)}) collective-permute-start(bf16[1024,256]{1,0:T(8,128)(2,1)S(1)} %bitcast.97), channel_id=1, source_target_pairs={{0,8},{8,16},{16,24},{24,32},{32,40},{40,48},{48,56},{56,64},{64,7... | collective-permute-start | bytes 1572872 | tf_op jit(solution)/shard_map/ppermute | solution.py:274
  15.5 2.1 %shard_map.50 = f32[2,256]{1,0:T(2,128)} custom-call(bf16[2048,256]{1,0:T(8,128)(2,1)} %bitcast.88), custom_call_target="tpu_custom_call" | custom-call | bytes 4000000 | tf_op jit(solution)/shard_map/pallas_call | solution.py:186
  19.5 7.0 %collective-permute-done = f32[2,256]{1,0:T(2,128)S(1)} collective-permute-done((f32[2,256]{1,0:T(2,128)}, f32[2,256]{1,0:T(2,128)S(1)}, u32[]{:S(2)}, u32[]{:S(2)}) %collective-permute-start) | collective-permute-done | bytes 2080 | tf_op jit(solution)/shard_map/ppermute | solution.py:207
  27.2 4.7 %collective-permute-start.1 = (f32[2,256]{1,0:T(2,128)S(1)}, f32[2,256]{1,0:T(2,128)S(1)}, u32[]{:S(2)}, u32[]{:S(2)}) collective-permute-start(f32[2,256]{1,0:T(2,128)S(1)} %add.181), channel_id=1, source_target_pairs={{0,24},{8,16},{16,8},{24,0},{32,56},{40,48},{48,40},{56,32},{64,88... | collective-permute-start | bytes 6152 | tf_op jit(solution)/shard_map/ppermute | solution.py:207
  33.5 2.1 %collective-permute-start.2 = (f32[2,256]{1,0:T(2,128)S(1)}, f32[2,256]{1,0:T(2,128)S(1)}, u32[]{:S(2)}, u32[]{:S(2)}) collective-permute-start(f32[2,256]{1,0:T(2,128)S(1)} %add.182), channel_id=1, source_target_pairs={{0,32},{8,40},{16,48},{24,56},{32,0},{40,8},{48,16},{56,24},{64,96... | collective-permute-start | bytes 6152 | tf_op jit(solution)/shard_map/ppermute | solution.py:207
  37.2 3.8 %collective-permute-start.3 = (f32[2,256]{1,0:T(2,128)S(1)}, f32[2,256]{1,0:T(2,128)S(1)}, u32[]{:S(2)}, u32[]{:S(2)}) collective-permute-start(f32[2,256]{1,0:T(2,128)S(1)} %add.183), channel_id=1, source_target_pairs={{0,96},{8,104},{16,112},{24,120},{32,64},{40,72},{48,80},{56,88},{... | collective-permute-start | bytes 6152 | tf_op jit(solution)/shard_map/ppermute | solution.py:207
  44.0 16.8 %shard_map.53 = (f32[3616,256]{1,0:T(8,128)}, bf16[3616,256]{1,0:T(8,128)(2,1)}) custom-call(s32[2]{0:T(128)} %pad_add_fusion.where, f32[2,256]{1,0:T(2,128)} %add.184.stats, bf16[2,1024,256]{2,1,0:T(8,128)(2,1)} %bitcast.89, bf16[1024,256]{1,0:T(8,128)(2,1)} %copy-done.2, bf16[2,1024,256]{2,1,0:T(8,128)(2,1)} %bitcast.92, bf16[1024,256]{1,0:T(8,128)(2,1)} %copy-done), custom_call_target="tpu_custom_call" | custom-call | flops 7247757312 | bytes 4000000 | tf_op jit(solution)/shard_map/pallas_call | solution.py:186
  62.4 2.5 %collective-permute-done.11 = bf16[3616,256]{1,0:T(8,128)(2,1)S(1)} collective-permute-done((bf16[3616,256]{1,0:T(8,128)(2,1)}, bf16[3616,256]{1,0:T(8,128)(2,1)S(1)}, u32[]{:S(2)}, u32[]{:S(2)}) %collective-permute-start.11) | collective-permute-done | bytes 1851424 | tf_op jit(solution)/shard_map/ppermute | solution.py:247
  64.9 2.4 %convert_add_fusion = f32[3584,256]{1,0:T(8,128)S(1)} fusion(f32[3616,256]{1,0:T(8,128)} %get-tuple-element.8, bf16[3616,256]{1,0:T(8,128)(2,1)S(1)} %collective-permute-done.11), kind=kLoop, calls=%fused_computation | loop fusion | flops 1835008 | bytes 9175040 | tf_op jit(solution)/shard_map/add | solution.py:248
  67.8 2.3 %collective-permute-start.22 = (bf16[2,2,2,112,128]{4,3,1,0,2:T(8,128)(2,1)S(1)}, bf16[2,2,2,112,128]{4,3,1,0,2:T(8,128)(2,1)S(1)}, u32[]{:S(2)}, u32[]{:S(2)}) collective-permute-start(bf16[2,2,2,112,128]{4,3,1,0,2:T(8,128)(2,1)S(1)} %fusion.6), channel_id=1, source_target_pairs={{0,32},{8,40},{16,48},{24,56},{32,0},{40,8},{48,16},{56,24},{64,96... | collective-permute-start | bytes 688136 | tf_op jit(solution)/shard_map/ppermute | solution.py:207
  74.0 10.1 %collective-permute-done.22 = bf16[2,2,2,112,128]{4,3,1,0,2:T(8,128)(2,1)S(1)} collective-permute-done((bf16[2,2,2,112,128]{4,3,1,0,2:T(8,128)(2,1)S(1)}, bf16[2,2,2,112,128]{4,3,1,0,2:T(8,128)(2,1)S(1)}, u32[]{:S(2)}, u32[]{:S(2)}) %collective-permute-start.22) | collective-permute-done | bytes 229408 | tf_op jit(solution)/shard_map/ppermute | solution.py:207
  84.4 2.0 %collective-permute-start.25 = (bf16[2,2,112,128]{3,2,1,0:T(8,128)(2,1)S(1)}, bf16[2,2,112,128]{3,2,1,0:T(8,128)(2,1)S(1)}, u32[]{:S(2)}, u32[]{:S(2)}) collective-permute-start(bf16[2,2,112,128]{3,2,1,0:T(8,128)(2,1)S(1)} %fusion.20), channel_id=1, source_target_pairs={{0,32},{8,40},{16,48},{24,56},{32,0},{40,8},{48,16},{56,24},{64,96... | collective-permute-start | bytes 344072 | tf_op jit(solution)/shard_map/ppermute | solution.py:207
  86.7 3.6 %collective-permute-done.23 = bf16[2,2,112,128]{3,2,1,0:T(8,128)(2,1)S(1)} collective-permute-done((bf16[2,2,112,128]{3,2,1,0:T(8,128)(2,1)S(1)}, bf16[2,2,112,128]{3,2,1,0:T(8,128)(2,1)S(1)}, u32[]{:S(2)}, u32[]{:S(2)}) %collective-permute-start.23) | collective-permute-done | bytes 114720 | tf_op jit(solution)/shard_map/ppermute | solution.py:207
  93.5 3.0 %collective-permute-done.26 = bf16[2,112,256]{2,1,0:T(8,128)(2,1)S(1)} collective-permute-done((bf16[2,112,256]{2,1,0:T(8,128)(2,1)S(1)}, bf16[2,112,256]{2,1,0:T(8,128)(2,1)S(1)}, u32[]{:S(2)}, u32[]{:S(2)}) %collective-permute-start.26) | collective-permute-done | bytes 114720 | tf_op jit(solution)/shard_map/ppermute | solution.py:207
  100.9 2.4 %collective-permute-done.17 = bf16[112,256]{1,0:T(8,128)(2,1)S(1)} collective-permute-done((bf16[112,256]{1,0:T(8,128)(2,1)S(1)}, bf16[112,256]{1,0:T(8,128)(2,1)S(1)}, u32[]{:S(2)}, u32[]{:S(2)}) %collective-permute-start.17) | collective-permute-done | bytes 57376 | tf_op jit(solution)/shard_map/ppermute | solution.py:207
  105.5 2.1 %collective-permute-done.18 = bf16[112,256]{1,0:T(8,128)(2,1)S(1)} collective-permute-done((bf16[112,256]{1,0:T(8,128)(2,1)S(1)}, bf16[112,256]{1,0:T(8,128)(2,1)S(1)}, u32[]{:S(2)}, u32[]{:S(2)}) %collective-permute-start.18) | collective-permute-done | bytes 57376 | tf_op jit(solution)/shard_map/ppermute | solution.py:207
  110.6 2.1 %collective-permute-start.30 = (bf16[112,256]{1,0:T(8,128)(2,1)S(1)}, bf16[112,256]{1,0:T(8,128)(2,1)S(1)}, u32[]{:S(2)}, u32[]{:S(2)}) collective-permute-start(bf16[112,256]{1,0:T(8,128)(2,1)S(1)} %add_convert_fusion), channel_id=1, source_target_pairs={{0,96},{8,104},{16,112},{24,120},{32,64},{40,72},{48,80},{56,88},{... | collective-permute-start | bytes 172040 | tf_op jit(solution)/shard_map/ppermute | solution.py:207
  116.2 2.4 %collective-permute-done.20 = bf16[112,256]{1,0:T(8,128)(2,1)S(1)} collective-permute-done((bf16[112,256]{1,0:T(8,128)(2,1)S(1)}, bf16[112,256]{1,0:T(8,128)(2,1)S(1)}, u32[]{:S(2)}, u32[]{:S(2)}) %collective-permute-start.20) | collective-permute-done | bytes 57376 | tf_op jit(solution)/shard_map/ppermute | solution.py:207
  119.8 19.0 %shard_map.51 = (f32[2,1024,256]{2,1,0:T(8,128)}, f32[2,256]{1,0:T(2,128)}) custom-call(f32[2,256]{1,0:T(2,128)} %add.184.stats, bf16[2,1024,256]{2,1,0:T(8,128)(2,1)} %bitcast.90, bf16[2,1024,256]{2,1,0:T(8,128)(2,1)} %bitcast.93, bf16[1024,256]{1,0:T(8,128)(2,1)} %copy-done, bf16[1024,256]{1,0:T(8,128)(2,1)} %copy-done.1, ...), custom_call_target="tpu_custom_call" | custom-call | flops 7247757312 | bytes 4000000 | tf_op jit(solution)/shard_map/pallas_call | solution.py:186
  138.8 2.0 %collective-permute-start.6 = (f32[2,256]{1,0:T(2,128)}, f32[2,256]{1,0:T(2,128)S(1)}, u32[]{:S(2)}, u32[]{:S(2)}) collective-permute-start(f32[2,256]{1,0:T(2,128)} %get-tuple-element.6), channel_id=1, source_target_pairs={{0,8},{8,0},{16,24},{24,16},{32,40},{40,32},{48,56},{56,48},{64,72... | collective-permute-start | bytes 6152 | tf_op jit(solution)/shard_map/ppermute | solution.py:207
  145.1 2.9 %collective-permute-done.7 = f32[2,256]{1,0:T(2,128)S(1)} collective-permute-done((f32[2,256]{1,0:T(2,128)S(1)}, f32[2,256]{1,0:T(2,128)S(1)}, u32[]{:S(2)}, u32[]{:S(2)}) %collective-permute-start.7) | collective-permute-done | bytes 2080 | tf_op jit(solution)/shard_map/ppermute | solution.py:207
  148.1 3.5 %collective-permute-done.8 = f32[2,256]{1,0:T(2,128)S(1)} collective-permute-done((f32[2,256]{1,0:T(2,128)S(1)}, f32[2,256]{1,0:T(2,128)S(1)}, u32[]{:S(2)}, u32[]{:S(2)}) %collective-permute-start.8) | collective-permute-done | bytes 2080 | tf_op jit(solution)/shard_map/ppermute | solution.py:207
  154.3 2.2 %collective-permute-done.9 = f32[2,256]{1,0:T(2,128)S(1)} collective-permute-done((f32[2,256]{1,0:T(2,128)S(1)}, f32[2,256]{1,0:T(2,128)S(1)}, u32[]{:S(2)}, u32[]{:S(2)}) %collective-permute-start.9) | collective-permute-done | bytes 2080 | tf_op jit(solution)/shard_map/ppermute | solution.py:207
  157.1 4.6 %shard_map.52 = bf16[2,1024,256]{2,1,0:T(8,128)(2,1)} custom-call(f32[2,256]{1,0:T(2,128)} %add.184.stats, f32[2,256]{1,0:T(2,128)} %add.188.sums, bf16[2,1024,256]{2,1,0:T(8,128)(2,1)} %bitcast.91, bf16[2,1024,256]{2,1,0:T(8,128)(2,1)} %bitcast.94, f32[2,1024,256]{2,1,0:T(8,128)} %get-tuple-element.7.grad), custom_call_target="tpu_custom_call" | custom-call | bytes 4000000 | tf_op jit(solution)/shard_map/pallas_call | solution.py:186
  (103 shorter events, 43.4 us)
Async XLA Ops:
  7.2 111.8 %all-gather.2.cloned.1.call-start = ((), (), s32[]{:S(2)}) async-start(), calls=%async_computation | async-start | bytes 3981312 | tf_op jit(solution)/shard_map/all_gather | solution.py:286
  8.5 34.5 %collective-permute-start.4 = (bf16[1024,256]{1,0:T(8,128)(2,1)S(1)}, bf16[1024,256]{1,0:T(8,128)(2,1)S(1)}, u32[]{:S(2)}, u32[]{:S(2)}) collective-permute-start(bf16[1024,256]{1,0:T(8,128)(2,1)S(1)} %bitcast.99), channel_id=1, source_target_pairs={{8,0},{16,8},{24,16},{32,24},{40,32},{48,40},{56,48},{64,56},{72,6... | collective-permute-start | bytes 1572872 | tf_op jit(solution)/shard_map/ppermute | solution.py:274
  10.9 32.2 %collective-permute-start.10 = (bf16[1024,256]{1,0:T(8,128)(2,1)S(1)}, bf16[1024,256]{1,0:T(8,128)(2,1)S(1)}, u32[]{:S(2)}, u32[]{:S(2)}) collective-permute-start(bf16[1024,256]{1,0:T(8,128)(2,1)S(1)} %bitcast.97), channel_id=1, source_target_pairs={{0,8},{8,16},{16,24},{24,32},{32,40},{40,48},{48,56},{56,64},{64,7... | collective-permute-start | bytes 1572872 | tf_op jit(solution)/shard_map/ppermute | solution.py:274
  17.6 8.9 %collective-permute-start = (f32[2,256]{1,0:T(2,128)}, f32[2,256]{1,0:T(2,128)S(1)}, u32[]{:S(2)}, u32[]{:S(2)}) collective-permute-start(f32[2,256]{1,0:T(2,128)} %shard_map.50), channel_id=1, source_target_pairs={{0,8},{8,0},{16,24},{24,16},{32,40},{40,32},{48,56},{56,48},{64,72... | collective-permute-start | bytes 6152 | tf_op jit(solution)/shard_map/ppermute | solution.py:207
  27.2 6.3 %collective-permute-start.1 = (f32[2,256]{1,0:T(2,128)S(1)}, f32[2,256]{1,0:T(2,128)S(1)}, u32[]{:S(2)}, u32[]{:S(2)}) collective-permute-start(f32[2,256]{1,0:T(2,128)S(1)} %add.181), channel_id=1, source_target_pairs={{0,24},{8,16},{16,8},{24,0},{32,56},{40,48},{48,40},{56,32},{64,88... | collective-permute-start | bytes 6152 | tf_op jit(solution)/shard_map/ppermute | solution.py:207
  37.2 5.3 %collective-permute-start.3 = (f32[2,256]{1,0:T(2,128)S(1)}, f32[2,256]{1,0:T(2,128)S(1)}, u32[]{:S(2)}, u32[]{:S(2)}) collective-permute-start(f32[2,256]{1,0:T(2,128)S(1)} %add.183), channel_id=1, source_target_pairs={{0,96},{8,104},{16,112},{24,120},{32,64},{40,72},{48,80},{56,88},{... | collective-permute-start | bytes 6152 | tf_op jit(solution)/shard_map/ppermute | solution.py:207
  60.9 58.1 %collective-permute-start.5 = (bf16[1024,256]{1,0:T(8,128)(2,1)S(1)}, bf16[1024,256]{1,0:T(8,128)(2,1)S(1)}, u32[]{:S(2)}, u32[]{:S(2)}) collective-permute-start(bf16[1024,256]{1,0:T(8,128)(2,1)S(1)} %bitcast.98), channel_id=1, source_target_pairs={{8,0},{16,8},{24,16},{32,24},{40,32},{48,40},{56,48},{64,56},{72,6... | collective-permute-start | bytes 1572872 | tf_op jit(solution)/shard_map/ppermute | solution.py:274
  67.8 16.3 %collective-permute-start.22 = (bf16[2,2,2,112,128]{4,3,1,0,2:T(8,128)(2,1)S(1)}, bf16[2,2,2,112,128]{4,3,1,0,2:T(8,128)(2,1)S(1)}, u32[]{:S(2)}, u32[]{:S(2)}) collective-permute-start(bf16[2,2,2,112,128]{4,3,1,0,2:T(8,128)(2,1)S(1)} %fusion.6), channel_id=1, source_target_pairs={{0,32},{8,40},{16,48},{24,56},{32,0},{40,8},{48,16},{56,24},{64,96... | collective-permute-start | bytes 688136 | tf_op jit(solution)/shard_map/ppermute | solution.py:207
  70.1 14.2 %collective-permute-start.24 = (bf16[2,2,2,112,128]{4,3,2,1,0:T(8,128)(2,1)S(1)}, bf16[2,2,2,112,128]{4,3,2,1,0:T(8,128)(2,1)S(1)}, u32[]{:S(2)}, u32[]{:S(2)}) collective-permute-start(bf16[2,2,2,112,128]{4,3,2,1,0:T(8,128)(2,1)S(1)} %fusion.3), channel_id=1, source_target_pairs={{0,96},{8,104},{16,112},{24,120},{32,64},{40,72},{48,80},{56,88},{... | collective-permute-start | bytes 688136 | tf_op jit(solution)/shard_map/ppermute | solution.py:207
  71.3 15.1 %collective-permute-start.12 = (bf16[2,2,2,112,128]{4,3,1,0,2:T(8,128)(2,1)S(1)}, bf16[2,2,2,112,128]{4,3,1,0,2:T(8,128)(2,1)S(1)}, u32[]{:S(2)}, u32[]{:S(2)}) collective-permute-start(bf16[2,2,2,112,128]{4,3,1,0,2:T(8,128)(2,1)S(1)} %fusion.4), channel_id=1, source_target_pairs={{0,8},{8,0},{16,24},{24,16},{32,40},{40,32},{48,56},{56,48},{64,72... | collective-permute-start | bytes 688136 | tf_op jit(solution)/shard_map/ppermute | solution.py:207
  72.7 13.9 %collective-permute-start.14 = (bf16[2,2,2,112,128]{4,3,1,0,2:T(8,128)(2,1)S(1)}, bf16[2,2,2,112,128]{4,3,1,0,2:T(8,128)(2,1)S(1)}, u32[]{:S(2)}, u32[]{:S(2)}) collective-permute-start(bf16[2,2,2,112,128]{4,3,1,0,2:T(8,128)(2,1)S(1)} %fusion.5), channel_id=1, source_target_pairs={{0,24},{8,16},{16,8},{24,0},{32,56},{40,48},{48,40},{56,32},{64,88... | collective-permute-start | bytes 688136 | tf_op jit(solution)/shard_map/ppermute | solution.py:207
  84.2 6.2 %collective-permute-start.23 = (bf16[2,2,112,128]{3,2,1,0:T(8,128)(2,1)S(1)}, bf16[2,2,112,128]{3,2,1,0:T(8,128)(2,1)S(1)}, u32[]{:S(2)}, u32[]{:S(2)}) collective-permute-start(bf16[2,2,112,128]{3,2,1,0:T(8,128)(2,1)S(1)} %fusion.19), channel_id=1, source_target_pairs={{0,96},{8,104},{16,112},{24,120},{32,64},{40,72},{48,80},{56,88},{... | collective-permute-start | bytes 344072 | tf_op jit(solution)/shard_map/ppermute | solution.py:207
  84.4 6.0 %collective-permute-start.25 = (bf16[2,2,112,128]{3,2,1,0:T(8,128)(2,1)S(1)}, bf16[2,2,112,128]{3,2,1,0:T(8,128)(2,1)S(1)}, u32[]{:S(2)}, u32[]{:S(2)}) collective-permute-start(bf16[2,2,112,128]{3,2,1,0:T(8,128)(2,1)S(1)} %fusion.20), channel_id=1, source_target_pairs={{0,32},{8,40},{16,48},{24,56},{32,0},{40,8},{48,16},{56,24},{64,96... | collective-permute-start | bytes 344072 | tf_op jit(solution)/shard_map/ppermute | solution.py:207
  86.4 6.1 %collective-permute-start.13 = (bf16[2,2,112,128]{3,2,1,0:T(8,128)(2,1)S(1)}, bf16[2,2,112,128]{3,2,1,0:T(8,128)(2,1)S(1)}, u32[]{:S(2)}, u32[]{:S(2)}) collective-permute-start(bf16[2,2,112,128]{3,2,1,0:T(8,128)(2,1)S(1)} %fusion.17), channel_id=1, source_target_pairs={{0,24},{8,16},{16,8},{24,0},{32,56},{40,48},{48,40},{56,32},{64,88... | collective-permute-start | bytes 344072 | tf_op jit(solution)/shard_map/ppermute | solution.py:207
  86.6 5.9 %collective-permute-start.15 = (bf16[2,2,112,128]{3,2,1,0:T(8,128)(2,1)S(1)}, bf16[2,2,112,128]{3,2,1,0:T(8,128)(2,1)S(1)}, u32[]{:S(2)}, u32[]{:S(2)}) collective-permute-start(bf16[2,2,112,128]{3,2,1,0:T(8,128)(2,1)S(1)} %fusion.18), channel_id=1, source_target_pairs={{0,8},{8,0},{16,24},{24,16},{32,40},{40,32},{48,56},{56,48},{64,72... | collective-permute-start | bytes 344072 | tf_op jit(solution)/shard_map/ppermute | solution.py:207
  90.4 6.1 %collective-permute-start.26 = (bf16[2,112,256]{2,1,0:T(8,128)(2,1)S(1)}, bf16[2,112,256]{2,1,0:T(8,128)(2,1)S(1)}, u32[]{:S(2)}, u32[]{:S(2)}) collective-permute-start(bf16[2,112,256]{2,1,0:T(8,128)(2,1)S(1)} %fusion.22), channel_id=1, source_target_pairs={{0,6},{1,7},{2,4},{3,5},{4,2},{5,3},{6,0},{7,1},{8,14},{9,15},{10,... | collective-permute-start | bytes 344072 | tf_op jit(solution)/shard_map/ppermute | solution.py:207
  92.6 5.2 %collective-permute-start.16 = (bf16[2,112,256]{2,1,0:T(8,128)(2,1)S(1)}, bf16[2,112,256]{2,1,0:T(8,128)(2,1)S(1)}, u32[]{:S(2)}, u32[]{:S(2)}) collective-permute-start(bf16[2,112,256]{2,1,0:T(8,128)(2,1)S(1)} %fusion.21), channel_id=1, source_target_pairs={{0,2},{1,3},{2,0},{3,1},{4,6},{5,7},{6,4},{7,5},{8,10},{9,11},{10,... | collective-permute-start | bytes 344072 | tf_op jit(solution)/shard_map/ppermute | solution.py:207
  97.9 5.5 %collective-permute-start.17 = (bf16[112,256]{1,0:T(8,128)(2,1)S(1)}, bf16[112,256]{1,0:T(8,128)(2,1)S(1)}, u32[]{:S(2)}, u32[]{:S(2)}) collective-permute-start(bf16[112,256]{1,0:T(8,128)(2,1)S(1)} %fusion.27), channel_id=1, source_target_pairs={{0,6},{1,7},{2,4},{3,5},{4,2},{5,3},{6,0},{7,1},{8,14},{9,15},{10,... | collective-permute-start | bytes 172040 | tf_op jit(solution)/shard_map/ppermute | solution.py:207
  105.1 5.5 %collective-permute-start.29 = (bf16[112,256]{1,0:T(8,128)(2,1)S(1)}, bf16[112,256]{1,0:T(8,128)(2,1)S(1)}, u32[]{:S(2)}, u32[]{:S(2)}) collective-permute-start(bf16[112,256]{1,0:T(8,128)(2,1)S(1)} %add_convert_fusion.1), channel_id=1, source_target_pairs={{0,24},{8,16},{16,8},{24,0},{32,56},{40,48},{48,40},{56,32},{64,88... | collective-permute-start | bytes 172040 | tf_op jit(solution)/shard_map/ppermute | solution.py:207
  107.7 5.5 %collective-permute-start.19 = (bf16[112,256]{1,0:T(8,128)(2,1)S(1)}, bf16[112,256]{1,0:T(8,128)(2,1)S(1)}, u32[]{:S(2)}, u32[]{:S(2)}) collective-permute-start(bf16[112,256]{1,0:T(8,128)(2,1)S(1)} %add_convert_fusion.3), channel_id=1, source_target_pairs={{0,96},{8,104},{16,112},{24,120},{32,64},{40,72},{48,80},{56,88},{... | collective-permute-start | bytes 172040 | tf_op jit(solution)/shard_map/ppermute | solution.py:207
  110.6 5.5 %collective-permute-start.30 = (bf16[112,256]{1,0:T(8,128)(2,1)S(1)}, bf16[112,256]{1,0:T(8,128)(2,1)S(1)}, u32[]{:S(2)}, u32[]{:S(2)}) collective-permute-start(bf16[112,256]{1,0:T(8,128)(2,1)S(1)} %add_convert_fusion), channel_id=1, source_target_pairs={{0,96},{8,104},{16,112},{24,120},{32,64},{40,72},{48,80},{56,88},{... | collective-permute-start | bytes 172040 | tf_op jit(solution)/shard_map/ppermute | solution.py:207
  113.1 5.5 %collective-permute-start.20 = (bf16[112,256]{1,0:T(8,128)(2,1)S(1)}, bf16[112,256]{1,0:T(8,128)(2,1)S(1)}, u32[]{:S(2)}, u32[]{:S(2)}) collective-permute-start(bf16[112,256]{1,0:T(8,128)(2,1)S(1)} %add_convert_fusion.2), channel_id=1, source_target_pairs={{0,24},{8,16},{16,8},{24,0},{32,56},{40,48},{48,40},{56,32},{64,88... | collective-permute-start | bytes 172040 | tf_op jit(solution)/shard_map/ppermute | solution.py:207
  116.1 24.7 %collective-permute-start.31 = (bf16[2,112,256]{2,1,0:T(8,128)(2,1)S(1)}, bf16[2,112,256]{2,1,0:T(8,128)(2,1)S(1)}, u32[]{:S(2)}, u32[]{:S(2)}) collective-permute-start(bf16[2,112,256]{2,1,0:T(8,128)(2,1)S(1)} %maximum_select_fusion.5), channel_id=1, source_target_pairs={{0,32},{8,40},{16,48},{24,56},{32,0},{40,8},{48,16},{56,24},{64,96... | collective-permute-start | bytes 344072 | tf_op jit(solution)/shard_map/ppermute | solution.py:207
  118.6 26.5 %collective-permute-start.21 = (bf16[2,112,256]{2,1,0:T(8,128)(2,1)S(1)}, bf16[2,112,256]{2,1,0:T(8,128)(2,1)S(1)}, u32[]{:S(2)}, u32[]{:S(2)}) collective-permute-start(bf16[2,112,256]{2,1,0:T(8,128)(2,1)S(1)} %maximum_select_fusion.3), channel_id=1, source_target_pairs={{0,8},{8,0},{16,24},{24,16},{32,40},{40,32},{48,56},{56,48},{64,72... | collective-permute-start | bytes 344072 | tf_op jit(solution)/shard_map/ppermute | solution.py:207
  (12 other events, 40.0 us)
Sparse Core Ops, SparseCore 0:
  62.3 30.0 all-gather.1

commit v2 on v1

v2 whole, which is shorter than its diff:
```python
import functools
import math

import jax
import jax.numpy as jnp
from jax import lax
from jax.experimental import pallas as pl
from jax.experimental.pallas import tpu as pltpu
from jax.sharding import PartitionSpec as P

GROUPS = 32
C = 256
H = 16
W = 64
ROWS = H * W
PADDED = ROWS + 2 * W
HALF = C // 2
SHARD = 864
SHARD_PAD = 896
QUARTER = 224
UNIT = 32
VMEM = 28 * 1024 * 1024
epsilon = 1e-06
f32 = jnp.float32
bf16 = jnp.bfloat16


def group_total(rows):
    lane = lax.broadcasted_iota(jnp.int32, rows.shape, 1)
    for s in (1, 2, 4):
        up = pltpu.roll(rows, s, 1)
        down = pltpu.roll(rows, C - s, 1)
        rows = rows + jnp.where((lane & s) != 0, up, down)
    return rows


def center_inverse(stats, count):
    sums = group_total(stats) / count
    center = sums[0:1]
    spread = sums[1:2] - center * center
    return center, lax.rsqrt(spread + epsilon)


def sigmoid(v):
    return 1.0 / (1.0 + jnp.exp(-v))


def widths(target, cot, slot):
    zero = jnp.zeros((W, C), bf16)
    for kw in range(3):
        target[kw, slot, 0:W] = zero
        target[kw, slot, W + ROWS : PADDED] = zero
    column = lax.broadcasted_iota(jnp.int32, (W, C), 0)

    @pl.loop(0, H)
    def _(h):
        row = cot(pl.multiple_of(h * W, W))
        at = pl.ds(pl.multiple_of(h * W + W, W), W)
        wide = row.astype(f32)
        target[1, slot, at] = row
        target[0, slot, at] = jnp.where(column == W - 1, 0.0, pltpu.roll(wide, W - 1, 0)).astype(bf16)
        target[2, slot, at] = jnp.where(column == 0, 0.0, pltpu.roll(wide, 1, 0)).astype(bf16)


def stats_kernel(clip, out):
    def step(i, carry):
        a, b = carry
        v = clip[pl.ds(pl.multiple_of(i * 128, 128), 128)].astype(f32)
        v = v.reshape(16, 8, C)
        return a + v.sum(0), b + (v * v).sum(0)

    zero = jnp.zeros((8, C), f32)
    a, b = lax.fori_loop(0, clip.shape[0] // 128, step, (zero, zero))
    out[0:1] = a.sum(0, keepdims=True)
    out[1:2] = b.sum(0, keepdims=True)


def widths_kernel(cot, wide):
    for t in range(cot.shape[0]):
        widths(wide, lambda r, t=t: cot[t, pl.ds(r, W)], t)


def tap_rows(kh):
    return pl.ds(pl.multiple_of((2 - kh) * W, W), ROWS)


CONTRACT_ROWS = (((0,), (0,)), ((), ()))
CONTRACT_COLUMNS = (((1,), (1,)), ((), ()))


def tap_product(frames, views, channels):
    total = None
    for frame, view in zip(frames, views):
        part = lax.dot_general(frame[:, channels], view, CONTRACT_ROWS, preferred_element_type=f32)
        total = part if total is None else total + part
    return total


def store_tap(tap, total, first_unit, core, keep, send):
    spare = 2 * SHARD_PAD
    for u in range(total.shape[0] // UNIT):
        unit = tap * (C // UNIT) + first_unit + u
        shard = unit // (SHARD // UNIT)
        dest = (shard // 2 % 2) * SHARD_PAD + (unit - shard * (SHARD // UNIT)) * UNIT
        mine = (shard % 2) == core
        piece = total[u * UNIT : (u + 1) * UNIT]
        keep[pl.ds(pl.multiple_of(jnp.where(mine, dest, spare), UNIT), UNIT)] = piece
        send[pl.ds(pl.multiple_of(jnp.where(mine, spare, dest), UNIT), UNIT)] = piece.astype(bf16)


def clear_tails(keep, send):
    for place in range(2):
        tail = slice(place * SHARD_PAD + SHARD, (place + 1) * SHARD_PAD)
        keep[tail] = jnp.zeros((SHARD_PAD - SHARD, C), f32)
        send[tail] = jnp.zeros((SHARD_PAD - SHARD, C), bf16)
    keep[2 * SHARD_PAD :] = jnp.zeros((UNIT, C), f32)
    send[2 * SHARD_PAD :] = jnp.zeros((UNIT, C), bf16)


def upper_kernel(count, scale, where, stats, clip, before, near, after, act, keep, send):
    center, inverse = center_inverse(stats[...], count)
    core = where[1]

    def activate(frame, slot, gain):
        @pl.loop(0, ROWS // 64)
        def _(i):
            at = pl.ds(pl.multiple_of(i * 64, 64), 64)
            v = (frame(at).astype(f32) - center) * inverse
            v = v * sigmoid(v)
            if gain is not None:
                v = v * gain
            act[slot, at] = v.astype(bf16)

    activate(lambda at: before[at], 0, jnp.where(where[0] == 1, 0.0, 1.0))
    activate(lambda at: clip[0, at], 1, None)
    activate(lambda at: clip[1, at], 2, None)

    @pl.loop(0, 9)
    def _(t):
        rows = tap_rows(t // 3)
        kw = t % 3
        total = tap_product((act[1], act[2]), (near[kw, 0, rows], near[kw, 1, rows]), slice(None))
        store_tap(18 + t, total * scale, 0, core, keep, send)

    @pl.loop(5, 9)
    def _(t):
        rows = tap_rows(t // 3)
        kw = t % 3
        total = tap_product((act[1], act[2]), (near[kw, 1, rows], after[kw, 0, rows]), slice(None))
        store_tap(9 + t, total * scale, 0, core, keep, send)

    rows = slice(W, W + ROWS)
    total = tap_product((act[1], act[2]), (near[1, 1, rows], after[1, 0, rows]), slice(HALF, C))
    store_tap(13, total * scale, HALF // UNIT, core, keep, send)
    clear_tails(keep, send)


def lower_kernel(scale, where, act, near, after, keep, send):
    core = where[1]

    @pl.loop(0, 9)
    def _(t):
        rows = tap_rows(t // 3)
        kw = t % 3
        total = tap_product((act[0], act[1]), (near[kw, 1, rows], after[kw, 0, rows]), slice(None))
        store_tap(t, total * scale, 0, core, keep, send)

    @pl.loop(0, 4)
    def _(t):
        rows = tap_rows(t // 3)
        kw = t % 3
        total = tap_product((act[1], act[2]), (near[kw, 1, rows], after[kw, 0, rows]), slice(None))
        store_tap(9 + t, total * scale, 0, core, keep, send)

    rows = slice(W, W + ROWS)
    total = tap_product((act[1], act[2]), (near[1, 1, rows], after[1, 0, rows]), slice(0, HALF))
    store_tap(13, total * scale, 0, core, keep, send)
    clear_tails(keep, send)


def pack_kernel(where, own, left, right, far, packed):
    x = where[2]
    for block, distance in ((own, 0), (left, 3), (right, 1), (far, 2)):
        packed[(x + distance) % 4] = block[...]


def frame_grad(count, frame, stats, clip, views, weights, grad, sums):
    center, inverse = center_inverse(stats[...], count)
    rows_per = 256

    @pl.loop(0, ROWS // rows_per)
    def _(i):
        start = i * rows_per
        total = jnp.zeros((rows_per, C), f32)
        for tap in range(27):
            kt, kh, kw = tap // 9, tap // 3 % 3, tap % 3
            rows = pl.ds(pl.multiple_of((2 - kh) * W + start, W), rows_per)
            w = weights[tap * C : (tap + 1) * C]
            total += lax.dot_general(
                views[2 - kt](kw, rows), w, CONTRACT_COLUMNS, preferred_element_type=f32
            )
        grad[pl.ds(pl.multiple_of(start, rows_per), rows_per)] = total

    zero = jnp.zeros((8, C), f32)

    def finish(i, carry):
        a, b = carry
        at = pl.ds(pl.multiple_of(i * 64, 64), 64)
        v = (clip[frame, at].astype(f32) - center) * inverse
        s = sigmoid(v)
        g = grad[at] * (s * (1.0 + v * (1.0 - s)))
        grad[at] = g
        return a + g.reshape(8, 8, C).sum(0), b + (g * v).reshape(8, 8, C).sum(0)

    a, b = lax.fori_loop(0, ROWS // 64, finish, (zero, zero))
    sums[0:1] = a.sum(0, keepdims=True)
    sums[1:2] = b.sum(0, keepdims=True)


def first_grad_kernel(count, where, stats, clip, near, after, mine, other, order, grad, sums, full):
    core = where[1]
    for x in range(4):
        full[pl.ds(pl.multiple_of((2 * x + core) * SHARD, UNIT), SHARD)] = mine[x]
        full[pl.ds(pl.multiple_of((2 * x + 1 - core) * SHARD, UNIT), SHARD)] = other[x]
    views = (
        lambda kw, rows: near[kw, 0, rows],
        lambda kw, rows: near[kw, 1, rows],
        lambda kw, rows: after[kw, 0, rows],
    )
    frame_grad(count, 0, stats, clip, views, full, grad, sums)


def second_grad_kernel(count, stats, clip, near, after, later, full, order, grad, sums, wide):
    widths(wide, lambda r: later[pl.ds(r, W)], 0)
    views = (
        lambda kw, rows: near[kw, 1, rows],
        lambda kw, rows: after[kw, 0, rows],
        lambda kw, rows: wide[kw, 0, rows],
    )
    frame_grad(count, 1, stats, clip, views, full, grad, sums)


def final_kernel(count, stats, sums, clip, cot, grad0, grad1, out):
    center, inverse = center_inverse(stats[...], count)
    means = group_total(sums[...]) / count
    total, cross = means[0:1], means[1:2]
    for frame, grad in enumerate((grad0, grad1)):

        @pl.loop(0, ROWS // 64)
        def _(i, frame=frame, grad=grad):
            at = pl.ds(pl.multiple_of(i * 64, 64), 64)
            v = (clip[frame, at].astype(f32) - center) * inverse
            g = cot[frame, at].astype(f32) + inverse * (grad[at] - total - v * cross)
            out[frame, at] = g.astype(bf16)


def split_core_kernel(where, keep_up, keep_low, got_up, got_low, order, left, right, left_out, right_out):
    a, b = where[3], where[4]
    places = ((keep_low, got_low, 0), (keep_up, got_up, 1), (keep_low, got_low, 1), (keep_up, got_up, 0))
    for place, (keep, got, x) in enumerate(places):

        def block(quarter, columns):
            at = pl.ds(pl.multiple_of(x * SHARD_PAD + quarter * QUARTER, UNIT), QUARTER)
            return keep[at, columns] + got[at, columns].astype(f32)

        for i in range(2):
            left[place, i] = block(2 * a + i, slice(0, HALF))
            left_out[place, i] = block(2 * (1 - a) + i, slice(0, HALF)).astype(bf16)
            right[place, i] = block(2 * i + b, slice(HALF, C))
            right_out[place, i] = block(2 * i + 1 - b, slice(HALF, C)).astype(bf16)


def split_z_kernel(where, left, right, left_in, right_in, order, left_next, right_next, left_out, right_out):
    for place in range(4):
        for held, got, keep, out, mine in (
            (left, left_in, left_next, left_out, where[4]),
            (right, right_in, right_next, right_out, where[3]),
        ):
            keep[place] = held[place, mine] + got[place, mine].astype(f32)
            out[place] = (held[place, 1 - mine] + got[place, 1 - mine].astype(f32)).astype(bf16)


def split_x_kernel(where, left, right, left_in, right_in, left_next, right_next, left_out, right_out):
    a, b = where[5], where[6]
    for i in range(2):
        for held, got, keep, out, mine, its in (
            (left, left_in, left_next, left_out, 2 * a + i, 2 * (1 - a) + i),
            (right, right_in, right_next, right_out, 2 * i + b, 2 * i + 1 - b),
        ):
            keep[i] = held[mine] + got[mine].astype(f32)
            out[i] = (held[its] + got[its].astype(f32)).astype(bf16)


def split_last_kernel(where, left, right, left_in, right_in, left_next, right_next, left_out, right_out):
    for held, got, keep, out, mine in (
        (left, left_in, left_next, left_out, where[6]),
        (right, right_in, right_next, right_out, where[5]),
    ):
        keep[...] = held[mine] + got[mine].astype(f32)
        out[...] = (held[1 - mine] + got[1 - mine].astype(f32)).astype(bf16)


def write_sums(sums, rows, out):
    rows[12:16] = jnp.zeros((4, HALF), f32)
    rest = sums
    for k in range(3):
        term = rest.astype(bf16).astype(f32)
        rest = rest - term
        rows[4 * k : 4 * k + 2] = term[:, :HALF]
        rows[4 * k + 2 : 4 * k + 4] = term[:, HALF:]
    out[...] = rows[...].astype(bf16)


def read_sums(block):
    wide = block.astype(f32)
    total = wide[0:4] + wide[4:8] + wide[8:12]
    return jnp.concatenate([total[0:2], total[2:4]], axis=1)


def start_sum_kernel(left, right, left_in, right_in, sums0, sums1, left_out, right_out, rows):
    left_out[:QUARTER] = (left[...] + left_in[...].astype(f32)).astype(bf16)
    right_out[...] = (right[...] + right_in[...].astype(f32)).astype(bf16)
    write_sums(sums0[...] + sums1[...], rows, left_out.at[QUARTER:])


def next_sum_kernel(left, right, left_in, right_in, left_out, right_out, rows):
    at = slice(0, QUARTER)
    left_out[at] = (left[at].astype(f32) + left_in[at].astype(f32)).astype(bf16)
    right_out[...] = (right[...].astype(f32) + right_in[...].astype(f32)).astype(bf16)
    total = read_sums(left[QUARTER:]) + read_sums(left_in[QUARTER:])
    write_sums(total, rows, left_out.at[QUARTER:])


def join_kernel(where, left, right, left_in, right_in, left_out, right_out, rows):
    a, b = where[3], where[4]
    left_out[pl.ds(pl.multiple_of(b * QUARTER, UNIT), QUARTER)] = left[:QUARTER]
    left_out[pl.ds(pl.multiple_of((1 - b) * QUARTER, UNIT), QUARTER)] = left_in[:QUARTER]
    right_out[pl.ds(pl.multiple_of(a * QUARTER, UNIT), QUARTER)] = right[...]
    right_out[pl.ds(pl.multiple_of((1 - a) * QUARTER, UNIT), QUARTER)] = right_in[...]
    total = read_sums(left[QUARTER:]) + read_sums(left_in[QUARTER:])
    write_sums(total, rows, left_out.at[2 * QUARTER :])


def finish_kernel(where, left, right, left_in, right_in, grad_weight, sums, full):
    a, b = where[3], where[4]
    for i in range(2):
        held = slice(i * QUARTER, (i + 1) * QUARTER)
        for block, quarter in ((left, 2 * a + i), (left_in, 2 * (1 - a) + i)):
            at = pl.ds(pl.multiple_of(quarter * QUARTER, UNIT), QUARTER)
            full[at, :HALF] = block[held].astype(f32)
        for block, quarter in ((right, 2 * i + b), (right_in, 2 * i + 1 - b)):
            at = pl.ds(pl.multiple_of(quarter * QUARTER, UNIT), QUARTER)
            full[at, HALF:] = block[held].astype(f32)
    grad_weight[...] = full[:SHARD]
    sums[...] = read_sums(left[2 * QUARTER :]) + read_sums(left_in[2 * QUARTER :])


def call(kernel, out_shape, args, scratch=(), flops=0, bytes_accessed=1_000_000, scalars=0, order=()):
    specs = [pl.BlockSpec(memory_space=pltpu.SMEM)] * scalars
    specs += [pl.BlockSpec(memory_space=pltpu.VMEM)] * (len(args) - scalars)
    specs += [pl.BlockSpec(memory_space=pl.ANY)] * len(order)
    return pl.pallas_call(
        kernel,
        out_shape=out_shape,
        in_specs=specs,
        out_specs=jax.tree.map(lambda _: pl.BlockSpec(memory_space=pltpu.VMEM), out_shape),
        scratch_shapes=list(scratch),
        compiler_params=pltpu.CompilerParams(vmem_limit_bytes=VMEM),
        cost_estimate=pl.CostEstimate(flops=flops, bytes_accessed=bytes_accessed, transcendentals=0),
    )(*args, *order)


FLIP = {"a": (1, 0, 3, 2), "b": (3, 2, 1, 0), "left": (1, 2, 3, 0), "right": (3, 0, 1, 2), "far": (2, 3, 0, 1)}
AXES = {"z": ("tm", 16, 1), "y": ("tm", 16, 4), "x": ("fsdp", 8, 2)}


def swap(block, axis, step):
    name, size, stride = AXES[axis]
    route = []
    for i in range(size):
        place = (i // stride) % 4
        route.append((i, i + (FLIP[step][place] - place) * stride))
    return lax.ppermute(block, name, route)


def swap_core(block):
    return lax.ppermute(block, "fsdp", [(i, i ^ 1) for i in range(8)])


def all_sum(values):
    for axis, step in (("y", "a"), ("y", "b"), ("z", "a"), ("z", "b")):
        values = values + swap(values, axis, step)
    return values


def passed(block, distance):
    route = [(i - distance, i) for i in range(16) if 0 <= i - distance < 16]
    return lax.ppermute(block, "tm", route)


def per_device(clip, cotangent, weights):
    shape = clip.shape
    clip = clip.reshape(2, ROWS, C)
    cot = cotangent.reshape(2, ROWS, C)
    count = 32 * ROWS * (C // GROUPS)
    scale = 1.0 / math.sqrt(8 * 32 * ROWS)
    partial = functools.partial
    S = jax.ShapeDtypeStruct
    tm = lax.axis_index("tm")
    fsdp = lax.axis_index("fsdp")
    z, x = tm % 4, fsdp // 2
    where = [tm == 0, fsdp % 2, x, z // 2 ^ z % 2, z // 2, x // 2 ^ x % 2, x // 2]
    where = jnp.stack([jnp.asarray(v, jnp.int32) for v in where])

    after = passed(cot[0], -1)
    before = passed(clip[1], 1)
    later = passed(cot[1], -1)
    mine = call(
        pack_kernel,
        S((4, SHARD, C), bf16),
        (where, weights, swap(weights, "x", "left"), swap(weights, "x", "right"), swap(weights, "x", "far")),
        scalars=1,
    )
    other = swap_core(mine)
    stats = call(stats_kernel, S((2, C), f32), (clip.reshape(2 * ROWS, C),))
    stats = all_sum(stats)
    near = call(widths_kernel, S((3, 2, PADDED, C), bf16), (cot,))
    after = call(widths_kernel, S((3, 1, PADDED, C), bf16), (after[None],))

    rows = 2 * SHARD_PAD + UNIT
    half_flops = 27 * C * C * 2 * ROWS
    act, keep_up, send_up = call(
        partial(upper_kernel, count, scale),
        (S((3, ROWS, C), bf16), S((rows, C), f32), S((rows, C), bf16)),
        (where, stats, clip, before, near, after),
        flops=half_flops,
        scalars=1,
    )
    got_up = swap_core(send_up)
    keep_low, send_low = call(
        partial(lower_kernel, scale),
        (S((rows, C), f32), S((rows, C), bf16)),
        (where, act, near, after),
        flops=half_flops,
        scalars=1,
    )
    got_low = swap_core(send_low)
    grad0, sums0, full = call(
        partial(first_grad_kernel, count),
        (S((ROWS, C), f32), S((2, C), f32), S((8 * SHARD, C), bf16)),
        (where, stats, clip, near, after, mine, other),
        flops=half_flops,
        scalars=1,
        order=(keep_low,),
    )

    block = lambda *dims: (S(dims + (QUARTER, HALF), f32),) * 2 + (S(dims + (QUARTER, HALF), bf16),) * 2
    left, right, left_out, right_out = call(
        split_core_kernel, block(4, 2), (where, keep_up, keep_low, got_up, got_low), scalars=1, order=(sums0,)
    )
    grad1, sums1 = call(
        partial(second_grad_kernel, count),
        (S((ROWS, C), f32), S((2, C), f32)),
        (stats, clip, near, after, later, full),
        [pltpu.VMEM((3, 1, PADDED, C), bf16)],
        flops=half_flops,
        order=(left_out,),
    )
    got = swap(left_out, "z", "a"), swap(right_out, "z", "b")
    left, right, left_out, right_out = call(
        split_z_kernel, block(4), (where, left, right, *got), scalars=1, order=(sums1,)
    )
    got = swap(left_out, "z", "b"), swap(right_out, "z", "a")
    left, right, left_out, right_out = call(split_x_kernel, block(2), (where, left, right, *got), scalars=1)
    got = swap(left_out, "x", "a"), swap(right_out, "x", "b")
    left, right, left_out, right_out = call(split_last_kernel, block(), (where, left, right, *got), scalars=1)
    got = swap(left_out, "x", "b"), swap(right_out, "x", "a")

    pair = lambda n: (S((n * QUARTER + 16, HALF), bf16), S((n * QUARTER, HALF), bf16))
    rows16 = [pltpu.VMEM((16, HALF), f32)]
    left, right = call(start_sum_kernel, pair(1), (left, right, *got, sums0, sums1), rows16)
    got = swap(left, "y", "a"), swap(right, "y", "b")
    left, right = call(next_sum_kernel, pair(1), (left, right, *got), rows16)
    got = swap(left, "y", "b"), swap(right, "y", "a")
    left, right = call(next_sum_kernel, pair(1), (left, right, *got), rows16)
    got = swap(left, "z", "b"), swap(right, "z", "a")
    left, right = call(join_kernel, pair(2), (where, left, right, *got), rows16, scalars=1)
    got = swap(left, "z", "a"), swap(right, "z", "b")
    grad_weight, sums = call(
        finish_kernel,
        (S((SHARD, C), f32), S((2, C), f32)),
        (where, left, right, *got),
        [pltpu.VMEM((SHARD_PAD, C), f32)],
        scalars=1,
    )
    grad_input = call(
        partial(final_kernel, count), S((2, ROWS, C), bf16), (stats, sums, clip, cot, grad0, grad1)
    )
    return grad_input.reshape(shape), grad_weight


def solution(mesh):
    in_specs = (
        P("fsdp", "tm", None, None, None),
        P("fsdp", "tm", None, None, None),
        P("fsdp", None),
    )
    out_specs = (P("fsdp", "tm", None, None, None), P("fsdp", None))
    return jax.shard_map(
        per_device, mesh=mesh, in_specs=in_specs, out_specs=out_specs, check_vma=False
    )
```

time: 170 us -> 145 us (0.85)
  between operations: 14.6 us -> 0.84 us
  other arithmetic: 7.14 us -> 0.01 us
  Pallas kernels: 42.6 us -> 38.4 us
    ppermute x3, waiting for transfers between devices: 0.01 us -> 4.32 us  [passed(): return lax.ppermute(block, 'tm', route)]
    pallas_call x4 -> x18, Pallas kernels: 42.6 us -> 38.4 us  [call(): pl.pallas_call(kernel, out_shape=out_shape, in_specs=specs, out_specs=jax...]
    add x11 -> x0, other arithmetic: 2.71 us -> none  [the longest x1 2.39 us: reduce_weight_grad(): local = keep[:4 * SHARD_PAD] + arrived[:4 * SHARD_PAD].astype(f32)]
    add x8 -> x4, other arithmetic: 2.51 us -> 0.01 us  [all_sum(): values = values + swap(values, axis, step)]
    ppermute x1 -> x3, waiting for transfers between devices: 2.5 us -> 0.01 us  [swap_core(): return lax.ppermute(block, 'fsdp', [(i, i ^ 1) for i in range(8)])]
    ppermute x28 -> x23, waiting for transfers between devices: 53.5 us -> 52.2 us  [swap(): return lax.ppermute(block, name, route)]
    ppermute x28 -> x23, starting transfers between devices: 36 us -> 35.7 us  [swap(): return lax.ppermute(block, name, route)]
  transfers between devices with their start and end apart: 33 -> 29, of which waited for: 22 -> 17; matrix products, arithmetic and copies ran while one was open for 5% -> 2% of each run, Pallas kernels for 13% -> 22%
where the time goes in v2:
time: 145 us; the launch traced here: 143 us
  waiting for transfers between devices  56.5 us (39%)
  starting transfers between devices  44.3 us (31%)
  Pallas kernels  38.4 us (26%)
  local copies, waits for them, and re-layouts  3.25 us (2%)
    ppermute x23, waiting for transfers between devices, swap(): return lax.ppermute(block, name, route)  52.2 us
    pallas_call x18, Pallas kernels, call(): pl.pallas_call(kernel, out_shape=out_shape, in_specs=specs, out_specs=jax...  38.4 us
    ppermute x23, starting transfers between devices, swap(): return lax.ppermute(block, name, route)  35.7 us
    ppermute x3, starting transfers between devices, passed(): return lax.ppermute(block, 'tm', route)  7.91 us
    ppermute x3, waiting for transfers between devices, passed(): return lax.ppermute(block, 'tm', route)  4.32 us
  transfers between devices with their start and end apart: 29, of which 17 were waited for; matrix products, arithmetic and copies ran while one was open for 2% of the time, Pallas kernels for 22%

profile of v2, /device:TPU:6, one launch (start us, length us, event | category | flops | bytes accessed | tf_op | source)
XLA Modules:
  0.0 143.3 jit_solution(10672404362584298062)
XLA Ops:
  1.5 2.4 %collective-permute-start.8 = (bf16[864,256]{1,0:T(8,128)(2,1)}, bf16[864,256]{1,0:T(8,128)(2,1)S(1)}, u32[]{:S(2)}, u32[]{:S(2)}) collective-permute-start(bf16[864,256]{1,0:T(8,128)(2,1)} %own.1), channel_id=1, source_target_pairs={{0,2},{1,3},{2,4},{3,5},{4,6},{5,7},{6,0},{7,1},{8,10},{9,11},{10,... | collective-permute-start | bytes 1327112 | tf_op jit(solution)/shard_map/ppermute | solution.py:383
  4.2 2.3 %fusion = (bf16[1,1,16,64,256]{4,3,2,1,0:T(8,128)(2,1)}, bf16[1,1,16,64,256]{4,3,2,1,0:T(8,128)(2,1)}) fusion(bf16[1,2,16,64,256]{4,3,2,1,0:T(8,128)(2,1)} %param.4), kind=kLoop, calls=%fused_computation | loop fusion | bytes 2097152 | tf_op jit(solution)/shard_map/slice | solution.py:417
  8.6 5.3 %collective-permute-start.4 = (bf16[1024,256]{1,0:T(8,128)(2,1)}, bf16[1024,256]{1,0:T(8,128)(2,1)}, u32[]{:S(2)}, u32[]{:S(2)}) collective-permute-start(bf16[1024,256]{1,0:T(8,128)(2,1)} %bitcast.9), channel_id=1, source_target_pairs={{0,8},{8,16},{16,24},{24,32},{32,40},{40,48},{48,56},{56,64},{64,7... | collective-permute-start | bytes 1572872 | tf_op jit(solution)/shard_map/ppermute | solution.py:398
  14.0 9.5 %collective-permute-done.9.right = bf16[864,256]{1,0:T(8,128)(2,1)S(1)} collective-permute-done((bf16[864,256]{1,0:T(8,128)(2,1)}, bf16[864,256]{1,0:T(8,128)(2,1)S(1)}, u32[]{:S(2)}, u32[]{:S(2)}) %collective-permute-start.9) | collective-permute-done | bytes 442400 | tf_op jit(solution)/shard_map/ppermute | solution.py:383
  28.3 3.0 %collective-permute-start.1 = (f32[2,256]{1,0:T(2,128)S(1)}, f32[2,256]{1,0:T(2,128)S(1)}, u32[]{:S(2)}, u32[]{:S(2)}) collective-permute-start(f32[2,256]{1,0:T(2,128)S(1)} %add.28), channel_id=1, source_target_pairs={{0,96},{8,104},{16,112},{24,120},{32,64},{40,72},{48,80},{56,88},{... | collective-permute-start | bytes 6152 | tf_op jit(solution)/shard_map/ppermute | solution.py:383
  36.7 4.0 %collective-permute-start.3 = (f32[2,256]{1,0:T(2,128)S(1)}, f32[2,256]{1,0:T(2,128)S(1)}, u32[]{:S(2)}, u32[]{:S(2)}) collective-permute-start(f32[2,256]{1,0:T(2,128)S(1)} %add.30), channel_id=1, source_target_pairs={{0,24},{8,16},{16,8},{24,0},{32,56},{40,48},{48,40},{56,32},{64,88... | collective-permute-start | bytes 6152 | tf_op jit(solution)/shard_map/ppermute | solution.py:383
  42.6 10.0 %shard_map.53 = (bf16[3,1024,256]{2,1,0:T(8,128)(2,1)S(1)}, f32[1824,256]{1,0:T(8,128)S(1)}, bf16[1824,256]{1,0:T(8,128)(2,1)S(1)}) custom-call(s32[7]{0:T(128)S(1)} %stack.35.where, f32[2,256]{1,0:T(2,128)S(1)} %add.31.stats, bf16[2,1024,256]{2,1,0:T(8,128)(2,1)S(1)} %bitcast.18, bf16[1024,256]{1,0:T(8,128)(2,1)} %collective-permute-done.4.before, ...), custom_call_target="tpu_custom_call" | custom-call | flops 3623878656 | bytes 1000000 | tf_op jit(solution)/shard_map/pallas_call | solution.py:362
  52.7 7.4 %shard_map.54 = (f32[1824,256]{1,0:T(8,128)S(1)}, bf16[1824,256]{1,0:T(8,128)(2,1)S(1)}) custom-call(s32[7]{0:T(128)S(1)} %stack.35.where, bf16[3,1024,256]{2,1,0:T(8,128)(2,1)S(1)} %get-tuple-element.39.act, bf16[3,2,1152,256]{3,2,1,0:T(8,128)(2,1)S(1)} %shard_map.51.near, bf16[3,1,1152,256]{3,2,1,0:T(8,128)(2,1)S(1)} %shard_map.52.after), custom_call_target="tpu_custom_call" | custom-call | flops 3623878656 | bytes 1000000 | tf_op jit(solution)/shard_map/pallas_call | solution.py:362
  62.1 6.1 %shard_map.56 = (f32[1024,256]{1,0:T(8,128)S(1)}, f32[2,256]{1,0:T(2,128)S(1)}, bf16[6912,256]{1,0:T(8,128)(2,1)S(1)}) custom-call(s32[7]{0:T(128)S(1)} %stack.35.where, f32[2,256]{1,0:T(2,128)S(1)} %add.31.stats, bf16[2,1024,256]{2,1,0:T(8,128)(2,1)S(1)} %bitcast.19, bf16[3,2,1152,256]{3,2,1,0:T(8,128)(2,1)S(1)} %shard_map.51.near, ...), custom_call_target="tpu_custom_call" | custom-call | flops 3623878656 | bytes 1000000 | tf_op jit(solution)/shard_map/pallas_call | solution.py:362
  69.2 3.9 %collective-permute-start.13 = (bf16[4,2,224,128]{3,2,1,0:T(8,128)(2,1)S(1)}, bf16[4,2,224,128]{3,2,1,0:T(8,128)(2,1)S(1)}, u32[]{:S(2)}, u32[]{:S(2)}) collective-permute-start(bf16[4,2,224,128]{3,2,1,0:T(8,128)(2,1)S(1)} %get-tuple-element.47), channel_id=1, source_target_pairs={{0,24},{8,16},{16,8},{24,0},{32,56},{40,48},{48,40},{56,32},{64,88... | collective-permute-start | bytes 1376264 | tf_op jit(solution)/shard_map/ppermute | solution.py:383
  73.1 4.3 %collective-permute-done.14.later = bf16[1024,256]{1,0:T(8,128)(2,1)S(1)} collective-permute-done((bf16[1024,256]{1,0:T(8,128)(2,1)S(1)}, bf16[1024,256]{1,0:T(8,128)(2,1)S(1)}, u32[]{:S(2)}, u32[]{:S(2)}) %collective-permute-start.14) | collective-permute-done | bytes 524320 | tf_op jit(solution)/shard_map/ppermute | solution.py:398
  77.4 5.7 %shard_map.58 = (f32[1024,256]{1,0:T(8,128)S(1)}, f32[2,256]{1,0:T(2,128)S(1)}) custom-call(f32[2,256]{1,0:T(2,128)S(1)} %add.31.stats, bf16[2,1024,256]{2,1,0:T(8,128)(2,1)S(1)} %bitcast.20, bf16[3,2,1152,256]{3,2,1,0:T(8,128)(2,1)S(1)} %shard_map.51.near, bf16[3,1,1152,256]{3,2,1,0:T(8,128)(2,1)S(1)} %shard_map.52.after, ...), custom_call_target="tpu_custom_call" | custom-call | flops 3623878656 | bytes 1000000 | tf_op jit(solution)/shard_map/pallas_call | solution.py:362
  83.1 4.8 %collective-permute-done.13.right_in = bf16[4,2,224,128]{3,2,1,0:T(8,128)(2,1)S(1)} collective-permute-done((bf16[4,2,224,128]{3,2,1,0:T(8,128)(2,1)S(1)}, bf16[4,2,224,128]{3,2,1,0:T(8,128)(2,1)S(1)}, u32[]{:S(2)}, u32[]{:S(2)}) %collective-permute-start.13) | collective-permute-done | bytes 458784 | tf_op jit(solution)/shard_map/ppermute | solution.py:383
  88.7 3.8 %collective-permute-start.15 = (bf16[4,224,128]{2,1,0:T(8,128)(2,1)S(1)}, bf16[4,224,128]{2,1,0:T(8,128)(2,1)S(1)}, u32[]{:S(2)}, u32[]{:S(2)}) collective-permute-start(bf16[4,224,128]{2,1,0:T(8,128)(2,1)S(1)} %get-tuple-element.52), channel_id=1, source_target_pairs={{0,24},{8,16},{16,8},{24,0},{32,56},{40,48},{48,40},{56,32},{64,88... | collective-permute-start | bytes 688136 | tf_op jit(solution)/shard_map/ppermute | solution.py:383
  92.5 5.8 %collective-permute-done.15.left_in = bf16[4,224,128]{2,1,0:T(8,128)(2,1)S(1)} collective-permute-done((bf16[4,224,128]{2,1,0:T(8,128)(2,1)S(1)}, bf16[4,224,128]{2,1,0:T(8,128)(2,1)S(1)}, u32[]{:S(2)}, u32[]{:S(2)}) %collective-permute-start.15) | collective-permute-done | bytes 229408 | tf_op jit(solution)/shard_map/ppermute | solution.py:383
  101.3 2.2 %collective-permute-start.18 = (bf16[2,224,128]{2,1,0:T(8,128)(2,1)S(1)}, bf16[2,224,128]{2,1,0:T(8,128)(2,1)S(1)}, u32[]{:S(2)}, u32[]{:S(2)}) collective-permute-start(bf16[2,224,128]{2,1,0:T(8,128)(2,1)S(1)} %get-tuple-element.57), channel_id=1, source_target_pairs={{0,6},{1,7},{2,4},{3,5},{4,2},{5,3},{6,0},{7,1},{8,14},{9,15},{10,... | collective-permute-start | bytes 344072 | tf_op jit(solution)/shard_map/ppermute | solution.py:383
  107.9 2.2 %collective-permute-start.19 = (bf16[224,128]{1,0:T(8,128)(2,1)S(1)}, bf16[224,128]{1,0:T(8,128)(2,1)S(1)}, u32[]{:S(2)}, u32[]{:S(2)}) collective-permute-start(bf16[224,128]{1,0:T(8,128)(2,1)S(1)} %get-tuple-element.60), channel_id=1, source_target_pairs={{0,6},{1,7},{2,4},{3,5},{4,2},{5,3},{6,0},{7,1},{8,14},{9,15},{10,... | collective-permute-start | bytes 172040 | tf_op jit(solution)/shard_map/ppermute | solution.py:383
  110.3 3.1 %collective-permute-done.19.left_in = bf16[224,128]{1,0:T(8,128)(2,1)S(1)} collective-permute-done((bf16[224,128]{1,0:T(8,128)(2,1)S(1)}, bf16[224,128]{1,0:T(8,128)(2,1)S(1)}, u32[]{:S(2)}, u32[]{:S(2)}) %collective-permute-start.19) | collective-permute-done | bytes 57376 | tf_op jit(solution)/shard_map/ppermute | solution.py:383
  114.8 2.2 %collective-permute-start.22 = (bf16[224,128]{1,0:T(8,128)(2,1)S(1)}, bf16[224,128]{1,0:T(8,128)(2,1)S(1)}, u32[]{:S(2)}, u32[]{:S(2)}) collective-permute-start(bf16[224,128]{1,0:T(8,128)(2,1)S(1)} %get-tuple-element.63.right), channel_id=1, source_target_pairs={{0,96},{8,104},{16,112},{24,120},{32,64},{40,72},{48,80},{56,88},{... | collective-permute-start | bytes 172040 | tf_op jit(solution)/shard_map/ppermute | solution.py:383
  117.0 3.3 %collective-permute-done.22.right_in = bf16[224,128]{1,0:T(8,128)(2,1)S(1)} collective-permute-done((bf16[224,128]{1,0:T(8,128)(2,1)S(1)}, bf16[224,128]{1,0:T(8,128)(2,1)S(1)}, u32[]{:S(2)}, u32[]{:S(2)}) %collective-permute-start.22) | collective-permute-done | bytes 57376 | tf_op jit(solution)/shard_map/ppermute | solution.py:383
  120.3 2.2 %collective-permute-start.23 = (bf16[240,128]{1,0:T(8,128)(2,1)S(1)}, bf16[240,128]{1,0:T(8,128)(2,1)S(1)}, u32[]{:S(2)}, u32[]{:S(2)}) collective-permute-start(bf16[240,128]{1,0:T(8,128)(2,1)S(1)} %get-tuple-element.64.left), channel_id=1, source_target_pairs={{0,96},{8,104},{16,112},{24,120},{32,64},{40,72},{48,80},{56,88},{... | collective-permute-start | bytes 184328 | tf_op jit(solution)/shard_map/ppermute | solution.py:383
  122.6 4.2 %collective-permute-done.24.right_in = bf16[224,128]{1,0:T(8,128)(2,1)S(1)} collective-permute-done((bf16[224,128]{1,0:T(8,128)(2,1)S(1)}, bf16[224,128]{1,0:T(8,128)(2,1)S(1)}, u32[]{:S(2)}, u32[]{:S(2)}) %collective-permute-start.24) | collective-permute-done | bytes 57376 | tf_op jit(solution)/shard_map/ppermute | solution.py:383
  128.7 4.2 %collective-permute-done.26.right_in = bf16[224,128]{1,0:T(8,128)(2,1)S(1)} collective-permute-done((bf16[224,128]{1,0:T(8,128)(2,1)S(1)}, bf16[224,128]{1,0:T(8,128)(2,1)S(1)}, u32[]{:S(2)}, u32[]{:S(2)}) %collective-permute-start.26) | collective-permute-done | bytes 57376 | tf_op jit(solution)/shard_map/ppermute | solution.py:383
  135.1 4.6 %collective-permute-done.28.right_in = bf16[448,128]{1,0:T(8,128)(2,1)S(1)} collective-permute-done((bf16[448,128]{1,0:T(8,128)(2,1)S(1)}, bf16[448,128]{1,0:T(8,128)(2,1)S(1)}, u32[]{:S(2)}, u32[]{:S(2)}) %collective-permute-start.28) | collective-permute-done | bytes 114720 | tf_op jit(solution)/shard_map/ppermute | solution.py:383
  (67 shorter events, 35.7 us)
Async XLA Ops:
  0.6 22.9 %collective-permute-start.9 = (bf16[864,256]{1,0:T(8,128)(2,1)}, bf16[864,256]{1,0:T(8,128)(2,1)S(1)}, u32[]{:S(2)}, u32[]{:S(2)}) collective-permute-start(bf16[864,256]{1,0:T(8,128)(2,1)} %own.1), channel_id=1, source_target_pairs={{0,6},{1,7},{2,0},{3,1},{4,2},{5,3},{6,4},{7,5},{8,14},{9,15},{10,... | collective-permute-start | bytes 1327112 | tf_op jit(solution)/shard_map/ppermute | solution.py:383
  1.5 22.0 %collective-permute-start.8 = (bf16[864,256]{1,0:T(8,128)(2,1)}, bf16[864,256]{1,0:T(8,128)(2,1)S(1)}, u32[]{:S(2)}, u32[]{:S(2)}) collective-permute-start(bf16[864,256]{1,0:T(8,128)(2,1)} %own.1), channel_id=1, source_target_pairs={{0,2},{1,3},{2,4},{3,5},{4,6},{5,7},{6,0},{7,1},{8,10},{9,11},{10,... | collective-permute-start | bytes 1327112 | tf_op jit(solution)/shard_map/ppermute | solution.py:383
  4.0 19.6 %collective-permute-start.10 = (bf16[864,256]{1,0:T(8,128)(2,1)}, bf16[864,256]{1,0:T(8,128)(2,1)S(1)}, u32[]{:S(2)}, u32[]{:S(2)}) collective-permute-start(bf16[864,256]{1,0:T(8,128)(2,1)} %own.1), channel_id=1, source_target_pairs={{0,4},{1,5},{2,6},{3,7},{4,0},{5,1},{6,2},{7,3},{8,12},{9,13},{10,... | collective-permute-start | bytes 1327112 | tf_op jit(solution)/shard_map/ppermute | solution.py:383
  6.5 35.9 %collective-permute-start.5 = (bf16[1024,256]{1,0:T(8,128)(2,1)}, bf16[1024,256]{1,0:T(8,128)(2,1)S(1)}, u32[]{:S(2)}, u32[]{:S(2)}) collective-permute-start(bf16[1024,256]{1,0:T(8,128)(2,1)} %bitcast.11), channel_id=1, source_target_pairs={{8,0},{16,8},{24,16},{32,24},{40,32},{48,40},{56,48},{64,56},{72,6... | collective-permute-start | bytes 1572872 | tf_op jit(solution)/shard_map/ppermute | solution.py:398
  8.6 34.0 %collective-permute-start.4 = (bf16[1024,256]{1,0:T(8,128)(2,1)}, bf16[1024,256]{1,0:T(8,128)(2,1)}, u32[]{:S(2)}, u32[]{:S(2)}) collective-permute-start(bf16[1024,256]{1,0:T(8,128)(2,1)} %bitcast.9), channel_id=1, source_target_pairs={{0,8},{8,16},{16,24},{24,32},{32,40},{40,48},{48,56},{56,64},{64,7... | collective-permute-start | bytes 1572872 | tf_op jit(solution)/shard_map/ppermute | solution.py:398
  24.2 37.8 %collective-permute-start.11 = (bf16[4,864,256]{2,1,0:T(8,128)(2,1)S(1)}, bf16[4,864,256]{2,1,0:T(8,128)(2,1)S(1)}, u32[]{:S(2)}, u32[]{:S(2)}) collective-permute-start(bf16[4,864,256]{2,1,0:T(8,128)(2,1)S(1)} %shard_map.55.mine), channel_id=1, source_target_pairs={{0,1},{1,0},{2,3},{3,2},{4,5},{5,4},{6,7},{7,6},{8,9},{9,8},{10,11... | collective-permute-start | bytes 5308424 | tf_op jit(solution)/shard_map/ppermute | solution.py:387
  28.3 4.8 %collective-permute-start.1 = (f32[2,256]{1,0:T(2,128)S(1)}, f32[2,256]{1,0:T(2,128)S(1)}, u32[]{:S(2)}, u32[]{:S(2)}) collective-permute-start(f32[2,256]{1,0:T(2,128)S(1)} %add.28), channel_id=1, source_target_pairs={{0,96},{8,104},{16,112},{24,120},{32,64},{40,72},{48,80},{56,88},{... | collective-permute-start | bytes 6152 | tf_op jit(solution)/shard_map/ppermute | solution.py:383
  36.7 5.6 %collective-permute-start.3 = (f32[2,256]{1,0:T(2,128)S(1)}, f32[2,256]{1,0:T(2,128)S(1)}, u32[]{:S(2)}, u32[]{:S(2)}) collective-permute-start(f32[2,256]{1,0:T(2,128)S(1)} %add.30), channel_id=1, source_target_pairs={{0,24},{8,16},{16,8},{24,0},{32,56},{40,48},{48,40},{56,32},{64,88... | collective-permute-start | bytes 6152 | tf_op jit(solution)/shard_map/ppermute | solution.py:383
  52.6 15.6 %collective-permute-start.6 = (bf16[1824,256]{1,0:T(8,128)(2,1)S(1)}, bf16[1824,256]{1,0:T(8,128)(2,1)S(1)}, u32[]{:S(2)}, u32[]{:S(2)}) collective-permute-start(bf16[1824,256]{1,0:T(8,128)(2,1)S(1)} %get-tuple-element.41), channel_id=1, source_target_pairs={{0,1},{1,0},{2,3},{3,2},{4,5},{5,4},{6,7},{7,6},{8,9},{9,8},{10,11... | collective-permute-start | bytes 2801672 | tf_op jit(solution)/shard_map/ppermute | solution.py:387
  60.2 8.0 %collective-permute-start.7 = (bf16[1824,256]{1,0:T(8,128)(2,1)S(1)}, bf16[1824,256]{1,0:T(8,128)(2,1)S(1)}, u32[]{:S(2)}, u32[]{:S(2)}) collective-permute-start(bf16[1824,256]{1,0:T(8,128)(2,1)S(1)} %get-tuple-element.42), channel_id=1, source_target_pairs={{0,1},{1,0},{2,3},{3,2},{4,5},{5,4},{6,7},{7,6},{8,9},{9,8},{10,11... | collective-permute-start | bytes 2801672 | tf_op jit(solution)/shard_map/ppermute | solution.py:387
  60.8 16.7 %collective-permute-start.14 = (bf16[1024,256]{1,0:T(8,128)(2,1)S(1)}, bf16[1024,256]{1,0:T(8,128)(2,1)S(1)}, u32[]{:S(2)}, u32[]{:S(2)}) collective-permute-start(bf16[1024,256]{1,0:T(8,128)(2,1)S(1)} %bitcast.24), channel_id=1, source_target_pairs={{8,0},{16,8},{24,16},{32,24},{40,32},{48,40},{56,48},{64,56},{72,6... | collective-permute-start | bytes 1572872 | tf_op jit(solution)/shard_map/ppermute | solution.py:398
  69.2 18.8 %collective-permute-start.13 = (bf16[4,2,224,128]{3,2,1,0:T(8,128)(2,1)S(1)}, bf16[4,2,224,128]{3,2,1,0:T(8,128)(2,1)S(1)}, u32[]{:S(2)}, u32[]{:S(2)}) collective-permute-start(bf16[4,2,224,128]{3,2,1,0:T(8,128)(2,1)S(1)} %get-tuple-element.47), channel_id=1, source_target_pairs={{0,24},{8,16},{16,8},{24,0},{32,56},{40,48},{48,40},{56,32},{64,88... | collective-permute-start | bytes 1376264 | tf_op jit(solution)/shard_map/ppermute | solution.py:383
  73.1 14.9 %collective-permute-start.12 = (bf16[4,2,224,128]{3,2,1,0:T(8,128)(2,1)S(1)}, bf16[4,2,224,128]{3,2,1,0:T(8,128)(2,1)S(1)}, u32[]{:S(2)}, u32[]{:S(2)}) collective-permute-start(bf16[4,2,224,128]{3,2,1,0:T(8,128)(2,1)S(1)} %get-tuple-element.46.order), channel_id=1, source_target_pairs={{0,8},{8,0},{16,24},{24,16},{32,40},{40,32},{48,56},{56,48},{64,72... | collective-permute-start | bytes 1376264 | tf_op jit(solution)/shard_map/ppermute | solution.py:383
  88.7 9.6 %collective-permute-start.15 = (bf16[4,224,128]{2,1,0:T(8,128)(2,1)S(1)}, bf16[4,224,128]{2,1,0:T(8,128)(2,1)S(1)}, u32[]{:S(2)}, u32[]{:S(2)}) collective-permute-start(bf16[4,224,128]{2,1,0:T(8,128)(2,1)S(1)} %get-tuple-element.52), channel_id=1, source_target_pairs={{0,24},{8,16},{16,8},{24,0},{32,56},{40,48},{48,40},{56,32},{64,88... | collective-permute-start | bytes 688136 | tf_op jit(solution)/shard_map/ppermute | solution.py:383
  92.5 7.3 %collective-permute-start.16 = (bf16[4,224,128]{2,1,0:T(8,128)(2,1)S(1)}, bf16[4,224,128]{2,1,0:T(8,128)(2,1)S(1)}, u32[]{:S(2)}, u32[]{:S(2)}) collective-permute-start(bf16[4,224,128]{2,1,0:T(8,128)(2,1)S(1)} %get-tuple-element.53), channel_id=1, source_target_pairs={{0,8},{8,0},{16,24},{24,16},{32,40},{40,32},{48,56},{56,48},{64,72... | collective-permute-start | bytes 688136 | tf_op jit(solution)/shard_map/ppermute | solution.py:383
  100.4 4.9 %collective-permute-start.17 = (bf16[2,224,128]{2,1,0:T(8,128)(2,1)S(1)}, bf16[2,224,128]{2,1,0:T(8,128)(2,1)S(1)}, u32[]{:S(2)}, u32[]{:S(2)}) collective-permute-start(bf16[2,224,128]{2,1,0:T(8,128)(2,1)S(1)} %get-tuple-element.56), channel_id=1, source_target_pairs={{0,2},{1,3},{2,0},{3,1},{4,6},{5,7},{6,4},{7,5},{8,10},{9,11},{10,... | collective-permute-start | bytes 344072 | tf_op jit(solution)/shard_map/ppermute | solution.py:383
  101.3 6.0 %collective-permute-start.18 = (bf16[2,224,128]{2,1,0:T(8,128)(2,1)S(1)}, bf16[2,224,128]{2,1,0:T(8,128)(2,1)S(1)}, u32[]{:S(2)}, u32[]{:S(2)}) collective-permute-start(bf16[2,224,128]{2,1,0:T(8,128)(2,1)S(1)} %get-tuple-element.57), channel_id=1, source_target_pairs={{0,6},{1,7},{2,4},{3,5},{4,2},{5,3},{6,0},{7,1},{8,14},{9,15},{10,... | collective-permute-start | bytes 344072 | tf_op jit(solution)/shard_map/ppermute | solution.py:383
  107.9 5.5 %collective-permute-start.19 = (bf16[224,128]{1,0:T(8,128)(2,1)S(1)}, bf16[224,128]{1,0:T(8,128)(2,1)S(1)}, u32[]{:S(2)}, u32[]{:S(2)}) collective-permute-start(bf16[224,128]{1,0:T(8,128)(2,1)S(1)} %get-tuple-element.60), channel_id=1, source_target_pairs={{0,6},{1,7},{2,4},{3,5},{4,2},{5,3},{6,0},{7,1},{8,14},{9,15},{10,... | collective-permute-start | bytes 172040 | tf_op jit(solution)/shard_map/ppermute | solution.py:383
  114.4 5.9 %collective-permute-start.21 = (bf16[240,128]{1,0:T(8,128)(2,1)S(1)}, bf16[240,128]{1,0:T(8,128)(2,1)S(1)}, u32[]{:S(2)}, u32[]{:S(2)}) collective-permute-start(bf16[240,128]{1,0:T(8,128)(2,1)S(1)} %get-tuple-element.62.left), channel_id=1, source_target_pairs={{0,32},{8,40},{16,48},{24,56},{32,0},{40,8},{48,16},{56,24},{64,96... | collective-permute-start | bytes 184328 | tf_op jit(solution)/shard_map/ppermute | solution.py:383
  114.8 5.5 %collective-permute-start.22 = (bf16[224,128]{1,0:T(8,128)(2,1)S(1)}, bf16[224,128]{1,0:T(8,128)(2,1)S(1)}, u32[]{:S(2)}, u32[]{:S(2)}) collective-permute-start(bf16[224,128]{1,0:T(8,128)(2,1)S(1)} %get-tuple-element.63.right), channel_id=1, source_target_pairs={{0,96},{8,104},{16,112},{24,120},{32,64},{40,72},{48,80},{56,88},{... | collective-permute-start | bytes 172040 | tf_op jit(solution)/shard_map/ppermute | solution.py:383
  120.3 6.4 %collective-permute-start.23 = (bf16[240,128]{1,0:T(8,128)(2,1)S(1)}, bf16[240,128]{1,0:T(8,128)(2,1)S(1)}, u32[]{:S(2)}, u32[]{:S(2)}) collective-permute-start(bf16[240,128]{1,0:T(8,128)(2,1)S(1)} %get-tuple-element.64.left), channel_id=1, source_target_pairs={{0,96},{8,104},{16,112},{24,120},{32,64},{40,72},{48,80},{56,88},{... | collective-permute-start | bytes 184328 | tf_op jit(solution)/shard_map/ppermute | solution.py:383
  126.8 6.1 %collective-permute-start.25 = (bf16[240,128]{1,0:T(8,128)(2,1)S(1)}, bf16[240,128]{1,0:T(8,128)(2,1)S(1)}, u32[]{:S(2)}, u32[]{:S(2)}) collective-permute-start(bf16[240,128]{1,0:T(8,128)(2,1)S(1)} %get-tuple-element.66.left), channel_id=1, source_target_pairs={{0,24},{8,16},{16,8},{24,0},{32,56},{40,48},{48,40},{56,32},{64,88... | collective-permute-start | bytes 184328 | tf_op jit(solution)/shard_map/ppermute | solution.py:383
  133.5 6.2 %collective-permute-start.27 = (bf16[464,128]{1,0:T(8,128)(2,1)S(1)}, bf16[464,128]{1,0:T(8,128)(2,1)S(1)}, u32[]{:S(2)}, u32[]{:S(2)}) collective-permute-start(bf16[464,128]{1,0:T(8,128)(2,1)S(1)} %get-tuple-element.68.left), channel_id=1, source_target_pairs={{0,8},{8,0},{16,24},{24,16},{32,40},{40,32},{48,56},{56,48},{64,72... | collective-permute-start | bytes 356360 | tf_op jit(solution)/shard_map/ppermute | solution.py:383
  133.6 6.1 %collective-permute-start.28 = (bf16[448,128]{1,0:T(8,128)(2,1)S(1)}, bf16[448,128]{1,0:T(8,128)(2,1)S(1)}, u32[]{:S(2)}, u32[]{:S(2)}) collective-permute-start(bf16[448,128]{1,0:T(8,128)(2,1)S(1)} %get-tuple-element.69.right), channel_id=1, source_target_pairs={{0,24},{8,16},{16,8},{24,0},{32,56},{40,48},{48,40},{56,32},{64,88... | collective-permute-start | bytes 344072 | tf_op jit(solution)/shard_map/ppermute | solution.py:383
  (9 other events, 84.6 us)

commit v3 on v2

v3 whole, which is shorter than its diff:
```python
import functools
import math

import jax
import jax.numpy as jnp
from jax import lax
from jax.experimental import pallas as pl
from jax.experimental.pallas import tpu as pltpu
from jax.sharding import PartitionSpec as P

GROUPS = 32
C = 256
H = 16
W = 64
ROWS = H * W
PADDED = ROWS + 2 * W
HALF = C // 2
SHARD = 864
SHARD_PAD = 896
QUARTER = 224
UNIT = 32
VMEM = 20 * 1024 * 1024
epsilon = 1e-06
f32 = jnp.float32
bf16 = jnp.bfloat16


def group_total(rows):
    lane = lax.broadcasted_iota(jnp.int32, rows.shape, 1)
    for s in (1, 2, 4):
        up = pltpu.roll(rows, s, 1)
        down = pltpu.roll(rows, C - s, 1)
        rows = rows + jnp.where((lane & s) != 0, up, down)
    return rows


def center_inverse(stats, count):
    sums = group_total(stats) / count
    center = sums[0:1]
    spread = sums[1:2] - center * center
    return center, lax.rsqrt(spread + epsilon)


def sigmoid(v):
    return 1.0 / (1.0 + jnp.exp(-v))


def widths(target, cot, slot):
    zero = jnp.zeros((W, C), bf16)
    for kw in range(3):
        target[kw, slot, 0:W] = zero
        target[kw, slot, W + ROWS : PADDED] = zero
    column = lax.broadcasted_iota(jnp.int32, (W, C), 0)

    @pl.loop(0, H)
    def _(h):
        row = cot(pl.multiple_of(h * W, W))
        at = pl.ds(pl.multiple_of(h * W + W, W), W)
        wide = row.astype(f32)
        target[1, slot, at] = row
        target[0, slot, at] = jnp.where(column == W - 1, 0.0, pltpu.roll(wide, W - 1, 0)).astype(bf16)
        target[2, slot, at] = jnp.where(column == 0, 0.0, pltpu.roll(wide, 1, 0)).astype(bf16)


def stats_kernel(clip, out):
    def step(i, carry):
        a, b = carry
        v = clip[pl.ds(pl.multiple_of(i * 128, 128), 128)].astype(f32)
        v = v.reshape(16, 8, C)
        return a + v.sum(0), b + (v * v).sum(0)

    zero = jnp.zeros((8, C), f32)
    a, b = lax.fori_loop(0, clip.shape[0] // 128, step, (zero, zero))
    out[0:1] = a.sum(0, keepdims=True)
    out[1:2] = b.sum(0, keepdims=True)


def copy_kernel(clip, cot, order, first, second, last):
    first[...] = cot[0]
    second[...] = cot[1]
    last[...] = clip[1]


def widths_kernel(cot, *refs):
    wide = refs[-1]
    for t in range(cot.shape[0]):
        widths(wide, lambda r, t=t: cot[t, pl.ds(r, W)], t)


def ring_sum_kernel(own, before, after, far, out):
    out[...] = (own[...] + far[...]) + (before[...] + after[...])


def tap_rows(kh):
    return pl.ds(pl.multiple_of((2 - kh) * W, W), ROWS)


CONTRACT_ROWS = (((0,), (0,)), ((), ()))
CONTRACT_COLUMNS = (((1,), (1,)), ((), ()))


def tap_product(frames, views, channels):
    total = None
    for frame, view in zip(frames, views):
        part = lax.dot_general(frame[:, channels], view, CONTRACT_ROWS, preferred_element_type=f32)
        total = part if total is None else total + part
    return total


def store_tap(tap, total, first_unit, core, keep, send):
    spare = 2 * SHARD_PAD
    for u in range(total.shape[0] // UNIT):
        unit = tap * (C // UNIT) + first_unit + u
        shard = (unit * 1214) >> 15
        dest = ((shard >> 1) & 1) * SHARD_PAD + (unit - shard * (SHARD // UNIT)) * UNIT
        mine = (shard & 1) == core
        piece = total[u * UNIT : (u + 1) * UNIT]
        keep[pl.ds(pl.multiple_of(jnp.where(mine, dest, spare), UNIT), UNIT)] = piece
        send[pl.ds(pl.multiple_of(jnp.where(mine, spare, dest), UNIT), UNIT)] = piece.astype(bf16)


def clear_tails(keep, send):
    for place in range(2):
        tail = slice(place * SHARD_PAD + SHARD, (place + 1) * SHARD_PAD)
        keep[tail] = jnp.zeros((SHARD_PAD - SHARD, C), f32)
        send[tail] = jnp.zeros((SHARD_PAD - SHARD, C), bf16)
    keep[2 * SHARD_PAD :] = jnp.zeros((UNIT, C), f32)
    send[2 * SHARD_PAD :] = jnp.zeros((UNIT, C), bf16)


def middle_taps(low, high, channels, scale, core, act, near, after, keep, send):
    for tap in range(low, high):
        kh, kw = tap // 3 % 3, tap % 3
        rows = slice((2 - kh) * W, (2 - kh) * W + ROWS)
        total = tap_product((act[1], act[2]), (near[kw, 1, rows], after[kw, 0, rows]), channels)
        store_tap(tap, total * scale, channels.start // UNIT, core, keep, send)


def upper_kernel(count, scale, where, stats, clip, before, near, after, act, keep, send):
    center, inverse = center_inverse(stats[...], count)
    core = where[1]

    def activate(frame, slot, gain):
        @pl.loop(0, ROWS // 64)
        def _(i):
            at = pl.ds(pl.multiple_of(i * 64, 64), 64)
            v = (frame(at).astype(f32) - center) * inverse
            v = v * sigmoid(v)
            if gain is not None:
                v = v * gain
            act[slot, at] = v.astype(bf16)

    activate(lambda at: before[at], 0, jnp.where(where[0] == 1, 0.0, 1.0))
    activate(lambda at: clip[0, at], 1, None)
    activate(lambda at: clip[1, at], 2, None)

    @pl.loop(0, 3)
    def _(kh):
        rows = tap_rows(kh)
        for kw in range(3):
            total = tap_product((act[1], act[2]), (near[kw, 0, rows], near[kw, 1, rows]), slice(None))
            store_tap(18 + kh * 3 + kw, total * scale, 0, core, keep, send)

    middle_taps(14, 18, slice(0, C), scale, core, act, near, after, keep, send)
    middle_taps(13, 14, slice(HALF, C), scale, core, act, near, after, keep, send)
    clear_tails(keep, send)


def lower_kernel(scale, where, act, near, after, order, keep, send):
    core = where[1]

    @pl.loop(0, 3)
    def _(kh):
        rows = tap_rows(kh)
        for kw in range(3):
            total = tap_product((act[0], act[1]), (near[kw, 1, rows], after[kw, 0, rows]), slice(None))
            store_tap(kh * 3 + kw, total * scale, 0, core, keep, send)

    middle_taps(9, 13, slice(0, C), scale, core, act, near, after, keep, send)
    middle_taps(13, 14, slice(0, HALF), scale, core, act, near, after, keep, send)
    clear_tails(keep, send)


def pack_kernel(where, own, left, right, far, order, packed):
    x = where[2]
    for block, distance in ((own, 0), (left, 3), (right, 1), (far, 2)):
        packed[(x + distance) % 4] = block[...]


def frame_grad(count, frame, stats, clip, views, weights, grad, sums):
    center, inverse = center_inverse(stats[...], count)
    rows_per = 256

    @pl.loop(0, ROWS // rows_per)
    def _(i):
        start = i * rows_per
        total = jnp.zeros((rows_per, C), f32)
        for tap in range(27):
            kt, kh, kw = tap // 9, tap // 3 % 3, tap % 3
            rows = pl.ds(pl.multiple_of((2 - kh) * W + start, W), rows_per)
            w = weights[tap * C : (tap + 1) * C]
            total += lax.dot_general(
                views[2 - kt](kw, rows), w, CONTRACT_COLUMNS, preferred_element_type=f32
            )
        grad[pl.ds(pl.multiple_of(start, rows_per), rows_per)] = total

    zero = jnp.zeros((8, C), f32)

    def finish(i, carry):
        a, b = carry
        at = pl.ds(pl.multiple_of(i * 64, 64), 64)
        v = (clip[frame, at].astype(f32) - center) * inverse
        s = sigmoid(v)
        g = grad[at] * (s * (1.0 + v * (1.0 - s)))
        grad[at] = g
        return a + g.reshape(8, 8, C).sum(0), b + (g * v).reshape(8, 8, C).sum(0)

    a, b = lax.fori_loop(0, ROWS // 64, finish, (zero, zero))
    sums[0:1] = a.sum(0, keepdims=True)
    sums[1:2] = b.sum(0, keepdims=True)


def first_grad_kernel(count, where, stats, clip, near, after, mine, other, order0, order1, grad, sums, full):
    core = where[1]
    for x in range(4):
        full[pl.ds(pl.multiple_of((2 * x + core) * SHARD, UNIT), SHARD)] = mine[x]
        full[pl.ds(pl.multiple_of((2 * x + 1 - core) * SHARD, UNIT), SHARD)] = other[x]
    views = (
        lambda kw, rows: near[kw, 0, rows],
        lambda kw, rows: near[kw, 1, rows],
        lambda kw, rows: after[kw, 0, rows],
    )
    frame_grad(count, 0, stats, clip, views, full, grad, sums)


def second_grad_kernel(count, stats, clip, near, after, later, full, order, grad, sums):
    views = (
        lambda kw, rows: near[kw, 1, rows],
        lambda kw, rows: after[kw, 0, rows],
        lambda kw, rows: later[kw, 0, rows],
    )
    frame_grad(count, 1, stats, clip, views, full, grad, sums)


def final_kernel(count, stats, sums, clip, cot, grad0, grad1, out):
    center, inverse = center_inverse(stats[...], count)
    means = group_total(sums[...]) / count
    total, cross = means[0:1], means[1:2]
    for frame, grad in enumerate((grad0, grad1)):

        @pl.loop(0, ROWS // 64)
        def _(i, frame=frame, grad=grad):
            at = pl.ds(pl.multiple_of(i * 64, 64), 64)
            v = (clip[frame, at].astype(f32) - center) * inverse
            g = cot[frame, at].astype(f32) + inverse * (grad[at] - total - v * cross)
            out[frame, at] = g.astype(bf16)


STEPS = (1, 3, 2)


def split_core_kernel(where, keep, got, order, held, *out):
    z = where[3]

    def add(x, quarter):
        at = pl.ds(pl.multiple_of(x * SHARD_PAD + quarter * QUARTER, UNIT), QUARTER)
        return keep[at] + got[at].astype(f32)

    for x in range(2):
        held[x] = add(x, z)
        for step, to in zip(STEPS, out):
            to[x] = add(x, (z + step) & 3).astype(bf16)


def ring_add(own, arrived, at):
    return (own[at].astype(f32) + arrived[2][at].astype(f32)) + (arrived[0][at].astype(f32) + arrived[1][at].astype(f32))


def split_z_kernel(where, low, l0, l1, l2, up, u0, u1, u2, order, held, *out):
    x_own = where[2]

    def total(x, use):
        @pl.when(x < 2)
        def _():
            use(ring_add(low, (l0, l1, l2), x & 1))

        @pl.when(x >= 2)
        def _():
            use(ring_add(up, (u0, u1, u2), x & 1))

    def hold(value):
        held[...] = value

    total(x_own, hold)
    for step, to in zip(STEPS, out):

        def give(value, to=to):
            to[...] = value.astype(bf16)

        total((x_own + step) & 3, give)


def write_sums(sums, rows, out):
    rows[...] = jnp.zeros((16, C), f32)
    rest = sums
    for k in range(3):
        term = rest.astype(bf16).astype(f32)
        rest = rest - term
        rows[2 * k : 2 * k + 2] = term
    out[QUARTER:] = rows[...].astype(bf16)


def read_sums(block):
    wide = block[QUARTER:].astype(f32)
    return wide[0:2] + wide[2:4] + wide[4:6]


def ring_sums(own, arrived):
    return (read_sums(own) + read_sums(arrived[2])) + (read_sums(arrived[0]) + read_sums(arrived[1]))


def split_x_kernel(held, a0, a1, a2, sums0, sums1, out, rows):
    out[:QUARTER] = ring_add(held, (a0, a1, a2), slice(None)).astype(bf16)
    write_sums(sums0[...] + sums1[...], rows, out)


def reduced_kernel(own, a0, a1, a2, out, rows):
    out[:QUARTER] = ring_add(own, (a0, a1, a2), slice(0, QUARTER)).astype(bf16)
    write_sums(ring_sums(own, (a0, a1, a2)), rows, out)


def finish_kernel(where, own, a0, a1, a2, grad_weight, sums, full):
    z = where[3]
    for block, distance in ((own, 0), (a0, 3), (a1, 1), (a2, 2)):
        at = pl.ds(pl.multiple_of(((z + distance) & 3) * QUARTER, UNIT), QUARTER)
        full[at] = block[:QUARTER].astype(f32)
    grad_weight[...] = full[:SHARD]
    sums[...] = ring_sums(own, (a0, a1, a2))


def call(kernel, out_shape, args, scratch=(), flops=0, bytes_accessed=1_000_000, scalars=0, order=()):
    specs = [pl.BlockSpec(memory_space=pltpu.SMEM)] * scalars
    specs += [pl.BlockSpec(memory_space=pltpu.VMEM)] * (len(args) - scalars)
    specs += [pl.BlockSpec(memory_space=pl.ANY)] * len(order)
    return pl.pallas_call(
        kernel,
        out_shape=out_shape,
        in_specs=specs,
        out_specs=jax.tree.map(lambda _: pl.BlockSpec(memory_space=pltpu.VMEM), out_shape),
        scratch_shapes=list(scratch),
        compiler_params=pltpu.CompilerParams(vmem_limit_bytes=VMEM),
        cost_estimate=pl.CostEstimate(flops=flops, bytes_accessed=bytes_accessed, transcendentals=0),
    )(*args, *order)


AXES = {"z": ("tm", 16, 1), "y": ("tm", 16, 4), "x": ("fsdp", 8, 2)}


def ring(axis, blocks):
    name, size, stride = AXES[axis]
    got = []
    for block, distance in zip(blocks, STEPS):
        route = []
        for i in range(size):
            place = (i // stride) % 4
            route.append((i, i + ((place + distance) % 4 - place) * stride))
        got.append(lax.ppermute(block, name, route))
    return got


def swap_core(block):
    return lax.ppermute(block, "fsdp", [(i, i ^ 1) for i in range(8)])


def ring_sum(values, axis):
    return call(ring_sum_kernel, jax.ShapeDtypeStruct(values.shape, f32), (values, *ring(axis, [values] * 3)))


def passed(block, distance):
    route = [(i - distance, i) for i in range(16) if 0 <= i - distance < 16]
    return lax.ppermute(block, "tm", route)


def per_device(clip, cotangent, weights):
    shape = clip.shape
    clip = clip.reshape(2, ROWS, C)
    cot = cotangent.reshape(2, ROWS, C)
    count = 32 * ROWS * (C // GROUPS)
    scale = 1.0 / math.sqrt(8 * 32 * ROWS)
    partial = functools.partial
    S = jax.ShapeDtypeStruct
    tm = lax.axis_index("tm")
    fsdp = lax.axis_index("fsdp")
    where = [tm == 0, fsdp & 1, fsdp >> 1, tm & 3]
    where = jnp.stack([jnp.asarray(v, jnp.int32) for v in where])
    frame = S((ROWS, C), bf16)

    sums = call(stats_kernel, S((2, C), f32), (clip.reshape(2 * ROWS, C),))
    first, second, last = call(copy_kernel, (frame, frame, frame), (clip, cot), order=(sums,))
    sums = ring_sum(sums, "y")
    near = call(widths_kernel, S((3, 2, PADDED, C), bf16), (cot,), order=(sums,))
    stats = ring_sum(sums, "z")
    after = call(widths_kernel, S((3, 1, PADDED, C), bf16), (passed(first, -1)[None],))
    before = passed(last, 1)
    later = call(widths_kernel, S((3, 1, PADDED, C), bf16), (passed(second, -1)[None],))
    gathered = ring("x", [weights] * 3)

    rows = 2 * SHARD_PAD + UNIT
    half_flops = 27 * C * C * 2 * ROWS // 4
    act, keep_up, send_up = call(
        partial(upper_kernel, count, scale),
        (S((3, ROWS, C), bf16), S((rows, C), f32), S((rows, C), bf16)),
        (where, stats, clip, before, near, after),
        flops=half_flops,
        scalars=1,
    )
    got_up = swap_core(send_up)
    keep_low, send_low = call(
        partial(lower_kernel, scale),
        (S((rows, C), f32), S((rows, C), bf16)),
        (where, act, near, after),
        flops=half_flops,
        scalars=1,
        order=(send_up,),
    )
    got_low = swap_core(send_low)
    block = lambda *dims: (S(dims + (QUARTER, C), f32),) + (S(dims + (QUARTER, C), bf16),) * 3
    up, *out_up = call(split_core_kernel, block(2), (where, keep_up, got_up), scalars=1, order=(keep_low,))
    low, *out_low = call(split_core_kernel, block(2), (where, keep_low, got_low), scalars=1, order=(up,))
    arrived_up = ring("z", out_up)
    mine = call(pack_kernel, S((4, SHARD, C), bf16), (where, weights, *gathered), scalars=1, order=(arrived_up[0],))
    other = swap_core(mine)
    grad0, sums0, full = call(
        partial(first_grad_kernel, count),
        (S((ROWS, C), f32), S((2, C), f32), S((8 * SHARD, C), bf16)),
        (where, stats, clip, near, after, mine, other),
        flops=half_flops,
        scalars=1,
        order=(later, low),
    )
    grad1, sums1 = call(
        partial(second_grad_kernel, count),
        (S((ROWS, C), f32), S((2, C), f32)),
        (stats, clip, near, after, later, full),
        flops=half_flops,
        order=(sums0,),
    )
    got = (low, *ring("z", out_low), up, *arrived_up)
    held, *out = call(split_z_kernel, block(), (where, *got), scalars=1, order=(sums1,))
    rows16 = [pltpu.VMEM((16, C), f32)]
    message = S((QUARTER + 16, C), bf16)
    own = call(split_x_kernel, message, (held, *ring("x", out), sums0, sums1), rows16)
    own = call(reduced_kernel, message, (own, *ring("y", [own] * 3)), rows16)
    grad_weight, sums = call(
        finish_kernel,
        (S((SHARD, C), f32), S((2, C), f32)),
        (where, own, *ring("z", [own] * 3)),
        [pltpu.VMEM((SHARD_PAD, C), f32)],
        scalars=1,
    )
    grad_input = call(
        partial(final_kernel, count), S((2, ROWS, C), bf16), (stats, sums, clip, cot, grad0, grad1)
    )
    return grad_input.reshape(shape), grad_weight


def solution(mesh):
    in_specs = (
        P("fsdp", "tm", None, None, None),
        P("fsdp", "tm", None, None, None),
        P("fsdp", None),
    )
    out_specs = (P("fsdp", "tm", None, None, None), P("fsdp", None))
    return jax.shard_map(
        per_device, mesh=mesh, in_specs=in_specs, out_specs=out_specs, check_vma=False
    )
```

time: 145 us -> 138 us (0.952)
  Pallas kernels: 38.4 us -> 33.1 us
  waiting for transfers between devices: 56.5 us -> 51.5 us
  starting transfers between devices: 44.3 us -> 48.7 us
    ppermute x23 -> x24, waiting for transfers between devices: 52.2 us -> 41.7 us  [ring(): got.append(lax.ppermute(block, name, route))]
    ppermute x3, waiting for transfers between devices: 4.32 us -> 9.8 us  [passed(): return lax.ppermute(block, 'tm', route)]
    pallas_call x18 -> x19, Pallas kernels: 38.4 us -> 33.1 us  [call(): pl.pallas_call(kernel, out_shape=out_shape, in_specs=specs, out_specs=jax...]
    ppermute x23 -> x24, starting transfers between devices: 35.7 us -> 40.9 us  [ring(): got.append(lax.ppermute(block, name, route))]
    slice x2 -> x0, local copies, waits for them, and re-layouts: 3.14 us -> none  [the longest x1 2.31 us: per_device(): later = passed(cot[1], -1)]
    unnamed x8, local copies, waits for them, and re-layouts: 0.02 us -> 2.12 us
  transfers between devices with their start and end apart: 29 -> 30, of which waited for: 17 -> 12; matrix products, arithmetic and copies ran while one was open for 2% -> 0% of each run, Pallas kernels for 22% -> 14%
where the time goes in v3:
time: 138 us; the launch traced here: 136 us
  waiting for transfers between devices  51.5 us (37%)
  starting transfers between devices  48.7 us (35%)
  Pallas kernels  33.1 us (24%)
  local copies, waits for them, and re-layouts  2.12 us (2%)
    ppermute x24, waiting for transfers between devices, ring(): got.append(lax.ppermute(block, name, route))  41.7 us
    ppermute x24, starting transfers between devices, ring(): got.append(lax.ppermute(block, name, route))  40.9 us
    pallas_call x19, Pallas kernels, call(): pl.pallas_call(kernel, out_shape=out_shape, in_specs=specs, out_specs=jax...  33.1 us
    ppermute x3, waiting for transfers between devices, passed(): return lax.ppermute(block, 'tm', route)  9.8 us
    ppermute x3, starting transfers between devices, passed(): return lax.ppermute(block, 'tm', route)  7.14 us
  transfers between devices with their start and end apart: 30, of which 12 were waited for; matrix products, arithmetic and copies ran while one was open for 0% of the time, Pallas kernels for 14%

profile of v3, /device:TPU:6, one launch (start us, length us, event | category | flops | bytes accessed | tf_op | source)
XLA Modules:
  0.0 136.3 jit_solution(14058423156074503092)
XLA Ops:
  5.3 4.6 %collective-permute-start.6 = (bf16[1024,256]{1,0:T(8,128)(2,1)S(1)}, bf16[1024,256]{1,0:T(8,128)(2,1)S(1)}, u32[]{:S(2)}, u32[]{:S(2)}) collective-permute-start(bf16[1024,256]{1,0:T(8,128)(2,1)S(1)} %get-tuple-element.29), channel_id=1, source_target_pairs={{0,8},{8,16},{16,24},{24,32},{32,40},{40,48},{48,56},{56,64},{64,7... | collective-permute-start | bytes 1572872 | tf_op jit(solution)/shard_map/ppermute | solution.py:381
  9.9 5.2 %collective-permute-start.2 = (f32[2,256]{1,0:T(2,128)S(1)}, f32[2,256]{1,0:T(2,128)S(1)}, u32[]{:S(2)}, u32[]{:S(2)}) collective-permute-start(f32[2,256]{1,0:T(2,128)S(1)} %shard_map.50.own.order), channel_id=1, source_target_pairs={{0,64},{8,72},{16,80},{24,88},{32,96},{40,104},{48,112},{56,120},{... | collective-permute-start | bytes 6152 | tf_op jit(solution)/shard_map/ppermute | solution.py:367
  17.0 6.3 %collective-permute-done.1.after = f32[2,256]{1,0:T(2,128)S(1)} collective-permute-done((f32[2,256]{1,0:T(2,128)S(1)}, f32[2,256]{1,0:T(2,128)S(1)}, u32[]{:S(2)}, u32[]{:S(2)}) %collective-permute-start.1) | collective-permute-done | bytes 2080 | tf_op jit(solution)/shard_map/ppermute | solution.py:367
  23.4 7.3 %collective-permute-start.4 = (f32[2,256]{1,0:T(2,128)S(1)}, f32[2,256]{1,0:T(2,128)S(1)}, u32[]{:S(2)}, u32[]{:S(2)}) collective-permute-start(f32[2,256]{1,0:T(2,128)S(1)} %shard_map.51.own.refs_0_), channel_id=1, source_target_pairs={{0,24},{8,0},{16,8},{24,16},{32,56},{40,32},{48,40},{56,48},{64,88... | collective-permute-start | bytes 6152 | tf_op jit(solution)/shard_map/ppermute | solution.py:367
  33.1 2.4 %collective-permute-done.3.before = f32[2,256]{1,0:T(2,128)S(1)} collective-permute-done((f32[2,256]{1,0:T(2,128)S(1)}, f32[2,256]{1,0:T(2,128)S(1)}, u32[]{:S(2)}, u32[]{:S(2)}) %collective-permute-start.3) | collective-permute-done | bytes 2080 | tf_op jit(solution)/shard_map/ppermute | solution.py:367
  35.9 7.2 %shard_map.56 = (bf16[3,1024,256]{2,1,0:T(8,128)(2,1)S(1)}, f32[1824,256]{1,0:T(8,128)S(1)}, bf16[1824,256]{1,0:T(8,128)(2,1)S(1)}) custom-call(s32[4]{0:T(128)S(1)} %pad_add_fusion.where, f32[2,256]{1,0:T(2,128)S(1)} %shard_map.52.stats, bf16[2,1024,256]{2,1,0:T(8,128)(2,1)S(1)} %bitcast.12, bf16[1024,256]{1,0:T(8,128)(2,1)S(1)} %collective-permute-done.6.before, ...), custom_call_target="tpu_custom_call" | custom-call | flops 905969664 | bytes 1000000 | tf_op jit(solution)/shard_map/pallas_call | solution.py:345
  44.1 2.4 %collective-permute-start.17 = (bf16[864,256]{1,0:T(8,128)(2,1)S(1)}, bf16[864,256]{1,0:T(8,128)(2,1)S(1)}, u32[]{:S(2)}, u32[]{:S(2)}) collective-permute-start(bf16[864,256]{1,0:T(8,128)(2,1)S(1)} %copy-done.3), channel_id=1, source_target_pairs={{0,2},{1,3},{2,4},{3,5},{4,6},{5,7},{6,0},{7,1},{8,10},{9,11},{10,... | collective-permute-start | bytes 1327112 | tf_op jit(solution)/shard_map/ppermute | solution.py:367
  46.7 5.2 %shard_map.57 = (f32[1824,256]{1,0:T(8,128)S(1)}, bf16[1824,256]{1,0:T(8,128)(2,1)S(1)}) custom-call(s32[4]{0:T(128)S(1)} %pad_add_fusion.where, bf16[3,1024,256]{2,1,0:T(8,128)(2,1)S(1)} %get-tuple-element.31.act, bf16[3,2,1152,256]{3,2,1,0:T(8,128)(2,1)S(1)} %shard_map.54.near, bf16[3,1,1152,256]{3,2,1,0:T(8,128)(2,1)S(1)} %shard_map.55.after, ...), custom_call_target="tpu_custom_call" | custom-call | flops 905969664 | bytes 1000000 | tf_op jit(solution)/shard_map/pallas_call | solution.py:345
  52.7 13.7 %collective-permute-done.18.right = bf16[864,256]{1,0:T(8,128)(2,1)S(1)} collective-permute-done((bf16[864,256]{1,0:T(8,128)(2,1)S(1)}, bf16[864,256]{1,0:T(8,128)(2,1)S(1)}, u32[]{:S(2)}, u32[]{:S(2)}) %collective-permute-start.18) | collective-permute-done | bytes 442400 | tf_op jit(solution)/shard_map/ppermute | solution.py:367
  69.0 2.9 %collective-permute-start.14 = (bf16[2,224,256]{2,1,0:T(8,128)(2,1)S(1)}, bf16[2,224,256]{2,1,0:T(8,128)(2,1)S(1)}, u32[]{:S(2)}, u32[]{:S(2)}) collective-permute-start(bf16[2,224,256]{2,1,0:T(8,128)(2,1)S(1)} %get-tuple-element.42), channel_id=1, source_target_pairs={{0,24},{8,0},{16,8},{24,16},{32,56},{40,32},{48,40},{56,48},{64,88... | collective-permute-start | bytes 688136 | tf_op jit(solution)/shard_map/ppermute | solution.py:367
  71.9 1.9 %collective-permute-start.15 = (bf16[2,224,256]{2,1,0:T(8,128)(2,1)S(1)}, bf16[2,224,256]{2,1,0:T(8,128)(2,1)S(1)}, u32[]{:S(2)}, u32[]{:S(2)}) collective-permute-start(bf16[2,224,256]{2,1,0:T(8,128)(2,1)S(1)} %get-tuple-element.43), channel_id=1, source_target_pairs={{0,16},{8,24},{16,0},{24,8},{32,48},{40,56},{48,32},{56,40},{64,80... | collective-permute-start | bytes 688136 | tf_op jit(solution)/shard_map/ppermute | solution.py:367
  74.6 9.8 %collective-permute-done.16 = bf16[1024,256]{1,0:T(8,128)(2,1)S(1)} collective-permute-done((bf16[1024,256]{1,0:T(8,128)(2,1)S(1)}, bf16[1024,256]{1,0:T(8,128)(2,1)S(1)}, u32[]{:S(2)}, u32[]{:S(2)}) %collective-permute-start.16) | collective-permute-done | bytes 524320 | tf_op jit(solution)/shard_map/ppermute | solution.py:381
  84.4 1.6 %collective-permute-start.11 = (bf16[2,224,256]{2,1,0:T(8,128)(2,1)S(1)}, bf16[2,224,256]{2,1,0:T(8,128)(2,1)S(1)}, u32[]{:S(2)}, u32[]{:S(2)}) collective-permute-start(bf16[2,224,256]{2,1,0:T(8,128)(2,1)S(1)} %get-tuple-element.39), channel_id=1, source_target_pairs={{0,24},{8,0},{16,8},{24,16},{32,56},{40,32},{48,40},{56,48},{64,88... | collective-permute-start | bytes 688136 | tf_op jit(solution)/shard_map/ppermute | solution.py:367
  86.3 6.1 %shard_map.62 = (f32[1024,256]{1,0:T(8,128)S(1)}, f32[2,256]{1,0:T(2,128)S(1)}, bf16[6912,256]{1,0:T(8,128)(2,1)S(1)}) custom-call(s32[4]{0:T(128)S(1)} %pad_add_fusion.where, f32[2,256]{1,0:T(2,128)S(1)} %shard_map.52.stats, bf16[2,1024,256]{2,1,0:T(8,128)(2,1)S(1)} %bitcast.13, bf16[3,2,1152,256]{3,2,1,0:T(8,128)(2,1)S(1)} %shard_map.54.near, ...), custom_call_target="tpu_custom_call" | custom-call | flops 905969664 | bytes 1000000 | tf_op jit(solution)/shard_map/pallas_call | solution.py:345
  92.4 5.4 %shard_map.63 = (f32[1024,256]{1,0:T(8,128)S(1)}, f32[2,256]{1,0:T(2,128)S(1)}) custom-call(f32[2,256]{1,0:T(2,128)S(1)} %shard_map.52.stats, bf16[2,1024,256]{2,1,0:T(8,128)(2,1)S(1)} %bitcast.14, bf16[3,2,1152,256]{3,2,1,0:T(8,128)(2,1)S(1)} %shard_map.54.near, bf16[3,1,1152,256]{3,2,1,0:T(8,128)(2,1)S(1)} %shard_map.55.after, ...), custom_call_target="tpu_custom_call" | custom-call | flops 905969664 | bytes 1000000 | tf_op jit(solution)/shard_map/pallas_call | solution.py:345
  100.0 3.0 %collective-permute-start.21 = (bf16[224,256]{1,0:T(8,128)(2,1)S(1)}, bf16[224,256]{1,0:T(8,128)(2,1)S(1)}, u32[]{:S(2)}, u32[]{:S(2)}) collective-permute-start(bf16[224,256]{1,0:T(8,128)(2,1)S(1)} %get-tuple-element.49), channel_id=1, source_target_pairs={{0,2},{1,3},{2,4},{3,5},{4,6},{5,7},{6,0},{7,1},{8,10},{9,11},{10,... | collective-permute-start | bytes 344072 | tf_op jit(solution)/shard_map/ppermute | solution.py:367
  104.5 2.0 %collective-permute-done.21.a0 = bf16[224,256]{1,0:T(8,128)(2,1)S(1)} collective-permute-done((bf16[224,256]{1,0:T(8,128)(2,1)S(1)}, bf16[224,256]{1,0:T(8,128)(2,1)S(1)}, u32[]{:S(2)}, u32[]{:S(2)}) %collective-permute-start.21) | collective-permute-done | bytes 114720 | tf_op jit(solution)/shard_map/ppermute | solution.py:367
  106.6 3.7 %collective-permute-done.22.a1 = bf16[224,256]{1,0:T(8,128)(2,1)S(1)} collective-permute-done((bf16[224,256]{1,0:T(8,128)(2,1)S(1)}, bf16[224,256]{1,0:T(8,128)(2,1)S(1)}, u32[]{:S(2)}, u32[]{:S(2)}) %collective-permute-start.22) | collective-permute-done | bytes 114720 | tf_op jit(solution)/shard_map/ppermute | solution.py:367
  112.8 3.9 %collective-permute-done.26.a2 = bf16[240,256]{1,0:T(8,128)(2,1)S(1)} collective-permute-done((bf16[240,256]{1,0:T(8,128)(2,1)S(1)}, bf16[240,256]{1,0:T(8,128)(2,1)S(1)}, u32[]{:S(2)}, u32[]{:S(2)}) %collective-permute-start.26) | collective-permute-done | bytes 122912 | tf_op jit(solution)/shard_map/ppermute | solution.py:367
  118.2 2.5 %collective-permute-start.29 = (bf16[240,256]{1,0:T(8,128)(2,1)S(1)}, bf16[240,256]{1,0:T(8,128)(2,1)S(1)}, u32[]{:S(2)}, u32[]{:S(2)}) collective-permute-start(bf16[240,256]{1,0:T(8,128)(2,1)S(1)} %shard_map.66.own), channel_id=1, source_target_pairs={{0,16},{8,24},{16,0},{24,8},{32,48},{40,56},{48,32},{56,40},{64,80... | collective-permute-start | bytes 368648 | tf_op jit(solution)/shard_map/ppermute | solution.py:367
  120.7 5.8 %collective-permute-start.28 = (bf16[240,256]{1,0:T(8,128)(2,1)S(1)}, bf16[240,256]{1,0:T(8,128)(2,1)S(1)}, u32[]{:S(2)}, u32[]{:S(2)}) collective-permute-start(bf16[240,256]{1,0:T(8,128)(2,1)S(1)} %shard_map.66.own), channel_id=1, source_target_pairs={{0,24},{8,0},{16,8},{24,16},{32,56},{40,32},{48,40},{56,48},{64,88... | collective-permute-start | bytes 368648 | tf_op jit(solution)/shard_map/ppermute | solution.py:367
  126.5 4.0 %collective-permute-done.28.a1 = bf16[240,256]{1,0:T(8,128)(2,1)S(1)} collective-permute-done((bf16[240,256]{1,0:T(8,128)(2,1)S(1)}, bf16[240,256]{1,0:T(8,128)(2,1)S(1)}, u32[]{:S(2)}, u32[]{:S(2)}) %collective-permute-start.28) | collective-permute-done | bytes 122912 | tf_op jit(solution)/shard_map/ppermute | solution.py:367
  130.5 2.1 %collective-permute-done.27.a0 = bf16[240,256]{1,0:T(8,128)(2,1)S(1)} collective-permute-done((bf16[240,256]{1,0:T(8,128)(2,1)S(1)}, bf16[240,256]{1,0:T(8,128)(2,1)S(1)}, u32[]{:S(2)}, u32[]{:S(2)}) %collective-permute-start.27) | collective-permute-done | bytes 122912 | tf_op jit(solution)/shard_map/ppermute | solution.py:367
  134.2 2.1 %shard_map.68 = bf16[2,1024,256]{2,1,0:T(8,128)(2,1)} custom-call(f32[2,256]{1,0:T(2,128)S(1)} %shard_map.52.stats, f32[2,256]{1,0:T(2,128)S(1)} %get-tuple-element.52.sums, bf16[2,1024,256]{2,1,0:T(8,128)(2,1)S(1)} %bitcast.15, bf16[2,1024,256]{2,1,0:T(8,128)(2,1)S(1)} %bitcast.18, f32[1024,256]{1,0:T(8,128)S(1)} %get-tuple-element.53.grad0, ...), custom_call_target="tpu_custom_call" | custom-call | bytes 1000000 | tf_op jit(solution)/shard_map/pallas_call | solution.py:345
  (64 shorter events, 24.2 us)
Async XLA Ops:
  4.0 31.6 %collective-permute-start.7 = (bf16[1024,256]{1,0:T(8,128)(2,1)}, bf16[1024,256]{1,0:T(8,128)(2,1)S(1)}, u32[]{:S(2)}, u32[]{:S(2)}) collective-permute-start(bf16[1024,256]{1,0:T(8,128)(2,1)} %get-tuple-element.30), channel_id=1, source_target_pairs={{8,0},{16,8},{24,16},{32,24},{40,32},{48,40},{56,48},{64,56},{72,6... | collective-permute-start | bytes 1572872 | tf_op jit(solution)/shard_map/ppermute | solution.py:381
  5.3 30.6 %collective-permute-start.6 = (bf16[1024,256]{1,0:T(8,128)(2,1)S(1)}, bf16[1024,256]{1,0:T(8,128)(2,1)S(1)}, u32[]{:S(2)}, u32[]{:S(2)}) collective-permute-start(bf16[1024,256]{1,0:T(8,128)(2,1)S(1)} %get-tuple-element.29), channel_id=1, source_target_pairs={{0,8},{8,16},{16,24},{24,32},{32,40},{40,48},{48,56},{56,64},{64,7... | collective-permute-start | bytes 1572872 | tf_op jit(solution)/shard_map/ppermute | solution.py:381
  9.9 7.2 %collective-permute-start.2 = (f32[2,256]{1,0:T(2,128)S(1)}, f32[2,256]{1,0:T(2,128)S(1)}, u32[]{:S(2)}, u32[]{:S(2)}) collective-permute-start(f32[2,256]{1,0:T(2,128)S(1)} %shard_map.50.own.order), channel_id=1, source_target_pairs={{0,64},{8,72},{16,80},{24,88},{32,96},{40,104},{48,112},{56,120},{... | collective-permute-start | bytes 6152 | tf_op jit(solution)/shard_map/ppermute | solution.py:367
  15.0 8.3 %collective-permute-start.1 = (f32[2,256]{1,0:T(2,128)S(1)}, f32[2,256]{1,0:T(2,128)S(1)}, u32[]{:S(2)}, u32[]{:S(2)}) collective-permute-start(f32[2,256]{1,0:T(2,128)S(1)} %shard_map.50.own.order), channel_id=1, source_target_pairs={{0,96},{8,104},{16,112},{24,120},{32,0},{40,8},{48,16},{56,24},{64... | collective-permute-start | bytes 6152 | tf_op jit(solution)/shard_map/ppermute | solution.py:367
  16.1 7.2 %collective-permute-start = (f32[2,256]{1,0:T(2,128)S(1)}, f32[2,256]{1,0:T(2,128)S(1)}, u32[]{:S(2)}, u32[]{:S(2)}) collective-permute-start(f32[2,256]{1,0:T(2,128)S(1)} %shard_map.50.own.order), channel_id=1, source_target_pairs={{0,32},{8,40},{16,48},{24,56},{32,64},{40,72},{48,80},{56,88},{64,... | collective-permute-start | bytes 6152 | tf_op jit(solution)/shard_map/ppermute | solution.py:367
  23.3 8.9 %collective-permute-start.5 = (f32[2,256]{1,0:T(2,128)S(1)}, f32[2,256]{1,0:T(2,128)S(1)}, u32[]{:S(2)}, u32[]{:S(2)}) collective-permute-start(f32[2,256]{1,0:T(2,128)S(1)} %shard_map.51.own.refs_0_), channel_id=1, source_target_pairs={{0,16},{8,24},{16,0},{24,8},{32,48},{40,56},{48,32},{56,40},{64,80... | collective-permute-start | bytes 6152 | tf_op jit(solution)/shard_map/ppermute | solution.py:367
  23.4 9.7 %collective-permute-start.4 = (f32[2,256]{1,0:T(2,128)S(1)}, f32[2,256]{1,0:T(2,128)S(1)}, u32[]{:S(2)}, u32[]{:S(2)}) collective-permute-start(f32[2,256]{1,0:T(2,128)S(1)} %shard_map.51.own.refs_0_), channel_id=1, source_target_pairs={{0,24},{8,0},{16,8},{24,16},{32,56},{40,32},{48,40},{56,48},{64,88... | collective-permute-start | bytes 6152 | tf_op jit(solution)/shard_map/ppermute | solution.py:367
  43.1 8.8 %collective-permute-start.9 = (bf16[1824,256]{1,0:T(8,128)(2,1)S(1)}, bf16[1824,256]{1,0:T(8,128)(2,1)S(1)}, u32[]{:S(2)}, u32[]{:S(2)}) collective-permute-start(bf16[1824,256]{1,0:T(8,128)(2,1)S(1)} %get-tuple-element.32.order), channel_id=1, source_target_pairs={{0,1},{1,0},{2,3},{3,2},{4,5},{5,4},{6,7},{7,6},{8,9},{9,8},{10,11... | collective-permute-start | bytes 2801672 | tf_op jit(solution)/shard_map/ppermute | solution.py:372
  43.2 23.3 %collective-permute-start.18 = (bf16[864,256]{1,0:T(8,128)(2,1)S(1)}, bf16[864,256]{1,0:T(8,128)(2,1)S(1)}, u32[]{:S(2)}, u32[]{:S(2)}) collective-permute-start(bf16[864,256]{1,0:T(8,128)(2,1)S(1)} %copy-done.3), channel_id=1, source_target_pairs={{0,6},{1,7},{2,0},{3,1},{4,2},{5,3},{6,4},{7,5},{8,14},{9,15},{10,... | collective-permute-start | bytes 1327112 | tf_op jit(solution)/shard_map/ppermute | solution.py:367
  44.1 22.4 %collective-permute-start.17 = (bf16[864,256]{1,0:T(8,128)(2,1)S(1)}, bf16[864,256]{1,0:T(8,128)(2,1)S(1)}, u32[]{:S(2)}, u32[]{:S(2)}) collective-permute-start(bf16[864,256]{1,0:T(8,128)(2,1)S(1)} %copy-done.3), channel_id=1, source_target_pairs={{0,2},{1,3},{2,4},{3,5},{4,6},{5,7},{6,0},{7,1},{8,10},{9,11},{10,... | collective-permute-start | bytes 1327112 | tf_op jit(solution)/shard_map/ppermute | solution.py:367
  46.5 20.0 %collective-permute-start.19 = (bf16[864,256]{1,0:T(8,128)(2,1)S(1)}, bf16[864,256]{1,0:T(8,128)(2,1)S(1)}, u32[]{:S(2)}, u32[]{:S(2)}) collective-permute-start(bf16[864,256]{1,0:T(8,128)(2,1)S(1)} %copy-done.3), channel_id=1, source_target_pairs={{0,4},{1,5},{2,6},{3,7},{4,0},{5,1},{6,2},{7,3},{8,12},{9,13},{10,... | collective-permute-start | bytes 1327112 | tf_op jit(solution)/shard_map/ppermute | solution.py:367
  52.6 13.8 %collective-permute-start.13 = (bf16[2,224,256]{2,1,0:T(8,128)(2,1)S(1)}, bf16[2,224,256]{2,1,0:T(8,128)(2,1)S(1)}, u32[]{:S(2)}, u32[]{:S(2)}) collective-permute-start(bf16[2,224,256]{2,1,0:T(8,128)(2,1)S(1)} %get-tuple-element.41), channel_id=1, source_target_pairs={{0,8},{8,16},{16,24},{24,0},{32,40},{40,48},{48,56},{56,32},{64,72... | collective-permute-start | bytes 688136 | tf_op jit(solution)/shard_map/ppermute | solution.py:367
  67.1 18.8 %collective-permute-start.20 = (bf16[4,864,256]{2,1,0:T(8,128)(2,1)S(1)}, bf16[4,864,256]{2,1,0:T(8,128)(2,1)S(1)}, u32[]{:S(2)}, u32[]{:S(2)}) collective-permute-start(bf16[4,864,256]{2,1,0:T(8,128)(2,1)S(1)} %shard_map.61.mine), channel_id=1, source_target_pairs={{0,1},{1,0},{2,3},{3,2},{4,5},{5,4},{6,7},{7,6},{8,9},{9,8},{10,11... | collective-permute-start | bytes 5308424 | tf_op jit(solution)/shard_map/ppermute | solution.py:372
  67.7 16.7 %collective-permute-start.16 = (bf16[1024,256]{1,0:T(8,128)(2,1)S(1)}, bf16[1024,256]{1,0:T(8,128)(2,1)S(1)}, u32[]{:S(2)}, u32[]{:S(2)}) collective-permute-start(bf16[1024,256]{1,0:T(8,128)(2,1)S(1)} %get-tuple-element.44), channel_id=1, source_target_pairs={{8,0},{16,8},{24,16},{32,24},{40,32},{48,40},{56,48},{64,56},{72,6... | collective-permute-start | bytes 1572872 | tf_op jit(solution)/shard_map/ppermute | solution.py:381
  69.0 28.9 %collective-permute-start.14 = (bf16[2,224,256]{2,1,0:T(8,128)(2,1)S(1)}, bf16[2,224,256]{2,1,0:T(8,128)(2,1)S(1)}, u32[]{:S(2)}, u32[]{:S(2)}) collective-permute-start(bf16[2,224,256]{2,1,0:T(8,128)(2,1)S(1)} %get-tuple-element.42), channel_id=1, source_target_pairs={{0,24},{8,0},{16,8},{24,16},{32,56},{40,32},{48,40},{56,48},{64,88... | collective-permute-start | bytes 688136 | tf_op jit(solution)/shard_map/ppermute | solution.py:367
  71.9 26.0 %collective-permute-start.15 = (bf16[2,224,256]{2,1,0:T(8,128)(2,1)S(1)}, bf16[2,224,256]{2,1,0:T(8,128)(2,1)S(1)}, u32[]{:S(2)}, u32[]{:S(2)}) collective-permute-start(bf16[2,224,256]{2,1,0:T(8,128)(2,1)S(1)} %get-tuple-element.43), channel_id=1, source_target_pairs={{0,16},{8,24},{16,0},{24,8},{32,48},{40,56},{48,32},{56,40},{64,80... | collective-permute-start | bytes 688136 | tf_op jit(solution)/shard_map/ppermute | solution.py:367
  74.5 23.4 %collective-permute-start.10 = (bf16[2,224,256]{2,1,0:T(8,128)(2,1)S(1)}, bf16[2,224,256]{2,1,0:T(8,128)(2,1)S(1)}, u32[]{:S(2)}, u32[]{:S(2)}) collective-permute-start(bf16[2,224,256]{2,1,0:T(8,128)(2,1)S(1)} %get-tuple-element.38), channel_id=1, source_target_pairs={{0,8},{8,16},{16,24},{24,0},{32,40},{40,48},{48,56},{56,32},{64,72... | collective-permute-start | bytes 688136 | tf_op jit(solution)/shard_map/ppermute | solution.py:367
  84.4 14.8 %collective-permute-start.11 = (bf16[2,224,256]{2,1,0:T(8,128)(2,1)S(1)}, bf16[2,224,256]{2,1,0:T(8,128)(2,1)S(1)}, u32[]{:S(2)}, u32[]{:S(2)}) collective-permute-start(bf16[2,224,256]{2,1,0:T(8,128)(2,1)S(1)} %get-tuple-element.39), channel_id=1, source_target_pairs={{0,24},{8,0},{16,8},{24,16},{32,56},{40,32},{48,40},{56,48},{64,88... | collective-permute-start | bytes 688136 | tf_op jit(solution)/shard_map/ppermute | solution.py:367
  86.0 13.2 %collective-permute-start.12 = (bf16[2,224,256]{2,1,0:T(8,128)(2,1)S(1)}, bf16[2,224,256]{2,1,0:T(8,128)(2,1)S(1)}, u32[]{:S(2)}, u32[]{:S(2)}) collective-permute-start(bf16[2,224,256]{2,1,0:T(8,128)(2,1)S(1)} %get-tuple-element.40), channel_id=1, source_target_pairs={{0,16},{8,24},{16,0},{24,8},{32,48},{40,56},{48,32},{56,40},{64,80... | collective-permute-start | bytes 688136 | tf_op jit(solution)/shard_map/ppermute | solution.py:367
  100.0 6.6 %collective-permute-start.21 = (bf16[224,256]{1,0:T(8,128)(2,1)S(1)}, bf16[224,256]{1,0:T(8,128)(2,1)S(1)}, u32[]{:S(2)}, u32[]{:S(2)}) collective-permute-start(bf16[224,256]{1,0:T(8,128)(2,1)S(1)} %get-tuple-element.49), channel_id=1, source_target_pairs={{0,2},{1,3},{2,4},{3,5},{4,6},{5,7},{6,0},{7,1},{8,10},{9,11},{10,... | collective-permute-start | bytes 344072 | tf_op jit(solution)/shard_map/ppermute | solution.py:367
  103.0 7.2 %collective-permute-start.22 = (bf16[224,256]{1,0:T(8,128)(2,1)S(1)}, bf16[224,256]{1,0:T(8,128)(2,1)S(1)}, u32[]{:S(2)}, u32[]{:S(2)}) collective-permute-start(bf16[224,256]{1,0:T(8,128)(2,1)S(1)} %get-tuple-element.50), channel_id=1, source_target_pairs={{0,6},{1,7},{2,0},{3,1},{4,2},{5,3},{6,4},{7,5},{8,14},{9,15},{10,... | collective-permute-start | bytes 344072 | tf_op jit(solution)/shard_map/ppermute | solution.py:367
  103.0 7.2 %collective-permute-start.23 = (bf16[224,256]{1,0:T(8,128)(2,1)S(1)}, bf16[224,256]{1,0:T(8,128)(2,1)S(1)}, u32[]{:S(2)}, u32[]{:S(2)}) collective-permute-start(bf16[224,256]{1,0:T(8,128)(2,1)S(1)} %get-tuple-element.51), channel_id=1, source_target_pairs={{0,4},{1,5},{2,6},{3,7},{4,0},{5,1},{6,2},{7,3},{8,12},{9,13},{10,... | collective-permute-start | bytes 344072 | tf_op jit(solution)/shard_map/ppermute | solution.py:367
  118.2 8.3 %collective-permute-start.29 = (bf16[240,256]{1,0:T(8,128)(2,1)S(1)}, bf16[240,256]{1,0:T(8,128)(2,1)S(1)}, u32[]{:S(2)}, u32[]{:S(2)}) collective-permute-start(bf16[240,256]{1,0:T(8,128)(2,1)S(1)} %shard_map.66.own), channel_id=1, source_target_pairs={{0,16},{8,24},{16,0},{24,8},{32,48},{40,56},{48,32},{56,40},{64,80... | collective-permute-start | bytes 368648 | tf_op jit(solution)/shard_map/ppermute | solution.py:367
  120.7 9.8 %collective-permute-start.28 = (bf16[240,256]{1,0:T(8,128)(2,1)S(1)}, bf16[240,256]{1,0:T(8,128)(2,1)S(1)}, u32[]{:S(2)}, u32[]{:S(2)}) collective-permute-start(bf16[240,256]{1,0:T(8,128)(2,1)S(1)} %shard_map.66.own), channel_id=1, source_target_pairs={{0,24},{8,0},{16,8},{24,16},{32,56},{40,32},{48,40},{56,48},{64,88... | collective-permute-start | bytes 368648 | tf_op jit(solution)/shard_map/ppermute | solution.py:367
  (10 other events, 49.6 us)

commit v4 on v3

--- a/solution.py
+++ b/solution.py
@@ -132,48 +132,52 @@
     for tap in range(low, high):
         kh, kw = tap // 3 % 3, tap % 3
         rows = slice((2 - kh) * W, (2 - kh) * W + ROWS)
-        total = tap_product((act[1], act[2]), (near[kw, 1, rows], after[kw, 0, rows]), channels)
+        total = tap_product((act[0], act[1]), (near[kw, 1, rows], after[kw, 0, rows]), channels)
         store_tap(tap, total * scale, channels.start // UNIT, core, keep, send)
 
 
-def upper_kernel(count, scale, where, stats, clip, before, near, after, act, keep, send):
+def activate(center, inverse, frame, act, gain=None):
+    @pl.loop(0, ROWS // 64)
+    def _(i):
+        at = pl.ds(pl.multiple_of(i * 64, 64), 64)
+        v = (frame(at).astype(f32) - center) * inverse
+        v = v * sigmoid(v)
+        if gain is not None:
+            v = v * gain
+        act[at] = v.astype(bf16)
+
+
+def near_kernel(count, scale, where, stats, clip, near, act, keep, send):
     center, inverse = center_inverse(stats[...], count)
-    core = where[1]
-
-    def activate(frame, slot, gain):
-        @pl.loop(0, ROWS // 64)
-        def _(i):
-            at = pl.ds(pl.multiple_of(i * 64, 64), 64)
-            v = (frame(at).astype(f32) - center) * inverse
-            v = v * sigmoid(v)
-            if gain is not None:
-                v = v * gain
-            act[slot, at] = v.astype(bf16)
-
-    activate(lambda at: before[at], 0, jnp.where(where[0] == 1, 0.0, 1.0))
-    activate(lambda at: clip[0, at], 1, None)
-    activate(lambda at: clip[1, at], 2, None)
+    for t in range(2):
+        activate(center, inverse, lambda at, t=t: clip[t, at], act.at[t])
 
     @pl.loop(0, 3)
     def _(kh):
         rows = tap_rows(kh)
         for kw in range(3):
-            total = tap_product((act[1], act[2]), (near[kw, 0, rows], near[kw, 1, rows]), slice(None))
-            store_tap(18 + kh * 3 + kw, total * scale, 0, core, keep, send)
-
-    middle_taps(14, 18, slice(0, C), scale, core, act, near, after, keep, send)
-    middle_taps(13, 14, slice(HALF, C), scale, core, act, near, after, keep, send)
+            total = tap_product((act[0], act[1]), (near[kw, 0, rows], near[kw, 1, rows]), slice(None))
+            store_tap(18 + kh * 3 + kw, total * scale, 0, where[1], keep, send)
+
     clear_tails(keep, send)
 
 
-def lower_kernel(scale, where, act, near, after, order, keep, send):
+def upper_kernel(scale, where, act, near, after, keep_in, send_in, order, keep, send):
+    middle_taps(14, 18, slice(0, C), scale, where[1], act, near, after, keep, send)
+    middle_taps(13, 14, slice(HALF, C), scale, where[1], act, near, after, keep, send)
+
+
+def lower_kernel(count, scale, where, stats, act, before, near, after, order, keep, send, act_before):
     core = where[1]
+    center, inverse = center_inverse(stats[...], count)
+    gain = jnp.where(where[0] == 1, 0.0, 1.0)
+    activate(center, inverse, lambda at: before[at], act_before, gain)
 
     @pl.loop(0, 3)
     def _(kh):
         rows = tap_rows(kh)
         for kw in range(3):
-            total = tap_product((act[0], act[1]), (near[kw, 1, rows], after[kw, 0, rows]), slice(None))
+            total = tap_product((act_before, act[0]), (near[kw, 1, rows], after[kw, 0, rows]), slice(None))
             store_tap(kh * 3 + kw, total * scale, 0, core, keep, send)
 
     middle_taps(9, 13, slice(0, C), scale, core, act, near, after, keep, send)
@@ -220,7 +224,7 @@
     sums[1:2] = b.sum(0, keepdims=True)
 
 
-def first_grad_kernel(count, where, stats, clip, near, after, mine, other, order0, order1, grad, sums, full):
+def first_grad_kernel(count, where, stats, clip, near, after, mine, other, order, grad, sums, full):
     core = where[1]
     for x in range(4):
         full[pl.ds(pl.multiple_of((2 * x + core) * SHARD, UNIT), SHARD)] = mine[x]
@@ -259,24 +263,25 @@
 STEPS = (1, 3, 2)
 
 
-def split_core_kernel(where, keep, got, order, held, *out):
-    z = where[3]
+def split_core_kernel(where, keep, got, *refs):
+    y = where[3]
+    held, *out = refs[-4:]
 
     def add(x, quarter):
         at = pl.ds(pl.multiple_of(x * SHARD_PAD + quarter * QUARTER, UNIT), QUARTER)
         return keep[at] + got[at].astype(f32)
 
     for x in range(2):
-        held[x] = add(x, z)
+        held[x] = add(x, y)
         for step, to in zip(STEPS, out):
-            to[x] = add(x, (z + step) & 3).astype(bf16)
+            to[x] = add(x, (y + step) & 3).astype(bf16)
 
 
 def ring_add(own, arrived, at):
     return (own[at].astype(f32) + arrived[2][at].astype(f32)) + (arrived[0][at].astype(f32) + arrived[1][at].astype(f32))
 
 
-def split_z_kernel(where, low, l0, l1, l2, up, u0, u1, u2, order, held, *out):
+def split_y_kernel(where, low, l0, l1, l2, up, u0, u1, u2, order, held, *out):
     x_own = where[2]
 
     def total(x, use):
@@ -330,15 +335,15 @@
 
 
 def finish_kernel(where, own, a0, a1, a2, grad_weight, sums, full):
-    z = where[3]
+    y = where[3]
     for block, distance in ((own, 0), (a0, 3), (a1, 1), (a2, 2)):
-        at = pl.ds(pl.multiple_of(((z + distance) & 3) * QUARTER, UNIT), QUARTER)
+        at = pl.ds(pl.multiple_of(((y + distance) & 3) * QUARTER, UNIT), QUARTER)
         full[at] = block[:QUARTER].astype(f32)
     grad_weight[...] = full[:SHARD]
     sums[...] = ring_sums(own, (a0, a1, a2))
 
 
-def call(kernel, out_shape, args, scratch=(), flops=0, bytes_accessed=1_000_000, scalars=0, order=()):
+def call(kernel, out_shape, args, scratch=(), flops=0, bytes_accessed=0, scalars=0, order=(), aliases={}):
     specs = [pl.BlockSpec(memory_space=pltpu.SMEM)] * scalars
     specs += [pl.BlockSpec(memory_space=pltpu.VMEM)] * (len(args) - scalars)
     specs += [pl.BlockSpec(memory_space=pl.ANY)] * len(order)
@@ -348,6 +353,7 @@
         in_specs=specs,
         out_specs=jax.tree.map(lambda _: pl.BlockSpec(memory_space=pltpu.VMEM), out_shape),
         scratch_shapes=list(scratch),
+        input_output_aliases=aliases,
         compiler_params=pltpu.CompilerParams(vmem_limit_bytes=VMEM),
         cost_estimate=pl.CostEstimate(flops=flops, bytes_accessed=bytes_accessed, transcendentals=0),
     )(*args, *order)
@@ -368,12 +374,21 @@
     return got
 
 
+def swap(block, axis, partners):
+    name, size, stride = AXES[axis]
+    route = []
+    for i in range(size):
+        place = (i // stride) % 4
+        route.append((i, i + (partners[place] - place) * stride))
+    return lax.ppermute(block, name, route)
+
+
 def swap_core(block):
     return lax.ppermute(block, "fsdp", [(i, i ^ 1) for i in range(8)])
 
 
-def ring_sum(values, axis):
-    return call(ring_sum_kernel, jax.ShapeDtypeStruct(values.shape, f32), (values, *ring(axis, [values] * 3)))
+def ring_sum(values, got):
+    return call(ring_sum_kernel, jax.ShapeDtypeStruct(values.shape, f32), (values, *got))
 
 
 def passed(block, distance):
@@ -391,70 +406,81 @@
     S = jax.ShapeDtypeStruct
     tm = lax.axis_index("tm")
     fsdp = lax.axis_index("fsdp")
-    where = [tm == 0, fsdp & 1, fsdp >> 1, tm & 3]
+    where = [tm == 0, fsdp & 1, fsdp >> 1, tm >> 2]
     where = jnp.stack([jnp.asarray(v, jnp.int32) for v in where])
     frame = S((ROWS, C), bf16)
 
     sums = call(stats_kernel, S((2, C), f32), (clip.reshape(2 * ROWS, C),))
+    sums = ring_sum(sums, ring("z", [sums] * 3))
     first, second, last = call(copy_kernel, (frame, frame, frame), (clip, cot), order=(sums,))
-    sums = ring_sum(sums, "y")
     near = call(widths_kernel, S((3, 2, PADDED, C), bf16), (cot,), order=(sums,))
-    stats = ring_sum(sums, "z")
+    half = sums + swap(sums, "y", (1, 0, 3, 2))
+    stats = half + swap(half, "y", (3, 2, 1, 0))
     after = call(widths_kernel, S((3, 1, PADDED, C), bf16), (passed(first, -1)[None],))
     before = passed(last, 1)
     later = call(widths_kernel, S((3, 1, PADDED, C), bf16), (passed(second, -1)[None],))
-    gathered = ring("x", [weights] * 3)
 
     rows = 2 * SHARD_PAD + UNIT
-    half_flops = 27 * C * C * 2 * ROWS // 4
+    tap_flops = C * C * 2 * ROWS * 2
+    pieces = (S((rows, C), f32), S((rows, C), bf16))
     act, keep_up, send_up = call(
-        partial(upper_kernel, count, scale),
-        (S((3, ROWS, C), bf16), S((rows, C), f32), S((rows, C), bf16)),
-        (where, stats, clip, before, near, after),
-        flops=half_flops,
+        partial(near_kernel, count, scale),
+        (S((2, ROWS, C), bf16), *pieces),
+        (where, stats, clip, near),
+        flops=9 * tap_flops,
         scalars=1,
+    )
+    mine = call(pack_kernel, S((4, SHARD, C), bf16), (where, weights, *ring("x", [weights] * 3)), scalars=1, order=(act,))
+    other = swap_core(mine)
+    keep_up, send_up = call(
+        partial(upper_kernel, scale),
+        pieces,
+        (where, act, near, after, keep_up, send_up),
+        flops=9 * tap_flops // 2,
+        scalars=1,
+        order=(mine,),
+        aliases={4: 0, 5: 1},
     )
     got_up = swap_core(send_up)
     keep_low, send_low = call(
-        partial(lower_kernel, scale),
-        (S((rows, C), f32), S((rows, C), bf16)),
-        (where, act, near, after),
-        flops=half_flops,
+        partial(lower_kernel, count, scale),
+        pieces,
+        (where, stats, act, before, near, after),
+        [pltpu.VMEM((ROWS, C), bf16)],
+        flops=27 * tap_flops // 2,
         scalars=1,
         order=(send_up,),
     )
     got_low = swap_core(send_low)
+
     block = lambda *dims: (S(dims + (QUARTER, C), f32),) + (S(dims + (QUARTER, C), bf16),) * 3
     up, *out_up = call(split_core_kernel, block(2), (where, keep_up, got_up), scalars=1, order=(keep_low,))
     low, *out_low = call(split_core_kernel, block(2), (where, keep_low, got_low), scalars=1, order=(up,))
-    arrived_up = ring("z", out_up)
-    mine = call(pack_kernel, S((4, SHARD, C), bf16), (where, weights, *gathered), scalars=1, order=(arrived_up[0],))
-    other = swap_core(mine)
     grad0, sums0, full = call(
         partial(first_grad_kernel, count),
         (S((ROWS, C), f32), S((2, C), f32), S((8 * SHARD, C), bf16)),
         (where, stats, clip, near, after, mine, other),
-        flops=half_flops,
+        flops=27 * tap_flops // 2,
         scalars=1,
-        order=(later, low),
+        order=(low,),
     )
     grad1, sums1 = call(
         partial(second_grad_kernel, count),
         (S((ROWS, C), f32), S((2, C), f32)),
         (stats, clip, near, after, later, full),
-        flops=half_flops,
+        flops=27 * tap_flops // 2,
         order=(sums0,),
     )
-    got = (low, *ring("z", out_low), up, *arrived_up)
-    held, *out = call(split_z_kernel, block(), (where, *got), scalars=1, order=(sums1,))
+    got = (low, *ring("y", out_low), up, *ring("y", out_up))
+    held, *out = call(split_y_kernel, block(), (where, *got), scalars=1, order=(sums1,))
     rows16 = [pltpu.VMEM((16, C), f32)]
     message = S((QUARTER + 16, C), bf16)
     own = call(split_x_kernel, message, (held, *ring("x", out), sums0, sums1), rows16)
-    own = call(reduced_kernel, message, (own, *ring("y", [own] * 3)), rows16)
+    own = call(reduced_kernel, message, (own, *ring("z", [own] * 3)), rows16)
     grad_weight, sums = call(
         finish_kernel,
         (S((SHARD, C), f32), S((2, C), f32)),
-        (where, own, *ring("z", [own] * 3)),
+        (where, own, *ring("y", [own] * 3)),
         [pltpu.VMEM((SHARD_PAD, C), f32)],
         scalars=1,
     )

time: 138 us -> 127 us (0.920)
  waiting for transfers between devices: 51.5 us -> 39.8 us
  starting transfers between devices: 48.7 us -> 47.3 us
    ppermute x24 -> x21, waiting for transfers between devices: 41.7 us -> 22.9 us  [ring(): got.append(lax.ppermute(block, name, route))]
    ppermute x24 -> x21, starting transfers between devices: 40.9 us -> 34.8 us  [ring(): got.append(lax.ppermute(block, name, route))]
    ppermute x3, waiting for transfers between devices: 9.8 us -> 14.9 us  [passed(): return lax.ppermute(block, 'tm', route)]
    ppermute x0 -> x2, starting transfers between devices: none -> 4.59 us  [swap(): return lax.ppermute(block, name, route)]
    ppermute x0 -> x2, waiting for transfers between devices: none -> 2.01 us  [swap(): return lax.ppermute(block, name, route)]
    unnamed x8 -> x10, local copies, waits for them, and re-layouts: 2.12 us -> 3.43 us
  transfers between devices with their start and end apart: 30 -> 29, of which waited for: 12 -> 12; matrix products, arithmetic and copies ran while one was open for 0% -> 0% of each run, Pallas kernels for 14% -> 23%
where the time goes in v4:
time: 127 us; the launch traced here: 125 us
  starting transfers between devices  47.3 us (37%)
  waiting for transfers between devices  39.8 us (31%)
  Pallas kernels  33.1 us (26%)
  local copies, waits for them, and re-layouts  3.43 us (3%)
    ppermute x21, starting transfers between devices, ring(): got.append(lax.ppermute(block, name, route))  34.8 us
    pallas_call x19, Pallas kernels, call(): pl.pallas_call(kernel, out_shape=out_shape, in_specs=specs, out_specs=jax...  33.1 us
    ppermute x21, waiting for transfers between devices, ring(): got.append(lax.ppermute(block, name, route))  22.9 us
    ppermute x3, waiting for transfers between devices, passed(): return lax.ppermute(block, 'tm', route)  14.9 us
    ppermute x3, starting transfers between devices, passed(): return lax.ppermute(block, 'tm', route)  7.15 us
    ppermute x2, starting transfers between devices, swap(): return lax.ppermute(block, name, route)  4.59 us
    unnamed x10, local copies, waits for them, and re-layouts  3.43 us
  transfers between devices with their start and end apart: 29, of which 12 were waited for; matrix products, arithmetic and copies ran while one was open for 0% of the time, Pallas kernels for 23%

profile of v4, /device:TPU:6, one launch (start us, length us, event | category | flops | bytes accessed | tf_op | source)
XLA Modules:
  0.0 124.7 jit_solution(15066784186992090856)
XLA Ops:
  5.7 2.0 %collective-permute-start = (f32[2,256]{1,0:T(2,128)S(1)}, f32[2,256]{1,0:T(2,128)S(1)}, u32[]{:S(2)}, u32[]{:S(2)}) collective-permute-start(f32[2,256]{1,0:T(2,128)S(1)} %shard_map.50.own), channel_id=1, source_target_pairs={{0,8},{8,16},{16,24},{24,0},{32,40},{40,48},{48,56},{56,32},{64,72... | collective-permute-start | bytes 6152 | tf_op jit(solution)/shard_map/ppermute | solution.py:373
  7.7 2.2 %collective-permute-start.1 = (f32[2,256]{1,0:T(2,128)S(1)}, f32[2,256]{1,0:T(2,128)S(1)}, u32[]{:S(2)}, u32[]{:S(2)}) collective-permute-start(f32[2,256]{1,0:T(2,128)S(1)} %shard_map.50.own), channel_id=1, source_target_pairs={{0,24},{8,0},{16,8},{24,16},{32,56},{40,32},{48,40},{56,48},{64,88... | collective-permute-start | bytes 6152 | tf_op jit(solution)/shard_map/ppermute | solution.py:373
  13.2 3.2 %collective-permute-done.2.far = f32[2,256]{1,0:T(2,128)S(1)} collective-permute-done((f32[2,256]{1,0:T(2,128)S(1)}, f32[2,256]{1,0:T(2,128)S(1)}, u32[]{:S(2)}, u32[]{:S(2)}) %collective-permute-start.2) | collective-permute-done | bytes 2080 | tf_op jit(solution)/shard_map/ppermute | solution.py:373
  18.0 2.0 %collective-permute-done.3 = f32[2,256]{1,0:T(2,128)S(1)} collective-permute-done((f32[2,256]{1,0:T(2,128)S(1)}, f32[2,256]{1,0:T(2,128)S(1)}, u32[]{:S(2)}, u32[]{:S(2)}) %collective-permute-start.3) | collective-permute-done | bytes 2080 | tf_op jit(solution)/shard_map/ppermute | solution.py:383
  20.1 3.0 %collective-permute-start.4 = (f32[2,256]{1,0:T(2,128)S(1)}, f32[2,256]{1,0:T(2,128)S(1)}, u32[]{:S(2)}, u32[]{:S(2)}) collective-permute-start(f32[2,256]{1,0:T(2,128)S(1)} %add.6), channel_id=1, source_target_pairs={{0,96},{8,104},{16,112},{24,120},{32,64},{40,72},{48,80},{56,88},{... | collective-permute-start | bytes 6152 | tf_op jit(solution)/shard_map/ppermute | solution.py:383
  27.3 4.6 %collective-permute-start.5 = (bf16[1024,256]{1,0:T(8,128)(2,1)S(1)}, bf16[1024,256]{1,0:T(8,128)(2,1)S(1)}, u32[]{:S(2)}, u32[]{:S(2)}) collective-permute-start(bf16[1024,256]{1,0:T(8,128)(2,1)S(1)} %get-tuple-element.32), channel_id=1, source_target_pairs={{0,8},{8,16},{16,24},{24,32},{32,40},{40,48},{48,56},{56,64},{64,7... | collective-permute-start | bytes 1572872 | tf_op jit(solution)/shard_map/ppermute | solution.py:396
  31.9 5.2 %shard_map.53 = (bf16[2,1024,256]{2,1,0:T(8,128)(2,1)S(1)}, f32[1824,256]{1,0:T(8,128)S(1)}, bf16[1824,256]{1,0:T(8,128)(2,1)S(1)}) custom-call(s32[4]{0:T(128)S(1)} %pad_add_fusion.where, f32[2,256]{1,0:T(2,128)S(1)} %add.7.stats, bf16[2,1024,256]{2,1,0:T(8,128)(2,1)S(1)} %bitcast.12, bf16[3,2,1152,256]{3,2,1,0:T(8,128)(2,1)S(1)} %shard_map.52.near), custom_call_target="tpu_custom_call" | custom-call | flops 2415919104 | tf_op jit(solution)/shard_map/pallas_call | solution.py:350
  38.2 2.0 %shard_map.57 = (f32[1824,256]{1,0:T(8,128)S(1)}, bf16[1824,256]{1,0:T(8,128)(2,1)S(1)}) custom-call(s32[4]{0:T(128)S(1)} %pad_add_fusion.where, bf16[2,1024,256]{2,1,0:T(8,128)(2,1)S(1)} %get-tuple-element.31.order.act, bf16[3,2,1152,256]{3,2,1,0:T(8,128)(2,1)S(1)} %shard_map.52.near, ...), custom_call_target="tpu_custom_call", output_to_operand_aliasing={{0}: (4, {}), {1}: (5, {})} | custom-call | flops 1207959552 | tf_op jit(solution)/shard_map/pallas_call | solution.py:350
  40.8 6.1 %shard_map.58 = (f32[1824,256]{1,0:T(8,128)S(1)}, bf16[1824,256]{1,0:T(8,128)(2,1)S(1)}) custom-call(s32[4]{0:T(128)S(1)} %pad_add_fusion.where, f32[2,256]{1,0:T(2,128)S(1)} %add.7.stats, bf16[2,1024,256]{2,1,0:T(8,128)(2,1)S(1)} %get-tuple-element.31.order.act, bf16[1024,256]{1,0:T(8,128)(2,1)S(1)} %collective-permute-done.5.before, ...), custom_call_target="tpu_custom_call" | custom-call | flops 3623878656 | tf_op jit(solution)/shard_map/pallas_call | solution.py:350
  48.3 14.9 %collective-permute-done.18 = bf16[1024,256]{1,0:T(8,128)(2,1)S(1)} collective-permute-done((bf16[1024,256]{1,0:T(8,128)(2,1)S(1)}, bf16[1024,256]{1,0:T(8,128)(2,1)S(1)}, u32[]{:S(2)}, u32[]{:S(2)}) %collective-permute-start.18) | collective-permute-done | bytes 524320 | tf_op jit(solution)/shard_map/ppermute | solution.py:396
  64.9 4.1 %collective-permute-start.12 = (bf16[2,224,256]{2,1,0:T(8,128)(2,1)S(1)}, bf16[2,224,256]{2,1,0:T(8,128)(2,1)S(1)}, u32[]{:S(2)}, u32[]{:S(2)}) collective-permute-start(bf16[2,224,256]{2,1,0:T(8,128)(2,1)S(1)} %get-tuple-element.42), channel_id=1, source_target_pairs={{0,32},{8,40},{16,48},{24,56},{32,64},{40,72},{48,80},{56,88},{64,... | collective-permute-start | bytes 688136 | tf_op jit(solution)/shard_map/ppermute | solution.py:373
  69.0 2.2 %collective-permute-start.14 = (bf16[2,224,256]{2,1,0:T(8,128)(2,1)S(1)}, bf16[2,224,256]{2,1,0:T(8,128)(2,1)S(1)}, u32[]{:S(2)}, u32[]{:S(2)}) collective-permute-start(bf16[2,224,256]{2,1,0:T(8,128)(2,1)S(1)} %get-tuple-element.44), channel_id=1, source_target_pairs={{0,64},{8,72},{16,80},{24,88},{32,96},{40,104},{48,112},{56,120},{... | collective-permute-start | bytes 688136 | tf_op jit(solution)/shard_map/ppermute | solution.py:373
  71.2 3.2 %collective-permute-start.16 = (bf16[2,224,256]{2,1,0:T(8,128)(2,1)S(1)}, bf16[2,224,256]{2,1,0:T(8,128)(2,1)S(1)}, u32[]{:S(2)}, u32[]{:S(2)}) collective-permute-start(bf16[2,224,256]{2,1,0:T(8,128)(2,1)S(1)} %get-tuple-element.46), channel_id=1, source_target_pairs={{0,96},{8,104},{16,112},{24,120},{32,0},{40,8},{48,16},{56,24},{64... | collective-permute-start | bytes 688136 | tf_op jit(solution)/shard_map/ppermute | solution.py:373
  74.5 6.1 %shard_map.62 = (f32[1024,256]{1,0:T(8,128)S(1)}, f32[2,256]{1,0:T(2,128)S(1)}, bf16[6912,256]{1,0:T(8,128)(2,1)S(1)}) custom-call(s32[4]{0:T(128)S(1)} %pad_add_fusion.where, f32[2,256]{1,0:T(2,128)S(1)} %add.7.stats, bf16[2,1024,256]{2,1,0:T(8,128)(2,1)S(1)} %bitcast.13, bf16[3,2,1152,256]{3,2,1,0:T(8,128)(2,1)S(1)} %shard_map.52.near, ...), custom_call_target="tpu_custom_call" | custom-call | flops 3623878656 | tf_op jit(solution)/shard_map/pallas_call | solution.py:350
  81.4 5.4 %shard_map.63 = (f32[1024,256]{1,0:T(8,128)S(1)}, f32[2,256]{1,0:T(2,128)S(1)}) custom-call(f32[2,256]{1,0:T(2,128)S(1)} %add.7.stats, bf16[2,1024,256]{2,1,0:T(8,128)(2,1)S(1)} %bitcast.14, bf16[3,2,1152,256]{3,2,1,0:T(8,128)(2,1)S(1)} %shard_map.52.near, bf16[3,1,1152,256]{3,2,1,0:T(8,128)(2,1)S(1)} %shard_map.55.after, ...), custom_call_target="tpu_custom_call" | custom-call | flops 3623878656 | tf_op jit(solution)/shard_map/pallas_call | solution.py:350
  87.4 2.2 %collective-permute-done.17.u2 = bf16[2,224,256]{2,1,0:T(8,128)(2,1)S(1)} collective-permute-done((bf16[2,224,256]{2,1,0:T(8,128)(2,1)S(1)}, bf16[2,224,256]{2,1,0:T(8,128)(2,1)S(1)}, u32[]{:S(2)}, u32[]{:S(2)}) %collective-permute-start.17) | collective-permute-done | bytes 229408 | tf_op jit(solution)/shard_map/ppermute | solution.py:373
  90.4 2.2 %collective-permute-start.20 = (bf16[224,256]{1,0:T(8,128)(2,1)S(1)}, bf16[224,256]{1,0:T(8,128)(2,1)S(1)}, u32[]{:S(2)}, u32[]{:S(2)}) collective-permute-start(bf16[224,256]{1,0:T(8,128)(2,1)S(1)} %get-tuple-element.53), channel_id=1, source_target_pairs={{0,2},{1,3},{2,4},{3,5},{4,6},{5,7},{6,0},{7,1},{8,10},{9,11},{10,... | collective-permute-start | bytes 344072 | tf_op jit(solution)/shard_map/ppermute | solution.py:373
  92.6 2.1 %collective-permute-start.22 = (bf16[224,256]{1,0:T(8,128)(2,1)S(1)}, bf16[224,256]{1,0:T(8,128)(2,1)S(1)}, u32[]{:S(2)}, u32[]{:S(2)}) collective-permute-start(bf16[224,256]{1,0:T(8,128)(2,1)S(1)} %get-tuple-element.55), channel_id=1, source_target_pairs={{0,4},{1,5},{2,6},{3,7},{4,0},{5,1},{6,2},{7,3},{8,12},{9,13},{10,... | collective-permute-start | bytes 344072 | tf_op jit(solution)/shard_map/ppermute | solution.py:373
  96.2 3.7 %collective-permute-done.21.a1 = bf16[224,256]{1,0:T(8,128)(2,1)S(1)} collective-permute-done((bf16[224,256]{1,0:T(8,128)(2,1)S(1)}, bf16[224,256]{1,0:T(8,128)(2,1)S(1)}, u32[]{:S(2)}, u32[]{:S(2)}) %collective-permute-start.21) | collective-permute-done | bytes 114720 | tf_op jit(solution)/shard_map/ppermute | solution.py:373
  100.0 4.8 %collective-permute-start.24 = (bf16[240,256]{1,0:T(8,128)(2,1)S(1)}, bf16[240,256]{1,0:T(8,128)(2,1)S(1)}, u32[]{:S(2)}, u32[]{:S(2)}) collective-permute-start(bf16[240,256]{1,0:T(8,128)(2,1)S(1)} %shard_map.65.own), channel_id=1, source_target_pairs={{0,24},{8,0},{16,8},{24,16},{32,56},{40,32},{48,40},{56,48},{64,88... | collective-permute-start | bytes 368648 | tf_op jit(solution)/shard_map/ppermute | solution.py:373
  107.6 3.6 %collective-permute-done.25.a2 = bf16[240,256]{1,0:T(8,128)(2,1)S(1)} collective-permute-done((bf16[240,256]{1,0:T(8,128)(2,1)S(1)}, bf16[240,256]{1,0:T(8,128)(2,1)S(1)}, u32[]{:S(2)}, u32[]{:S(2)}) %collective-permute-start.25) | collective-permute-done | bytes 122912 | tf_op jit(solution)/shard_map/ppermute | solution.py:373
  112.3 2.3 %collective-permute-start.27 = (bf16[240,256]{1,0:T(8,128)(2,1)S(1)}, bf16[240,256]{1,0:T(8,128)(2,1)S(1)}, u32[]{:S(2)}, u32[]{:S(2)}) collective-permute-start(bf16[240,256]{1,0:T(8,128)(2,1)S(1)} %shard_map.66.own), channel_id=1, source_target_pairs={{0,96},{8,104},{16,112},{24,120},{32,0},{40,8},{48,16},{56,24},{64... | collective-permute-start | bytes 368648 | tf_op jit(solution)/shard_map/ppermute | solution.py:373
  117.5 3.5 %collective-permute-done.28.a2 = bf16[240,256]{1,0:T(8,128)(2,1)S(1)} collective-permute-done((bf16[240,256]{1,0:T(8,128)(2,1)S(1)}, bf16[240,256]{1,0:T(8,128)(2,1)S(1)}, u32[]{:S(2)}, u32[]{:S(2)}) %collective-permute-start.28) | collective-permute-done | bytes 122912 | tf_op jit(solution)/shard_map/ppermute | solution.py:373
  122.6 2.1 %shard_map.68 = bf16[2,1024,256]{2,1,0:T(8,128)(2,1)} custom-call(f32[2,256]{1,0:T(2,128)S(1)} %add.7.stats, f32[2,256]{1,0:T(2,128)S(1)} %get-tuple-element.56.sums, bf16[2,1024,256]{2,1,0:T(8,128)(2,1)S(1)} %bitcast.15, bf16[2,1024,256]{2,1,0:T(8,128)(2,1)S(1)} %bitcast.18, f32[1024,256]{1,0:T(8,128)S(1)} %get-tuple-element.57.grad0, ...), custom_call_target="tpu_custom_call" | custom-call | tf_op jit(solution)/shard_map/pallas_call | solution.py:350
  (66 shorter events, 31.1 us)
Async XLA Ops:
  0.6 36.5 %collective-permute-start.7 = (bf16[864,256]{1,0:T(8,128)(2,1)}, bf16[864,256]{1,0:T(8,128)(2,1)S(1)}, u32[]{:S(2)}, u32[]{:S(2)}) collective-permute-start(bf16[864,256]{1,0:T(8,128)(2,1)} %own.1), channel_id=1, source_target_pairs={{0,2},{1,3},{2,4},{3,5},{4,6},{5,7},{6,0},{7,1},{8,10},{9,11},{10,... | collective-permute-start | bytes 1327112 | tf_op jit(solution)/shard_map/ppermute | solution.py:373
  1.1 36.0 %collective-permute-start.8 = (bf16[864,256]{1,0:T(8,128)(2,1)}, bf16[864,256]{1,0:T(8,128)(2,1)S(1)}, u32[]{:S(2)}, u32[]{:S(2)}) collective-permute-start(bf16[864,256]{1,0:T(8,128)(2,1)} %own.1), channel_id=1, source_target_pairs={{0,6},{1,7},{2,0},{3,1},{4,2},{5,3},{6,4},{7,5},{8,14},{9,15},{10,... | collective-permute-start | bytes 1327112 | tf_op jit(solution)/shard_map/ppermute | solution.py:373
  2.7 34.4 %collective-permute-start.9 = (bf16[864,256]{1,0:T(8,128)(2,1)}, bf16[864,256]{1,0:T(8,128)(2,1)S(1)}, u32[]{:S(2)}, u32[]{:S(2)}) collective-permute-start(bf16[864,256]{1,0:T(8,128)(2,1)} %own.1), channel_id=1, source_target_pairs={{0,4},{1,5},{2,6},{3,7},{4,0},{5,1},{6,2},{7,3},{8,12},{9,13},{10,... | collective-permute-start | bytes 1327112 | tf_op jit(solution)/shard_map/ppermute | solution.py:373
  20.1 7.3 %collective-permute-start.4 = (f32[2,256]{1,0:T(2,128)S(1)}, f32[2,256]{1,0:T(2,128)S(1)}, u32[]{:S(2)}, u32[]{:S(2)}) collective-permute-start(f32[2,256]{1,0:T(2,128)S(1)} %add.6), channel_id=1, source_target_pairs={{0,96},{8,104},{16,112},{24,120},{32,64},{40,72},{48,80},{56,88},{... | collective-permute-start | bytes 6152 | tf_op jit(solution)/shard_map/ppermute | solution.py:383
  26.0 11.9 %collective-permute-start.6 = (bf16[1024,256]{1,0:T(8,128)(2,1)S(1)}, bf16[1024,256]{1,0:T(8,128)(2,1)S(1)}, u32[]{:S(2)}, u32[]{:S(2)}) collective-permute-start(bf16[1024,256]{1,0:T(8,128)(2,1)S(1)} %get-tuple-element.33), channel_id=1, source_target_pairs={{8,0},{16,8},{24,16},{32,24},{40,32},{48,40},{56,48},{64,56},{72,6... | collective-permute-start | bytes 1572872 | tf_op jit(solution)/shard_map/ppermute | solution.py:396
  27.3 13.5 %collective-permute-start.5 = (bf16[1024,256]{1,0:T(8,128)(2,1)S(1)}, bf16[1024,256]{1,0:T(8,128)(2,1)S(1)}, u32[]{:S(2)}, u32[]{:S(2)}) collective-permute-start(bf16[1024,256]{1,0:T(8,128)(2,1)S(1)} %get-tuple-element.32), channel_id=1, source_target_pairs={{0,8},{8,16},{16,24},{24,32},{32,40},{40,48},{48,56},{56,64},{64,7... | collective-permute-start | bytes 1572872 | tf_op jit(solution)/shard_map/ppermute | solution.py:396
  37.8 33.4 %collective-permute-start.19 = (bf16[4,864,256]{2,1,0:T(8,128)(2,1)S(1)}, bf16[4,864,256]{2,1,0:T(8,128)(2,1)S(1)}, u32[]{:S(2)}, u32[]{:S(2)}) collective-permute-start(bf16[4,864,256]{2,1,0:T(8,128)(2,1)S(1)} %shard_map.56.order.mine), channel_id=1, source_target_pairs={{0,1},{1,0},{2,3},{3,2},{4,5},{5,4},{6,7},{7,6},{8,9},{9,8},{10,11... | collective-permute-start | bytes 5308424 | tf_op jit(solution)/shard_map/ppermute | solution.py:387
  40.2 23.2 %collective-permute-start.11 = (bf16[1824,256]{1,0:T(8,128)(2,1)S(1)}, bf16[1824,256]{1,0:T(8,128)(2,1)S(1)}, u32[]{:S(2)}, u32[]{:S(2)}) collective-permute-start(bf16[1824,256]{1,0:T(8,128)(2,1)S(1)} %get-tuple-element.36.order), channel_id=1, source_target_pairs={{0,1},{1,0},{2,3},{3,2},{4,5},{5,4},{6,7},{7,6},{8,9},{9,8},{10,11... | collective-permute-start | bytes 2801672 | tf_op jit(solution)/shard_map/ppermute | solution.py:387
  46.9 17.3 %collective-permute-start.10 = (bf16[1824,256]{1,0:T(8,128)(2,1)S(1)}, bf16[1824,256]{1,0:T(8,128)(2,1)S(1)}, u32[]{:S(2)}, u32[]{:S(2)}) collective-permute-start(bf16[1824,256]{1,0:T(8,128)(2,1)S(1)} %get-tuple-element.38), channel_id=1, source_target_pairs={{0,1},{1,0},{2,3},{3,2},{4,5},{5,4},{6,7},{7,6},{8,9},{9,8},{10,11... | collective-permute-start | bytes 2801672 | tf_op jit(solution)/shard_map/ppermute | solution.py:387
  47.0 16.2 %collective-permute-start.18 = (bf16[1024,256]{1,0:T(8,128)(2,1)S(1)}, bf16[1024,256]{1,0:T(8,128)(2,1)S(1)}, u32[]{:S(2)}, u32[]{:S(2)}) collective-permute-start(bf16[1024,256]{1,0:T(8,128)(2,1)S(1)} %get-tuple-element.48), channel_id=1, source_target_pairs={{8,0},{16,8},{24,16},{32,24},{40,32},{48,40},{56,48},{64,56},{72,6... | collective-permute-start | bytes 1572872 | tf_op jit(solution)/shard_map/ppermute | solution.py:396
  64.9 15.7 %collective-permute-start.12 = (bf16[2,224,256]{2,1,0:T(8,128)(2,1)S(1)}, bf16[2,224,256]{2,1,0:T(8,128)(2,1)S(1)}, u32[]{:S(2)}, u32[]{:S(2)}) collective-permute-start(bf16[2,224,256]{2,1,0:T(8,128)(2,1)S(1)} %get-tuple-element.42), channel_id=1, source_target_pairs={{0,32},{8,40},{16,48},{24,56},{32,64},{40,72},{48,80},{56,88},{64,... | collective-permute-start | bytes 688136 | tf_op jit(solution)/shard_map/ppermute | solution.py:373
  69.0 17.8 %collective-permute-start.13 = (bf16[2,224,256]{2,1,0:T(8,128)(2,1)S(1)}, bf16[2,224,256]{2,1,0:T(8,128)(2,1)S(1)}, u32[]{:S(2)}, u32[]{:S(2)}) collective-permute-start(bf16[2,224,256]{2,1,0:T(8,128)(2,1)S(1)} %get-tuple-element.43), channel_id=1, source_target_pairs={{0,96},{8,104},{16,112},{24,120},{32,0},{40,8},{48,16},{56,24},{64... | collective-permute-start | bytes 688136 | tf_op jit(solution)/shard_map/ppermute | solution.py:373
  69.0 17.8 %collective-permute-start.14 = (bf16[2,224,256]{2,1,0:T(8,128)(2,1)S(1)}, bf16[2,224,256]{2,1,0:T(8,128)(2,1)S(1)}, u32[]{:S(2)}, u32[]{:S(2)}) collective-permute-start(bf16[2,224,256]{2,1,0:T(8,128)(2,1)S(1)} %get-tuple-element.44), channel_id=1, source_target_pairs={{0,64},{8,72},{16,80},{24,88},{32,96},{40,104},{48,112},{56,120},{... | collective-permute-start | bytes 688136 | tf_op jit(solution)/shard_map/ppermute | solution.py:373
  71.2 15.6 %collective-permute-start.15 = (bf16[2,224,256]{2,1,0:T(8,128)(2,1)S(1)}, bf16[2,224,256]{2,1,0:T(8,128)(2,1)S(1)}, u32[]{:S(2)}, u32[]{:S(2)}) collective-permute-start(bf16[2,224,256]{2,1,0:T(8,128)(2,1)S(1)} %get-tuple-element.45), channel_id=1, source_target_pairs={{0,32},{8,40},{16,48},{24,56},{32,64},{40,72},{48,80},{56,88},{64,... | collective-permute-start | bytes 688136 | tf_op jit(solution)/shard_map/ppermute | solution.py:373
  71.2 16.2 %collective-permute-start.16 = (bf16[2,224,256]{2,1,0:T(8,128)(2,1)S(1)}, bf16[2,224,256]{2,1,0:T(8,128)(2,1)S(1)}, u32[]{:S(2)}, u32[]{:S(2)}) collective-permute-start(bf16[2,224,256]{2,1,0:T(8,128)(2,1)S(1)} %get-tuple-element.46), channel_id=1, source_target_pairs={{0,96},{8,104},{16,112},{24,120},{32,0},{40,8},{48,16},{56,24},{64... | collective-permute-start | bytes 688136 | tf_op jit(solution)/shard_map/ppermute | solution.py:373
  80.6 9.0 %collective-permute-start.17 = (bf16[2,224,256]{2,1,0:T(8,128)(2,1)S(1)}, bf16[2,224,256]{2,1,0:T(8,128)(2,1)S(1)}, u32[]{:S(2)}, u32[]{:S(2)}) collective-permute-start(bf16[2,224,256]{2,1,0:T(8,128)(2,1)S(1)} %get-tuple-element.47), channel_id=1, source_target_pairs={{0,64},{8,72},{16,80},{24,88},{32,96},{40,104},{48,112},{56,120},{... | collective-permute-start | bytes 688136 | tf_op jit(solution)/shard_map/ppermute | solution.py:373
  90.4 5.7 %collective-permute-start.20 = (bf16[224,256]{1,0:T(8,128)(2,1)S(1)}, bf16[224,256]{1,0:T(8,128)(2,1)S(1)}, u32[]{:S(2)}, u32[]{:S(2)}) collective-permute-start(bf16[224,256]{1,0:T(8,128)(2,1)S(1)} %get-tuple-element.53), channel_id=1, source_target_pairs={{0,2},{1,3},{2,4},{3,5},{4,6},{5,7},{6,0},{7,1},{8,10},{9,11},{10,... | collective-permute-start | bytes 344072 | tf_op jit(solution)/shard_map/ppermute | solution.py:373
  92.6 7.3 %collective-permute-start.21 = (bf16[224,256]{1,0:T(8,128)(2,1)S(1)}, bf16[224,256]{1,0:T(8,128)(2,1)S(1)}, u32[]{:S(2)}, u32[]{:S(2)}) collective-permute-start(bf16[224,256]{1,0:T(8,128)(2,1)S(1)} %get-tuple-element.54), channel_id=1, source_target_pairs={{0,6},{1,7},{2,0},{3,1},{4,2},{5,3},{6,4},{7,5},{8,14},{9,15},{10,... | collective-permute-start | bytes 344072 | tf_op jit(solution)/shard_map/ppermute | solution.py:373
  92.6 7.3 %collective-permute-start.22 = (bf16[224,256]{1,0:T(8,128)(2,1)S(1)}, bf16[224,256]{1,0:T(8,128)(2,1)S(1)}, u32[]{:S(2)}, u32[]{:S(2)}) collective-permute-start(bf16[224,256]{1,0:T(8,128)(2,1)S(1)} %get-tuple-element.55), channel_id=1, source_target_pairs={{0,4},{1,5},{2,6},{3,7},{4,0},{5,1},{6,2},{7,3},{8,12},{9,13},{10,... | collective-permute-start | bytes 344072 | tf_op jit(solution)/shard_map/ppermute | solution.py:373
  100.0 7.6 %collective-permute-start.23 = (bf16[240,256]{1,0:T(8,128)(2,1)S(1)}, bf16[240,256]{1,0:T(8,128)(2,1)S(1)}, u32[]{:S(2)}, u32[]{:S(2)}) collective-permute-start(bf16[240,256]{1,0:T(8,128)(2,1)S(1)} %shard_map.65.own), channel_id=1, source_target_pairs={{0,8},{8,16},{16,24},{24,0},{32,40},{40,48},{48,56},{56,32},{64,72... | collective-permute-start | bytes 368648 | tf_op jit(solution)/shard_map/ppermute | solution.py:373
  100.0 7.6 %collective-permute-start.24 = (bf16[240,256]{1,0:T(8,128)(2,1)S(1)}, bf16[240,256]{1,0:T(8,128)(2,1)S(1)}, u32[]{:S(2)}, u32[]{:S(2)}) collective-permute-start(bf16[240,256]{1,0:T(8,128)(2,1)S(1)} %shard_map.65.own), channel_id=1, source_target_pairs={{0,24},{8,0},{16,8},{24,16},{32,56},{40,32},{48,40},{56,48},{64,88... | collective-permute-start | bytes 368648 | tf_op jit(solution)/shard_map/ppermute | solution.py:373
  104.8 6.4 %collective-permute-start.25 = (bf16[240,256]{1,0:T(8,128)(2,1)S(1)}, bf16[240,256]{1,0:T(8,128)(2,1)S(1)}, u32[]{:S(2)}, u32[]{:S(2)}) collective-permute-start(bf16[240,256]{1,0:T(8,128)(2,1)S(1)} %shard_map.65.own), channel_id=1, source_target_pairs={{0,16},{8,24},{16,0},{24,8},{32,48},{40,56},{48,32},{56,40},{64,80... | collective-permute-start | bytes 368648 | tf_op jit(solution)/shard_map/ppermute | solution.py:373
  111.3 6.2 %collective-permute-start.26 = (bf16[240,256]{1,0:T(8,128)(2,1)S(1)}, bf16[240,256]{1,0:T(8,128)(2,1)S(1)}, u32[]{:S(2)}, u32[]{:S(2)}) collective-permute-start(bf16[240,256]{1,0:T(8,128)(2,1)S(1)} %shard_map.66.own), channel_id=1, source_target_pairs={{0,32},{8,40},{16,48},{24,56},{32,64},{40,72},{48,80},{56,88},{64,... | collective-permute-start | bytes 368648 | tf_op jit(solution)/shard_map/ppermute | solution.py:373
  114.6 6.4 %collective-permute-start.28 = (bf16[240,256]{1,0:T(8,128)(2,1)S(1)}, bf16[240,256]{1,0:T(8,128)(2,1)S(1)}, u32[]{:S(2)}, u32[]{:S(2)}) collective-permute-start(bf16[240,256]{1,0:T(8,128)(2,1)S(1)} %shard_map.66.own), channel_id=1, source_target_pairs={{0,64},{8,72},{16,80},{24,88},{32,96},{40,104},{48,112},{56,120},{... | collective-permute-start | bytes 368648 | tf_op jit(solution)/shard_map/ppermute | solution.py:373
  (10 other events, 35.5 us)

commit v5 on v4

--- a/solution.py
+++ b/solution.py
@@ -62,20 +62,17 @@
         target[2, slot, at] = jnp.where(column == 0, 0.0, pltpu.roll(wide, 1, 0)).astype(bf16)
 
 
-def stats_kernel(clip, out):
+def first_kernel(clip, cot, out, first, second, last):
     def step(i, carry):
         a, b = carry
-        v = clip[pl.ds(pl.multiple_of(i * 128, 128), 128)].astype(f32)
-        v = v.reshape(16, 8, C)
+        at = pl.ds(pl.multiple_of((i & 7) * 128, 128), 128)
+        v = clip[i >> 3, at].astype(f32).reshape(16, 8, C)
         return a + v.sum(0), b + (v * v).sum(0)
 
     zero = jnp.zeros((8, C), f32)
-    a, b = lax.fori_loop(0, clip.shape[0] // 128, step, (zero, zero))
+    a, b = lax.fori_loop(0, 2 * ROWS // 128, step, (zero, zero))
     out[0:1] = a.sum(0, keepdims=True)
     out[1:2] = b.sum(0, keepdims=True)
-
-
-def copy_kernel(clip, cot, order, first, second, last):
     first[...] = cot[0]
     second[...] = cot[1]
     last[...] = clip[1]
@@ -87,7 +84,7 @@
         widths(wide, lambda r, t=t: cot[t, pl.ds(r, W)], t)
 
 
-def ring_sum_kernel(own, before, after, far, out):
+def ring_sum_kernel(own, before, after, far, held0, held1, out, pass0, pass1):
     out[...] = (own[...] + far[...]) + (before[...] + after[...])
 
 
@@ -343,15 +340,18 @@
     sums[...] = ring_sums(own, (a0, a1, a2))
 
 
-def call(kernel, out_shape, args, scratch=(), flops=0, bytes_accessed=0, scalars=0, order=(), aliases={}):
+def call(kernel, out_shape, args, scratch=(), flops=0, bytes_accessed=0, scalars=0, order=(), aliases={}, passed_out=0):
     specs = [pl.BlockSpec(memory_space=pltpu.SMEM)] * scalars
     specs += [pl.BlockSpec(memory_space=pltpu.VMEM)] * (len(args) - scalars)
     specs += [pl.BlockSpec(memory_space=pl.ANY)] * len(order)
+    out_specs = jax.tree.map(lambda _: pl.BlockSpec(memory_space=pltpu.VMEM), out_shape)
+    if passed_out:
+        out_specs = out_specs[:-passed_out] + (pl.BlockSpec(memory_space=pl.ANY),) * passed_out
     return pl.pallas_call(
         kernel,
         out_shape=out_shape,
         in_specs=specs,
-        out_specs=jax.tree.map(lambda _: pl.BlockSpec(memory_space=pltpu.VMEM), out_shape),
+        out_specs=out_specs,
         scratch_shapes=list(scratch),
         input_output_aliases=aliases,
         compiler_params=pltpu.CompilerParams(vmem_limit_bytes=VMEM),
@@ -385,10 +385,6 @@
 
 def swap_core(block):
     return lax.ppermute(block, "fsdp", [(i, i ^ 1) for i in range(8)])
-
-
-def ring_sum(values, got):
-    return call(ring_sum_kernel, jax.ShapeDtypeStruct(values.shape, f32), (values, *got))
 
 
 def passed(block, distance):
@@ -410,15 +406,22 @@
     where = jnp.stack([jnp.asarray(v, jnp.int32) for v in where])
     frame = S((ROWS, C), bf16)
 
-    sums = call(stats_kernel, S((2, C), f32), (clip.reshape(2 * ROWS, C),))
-    sums = ring_sum(sums, ring("z", [sums] * 3))
-    first, second, last = call(copy_kernel, (frame, frame, frame), (clip, cot), order=(sums,))
+    sums, first, second, last = call(first_kernel, (S((2, C), f32), frame, frame, frame), (clip, cot))
+    got = ring("z", [sums] * 3)
+    sums, first, last = call(
+        ring_sum_kernel,
+        (S((2, C), f32), frame, frame),
+        (sums, *got),
+        order=(first, last),
+        aliases={4: 1, 5: 2},
+        passed_out=2,
+    )
     near = call(widths_kernel, S((3, 2, PADDED, C), bf16), (cot,), order=(sums,))
     half = sums + swap(sums, "y", (1, 0, 3, 2))
     stats = half + swap(half, "y", (3, 2, 1, 0))
     after = call(widths_kernel, S((3, 1, PADDED, C), bf16), (passed(first, -1)[None],))
     before = passed(last, 1)
-    later = call(widths_kernel, S((3, 1, PADDED, C), bf16), (passed(second, -1)[None],))
+    later = passed(second, -1)[None]
 
     rows = 2 * SHARD_PAD + UNIT
     tap_flops = C * C * 2 * ROWS * 2
@@ -464,6 +467,7 @@
         scalars=1,
         order=(low,),
     )
+    later = call(widths_kernel, S((3, 1, PADDED, C), bf16), (later,), order=(sums0,))
     grad1, sums1 = call(
         partial(second_grad_kernel, count),
         (S((ROWS, C), f32), S((2, C), f32)),

time: 127 us -> 121 us (0.953)
  waiting for transfers between devices: 39.8 us -> 34.2 us
  starting transfers between devices: 47.3 us -> 48.7 us
    ppermute x3, waiting for transfers between devices: 14.9 us -> 4.54 us  [passed(): return lax.ppermute(block, 'tm', route)]
    ppermute x21, waiting for transfers between devices: 22.9 us -> 27.7 us  [ring(): got.append(lax.ppermute(block, name, route))]
    ppermute x21, starting transfers between devices: 34.8 us -> 38.9 us  [ring(): got.append(lax.ppermute(block, name, route))]
    ppermute x3, starting transfers between devices: 7.15 us -> 4.41 us  [passed(): return lax.ppermute(block, 'tm', route)]
    unnamed x10 -> x14, local copies, waits for them, and re-layouts: 3.43 us -> 2.47 us
    pallas_call x19 -> x18, Pallas kernels: 33.1 us -> 33.1 us  [call(): pl.pallas_call(kernel, out_shape=out_shape, in_specs=specs, out_specs=out...]
  transfers between devices with their start and end apart: 29 -> 29, of which waited for: 12 -> 12; matrix products, arithmetic and copies ran while one was open for 0% -> 0% of each run, Pallas kernels for 23% -> 24%
where the time goes in v5:
time: 121 us; the launch traced here: 120 us
  starting transfers between devices  48.7 us (40%)
  waiting for transfers between devices  34.2 us (28%)
  Pallas kernels  33.1 us (27%)
  local copies, waits for them, and re-layouts  2.47 us (2%)
    ppermute x21, starting transfers between devices, ring(): got.append(lax.ppermute(block, name, route))  38.9 us
    pallas_call x18, Pallas kernels, call(): pl.pallas_call(kernel, out_shape=out_shape, in_specs=specs, out_specs=out...  33.1 us
    ppermute x21, waiting for transfers between devices, ring(): got.append(lax.ppermute(block, name, route))  27.7 us
    ppermute x2, starting transfers between devices, swap(): return lax.ppermute(block, name, route)  4.66 us
    ppermute x3, waiting for transfers between devices, passed(): return lax.ppermute(block, 'tm', route)  4.54 us
    ppermute x3, starting transfers between devices, passed(): return lax.ppermute(block, 'tm', route)  4.41 us
    unnamed x14, local copies, waits for them, and re-layouts  2.47 us
  transfers between devices with their start and end apart: 29, of which 12 were waited for; matrix products, arithmetic and copies ran while one was open for 0% of the time, Pallas kernels for 24%

profile of v5, /device:TPU:6, one launch (start us, length us, event | category | flops | bytes accessed | tf_op | source)
XLA Modules:
  0.0 119.6 jit_solution(616279005079879613)
XLA Ops:
  1.5 2.4 %collective-permute-start.7 = (bf16[864,256]{1,0:T(8,128)(2,1)}, bf16[864,256]{1,0:T(8,128)(2,1)S(1)}, u32[]{:S(2)}, u32[]{:S(2)}) collective-permute-start(bf16[864,256]{1,0:T(8,128)(2,1)} %own.1), channel_id=1, source_target_pairs={{0,2},{1,3},{2,4},{3,5},{4,6},{5,7},{6,0},{7,1},{8,10},{9,11},{10,... | collective-permute-start | bytes 1327112 | tf_op jit(solution)/shard_map/ppermute | solution.py:373
  7.1 4.0 %collective-permute-start.2 = (f32[2,256]{1,0:T(2,128)S(1)}, f32[2,256]{1,0:T(2,128)S(1)}, u32[]{:S(2)}, u32[]{:S(2)}) collective-permute-start(f32[2,256]{1,0:T(2,128)S(1)} %get-tuple-element.35.own), channel_id=1, source_target_pairs={{0,16},{8,24},{16,0},{24,8},{32,48},{40,56},{48,32},{56,40},{64,80... | collective-permute-start | bytes 6152 | tf_op jit(solution)/shard_map/ppermute | solution.py:373
  14.6 3.2 %collective-permute-done.before = f32[2,256]{1,0:T(2,128)S(1)} collective-permute-done((f32[2,256]{1,0:T(2,128)S(1)}, f32[2,256]{1,0:T(2,128)S(1)}, u32[]{:S(2)}, u32[]{:S(2)}) %collective-permute-start) | collective-permute-done | bytes 2080 | tf_op jit(solution)/shard_map/ppermute | solution.py:373
  19.5 2.0 %collective-permute-done.3 = f32[2,256]{1,0:T(2,128)S(1)} collective-permute-done((f32[2,256]{1,0:T(2,128)S(1)}, f32[2,256]{1,0:T(2,128)S(1)}, u32[]{:S(2)}, u32[]{:S(2)}) %collective-permute-start.3) | collective-permute-done | bytes 2080 | tf_op jit(solution)/shard_map/ppermute | solution.py:383
  21.5 3.0 %collective-permute-start.4 = (f32[2,256]{1,0:T(2,128)S(1)}, f32[2,256]{1,0:T(2,128)S(1)}, u32[]{:S(2)}, u32[]{:S(2)}) collective-permute-start(f32[2,256]{1,0:T(2,128)S(1)} %add.6), channel_id=1, source_target_pairs={{0,96},{8,104},{16,112},{24,120},{32,64},{40,72},{48,80},{56,88},{... | collective-permute-start | bytes 6152 | tf_op jit(solution)/shard_map/ppermute | solution.py:383
  28.3 5.2 %shard_map.53 = (bf16[2,1024,256]{2,1,0:T(8,128)(2,1)S(1)}, f32[1824,256]{1,0:T(8,128)S(1)}, bf16[1824,256]{1,0:T(8,128)(2,1)S(1)}) custom-call(s32[4]{0:T(128)S(1)} %pad_add_fusion.where, f32[2,256]{1,0:T(2,128)S(1)} %add.7.stats, bf16[2,1024,256]{2,1,0:T(8,128)(2,1)S(1)} %bitcast.13, bf16[3,2,1152,256]{3,2,1,0:T(8,128)(2,1)S(1)} %shard_map.52.near), custom_call_target="tpu_custom_call" | custom-call | flops 2415919104 | tf_op jit(solution)/shard_map/pallas_call | solution.py:350
  34.3 4.5 %collective-permute-done.6 = bf16[1024,256]{1,0:T(8,128)(2,1)S(1)} collective-permute-done((bf16[1024,256]{1,0:T(8,128)(2,1)S(1)}, bf16[1024,256]{1,0:T(8,128)(2,1)S(1)}, u32[]{:S(2)}, u32[]{:S(2)}) %collective-permute-start.6) | collective-permute-done | bytes 524320 | tf_op jit(solution)/shard_map/ppermute | solution.py:392
  39.1 2.0 %shard_map.56 = (f32[1824,256]{1,0:T(8,128)S(1)}, bf16[1824,256]{1,0:T(8,128)(2,1)S(1)}) custom-call(s32[4]{0:T(128)S(1)} %pad_add_fusion.where, bf16[2,1024,256]{2,1,0:T(8,128)(2,1)S(1)} %get-tuple-element.39.order.act, bf16[3,2,1152,256]{3,2,1,0:T(8,128)(2,1)S(1)} %shard_map.52.near, ...), custom_call_target="tpu_custom_call", output_to_operand_aliasing={{0}: (4, {}), {1}: (5, {})} | custom-call | flops 1207959552 | tf_op jit(solution)/shard_map/pallas_call | solution.py:350
  41.3 6.1 %shard_map.57 = (f32[1824,256]{1,0:T(8,128)S(1)}, bf16[1824,256]{1,0:T(8,128)(2,1)S(1)}) custom-call(s32[4]{0:T(128)S(1)} %pad_add_fusion.where, f32[2,256]{1,0:T(2,128)S(1)} %add.7.stats, bf16[2,1024,256]{2,1,0:T(8,128)(2,1)S(1)} %get-tuple-element.39.order.act, bf16[1024,256]{1,0:T(8,128)(2,1)S(1)} %collective-permute-done.5.before, ...), custom_call_target="tpu_custom_call" | custom-call | flops 3623878656 | tf_op jit(solution)/shard_map/pallas_call | solution.py:350
  49.9 7.0 %collective-permute-start.15 = (bf16[2,224,256]{2,1,0:T(8,128)(2,1)S(1)}, bf16[2,224,256]{2,1,0:T(8,128)(2,1)S(1)}, u32[]{:S(2)}, u32[]{:S(2)}) collective-permute-start(bf16[2,224,256]{2,1,0:T(8,128)(2,1)S(1)} %get-tuple-element.53), channel_id=1, source_target_pairs={{0,32},{8,40},{16,48},{24,56},{32,64},{40,72},{48,80},{56,88},{64,... | collective-permute-start | bytes 688136 | tf_op jit(solution)/shard_map/ppermute | solution.py:373
  57.1 2.3 %collective-permute-start.17 = (bf16[2,224,256]{2,1,0:T(8,128)(2,1)S(1)}, bf16[2,224,256]{2,1,0:T(8,128)(2,1)S(1)}, u32[]{:S(2)}, u32[]{:S(2)}) collective-permute-start(bf16[2,224,256]{2,1,0:T(8,128)(2,1)S(1)} %get-tuple-element.55), channel_id=1, source_target_pairs={{0,64},{8,72},{16,80},{24,88},{32,96},{40,104},{48,112},{56,120},{... | collective-permute-start | bytes 688136 | tf_op jit(solution)/shard_map/ppermute | solution.py:373
  60.9 6.1 %shard_map.60 = (f32[1024,256]{1,0:T(8,128)S(1)}, f32[2,256]{1,0:T(2,128)S(1)}, bf16[6912,256]{1,0:T(8,128)(2,1)S(1)}) custom-call(s32[4]{0:T(128)S(1)} %pad_add_fusion.where, f32[2,256]{1,0:T(2,128)S(1)} %add.7.stats, bf16[2,1024,256]{2,1,0:T(8,128)(2,1)S(1)} %bitcast.14, bf16[3,2,1152,256]{3,2,1,0:T(8,128)(2,1)S(1)} %shard_map.52.near, ...), custom_call_target="tpu_custom_call" | custom-call | flops 3623878656 | tf_op jit(solution)/shard_map/pallas_call | solution.py:350
  67.1 2.8 %collective-permute-start.13 = (bf16[2,224,256]{2,1,0:T(8,128)(2,1)S(1)}, bf16[2,224,256]{2,1,0:T(8,128)(2,1)S(1)}, u32[]{:S(2)}, u32[]{:S(2)}) collective-permute-start(bf16[2,224,256]{2,1,0:T(8,128)(2,1)S(1)} %get-tuple-element.51), channel_id=1, source_target_pairs={{0,96},{8,104},{16,112},{24,120},{32,0},{40,8},{48,16},{56,24},{64... | collective-permute-start | bytes 688136 | tf_op jit(solution)/shard_map/ppermute | solution.py:373
  70.8 5.4 %shard_map.62 = (f32[1024,256]{1,0:T(8,128)S(1)}, f32[2,256]{1,0:T(2,128)S(1)}) custom-call(f32[2,256]{1,0:T(2,128)S(1)} %add.7.stats, bf16[2,1024,256]{2,1,0:T(8,128)(2,1)S(1)} %bitcast.15, bf16[3,2,1152,256]{3,2,1,0:T(8,128)(2,1)S(1)} %shard_map.52.near, bf16[3,1,1152,256]{3,2,1,0:T(8,128)(2,1)S(1)} %shard_map.54.after, ...), custom_call_target="tpu_custom_call" | custom-call | flops 3623878656 | tf_op jit(solution)/shard_map/pallas_call | solution.py:350
  76.3 7.3 %collective-permute-done.13.l1 = bf16[2,224,256]{2,1,0:T(8,128)(2,1)S(1)} collective-permute-done((bf16[2,224,256]{2,1,0:T(8,128)(2,1)S(1)}, bf16[2,224,256]{2,1,0:T(8,128)(2,1)S(1)}, u32[]{:S(2)}, u32[]{:S(2)}) %collective-permute-start.13) | collective-permute-done | bytes 229408 | tf_op jit(solution)/shard_map/ppermute | solution.py:373
  84.4 2.1 %collective-permute-start.20 = (bf16[224,256]{1,0:T(8,128)(2,1)S(1)}, bf16[224,256]{1,0:T(8,128)(2,1)S(1)}, u32[]{:S(2)}, u32[]{:S(2)}) collective-permute-start(bf16[224,256]{1,0:T(8,128)(2,1)S(1)} %get-tuple-element.61), channel_id=1, source_target_pairs={{0,2},{1,3},{2,4},{3,5},{4,6},{5,7},{6,0},{7,1},{8,10},{9,11},{10,... | collective-permute-start | bytes 344072 | tf_op jit(solution)/shard_map/ppermute | solution.py:373
  86.5 3.1 %collective-permute-start.22 = (bf16[224,256]{1,0:T(8,128)(2,1)S(1)}, bf16[224,256]{1,0:T(8,128)(2,1)S(1)}, u32[]{:S(2)}, u32[]{:S(2)}) collective-permute-start(bf16[224,256]{1,0:T(8,128)(2,1)S(1)} %get-tuple-element.63), channel_id=1, source_target_pairs={{0,4},{1,5},{2,6},{3,7},{4,0},{5,1},{6,2},{7,3},{8,12},{9,13},{10,... | collective-permute-start | bytes 344072 | tf_op jit(solution)/shard_map/ppermute | solution.py:373
  90.1 3.7 %collective-permute-done.21.a1 = bf16[224,256]{1,0:T(8,128)(2,1)S(1)} collective-permute-done((bf16[224,256]{1,0:T(8,128)(2,1)S(1)}, bf16[224,256]{1,0:T(8,128)(2,1)S(1)}, u32[]{:S(2)}, u32[]{:S(2)}) %collective-permute-start.21) | collective-permute-done | bytes 114720 | tf_op jit(solution)/shard_map/ppermute | solution.py:373
  94.0 2.0 %collective-permute-start.23 = (bf16[240,256]{1,0:T(8,128)(2,1)S(1)}, bf16[240,256]{1,0:T(8,128)(2,1)S(1)}, u32[]{:S(2)}, u32[]{:S(2)}) collective-permute-start(bf16[240,256]{1,0:T(8,128)(2,1)S(1)} %shard_map.64.own), channel_id=1, source_target_pairs={{0,8},{8,16},{16,24},{24,0},{32,40},{40,48},{48,56},{56,32},{64,72... | collective-permute-start | bytes 368648 | tf_op jit(solution)/shard_map/ppermute | solution.py:373
  96.0 4.4 %collective-permute-done.25.a2 = bf16[240,256]{1,0:T(8,128)(2,1)S(1)} collective-permute-done((bf16[240,256]{1,0:T(8,128)(2,1)S(1)}, bf16[240,256]{1,0:T(8,128)(2,1)S(1)}, u32[]{:S(2)}, u32[]{:S(2)}) %collective-permute-start.25) | collective-permute-done | bytes 122912 | tf_op jit(solution)/shard_map/ppermute | solution.py:373
  103.4 6.5 %collective-permute-start.27 = (bf16[240,256]{1,0:T(8,128)(2,1)S(1)}, bf16[240,256]{1,0:T(8,128)(2,1)S(1)}, u32[]{:S(2)}, u32[]{:S(2)}) collective-permute-start(bf16[240,256]{1,0:T(8,128)(2,1)S(1)} %shard_map.65.own), channel_id=1, source_target_pairs={{0,96},{8,104},{16,112},{24,120},{32,0},{40,8},{48,16},{56,24},{64... | collective-permute-start | bytes 368648 | tf_op jit(solution)/shard_map/ppermute | solution.py:373
  109.9 4.0 %collective-permute-done.27.a1 = bf16[240,256]{1,0:T(8,128)(2,1)S(1)} collective-permute-done((bf16[240,256]{1,0:T(8,128)(2,1)S(1)}, bf16[240,256]{1,0:T(8,128)(2,1)S(1)}, u32[]{:S(2)}, u32[]{:S(2)}) %collective-permute-start.27) | collective-permute-done | bytes 122912 | tf_op jit(solution)/shard_map/ppermute | solution.py:373
  113.9 2.1 %collective-permute-done.26.a0 = bf16[240,256]{1,0:T(8,128)(2,1)S(1)} collective-permute-done((bf16[240,256]{1,0:T(8,128)(2,1)S(1)}, bf16[240,256]{1,0:T(8,128)(2,1)S(1)}, u32[]{:S(2)}, u32[]{:S(2)}) %collective-permute-start.26) | collective-permute-done | bytes 122912 | tf_op jit(solution)/shard_map/ppermute | solution.py:373
  117.5 2.1 %shard_map.67 = bf16[2,1024,256]{2,1,0:T(8,128)(2,1)} custom-call(f32[2,256]{1,0:T(2,128)S(1)} %add.7.stats, f32[2,256]{1,0:T(2,128)S(1)} %get-tuple-element.64.sums, bf16[2,1024,256]{2,1,0:T(8,128)(2,1)S(1)} %bitcast.16, bf16[2,1024,256]{2,1,0:T(8,128)(2,1)S(1)} %bitcast.11, f32[1024,256]{1,0:T(8,128)S(1)} %get-tuple-element.65.grad0, ...), custom_call_target="tpu_custom_call" | custom-call | tf_op jit(solution)/shard_map/pallas_call | solution.py:350
  (69 shorter events, 25.5 us)
Async XLA Ops:
  0.6 32.9 %collective-permute-start.8 = (bf16[864,256]{1,0:T(8,128)(2,1)}, bf16[864,256]{1,0:T(8,128)(2,1)S(1)}, u32[]{:S(2)}, u32[]{:S(2)}) collective-permute-start(bf16[864,256]{1,0:T(8,128)(2,1)} %own.1), channel_id=1, source_target_pairs={{0,6},{1,7},{2,0},{3,1},{4,2},{5,3},{6,4},{7,5},{8,14},{9,15},{10,... | collective-permute-start | bytes 1327112 | tf_op jit(solution)/shard_map/ppermute | solution.py:373
  1.5 32.0 %collective-permute-start.7 = (bf16[864,256]{1,0:T(8,128)(2,1)}, bf16[864,256]{1,0:T(8,128)(2,1)S(1)}, u32[]{:S(2)}, u32[]{:S(2)}) collective-permute-start(bf16[864,256]{1,0:T(8,128)(2,1)} %own.1), channel_id=1, source_target_pairs={{0,2},{1,3},{2,4},{3,5},{4,6},{5,7},{6,0},{7,1},{8,10},{9,11},{10,... | collective-permute-start | bytes 1327112 | tf_op jit(solution)/shard_map/ppermute | solution.py:373
  3.9 29.6 %collective-permute-start.9 = (bf16[864,256]{1,0:T(8,128)(2,1)}, bf16[864,256]{1,0:T(8,128)(2,1)S(1)}, u32[]{:S(2)}, u32[]{:S(2)}) collective-permute-start(bf16[864,256]{1,0:T(8,128)(2,1)} %own.1), channel_id=1, source_target_pairs={{0,4},{1,5},{2,6},{3,7},{4,0},{5,1},{6,2},{7,3},{8,12},{9,13},{10,... | collective-permute-start | bytes 1327112 | tf_op jit(solution)/shard_map/ppermute | solution.py:373
  25.2 16.1 %collective-permute-start.5 = (bf16[1024,256]{1,0:T(8,128)(2,1)S(1)}, bf16[1024,256]{1,0:T(8,128)(2,1)S(1)}, u32[]{:S(2)}, u32[]{:S(2)}) collective-permute-start(bf16[1024,256]{1,0:T(8,128)(2,1)S(1)} %get-tuple-element.40), channel_id=1, source_target_pairs={{0,8},{8,16},{16,24},{24,32},{32,40},{40,48},{48,56},{56,64},{64,7... | collective-permute-start | bytes 1572872 | tf_op jit(solution)/shard_map/ppermute | solution.py:392
  27.0 11.8 %collective-permute-start.6 = (bf16[1024,256]{1,0:T(8,128)(2,1)S(1)}, bf16[1024,256]{1,0:T(8,128)(2,1)S(1)}, u32[]{:S(2)}, u32[]{:S(2)}) collective-permute-start(bf16[1024,256]{1,0:T(8,128)(2,1)S(1)} %get-tuple-element.41), channel_id=1, source_target_pairs={{8,0},{16,8},{24,16},{32,24},{40,32},{48,40},{56,48},{64,56},{72,6... | collective-permute-start | bytes 1572872 | tf_op jit(solution)/shard_map/ppermute | solution.py:392
  34.2 25.9 %collective-permute-start.19 = (bf16[4,864,256]{2,1,0:T(8,128)(2,1)S(1)}, bf16[4,864,256]{2,1,0:T(8,128)(2,1)S(1)}, u32[]{:S(2)}, u32[]{:S(2)}) collective-permute-start(bf16[4,864,256]{2,1,0:T(8,128)(2,1)S(1)} %shard_map.55.order.mine), channel_id=1, source_target_pairs={{0,1},{1,0},{2,3},{3,2},{4,5},{5,4},{6,7},{7,6},{8,9},{9,8},{10,11... | collective-permute-start | bytes 5308424 | tf_op jit(solution)/shard_map/ppermute | solution.py:387
  41.2 8.0 %collective-permute-start.11 = (bf16[1824,256]{1,0:T(8,128)(2,1)S(1)}, bf16[1824,256]{1,0:T(8,128)(2,1)S(1)}, u32[]{:S(2)}, u32[]{:S(2)}) collective-permute-start(bf16[1824,256]{1,0:T(8,128)(2,1)S(1)} %get-tuple-element.44.order), channel_id=1, source_target_pairs={{0,1},{1,0},{2,3},{3,2},{4,5},{5,4},{6,7},{7,6},{8,9},{9,8},{10,11... | collective-permute-start | bytes 2801672 | tf_op jit(solution)/shard_map/ppermute | solution.py:387
  47.3 9.8 %collective-permute-start.10 = (bf16[1824,256]{1,0:T(8,128)(2,1)S(1)}, bf16[1824,256]{1,0:T(8,128)(2,1)S(1)}, u32[]{:S(2)}, u32[]{:S(2)}) collective-permute-start(bf16[1824,256]{1,0:T(8,128)(2,1)S(1)} %get-tuple-element.46), channel_id=1, source_target_pairs={{0,1},{1,0},{2,3},{3,2},{4,5},{5,4},{6,7},{7,6},{8,9},{9,8},{10,11... | collective-permute-start | bytes 2801672 | tf_op jit(solution)/shard_map/ppermute | solution.py:387
  47.9 19.1 %collective-permute-start.18 = (bf16[1024,256]{1,0:T(8,128)(2,1)S(1)}, bf16[1024,256]{1,0:T(8,128)(2,1)S(1)}, u32[]{:S(2)}, u32[]{:S(2)}) collective-permute-start(bf16[1024,256]{1,0:T(8,128)(2,1)S(1)} %copy-done.6), channel_id=1, source_target_pairs={{8,0},{16,8},{24,16},{32,24},{40,32},{48,40},{56,48},{64,56},{72,6... | collective-permute-start | bytes 1572872 | tf_op jit(solution)/shard_map/ppermute | solution.py:392
  49.9 20.2 %collective-permute-start.15 = (bf16[2,224,256]{2,1,0:T(8,128)(2,1)S(1)}, bf16[2,224,256]{2,1,0:T(8,128)(2,1)S(1)}, u32[]{:S(2)}, u32[]{:S(2)}) collective-permute-start(bf16[2,224,256]{2,1,0:T(8,128)(2,1)S(1)} %get-tuple-element.53), channel_id=1, source_target_pairs={{0,32},{8,40},{16,48},{24,56},{32,64},{40,72},{48,80},{56,88},{64,... | collective-permute-start | bytes 688136 | tf_op jit(solution)/shard_map/ppermute | solution.py:373
  56.9 19.4 %collective-permute-start.16 = (bf16[2,224,256]{2,1,0:T(8,128)(2,1)S(1)}, bf16[2,224,256]{2,1,0:T(8,128)(2,1)S(1)}, u32[]{:S(2)}, u32[]{:S(2)}) collective-permute-start(bf16[2,224,256]{2,1,0:T(8,128)(2,1)S(1)} %get-tuple-element.54), channel_id=1, source_target_pairs={{0,96},{8,104},{16,112},{24,120},{32,0},{40,8},{48,16},{56,24},{64... | collective-permute-start | bytes 688136 | tf_op jit(solution)/shard_map/ppermute | solution.py:373
  57.1 19.2 %collective-permute-start.17 = (bf16[2,224,256]{2,1,0:T(8,128)(2,1)S(1)}, bf16[2,224,256]{2,1,0:T(8,128)(2,1)S(1)}, u32[]{:S(2)}, u32[]{:S(2)}) collective-permute-start(bf16[2,224,256]{2,1,0:T(8,128)(2,1)S(1)} %get-tuple-element.55), channel_id=1, source_target_pairs={{0,64},{8,72},{16,80},{24,88},{32,96},{40,104},{48,112},{56,120},{... | collective-permute-start | bytes 688136 | tf_op jit(solution)/shard_map/ppermute | solution.py:373
  60.2 16.1 %collective-permute-start.12 = (bf16[2,224,256]{2,1,0:T(8,128)(2,1)S(1)}, bf16[2,224,256]{2,1,0:T(8,128)(2,1)S(1)}, u32[]{:S(2)}, u32[]{:S(2)}) collective-permute-start(bf16[2,224,256]{2,1,0:T(8,128)(2,1)S(1)} %get-tuple-element.50), channel_id=1, source_target_pairs={{0,32},{8,40},{16,48},{24,56},{32,64},{40,72},{48,80},{56,88},{64,... | collective-permute-start | bytes 688136 | tf_op jit(solution)/shard_map/ppermute | solution.py:373
  67.1 16.6 %collective-permute-start.13 = (bf16[2,224,256]{2,1,0:T(8,128)(2,1)S(1)}, bf16[2,224,256]{2,1,0:T(8,128)(2,1)S(1)}, u32[]{:S(2)}, u32[]{:S(2)}) collective-permute-start(bf16[2,224,256]{2,1,0:T(8,128)(2,1)S(1)} %get-tuple-element.51), channel_id=1, source_target_pairs={{0,96},{8,104},{16,112},{24,120},{32,0},{40,8},{48,16},{56,24},{64... | collective-permute-start | bytes 688136 | tf_op jit(solution)/shard_map/ppermute | solution.py:373
  70.1 13.5 %collective-permute-start.14 = (bf16[2,224,256]{2,1,0:T(8,128)(2,1)S(1)}, bf16[2,224,256]{2,1,0:T(8,128)(2,1)S(1)}, u32[]{:S(2)}, u32[]{:S(2)}) collective-permute-start(bf16[2,224,256]{2,1,0:T(8,128)(2,1)S(1)} %get-tuple-element.52), channel_id=1, source_target_pairs={{0,64},{8,72},{16,80},{24,88},{32,96},{40,104},{48,112},{56,120},{... | collective-permute-start | bytes 688136 | tf_op jit(solution)/shard_map/ppermute | solution.py:373
  84.4 5.6 %collective-permute-start.20 = (bf16[224,256]{1,0:T(8,128)(2,1)S(1)}, bf16[224,256]{1,0:T(8,128)(2,1)S(1)}, u32[]{:S(2)}, u32[]{:S(2)}) collective-permute-start(bf16[224,256]{1,0:T(8,128)(2,1)S(1)} %get-tuple-element.61), channel_id=1, source_target_pairs={{0,2},{1,3},{2,4},{3,5},{4,6},{5,7},{6,0},{7,1},{8,10},{9,11},{10,... | collective-permute-start | bytes 344072 | tf_op jit(solution)/shard_map/ppermute | solution.py:373
  86.5 7.2 %collective-permute-start.21 = (bf16[224,256]{1,0:T(8,128)(2,1)S(1)}, bf16[224,256]{1,0:T(8,128)(2,1)S(1)}, u32[]{:S(2)}, u32[]{:S(2)}) collective-permute-start(bf16[224,256]{1,0:T(8,128)(2,1)S(1)} %get-tuple-element.62), channel_id=1, source_target_pairs={{0,6},{1,7},{2,0},{3,1},{4,2},{5,3},{6,4},{7,5},{8,14},{9,15},{10,... | collective-permute-start | bytes 344072 | tf_op jit(solution)/shard_map/ppermute | solution.py:373
  86.5 7.2 %collective-permute-start.22 = (bf16[224,256]{1,0:T(8,128)(2,1)S(1)}, bf16[224,256]{1,0:T(8,128)(2,1)S(1)}, u32[]{:S(2)}, u32[]{:S(2)}) collective-permute-start(bf16[224,256]{1,0:T(8,128)(2,1)S(1)} %get-tuple-element.63), channel_id=1, source_target_pairs={{0,4},{1,5},{2,6},{3,7},{4,0},{5,1},{6,2},{7,3},{8,12},{9,13},{10,... | collective-permute-start | bytes 344072 | tf_op jit(solution)/shard_map/ppermute | solution.py:373
  93.8 6.5 %collective-permute-start.25 = (bf16[240,256]{1,0:T(8,128)(2,1)S(1)}, bf16[240,256]{1,0:T(8,128)(2,1)S(1)}, u32[]{:S(2)}, u32[]{:S(2)}) collective-permute-start(bf16[240,256]{1,0:T(8,128)(2,1)S(1)} %shard_map.64.own), channel_id=1, source_target_pairs={{0,16},{8,24},{16,0},{24,8},{32,48},{40,56},{48,32},{56,40},{64,80... | collective-permute-start | bytes 368648 | tf_op jit(solution)/shard_map/ppermute | solution.py:373
  93.9 6.5 %collective-permute-start.24 = (bf16[240,256]{1,0:T(8,128)(2,1)S(1)}, bf16[240,256]{1,0:T(8,128)(2,1)S(1)}, u32[]{:S(2)}, u32[]{:S(2)}) collective-permute-start(bf16[240,256]{1,0:T(8,128)(2,1)S(1)} %shard_map.64.own), channel_id=1, source_target_pairs={{0,24},{8,0},{16,8},{24,16},{32,56},{40,32},{48,40},{56,48},{64,88... | collective-permute-start | bytes 368648 | tf_op jit(solution)/shard_map/ppermute | solution.py:373
  94.0 7.6 %collective-permute-start.23 = (bf16[240,256]{1,0:T(8,128)(2,1)S(1)}, bf16[240,256]{1,0:T(8,128)(2,1)S(1)}, u32[]{:S(2)}, u32[]{:S(2)}) collective-permute-start(bf16[240,256]{1,0:T(8,128)(2,1)S(1)} %shard_map.64.own), channel_id=1, source_target_pairs={{0,8},{8,16},{16,24},{24,0},{32,40},{40,48},{48,56},{56,32},{64,72... | collective-permute-start | bytes 368648 | tf_op jit(solution)/shard_map/ppermute | solution.py:373
  101.7 8.1 %collective-permute-start.28 = (bf16[240,256]{1,0:T(8,128)(2,1)S(1)}, bf16[240,256]{1,0:T(8,128)(2,1)S(1)}, u32[]{:S(2)}, u32[]{:S(2)}) collective-permute-start(bf16[240,256]{1,0:T(8,128)(2,1)S(1)} %shard_map.65.own), channel_id=1, source_target_pairs={{0,64},{8,72},{16,80},{24,88},{32,96},{40,104},{48,112},{56,120},{... | collective-permute-start | bytes 368648 | tf_op jit(solution)/shard_map/ppermute | solution.py:373
  103.4 10.5 %collective-permute-start.27 = (bf16[240,256]{1,0:T(8,128)(2,1)S(1)}, bf16[240,256]{1,0:T(8,128)(2,1)S(1)}, u32[]{:S(2)}, u32[]{:S(2)}) collective-permute-start(bf16[240,256]{1,0:T(8,128)(2,1)S(1)} %shard_map.65.own), channel_id=1, source_target_pairs={{0,96},{8,104},{16,112},{24,120},{32,0},{40,8},{48,16},{56,24},{64... | collective-permute-start | bytes 368648 | tf_op jit(solution)/shard_map/ppermute | solution.py:373
  109.8 6.1 %collective-permute-start.26 = (bf16[240,256]{1,0:T(8,128)(2,1)S(1)}, bf16[240,256]{1,0:T(8,128)(2,1)S(1)}, u32[]{:S(2)}, u32[]{:S(2)}) collective-permute-start(bf16[240,256]{1,0:T(8,128)(2,1)S(1)} %shard_map.65.own), channel_id=1, source_target_pairs={{0,32},{8,40},{16,48},{24,56},{32,64},{40,72},{48,80},{56,88},{64,... | collective-permute-start | bytes 368648 | tf_op jit(solution)/shard_map/ppermute | solution.py:373
  (12 other events, 70.5 us)

commit v6 on v5

--- a/solution.py
+++ b/solution.py
@@ -260,46 +260,39 @@
 STEPS = (1, 3, 2)
 
 
-def split_core_kernel(where, keep, got, *refs):
-    y = where[3]
-    held, *out = refs[-4:]
-
-    def add(x, quarter):
-        at = pl.ds(pl.multiple_of(x * SHARD_PAD + quarter * QUARTER, UNIT), QUARTER)
-        return keep[at] + got[at].astype(f32)
-
-    for x in range(2):
-        held[x] = add(x, y)
-        for step, to in zip(STEPS, out):
-            to[x] = add(x, (y + step) & 3).astype(bf16)
+def split_core_kernel(where, keep_up, got_up, keep_low, got_low, held, *out):
+    x_own = where[2]
+
+    def total(x, to):
+        at = pl.ds(pl.multiple_of((x & 1) * SHARD_PAD, UNIT), SHARD_PAD)
+
+        @pl.when(x < 2)
+        def _():
+            to[...] = (keep_low[at] + got_low[at].astype(f32)).astype(to.dtype)
+
+        @pl.when(x >= 2)
+        def _():
+            to[...] = (keep_up[at] + got_up[at].astype(f32)).astype(to.dtype)
+
+    total(x_own, held)
+    for step, to in zip(STEPS, out):
+        total((x_own + step) & 3, to)
 
 
 def ring_add(own, arrived, at):
     return (own[at].astype(f32) + arrived[2][at].astype(f32)) + (arrived[0][at].astype(f32) + arrived[1][at].astype(f32))
 
 
-def split_y_kernel(where, low, l0, l1, l2, up, u0, u1, u2, order, held, *out):
-    x_own = where[2]
-
-    def total(x, use):
-        @pl.when(x < 2)
-        def _():
-            use(ring_add(low, (l0, l1, l2), x & 1))
-
-        @pl.when(x >= 2)
-        def _():
-            use(ring_add(up, (u0, u1, u2), x & 1))
-
-    def hold(value):
-        held[...] = value
-
-    total(x_own, hold)
+def split_x_kernel(where, own, a0, a1, a2, order, held, *out):
+    y = where[3]
+
+    def total(quarter):
+        at = pl.ds(pl.multiple_of((quarter & 3) * QUARTER, UNIT), QUARTER)
+        return ring_add(own, (a0, a1, a2), at)
+
+    held[...] = total(y)
     for step, to in zip(STEPS, out):
-
-        def give(value, to=to):
-            to[...] = value.astype(bf16)
-
-        total((x_own + step) & 3, give)
+        to[...] = total(y + step).astype(bf16)
 
 
 def write_sums(sums, rows, out):
@@ -321,7 +314,7 @@
     return (read_sums(own) + read_sums(arrived[2])) + (read_sums(arrived[0]) + read_sums(arrived[1]))
 
 
-def split_x_kernel(held, a0, a1, a2, sums0, sums1, out, rows):
+def split_y_kernel(held, a0, a1, a2, sums0, sums1, out, rows):
     out[:QUARTER] = ring_add(held, (a0, a1, a2), slice(None)).astype(bf16)
     write_sums(sums0[...] + sums1[...], rows, out)
 
@@ -456,16 +449,17 @@
     )
     got_low = swap_core(send_low)
 
-    block = lambda *dims: (S(dims + (QUARTER, C), f32),) + (S(dims + (QUARTER, C), bf16),) * 3
-    up, *out_up = call(split_core_kernel, block(2), (where, keep_up, got_up), scalars=1, order=(keep_low,))
-    low, *out_low = call(split_core_kernel, block(2), (where, keep_low, got_low), scalars=1, order=(up,))
+    block = lambda rows: (S((rows, C), f32),) + (S((rows, C), bf16),) * 3
+    held, *out = call(
+        split_core_kernel, block(SHARD_PAD), (where, keep_up, got_up, keep_low, got_low), scalars=1
+    )
     grad0, sums0, full = call(
         partial(first_grad_kernel, count),
         (S((ROWS, C), f32), S((2, C), f32), S((8 * SHARD, C), bf16)),
         (where, stats, clip, near, after, mine, other),
         flops=27 * tap_flops // 2,
         scalars=1,
-        order=(low,),
+        order=(held,),
     )
     later = call(widths_kernel, S((3, 1, PADDED, C), bf16), (later,), order=(sums0,))
     grad1, sums1 = call(
@@ -475,11 +469,12 @@
         flops=27 * tap_flops // 2,
         order=(sums0,),
     )
-    got = (low, *ring("y", out_low), up, *ring("y", out_up))
-    held, *out = call(split_y_kernel, block(), (where, *got), scalars=1, order=(sums1,))
+    held, *out = call(
+        split_x_kernel, block(QUARTER), (where, held, *ring("x", out)), scalars=1, order=(sums1,)
+    )
     rows16 = [pltpu.VMEM((16, C), f32)]
     message = S((QUARTER + 16, C), bf16)
-    own = call(split_x_kernel, message, (held, *ring("x", out), sums0, sums1), rows16)
+    own = call(split_y_kernel, message, (held, *ring("y", out), sums0, sums1), rows16)
     own = call(reduced_kernel, message, (own, *ring("z", [own] * 3)), rows16)
     grad_weight, sums = call(
         finish_kernel,

time: 121 us -> 112 us (0.926)
  starting transfers between devices: 48.7 us -> 43.2 us
  waiting for transfers between devices: 34.2 us -> 32.2 us
    ppermute x21 -> x18, starting transfers between devices: 38.9 us -> 30.6 us  [ring(): got.append(lax.ppermute(block, name, route))]
    ppermute x3, waiting for transfers between devices: 4.54 us -> 1.3 us  [passed(): return lax.ppermute(block, 'tm', route)]
    ppermute x3, starting transfers between devices: 4.41 us -> 7.15 us  [passed(): return lax.ppermute(block, 'tm', route)]
    pallas_call x18 -> x17, Pallas kernels: 33.1 us -> 32.5 us  [call(): pl.pallas_call(kernel, out_shape=out_shape, in_specs=specs, out_specs=out...]
    ppermute x21 -> x18, waiting for transfers between devices: 27.7 us -> 27.8 us  [ring(): got.append(lax.ppermute(block, name, route))]
  transfers between devices with their start and end apart: 29 -> 26, of which waited for: 12 -> 17; matrix products, arithmetic and copies ran while one was open for 0% -> 0% of each run, Pallas kernels for 24% -> 25%
where the time goes in v6:
time: 112 us; the launch traced here: 111 us
  starting transfers between devices  43.2 us (39%)
  Pallas kernels  32.5 us (29%)
  waiting for transfers between devices  32.2 us (29%)
  local copies, waits for them, and re-layouts  2.47 us (2%)
    pallas_call x17, Pallas kernels, call(): pl.pallas_call(kernel, out_shape=out_shape, in_specs=specs, out_specs=out...  32.5 us
    ppermute x18, starting transfers between devices, ring(): got.append(lax.ppermute(block, name, route))  30.6 us
    ppermute x18, waiting for transfers between devices, ring(): got.append(lax.ppermute(block, name, route))  27.8 us
    ppermute x3, starting transfers between devices, passed(): return lax.ppermute(block, 'tm', route)  7.15 us
    ppermute x2, starting transfers between devices, swap(): return lax.ppermute(block, name, route)  4.66 us
    unnamed x14, local copies, waits for them, and re-layouts  2.47 us
  transfers between devices with their start and end apart: 26, of which 17 were waited for; matrix products, arithmetic and copies ran while one was open for 0% of the time, Pallas kernels for 25%

profile of v6, /device:TPU:6, one launch (start us, length us, event | category | flops | bytes accessed | tf_op | source)
XLA Modules:
  0.0 111.3 jit_solution(14045730607309628545)
XLA Ops:
  1.5 2.4 %collective-permute-start.6 = (bf16[864,256]{1,0:T(8,128)(2,1)}, bf16[864,256]{1,0:T(8,128)(2,1)S(1)}, u32[]{:S(2)}, u32[]{:S(2)}) collective-permute-start(bf16[864,256]{1,0:T(8,128)(2,1)} %own.1), channel_id=1, source_target_pairs={{0,2},{1,3},{2,4},{3,5},{4,6},{5,7},{6,0},{7,1},{8,10},{9,11},{10,... | collective-permute-start | bytes 1327112 | tf_op jit(solution)/shard_map/ppermute | solution.py:366
  7.1 4.0 %collective-permute-start.2 = (f32[2,256]{1,0:T(2,128)S(1)}, f32[2,256]{1,0:T(2,128)S(1)}, u32[]{:S(2)}, u32[]{:S(2)}) collective-permute-start(f32[2,256]{1,0:T(2,128)S(1)} %get-tuple-element.31.own), channel_id=1, source_target_pairs={{0,16},{8,24},{16,0},{24,8},{32,48},{40,56},{48,32},{56,40},{64,80... | collective-permute-start | bytes 6152 | tf_op jit(solution)/shard_map/ppermute | solution.py:366
  14.6 3.2 %collective-permute-done.before = f32[2,256]{1,0:T(2,128)S(1)} collective-permute-done((f32[2,256]{1,0:T(2,128)S(1)}, f32[2,256]{1,0:T(2,128)S(1)}, u32[]{:S(2)}, u32[]{:S(2)}) %collective-permute-start) | collective-permute-done | bytes 2080 | tf_op jit(solution)/shard_map/ppermute | solution.py:366
  19.5 2.0 %collective-permute-done.3 = f32[2,256]{1,0:T(2,128)S(1)} collective-permute-done((f32[2,256]{1,0:T(2,128)S(1)}, f32[2,256]{1,0:T(2,128)S(1)}, u32[]{:S(2)}, u32[]{:S(2)}) %collective-permute-start.3) | collective-permute-done | bytes 2080 | tf_op jit(solution)/shard_map/ppermute | solution.py:376
  21.5 3.0 %collective-permute-start.4 = (f32[2,256]{1,0:T(2,128)S(1)}, f32[2,256]{1,0:T(2,128)S(1)}, u32[]{:S(2)}, u32[]{:S(2)}) collective-permute-start(f32[2,256]{1,0:T(2,128)S(1)} %add.6), channel_id=1, source_target_pairs={{0,96},{8,104},{16,112},{24,120},{32,64},{40,72},{48,80},{56,88},{... | collective-permute-start | bytes 6152 | tf_op jit(solution)/shard_map/ppermute | solution.py:376
  26.5 4.6 %collective-permute-start.10 = (bf16[1024,256]{1,0:T(8,128)(2,1)S(1)}, bf16[1024,256]{1,0:T(8,128)(2,1)S(1)}, u32[]{:S(2)}, u32[]{:S(2)}) collective-permute-start(bf16[1024,256]{1,0:T(8,128)(2,1)S(1)} %get-tuple-element.41), channel_id=1, source_target_pairs={{0,8},{8,16},{16,24},{24,32},{32,40},{40,48},{48,56},{56,64},{64,7... | collective-permute-start | bytes 1572872 | tf_op jit(solution)/shard_map/ppermute | solution.py:385
  31.1 5.2 %shard_map.53 = (bf16[2,1024,256]{2,1,0:T(8,128)(2,1)S(1)}, f32[1824,256]{1,0:T(8,128)S(1)}, bf16[1824,256]{1,0:T(8,128)(2,1)S(1)}) custom-call(s32[4]{0:T(128)S(1)} %pad_add_fusion.where, f32[2,256]{1,0:T(2,128)S(1)} %add.7.stats, bf16[2,1024,256]{2,1,0:T(8,128)(2,1)S(1)} %bitcast.13, bf16[3,2,1152,256]{3,2,1,0:T(8,128)(2,1)S(1)} %shard_map.52.near), custom_call_target="tpu_custom_call" | custom-call | flops 2415919104 | tf_op jit(solution)/shard_map/pallas_call | solution.py:343
  37.4 2.0 %shard_map.56 = (f32[1824,256]{1,0:T(8,128)S(1)}, bf16[1824,256]{1,0:T(8,128)(2,1)S(1)}) custom-call(s32[4]{0:T(128)S(1)} %pad_add_fusion.where, bf16[2,1024,256]{2,1,0:T(8,128)(2,1)S(1)} %get-tuple-element.35.order.act, bf16[3,2,1152,256]{3,2,1,0:T(8,128)(2,1)S(1)} %shard_map.52.near, ...), custom_call_target="tpu_custom_call", output_to_operand_aliasing={{0}: (4, {}), {1}: (5, {})} | custom-call | flops 1207959552 | tf_op jit(solution)/shard_map/pallas_call | solution.py:343
  39.9 6.1 %shard_map.57 = (f32[1824,256]{1,0:T(8,128)S(1)}, bf16[1824,256]{1,0:T(8,128)(2,1)S(1)}) custom-call(s32[4]{0:T(128)S(1)} %pad_add_fusion.where, f32[2,256]{1,0:T(2,128)S(1)} %add.7.stats, bf16[2,1024,256]{2,1,0:T(8,128)(2,1)S(1)} %get-tuple-element.35.order.act, bf16[1024,256]{1,0:T(8,128)(2,1)S(1)} %collective-permute-done.10.before, ...), custom_call_target="tpu_custom_call" | custom-call | flops 3623878656 | tf_op jit(solution)/shard_map/pallas_call | solution.py:343
  49.5 2.2 %collective-permute-start.12 = (bf16[896,256]{1,0:T(8,128)(2,1)S(1)}, bf16[896,256]{1,0:T(8,128)(2,1)S(1)}, u32[]{:S(2)}, u32[]{:S(2)}) collective-permute-start(bf16[896,256]{1,0:T(8,128)(2,1)S(1)} %get-tuple-element.45), channel_id=1, source_target_pairs={{0,2},{1,3},{2,4},{3,5},{4,6},{5,7},{6,0},{7,1},{8,10},{9,11},{10,... | collective-permute-start | bytes 1376264 | tf_op jit(solution)/shard_map/ppermute | solution.py:366
  51.7 3.3 %collective-permute-start.14 = (bf16[896,256]{1,0:T(8,128)(2,1)S(1)}, bf16[896,256]{1,0:T(8,128)(2,1)S(1)}, u32[]{:S(2)}, u32[]{:S(2)}) collective-permute-start(bf16[896,256]{1,0:T(8,128)(2,1)S(1)} %get-tuple-element.47), channel_id=1, source_target_pairs={{0,4},{1,5},{2,6},{3,7},{4,0},{5,1},{6,2},{7,3},{8,12},{9,13},{10,... | collective-permute-start | bytes 1376264 | tf_op jit(solution)/shard_map/ppermute | solution.py:366
  54.9 6.1 %shard_map.59 = (f32[1024,256]{1,0:T(8,128)S(1)}, f32[2,256]{1,0:T(2,128)S(1)}, bf16[6912,256]{1,0:T(8,128)(2,1)S(1)}) custom-call(s32[4]{0:T(128)S(1)} %pad_add_fusion.where, f32[2,256]{1,0:T(2,128)S(1)} %add.7.stats, bf16[2,1024,256]{2,1,0:T(8,128)(2,1)S(1)} %bitcast.14, bf16[3,2,1152,256]{3,2,1,0:T(8,128)(2,1)S(1)} %shard_map.52.near, ...), custom_call_target="tpu_custom_call" | custom-call | flops 3623878656 | tf_op jit(solution)/shard_map/pallas_call | solution.py:343
  62.6 5.4 %shard_map.61 = (f32[1024,256]{1,0:T(8,128)S(1)}, f32[2,256]{1,0:T(2,128)S(1)}) custom-call(f32[2,256]{1,0:T(2,128)S(1)} %add.7.stats, bf16[2,1024,256]{2,1,0:T(8,128)(2,1)S(1)} %bitcast.15, bf16[3,2,1152,256]{3,2,1,0:T(8,128)(2,1)S(1)} %shard_map.52.near, bf16[3,1,1152,256]{3,2,1,0:T(8,128)(2,1)S(1)} %shard_map.54.after, ...), custom_call_target="tpu_custom_call" | custom-call | flops 3623878656 | tf_op jit(solution)/shard_map/pallas_call | solution.py:343
  68.0 3.6 %collective-permute-done.12.a0 = bf16[896,256]{1,0:T(8,128)(2,1)S(1)} collective-permute-done((bf16[896,256]{1,0:T(8,128)(2,1)S(1)}, bf16[896,256]{1,0:T(8,128)(2,1)S(1)}, u32[]{:S(2)}, u32[]{:S(2)}) %collective-permute-start.12) | collective-permute-done | bytes 458784 | tf_op jit(solution)/shard_map/ppermute | solution.py:366
  71.6 3.4 %collective-permute-done.14.a2 = bf16[896,256]{1,0:T(8,128)(2,1)S(1)} collective-permute-done((bf16[896,256]{1,0:T(8,128)(2,1)S(1)}, bf16[896,256]{1,0:T(8,128)(2,1)S(1)}, u32[]{:S(2)}, u32[]{:S(2)}) %collective-permute-start.14) | collective-permute-done | bytes 458784 | tf_op jit(solution)/shard_map/ppermute | solution.py:366
  75.8 5.1 %collective-permute-start.17 = (bf16[224,256]{1,0:T(8,128)(2,1)S(1)}, bf16[224,256]{1,0:T(8,128)(2,1)S(1)}, u32[]{:S(2)}, u32[]{:S(2)}) collective-permute-start(bf16[224,256]{1,0:T(8,128)(2,1)S(1)} %get-tuple-element.53), channel_id=1, source_target_pairs={{0,32},{8,40},{16,48},{24,56},{32,64},{40,72},{48,80},{56,88},{64,... | collective-permute-start | bytes 344072 | tf_op jit(solution)/shard_map/ppermute | solution.py:366
  80.9 2.2 %collective-permute-start.19 = (bf16[224,256]{1,0:T(8,128)(2,1)S(1)}, bf16[224,256]{1,0:T(8,128)(2,1)S(1)}, u32[]{:S(2)}, u32[]{:S(2)}) collective-permute-start(bf16[224,256]{1,0:T(8,128)(2,1)S(1)} %get-tuple-element.55), channel_id=1, source_target_pairs={{0,64},{8,72},{16,80},{24,88},{32,96},{40,104},{48,112},{56,120},{... | collective-permute-start | bytes 344072 | tf_op jit(solution)/shard_map/ppermute | solution.py:366
  87.8 2.7 %collective-permute-start.21 = (bf16[240,256]{1,0:T(8,128)(2,1)S(1)}, bf16[240,256]{1,0:T(8,128)(2,1)S(1)}, u32[]{:S(2)}, u32[]{:S(2)}) collective-permute-start(bf16[240,256]{1,0:T(8,128)(2,1)S(1)} %shard_map.63.own), channel_id=1, source_target_pairs={{0,24},{8,0},{16,8},{24,16},{32,56},{40,32},{48,40},{56,48},{64,88... | collective-permute-start | bytes 368648 | tf_op jit(solution)/shard_map/ppermute | solution.py:366
  90.6 3.3 %collective-permute-done.22.a2 = bf16[240,256]{1,0:T(8,128)(2,1)S(1)} collective-permute-done((bf16[240,256]{1,0:T(8,128)(2,1)S(1)}, bf16[240,256]{1,0:T(8,128)(2,1)S(1)}, u32[]{:S(2)}, u32[]{:S(2)}) %collective-permute-start.22) | collective-permute-done | bytes 122912 | tf_op jit(solution)/shard_map/ppermute | solution.py:366
  94.7 2.0 %collective-permute-done.20.a0 = bf16[240,256]{1,0:T(8,128)(2,1)S(1)} collective-permute-done((bf16[240,256]{1,0:T(8,128)(2,1)S(1)}, bf16[240,256]{1,0:T(8,128)(2,1)S(1)}, u32[]{:S(2)}, u32[]{:S(2)}) %collective-permute-start.20) | collective-permute-done | bytes 122912 | tf_op jit(solution)/shard_map/ppermute | solution.py:366
  96.8 2.5 %collective-permute-start.25 = (bf16[240,256]{1,0:T(8,128)(2,1)S(1)}, bf16[240,256]{1,0:T(8,128)(2,1)S(1)}, u32[]{:S(2)}, u32[]{:S(2)}) collective-permute-start(bf16[240,256]{1,0:T(8,128)(2,1)S(1)} %shard_map.64.own), channel_id=1, source_target_pairs={{0,64},{8,72},{16,80},{24,88},{32,96},{40,104},{48,112},{56,120},{... | collective-permute-start | bytes 368648 | tf_op jit(solution)/shard_map/ppermute | solution.py:366
  99.3 2.3 %collective-permute-start.24 = (bf16[240,256]{1,0:T(8,128)(2,1)S(1)}, bf16[240,256]{1,0:T(8,128)(2,1)S(1)}, u32[]{:S(2)}, u32[]{:S(2)}) collective-permute-start(bf16[240,256]{1,0:T(8,128)(2,1)S(1)} %shard_map.64.own), channel_id=1, source_target_pairs={{0,96},{8,104},{16,112},{24,120},{32,0},{40,8},{48,16},{56,24},{64... | collective-permute-start | bytes 368648 | tf_op jit(solution)/shard_map/ppermute | solution.py:366
  104.6 3.1 %collective-permute-done.23.a0 = bf16[240,256]{1,0:T(8,128)(2,1)S(1)} collective-permute-done((bf16[240,256]{1,0:T(8,128)(2,1)S(1)}, bf16[240,256]{1,0:T(8,128)(2,1)S(1)}, u32[]{:S(2)}, u32[]{:S(2)}) %collective-permute-start.23) | collective-permute-done | bytes 122912 | tf_op jit(solution)/shard_map/ppermute | solution.py:366
  109.2 2.1 %shard_map.66 = bf16[2,1024,256]{2,1,0:T(8,128)(2,1)} custom-call(f32[2,256]{1,0:T(2,128)S(1)} %add.7.stats, f32[2,256]{1,0:T(2,128)S(1)} %get-tuple-element.56.sums, bf16[2,1024,256]{2,1,0:T(8,128)(2,1)S(1)} %bitcast.16, bf16[2,1024,256]{2,1,0:T(8,128)(2,1)S(1)} %bitcast.11, f32[1024,256]{1,0:T(8,128)S(1)} %get-tuple-element.57.grad0, ...), custom_call_target="tpu_custom_call" | custom-call | tf_op jit(solution)/shard_map/pallas_call | solution.py:343
  (62 shorter events, 28.7 us)
Async XLA Ops:
  0.6 35.6 %collective-permute-start.7 = (bf16[864,256]{1,0:T(8,128)(2,1)}, bf16[864,256]{1,0:T(8,128)(2,1)S(1)}, u32[]{:S(2)}, u32[]{:S(2)}) collective-permute-start(bf16[864,256]{1,0:T(8,128)(2,1)} %own.1), channel_id=1, source_target_pairs={{0,6},{1,7},{2,0},{3,1},{4,2},{5,3},{6,4},{7,5},{8,14},{9,15},{10,... | collective-permute-start | bytes 1327112 | tf_op jit(solution)/shard_map/ppermute | solution.py:366
  1.5 34.7 %collective-permute-start.6 = (bf16[864,256]{1,0:T(8,128)(2,1)}, bf16[864,256]{1,0:T(8,128)(2,1)S(1)}, u32[]{:S(2)}, u32[]{:S(2)}) collective-permute-start(bf16[864,256]{1,0:T(8,128)(2,1)} %own.1), channel_id=1, source_target_pairs={{0,2},{1,3},{2,4},{3,5},{4,6},{5,7},{6,0},{7,1},{8,10},{9,11},{10,... | collective-permute-start | bytes 1327112 | tf_op jit(solution)/shard_map/ppermute | solution.py:366
  3.9 32.3 %collective-permute-start.8 = (bf16[864,256]{1,0:T(8,128)(2,1)}, bf16[864,256]{1,0:T(8,128)(2,1)S(1)}, u32[]{:S(2)}, u32[]{:S(2)}) collective-permute-start(bf16[864,256]{1,0:T(8,128)(2,1)} %own.1), channel_id=1, source_target_pairs={{0,4},{1,5},{2,6},{3,7},{4,0},{5,1},{6,2},{7,3},{8,12},{9,13},{10,... | collective-permute-start | bytes 1327112 | tf_op jit(solution)/shard_map/ppermute | solution.py:366
  7.1 5.5 %collective-permute-start.2 = (f32[2,256]{1,0:T(2,128)S(1)}, f32[2,256]{1,0:T(2,128)S(1)}, u32[]{:S(2)}, u32[]{:S(2)}) collective-permute-start(f32[2,256]{1,0:T(2,128)S(1)} %get-tuple-element.31.own), channel_id=1, source_target_pairs={{0,16},{8,24},{16,0},{24,8},{32,48},{40,56},{48,32},{56,40},{64,80... | collective-permute-start | bytes 6152 | tf_op jit(solution)/shard_map/ppermute | solution.py:366
  12.6 5.2 %collective-permute-start = (f32[2,256]{1,0:T(2,128)S(1)}, f32[2,256]{1,0:T(2,128)S(1)}, u32[]{:S(2)}, u32[]{:S(2)}) collective-permute-start(f32[2,256]{1,0:T(2,128)S(1)} %get-tuple-element.31.own), channel_id=1, source_target_pairs={{0,8},{8,16},{16,24},{24,0},{32,40},{40,48},{48,56},{56,32},{64,72... | collective-permute-start | bytes 6152 | tf_op jit(solution)/shard_map/ppermute | solution.py:366
  17.8 3.7 %collective-permute-start.3 = (f32[2,256]{1,0:T(2,128)S(1)}, f32[2,256]{1,0:T(2,128)S(1)}, u32[]{:S(2)}, u32[]{:S(2)}) collective-permute-start(f32[2,256]{1,0:T(2,128)S(1)} %get-tuple-element.34.refs_0_), channel_id=1, source_target_pairs={{0,32},{8,40},{16,48},{24,56},{32,0},{40,8},{48,16},{56,24},{64,96... | collective-permute-start | bytes 6152 | tf_op jit(solution)/shard_map/ppermute | solution.py:376
  21.5 5.0 %collective-permute-start.4 = (f32[2,256]{1,0:T(2,128)S(1)}, f32[2,256]{1,0:T(2,128)S(1)}, u32[]{:S(2)}, u32[]{:S(2)}) collective-permute-start(f32[2,256]{1,0:T(2,128)S(1)} %add.6), channel_id=1, source_target_pairs={{0,96},{8,104},{16,112},{24,120},{32,64},{40,72},{48,80},{56,88},{... | collective-permute-start | bytes 6152 | tf_op jit(solution)/shard_map/ppermute | solution.py:376
  25.2 11.9 %collective-permute-start.5 = (bf16[1024,256]{1,0:T(8,128)(2,1)S(1)}, bf16[1024,256]{1,0:T(8,128)(2,1)S(1)}, u32[]{:S(2)}, u32[]{:S(2)}) collective-permute-start(bf16[1024,256]{1,0:T(8,128)(2,1)S(1)} %get-tuple-element.36), channel_id=1, source_target_pairs={{8,0},{16,8},{24,16},{32,24},{40,32},{48,40},{56,48},{64,56},{72,6... | collective-permute-start | bytes 1572872 | tf_op jit(solution)/shard_map/ppermute | solution.py:385
  26.5 13.5 %collective-permute-start.10 = (bf16[1024,256]{1,0:T(8,128)(2,1)S(1)}, bf16[1024,256]{1,0:T(8,128)(2,1)S(1)}, u32[]{:S(2)}, u32[]{:S(2)}) collective-permute-start(bf16[1024,256]{1,0:T(8,128)(2,1)S(1)} %get-tuple-element.41), channel_id=1, source_target_pairs={{0,8},{8,16},{16,24},{24,32},{32,40},{40,48},{48,56},{56,64},{64,7... | collective-permute-start | bytes 1572872 | tf_op jit(solution)/shard_map/ppermute | solution.py:385
  37.0 18.0 %collective-permute-start.16 = (bf16[4,864,256]{2,1,0:T(8,128)(2,1)S(1)}, bf16[4,864,256]{2,1,0:T(8,128)(2,1)S(1)}, u32[]{:S(2)}, u32[]{:S(2)}) collective-permute-start(bf16[4,864,256]{2,1,0:T(8,128)(2,1)S(1)} %shard_map.55.order.mine), channel_id=1, source_target_pairs={{0,1},{1,0},{2,3},{3,2},{4,5},{5,4},{6,7},{7,6},{8,9},{9,8},{10,11... | collective-permute-start | bytes 5308424 | tf_op jit(solution)/shard_map/ppermute | solution.py:380
  39.4 8.0 %collective-permute-start.9 = (bf16[1824,256]{1,0:T(8,128)(2,1)S(1)}, bf16[1824,256]{1,0:T(8,128)(2,1)S(1)}, u32[]{:S(2)}, u32[]{:S(2)}) collective-permute-start(bf16[1824,256]{1,0:T(8,128)(2,1)S(1)} %get-tuple-element.40.order), channel_id=1, source_target_pairs={{0,1},{1,0},{2,3},{3,2},{4,5},{5,4},{6,7},{7,6},{8,9},{9,8},{10,11... | collective-permute-start | bytes 2801672 | tf_op jit(solution)/shard_map/ppermute | solution.py:380
  46.2 16.2 %collective-permute-start.15 = (bf16[1024,256]{1,0:T(8,128)(2,1)S(1)}, bf16[1024,256]{1,0:T(8,128)(2,1)S(1)}, u32[]{:S(2)}, u32[]{:S(2)}) collective-permute-start(bf16[1024,256]{1,0:T(8,128)(2,1)S(1)} %copy-done.6), channel_id=1, source_target_pairs={{8,0},{16,8},{24,16},{32,24},{40,32},{48,40},{56,48},{64,56},{72,6... | collective-permute-start | bytes 1572872 | tf_op jit(solution)/shard_map/ppermute | solution.py:385
  49.5 22.1 %collective-permute-start.12 = (bf16[896,256]{1,0:T(8,128)(2,1)S(1)}, bf16[896,256]{1,0:T(8,128)(2,1)S(1)}, u32[]{:S(2)}, u32[]{:S(2)}) collective-permute-start(bf16[896,256]{1,0:T(8,128)(2,1)S(1)} %get-tuple-element.45), channel_id=1, source_target_pairs={{0,2},{1,3},{2,4},{3,5},{4,6},{5,7},{6,0},{7,1},{8,10},{9,11},{10,... | collective-permute-start | bytes 1376264 | tf_op jit(solution)/shard_map/ppermute | solution.py:366
  51.7 19.9 %collective-permute-start.13 = (bf16[896,256]{1,0:T(8,128)(2,1)S(1)}, bf16[896,256]{1,0:T(8,128)(2,1)S(1)}, u32[]{:S(2)}, u32[]{:S(2)}) collective-permute-start(bf16[896,256]{1,0:T(8,128)(2,1)S(1)} %get-tuple-element.46), channel_id=1, source_target_pairs={{0,6},{1,7},{2,0},{3,1},{4,2},{5,3},{6,4},{7,5},{8,14},{9,15},{10,... | collective-permute-start | bytes 1376264 | tf_op jit(solution)/shard_map/ppermute | solution.py:366
  51.7 23.3 %collective-permute-start.14 = (bf16[896,256]{1,0:T(8,128)(2,1)S(1)}, bf16[896,256]{1,0:T(8,128)(2,1)S(1)}, u32[]{:S(2)}, u32[]{:S(2)}) collective-permute-start(bf16[896,256]{1,0:T(8,128)(2,1)S(1)} %get-tuple-element.47), channel_id=1, source_target_pairs={{0,4},{1,5},{2,6},{3,7},{4,0},{5,1},{6,2},{7,3},{8,12},{9,13},{10,... | collective-permute-start | bytes 1376264 | tf_op jit(solution)/shard_map/ppermute | solution.py:366
  75.8 8.7 %collective-permute-start.17 = (bf16[224,256]{1,0:T(8,128)(2,1)S(1)}, bf16[224,256]{1,0:T(8,128)(2,1)S(1)}, u32[]{:S(2)}, u32[]{:S(2)}) collective-permute-start(bf16[224,256]{1,0:T(8,128)(2,1)S(1)} %get-tuple-element.53), channel_id=1, source_target_pairs={{0,32},{8,40},{16,48},{24,56},{32,64},{40,72},{48,80},{56,88},{64,... | collective-permute-start | bytes 344072 | tf_op jit(solution)/shard_map/ppermute | solution.py:366
  80.9 5.1 %collective-permute-start.18 = (bf16[224,256]{1,0:T(8,128)(2,1)S(1)}, bf16[224,256]{1,0:T(8,128)(2,1)S(1)}, u32[]{:S(2)}, u32[]{:S(2)}) collective-permute-start(bf16[224,256]{1,0:T(8,128)(2,1)S(1)} %get-tuple-element.54), channel_id=1, source_target_pairs={{0,96},{8,104},{16,112},{24,120},{32,0},{40,8},{48,16},{56,24},{64... | collective-permute-start | bytes 344072 | tf_op jit(solution)/shard_map/ppermute | solution.py:366
  80.9 6.3 %collective-permute-start.19 = (bf16[224,256]{1,0:T(8,128)(2,1)S(1)}, bf16[224,256]{1,0:T(8,128)(2,1)S(1)}, u32[]{:S(2)}, u32[]{:S(2)}) collective-permute-start(bf16[224,256]{1,0:T(8,128)(2,1)S(1)} %get-tuple-element.55), channel_id=1, source_target_pairs={{0,64},{8,72},{16,80},{24,88},{32,96},{40,104},{48,112},{56,120},{... | collective-permute-start | bytes 344072 | tf_op jit(solution)/shard_map/ppermute | solution.py:366
  87.3 6.6 %collective-permute-start.22 = (bf16[240,256]{1,0:T(8,128)(2,1)S(1)}, bf16[240,256]{1,0:T(8,128)(2,1)S(1)}, u32[]{:S(2)}, u32[]{:S(2)}) collective-permute-start(bf16[240,256]{1,0:T(8,128)(2,1)S(1)} %shard_map.63.own), channel_id=1, source_target_pairs={{0,16},{8,24},{16,0},{24,8},{32,48},{40,56},{48,32},{56,40},{64,80... | collective-permute-start | bytes 368648 | tf_op jit(solution)/shard_map/ppermute | solution.py:366
  87.8 6.8 %collective-permute-start.21 = (bf16[240,256]{1,0:T(8,128)(2,1)S(1)}, bf16[240,256]{1,0:T(8,128)(2,1)S(1)}, u32[]{:S(2)}, u32[]{:S(2)}) collective-permute-start(bf16[240,256]{1,0:T(8,128)(2,1)S(1)} %shard_map.63.own), channel_id=1, source_target_pairs={{0,24},{8,0},{16,8},{24,16},{32,56},{40,32},{48,40},{56,48},{64,88... | collective-permute-start | bytes 368648 | tf_op jit(solution)/shard_map/ppermute | solution.py:366
  90.6 6.1 %collective-permute-start.20 = (bf16[240,256]{1,0:T(8,128)(2,1)S(1)}, bf16[240,256]{1,0:T(8,128)(2,1)S(1)}, u32[]{:S(2)}, u32[]{:S(2)}) collective-permute-start(bf16[240,256]{1,0:T(8,128)(2,1)S(1)} %shard_map.63.own), channel_id=1, source_target_pairs={{0,8},{8,16},{16,24},{24,0},{32,40},{40,48},{48,56},{56,32},{64,72... | collective-permute-start | bytes 368648 | tf_op jit(solution)/shard_map/ppermute | solution.py:366
  96.8 6.6 %collective-permute-start.25 = (bf16[240,256]{1,0:T(8,128)(2,1)S(1)}, bf16[240,256]{1,0:T(8,128)(2,1)S(1)}, u32[]{:S(2)}, u32[]{:S(2)}) collective-permute-start(bf16[240,256]{1,0:T(8,128)(2,1)S(1)} %shard_map.64.own), channel_id=1, source_target_pairs={{0,64},{8,72},{16,80},{24,88},{32,96},{40,104},{48,112},{56,120},{... | collective-permute-start | bytes 368648 | tf_op jit(solution)/shard_map/ppermute | solution.py:366
  99.3 5.3 %collective-permute-start.24 = (bf16[240,256]{1,0:T(8,128)(2,1)S(1)}, bf16[240,256]{1,0:T(8,128)(2,1)S(1)}, u32[]{:S(2)}, u32[]{:S(2)}) collective-permute-start(bf16[240,256]{1,0:T(8,128)(2,1)S(1)} %shard_map.64.own), channel_id=1, source_target_pairs={{0,96},{8,104},{16,112},{24,120},{32,0},{40,8},{48,16},{56,24},{64... | collective-permute-start | bytes 368648 | tf_op jit(solution)/shard_map/ppermute | solution.py:366
  101.5 6.1 %collective-permute-start.23 = (bf16[240,256]{1,0:T(8,128)(2,1)S(1)}, bf16[240,256]{1,0:T(8,128)(2,1)S(1)}, u32[]{:S(2)}, u32[]{:S(2)}) collective-permute-start(bf16[240,256]{1,0:T(8,128)(2,1)S(1)} %shard_map.64.own), channel_id=1, source_target_pairs={{0,32},{8,40},{16,48},{24,56},{32,64},{40,72},{48,80},{56,88},{64,... | collective-permute-start | bytes 368648 | tf_op jit(solution)/shard_map/ppermute | solution.py:366
  (9 other events, 55.8 us)

commit v7 on v6

--- a/solution.py
+++ b/solution.py
@@ -62,7 +62,7 @@
         target[2, slot, at] = jnp.where(column == 0, 0.0, pltpu.roll(wide, 1, 0)).astype(bf16)
 
 
-def first_kernel(clip, cot, out, first, second, last):
+def first_kernel(clip, out, last):
     def step(i, carry):
         a, b = carry
         at = pl.ds(pl.multiple_of((i & 7) * 128, 128), 128)
@@ -73,9 +73,12 @@
     a, b = lax.fori_loop(0, 2 * ROWS // 128, step, (zero, zero))
     out[0:1] = a.sum(0, keepdims=True)
     out[1:2] = b.sum(0, keepdims=True)
+    last[...] = clip[1]
+
+
+def copy_kernel(cot, order, first, second):
     first[...] = cot[0]
     second[...] = cot[1]
-    last[...] = clip[1]
 
 
 def widths_kernel(cot, *refs):
@@ -283,7 +286,8 @@
     return (own[at].astype(f32) + arrived[2][at].astype(f32)) + (arrived[0][at].astype(f32) + arrived[1][at].astype(f32))
 
 
-def split_x_kernel(where, own, a0, a1, a2, order, held, *out):
+def split_x_kernel(where, own, a0, a1, a2, sums0, sums1, held, sums, m0, m1, m2, rows):
+    out = (m0, m1, m2)
     y = where[3]
 
     def total(quarter):
@@ -291,8 +295,10 @@
         return ring_add(own, (a0, a1, a2), at)
 
     held[...] = total(y)
+    sums[...] = sums0[...] + sums1[...]
     for step, to in zip(STEPS, out):
-        to[...] = total(y + step).astype(bf16)
+        to[:QUARTER] = total(y + step).astype(bf16)
+        write_sums(sums[...], rows, to)
 
 
 def write_sums(sums, rows, out):
@@ -311,26 +317,26 @@
 
 
 def ring_sums(own, arrived):
-    return (read_sums(own) + read_sums(arrived[2])) + (read_sums(arrived[0]) + read_sums(arrived[1]))
-
-
-def split_y_kernel(held, a0, a1, a2, sums0, sums1, out, rows):
-    out[:QUARTER] = ring_add(held, (a0, a1, a2), slice(None)).astype(bf16)
-    write_sums(sums0[...] + sums1[...], rows, out)
-
-
-def reduced_kernel(own, a0, a1, a2, out, rows):
-    out[:QUARTER] = ring_add(own, (a0, a1, a2), slice(0, QUARTER)).astype(bf16)
-    write_sums(ring_sums(own, (a0, a1, a2)), rows, out)
-
-
-def finish_kernel(where, own, a0, a1, a2, grad_weight, sums, full):
+    return (own + read_sums(arrived[2])) + (read_sums(arrived[0]) + read_sums(arrived[1]))
+
+
+def split_y_kernel(held, sums, a0, a1, a2, out, next_sums, rows):
+    out[:QUARTER] = ring_add(held, (a0, a1, a2), slice(0, QUARTER)).astype(bf16)
+    next_sums[...] = ring_sums(sums[...], (a0, a1, a2))
+    write_sums(next_sums[...], rows, out)
+
+
+def reduced_kernel(own, sums, a0, a1, a2, out, next_sums):
+    out[...] = ring_add(own, (a0, a1, a2), slice(0, QUARTER)).astype(bf16)
+    next_sums[...] = ring_sums(sums[...], (a0, a1, a2))
+
+
+def finish_kernel(where, own, a0, a1, a2, grad_weight, full):
     y = where[3]
     for block, distance in ((own, 0), (a0, 3), (a1, 1), (a2, 2)):
         at = pl.ds(pl.multiple_of(((y + distance) & 3) * QUARTER, UNIT), QUARTER)
-        full[at] = block[:QUARTER].astype(f32)
+        full[at] = block[...].astype(f32)
     grad_weight[...] = full[:SHARD]
-    sums[...] = ring_sums(own, (a0, a1, a2))
 
 
 def call(kernel, out_shape, args, scratch=(), flops=0, bytes_accessed=0, scalars=0, order=(), aliases={}, passed_out=0):
@@ -399,8 +405,9 @@
     where = jnp.stack([jnp.asarray(v, jnp.int32) for v in where])
     frame = S((ROWS, C), bf16)
 
-    sums, first, second, last = call(first_kernel, (S((2, C), f32), frame, frame, frame), (clip, cot))
+    sums, last = call(first_kernel, (S((2, C), f32), frame), (clip,))
     got = ring("z", [sums] * 3)
+    first, second = call(copy_kernel, (frame, frame), (cot,), order=(sums,))
     sums, first, last = call(
         ring_sum_kernel,
         (S((2, C), f32), frame, frame),
@@ -414,7 +421,6 @@
     stats = half + swap(half, "y", (3, 2, 1, 0))
     after = call(widths_kernel, S((3, 1, PADDED, C), bf16), (passed(first, -1)[None],))
     before = passed(last, 1)
-    later = passed(second, -1)[None]
 
     rows = 2 * SHARD_PAD + UNIT
     tap_flops = C * C * 2 * ROWS * 2
@@ -453,6 +459,7 @@
     held, *out = call(
         split_core_kernel, block(SHARD_PAD), (where, keep_up, got_up, keep_low, got_low), scalars=1
     )
+    later = passed(second, -1)[None]
     grad0, sums0, full = call(
         partial(first_grad_kernel, count),
         (S((ROWS, C), f32), S((2, C), f32), S((8 * SHARD, C), bf16)),
@@ -469,22 +476,31 @@
         flops=27 * tap_flops // 2,
         order=(sums0,),
     )
-    held, *out = call(
-        split_x_kernel, block(QUARTER), (where, held, *ring("x", out)), scalars=1, order=(sums1,)
-    )
     rows16 = [pltpu.VMEM((16, C), f32)]
     message = S((QUARTER + 16, C), bf16)
-    own = call(split_y_kernel, message, (held, *ring("y", out), sums0, sums1), rows16)
-    own = call(reduced_kernel, message, (own, *ring("z", [own] * 3)), rows16)
-    grad_weight, sums = call(
+    held, sums, *out = call(
+        split_x_kernel,
+        (S((QUARTER, C), f32), S((2, C), f32), message, message, message),
+        (where, held, *ring("x", out), sums0, sums1),
+        rows16,
+        scalars=1,
+    )
+    own, sums = call(split_y_kernel, (message, S((2, C), f32)), (held, sums, *ring("y", out)), rows16)
+    own, sums = call(
+        reduced_kernel, (S((QUARTER, C), bf16), S((2, C), f32)), (own, sums, *ring("z", [own] * 3))
+    )
+    grad_input = call(
+        partial(final_kernel, count),
+        S((2, ROWS, C), bf16),
+        (stats, sums, clip, cot, grad0, grad1),
+        bytes_accessed=8_000_000,
+    )
+    grad_weight = call(
         finish_kernel,
-        (S((SHARD, C), f32), S((2, C), f32)),
+        S((SHARD, C), f32),
         (where, own, *ring("y", [own] * 3)),
         [pltpu.VMEM((SHARD_PAD, C), f32)],
         scalars=1,
-    )
-    grad_input = call(
-        partial(final_kernel, count), S((2, ROWS, C), bf16), (stats, sums, clip, cot, grad0, grad1)
     )
     return grad_input.reshape(shape), grad_weight
 

time: 112 us -> 108 us (0.964)
  waiting for transfers between devices: 32.2 us -> 28.8 us
    ppermute x18, waiting for transfers between devices: 27.8 us -> 24.3 us  [ring(): got.append(lax.ppermute(block, name, route))]
    pallas_call x17 -> x18, Pallas kernels: 32.5 us -> 32.6 us  [call(): pl.pallas_call(kernel, out_shape=out_shape, in_specs=specs, out_specs=out...]
  transfers between devices with their start and end apart: 26 -> 26, of which waited for: 17 -> 15; matrix products, arithmetic and copies ran while one was open for 0% -> 0% of each run, Pallas kernels for 25% -> 28%
where the time goes in v7:
time: 108 us
  starting transfers between devices  43.1 us (40%)
  Pallas kernels  32.6 us (30%)
  waiting for transfers between devices  28.8 us (27%)
  local copies, waits for them, and re-layouts  2.48 us (2%)
    pallas_call x18, Pallas kernels, call(): pl.pallas_call(kernel, out_shape=out_shape, in_specs=specs, out_specs=out...  32.6 us
    ppermute x18, starting transfers between devices, ring(): got.append(lax.ppermute(block, name, route))  30.5 us
    ppermute x18, waiting for transfers between devices, ring(): got.append(lax.ppermute(block, name, route))  24.3 us
    ppermute x3, starting transfers between devices, passed(): return lax.ppermute(block, 'tm', route)  7.15 us
    ppermute x2, starting transfers between devices, swap(): return lax.ppermute(block, name, route)  4.66 us
    unnamed x14, local copies, waits for them, and re-layouts  2.48 us
  transfers between devices with their start and end apart: 26, of which 15 were waited for; matrix products, arithmetic and copies ran while one was open for 0% of the time, Pallas kernels for 28%

profile of v7, /device:TPU:6, one launch (start us, length us, event | category | flops | bytes accessed | tf_op | source)
XLA Modules:
  0.0 108.0 jit_solution(15668345854318017063)
XLA Ops:
  1.5 2.4 %collective-permute-start.6 = (bf16[864,256]{1,0:T(8,128)(2,1)}, bf16[864,256]{1,0:T(8,128)(2,1)S(1)}, u32[]{:S(2)}, u32[]{:S(2)}) collective-permute-start(bf16[864,256]{1,0:T(8,128)(2,1)} %own.1), channel_id=1, source_target_pairs={{0,2},{1,3},{2,4},{3,5},{4,6},{5,7},{6,0},{7,1},{8,10},{9,11},{10,... | collective-permute-start | bytes 1327112 | tf_op jit(solution)/shard_map/ppermute | solution.py:372
  5.8 4.0 %collective-permute-start.2 = (f32[2,256]{1,0:T(2,128)S(1)}, f32[2,256]{1,0:T(2,128)S(1)}, u32[]{:S(2)}, u32[]{:S(2)}) collective-permute-start(f32[2,256]{1,0:T(2,128)S(1)} %get-tuple-element.34.order.own), channel_id=1, source_target_pairs={{0,16},{8,24},{16,0},{24,8},{32,48},{40,56},{48,32},{56,40},{64,80... | collective-permute-start | bytes 6152 | tf_op jit(solution)/shard_map/ppermute | solution.py:372
  14.2 2.4 %collective-permute-done.before = f32[2,256]{1,0:T(2,128)S(1)} collective-permute-done((f32[2,256]{1,0:T(2,128)S(1)}, f32[2,256]{1,0:T(2,128)S(1)}, u32[]{:S(2)}, u32[]{:S(2)}) %collective-permute-start) | collective-permute-done | bytes 2080 | tf_op jit(solution)/shard_map/ppermute | solution.py:372
  18.2 2.0 %collective-permute-done.3 = f32[2,256]{1,0:T(2,128)S(1)} collective-permute-done((f32[2,256]{1,0:T(2,128)S(1)}, f32[2,256]{1,0:T(2,128)S(1)}, u32[]{:S(2)}, u32[]{:S(2)}) %collective-permute-start.3) | collective-permute-done | bytes 2080 | tf_op jit(solution)/shard_map/ppermute | solution.py:382
  20.2 3.0 %collective-permute-start.4 = (f32[2,256]{1,0:T(2,128)S(1)}, f32[2,256]{1,0:T(2,128)S(1)}, u32[]{:S(2)}, u32[]{:S(2)}) collective-permute-start(f32[2,256]{1,0:T(2,128)S(1)} %add.6), channel_id=1, source_target_pairs={{0,96},{8,104},{16,112},{24,120},{32,64},{40,72},{48,80},{56,88},{... | collective-permute-start | bytes 6152 | tf_op jit(solution)/shard_map/ppermute | solution.py:382
  25.2 4.6 %collective-permute-start.10 = (bf16[1024,256]{1,0:T(8,128)(2,1)S(1)}, bf16[1024,256]{1,0:T(8,128)(2,1)S(1)}, u32[]{:S(2)}, u32[]{:S(2)}) collective-permute-start(bf16[1024,256]{1,0:T(8,128)(2,1)S(1)} %get-tuple-element.44), channel_id=1, source_target_pairs={{0,8},{8,16},{16,24},{24,32},{32,40},{40,48},{48,56},{56,64},{64,7... | collective-permute-start | bytes 1572872 | tf_op jit(solution)/shard_map/ppermute | solution.py:391
  29.8 5.2 %shard_map.54 = (bf16[2,1024,256]{2,1,0:T(8,128)(2,1)S(1)}, f32[1824,256]{1,0:T(8,128)S(1)}, bf16[1824,256]{1,0:T(8,128)(2,1)S(1)}) custom-call(s32[4]{0:T(128)S(1)} %pad_add_fusion.where, f32[2,256]{1,0:T(2,128)S(1)} %add.7.stats, bf16[2,1024,256]{2,1,0:T(8,128)(2,1)S(1)} %bitcast.13, bf16[3,2,1152,256]{3,2,1,0:T(8,128)(2,1)S(1)} %shard_map.53.near), custom_call_target="tpu_custom_call" | custom-call | flops 2415919104 | tf_op jit(solution)/shard_map/pallas_call | solution.py:349
  36.1 2.0 %shard_map.57 = (f32[1824,256]{1,0:T(8,128)S(1)}, bf16[1824,256]{1,0:T(8,128)(2,1)S(1)}) custom-call(s32[4]{0:T(128)S(1)} %pad_add_fusion.where, bf16[2,1024,256]{2,1,0:T(8,128)(2,1)S(1)} %get-tuple-element.38.order.act, bf16[3,2,1152,256]{3,2,1,0:T(8,128)(2,1)S(1)} %shard_map.53.near, ...), custom_call_target="tpu_custom_call", output_to_operand_aliasing={{0}: (4, {}), {1}: (5, {})} | custom-call | flops 1207959552 | tf_op jit(solution)/shard_map/pallas_call | solution.py:349
  38.7 6.1 %shard_map.58 = (f32[1824,256]{1,0:T(8,128)S(1)}, bf16[1824,256]{1,0:T(8,128)(2,1)S(1)}) custom-call(s32[4]{0:T(128)S(1)} %pad_add_fusion.where, f32[2,256]{1,0:T(2,128)S(1)} %add.7.stats, bf16[2,1024,256]{2,1,0:T(8,128)(2,1)S(1)} %get-tuple-element.38.order.act, bf16[1024,256]{1,0:T(8,128)(2,1)S(1)} %collective-permute-done.10.before, ...), custom_call_target="tpu_custom_call" | custom-call | flops 3623878656 | tf_op jit(solution)/shard_map/pallas_call | solution.py:349
  48.2 2.2 %collective-permute-start.12 = (bf16[896,256]{1,0:T(8,128)(2,1)S(1)}, bf16[896,256]{1,0:T(8,128)(2,1)S(1)}, u32[]{:S(2)}, u32[]{:S(2)}) collective-permute-start(bf16[896,256]{1,0:T(8,128)(2,1)S(1)} %get-tuple-element.48), channel_id=1, source_target_pairs={{0,2},{1,3},{2,4},{3,5},{4,6},{5,7},{6,0},{7,1},{8,10},{9,11},{10,... | collective-permute-start | bytes 1376264 | tf_op jit(solution)/shard_map/ppermute | solution.py:372
  50.4 3.3 %collective-permute-start.14 = (bf16[896,256]{1,0:T(8,128)(2,1)S(1)}, bf16[896,256]{1,0:T(8,128)(2,1)S(1)}, u32[]{:S(2)}, u32[]{:S(2)}) collective-permute-start(bf16[896,256]{1,0:T(8,128)(2,1)S(1)} %get-tuple-element.50), channel_id=1, source_target_pairs={{0,4},{1,5},{2,6},{3,7},{4,0},{5,1},{6,2},{7,3},{8,12},{9,13},{10,... | collective-permute-start | bytes 1376264 | tf_op jit(solution)/shard_map/ppermute | solution.py:372
  53.6 6.1 %shard_map.60 = (f32[1024,256]{1,0:T(8,128)S(1)}, f32[2,256]{1,0:T(2,128)S(1)}, bf16[6912,256]{1,0:T(8,128)(2,1)S(1)}) custom-call(s32[4]{0:T(128)S(1)} %pad_add_fusion.where, f32[2,256]{1,0:T(2,128)S(1)} %add.7.stats, bf16[2,1024,256]{2,1,0:T(8,128)(2,1)S(1)} %bitcast.14, bf16[3,2,1152,256]{3,2,1,0:T(8,128)(2,1)S(1)} %shard_map.53.near, ...), custom_call_target="tpu_custom_call" | custom-call | flops 3623878656 | tf_op jit(solution)/shard_map/pallas_call | solution.py:349
  61.3 5.4 %shard_map.62 = (f32[1024,256]{1,0:T(8,128)S(1)}, f32[2,256]{1,0:T(2,128)S(1)}) custom-call(f32[2,256]{1,0:T(2,128)S(1)} %add.7.stats, bf16[2,1024,256]{2,1,0:T(8,128)(2,1)S(1)} %bitcast.15, bf16[3,2,1152,256]{3,2,1,0:T(8,128)(2,1)S(1)} %shard_map.53.near, bf16[3,1,1152,256]{3,2,1,0:T(8,128)(2,1)S(1)} %shard_map.55.after, ...), custom_call_target="tpu_custom_call" | custom-call | flops 3623878656 | tf_op jit(solution)/shard_map/pallas_call | solution.py:349
  66.8 3.5 %collective-permute-done.12.a0 = bf16[896,256]{1,0:T(8,128)(2,1)S(1)} collective-permute-done((bf16[896,256]{1,0:T(8,128)(2,1)S(1)}, bf16[896,256]{1,0:T(8,128)(2,1)S(1)}, u32[]{:S(2)}, u32[]{:S(2)}) %collective-permute-start.12) | collective-permute-done | bytes 458784 | tf_op jit(solution)/shard_map/ppermute | solution.py:372
  70.3 3.4 %collective-permute-done.14.a2 = bf16[896,256]{1,0:T(8,128)(2,1)S(1)} collective-permute-done((bf16[896,256]{1,0:T(8,128)(2,1)S(1)}, bf16[896,256]{1,0:T(8,128)(2,1)S(1)}, u32[]{:S(2)}, u32[]{:S(2)}) %collective-permute-start.14) | collective-permute-done | bytes 458784 | tf_op jit(solution)/shard_map/ppermute | solution.py:372
  74.6 5.1 %collective-permute-start.17 = (bf16[240,256]{1,0:T(8,128)(2,1)S(1)}, bf16[240,256]{1,0:T(8,128)(2,1)S(1)}, u32[]{:S(2)}, u32[]{:S(2)}) collective-permute-start(bf16[240,256]{1,0:T(8,128)(2,1)S(1)} %get-tuple-element.57), channel_id=1, source_target_pairs={{0,32},{8,40},{16,48},{24,56},{32,64},{40,72},{48,80},{56,88},{64,... | collective-permute-start | bytes 368648 | tf_op jit(solution)/shard_map/ppermute | solution.py:372
  79.7 2.2 %collective-permute-start.19 = (bf16[240,256]{1,0:T(8,128)(2,1)S(1)}, bf16[240,256]{1,0:T(8,128)(2,1)S(1)}, u32[]{:S(2)}, u32[]{:S(2)}) collective-permute-start(bf16[240,256]{1,0:T(8,128)(2,1)S(1)} %get-tuple-element.59), channel_id=1, source_target_pairs={{0,64},{8,72},{16,80},{24,88},{32,96},{40,104},{48,112},{56,120},{... | collective-permute-start | bytes 368648 | tf_op jit(solution)/shard_map/ppermute | solution.py:372
  86.7 2.7 %collective-permute-start.21 = (bf16[240,256]{1,0:T(8,128)(2,1)S(1)}, bf16[240,256]{1,0:T(8,128)(2,1)S(1)}, u32[]{:S(2)}, u32[]{:S(2)}) collective-permute-start(bf16[240,256]{1,0:T(8,128)(2,1)S(1)} %get-tuple-element.60.own), channel_id=1, source_target_pairs={{0,24},{8,0},{16,8},{24,16},{32,56},{40,32},{48,40},{56,48},{64,88... | collective-permute-start | bytes 368648 | tf_op jit(solution)/shard_map/ppermute | solution.py:372
  89.5 3.4 %collective-permute-done.22.a2 = bf16[240,256]{1,0:T(8,128)(2,1)S(1)} collective-permute-done((bf16[240,256]{1,0:T(8,128)(2,1)S(1)}, bf16[240,256]{1,0:T(8,128)(2,1)S(1)}, u32[]{:S(2)}, u32[]{:S(2)}) %collective-permute-start.22) | collective-permute-done | bytes 122912 | tf_op jit(solution)/shard_map/ppermute | solution.py:372
  93.6 2.0 %collective-permute-done.20.a0 = bf16[240,256]{1,0:T(8,128)(2,1)S(1)} collective-permute-done((bf16[240,256]{1,0:T(8,128)(2,1)S(1)}, bf16[240,256]{1,0:T(8,128)(2,1)S(1)}, u32[]{:S(2)}, u32[]{:S(2)}) %collective-permute-start.20) | collective-permute-done | bytes 122912 | tf_op jit(solution)/shard_map/ppermute | solution.py:372
  95.6 2.7 %collective-permute-start.25 = (bf16[224,256]{1,0:T(8,128)(2,1)S(1)}, bf16[224,256]{1,0:T(8,128)(2,1)S(1)}, u32[]{:S(2)}, u32[]{:S(2)}) collective-permute-start(bf16[224,256]{1,0:T(8,128)(2,1)S(1)} %get-tuple-element.65.own), channel_id=1, source_target_pairs={{0,64},{8,72},{16,80},{24,88},{32,96},{40,104},{48,112},{56,120},{... | collective-permute-start | bytes 344072 | tf_op jit(solution)/shard_map/ppermute | solution.py:372
  98.3 2.1 %collective-permute-start.24 = (bf16[224,256]{1,0:T(8,128)(2,1)S(1)}, bf16[224,256]{1,0:T(8,128)(2,1)S(1)}, u32[]{:S(2)}, u32[]{:S(2)}) collective-permute-start(bf16[224,256]{1,0:T(8,128)(2,1)S(1)} %get-tuple-element.65.own), channel_id=1, source_target_pairs={{0,96},{8,104},{16,112},{24,120},{32,0},{40,8},{48,16},{56,24},{64... | collective-permute-start | bytes 344072 | tf_op jit(solution)/shard_map/ppermute | solution.py:372
  100.4 2.1 %shard_map.66 = bf16[2,1024,256]{2,1,0:T(8,128)(2,1)} custom-call(f32[2,256]{1,0:T(2,128)S(1)} %add.7.stats, f32[2,256]{1,0:T(2,128)S(1)} %get-tuple-element.62.sums, bf16[2,1024,256]{2,1,0:T(8,128)(2,1)S(1)} %bitcast.16, bf16[2,1024,256]{2,1,0:T(8,128)(2,1)S(1)} %bitcast.11, f32[1024,256]{1,0:T(8,128)S(1)} %get-tuple-element.63.grad0, ...), custom_call_target="tpu_custom_call" | custom-call | bytes 8000000 | tf_op jit(solution)/shard_map/pallas_call | solution.py:349
  103.5 2.9 %collective-permute-done.23.a0 = bf16[224,256]{1,0:T(8,128)(2,1)S(1)} collective-permute-done((bf16[224,256]{1,0:T(8,128)(2,1)S(1)}, bf16[224,256]{1,0:T(8,128)(2,1)S(1)}, u32[]{:S(2)}, u32[]{:S(2)}) %collective-permute-start.23) | collective-permute-done | bytes 114720 | tf_op jit(solution)/shard_map/ppermute | solution.py:372
  (63 shorter events, 26.4 us)
Async XLA Ops:
  0.6 34.3 %collective-permute-start.7 = (bf16[864,256]{1,0:T(8,128)(2,1)}, bf16[864,256]{1,0:T(8,128)(2,1)S(1)}, u32[]{:S(2)}, u32[]{:S(2)}) collective-permute-start(bf16[864,256]{1,0:T(8,128)(2,1)} %own.1), channel_id=1, source_target_pairs={{0,6},{1,7},{2,0},{3,1},{4,2},{5,3},{6,4},{7,5},{8,14},{9,15},{10,... | collective-permute-start | bytes 1327112 | tf_op jit(solution)/shard_map/ppermute | solution.py:372
  1.5 33.4 %collective-permute-start.6 = (bf16[864,256]{1,0:T(8,128)(2,1)}, bf16[864,256]{1,0:T(8,128)(2,1)S(1)}, u32[]{:S(2)}, u32[]{:S(2)}) collective-permute-start(bf16[864,256]{1,0:T(8,128)(2,1)} %own.1), channel_id=1, source_target_pairs={{0,2},{1,3},{2,4},{3,5},{4,6},{5,7},{6,0},{7,1},{8,10},{9,11},{10,... | collective-permute-start | bytes 1327112 | tf_op jit(solution)/shard_map/ppermute | solution.py:372
  3.9 31.0 %collective-permute-start.8 = (bf16[864,256]{1,0:T(8,128)(2,1)}, bf16[864,256]{1,0:T(8,128)(2,1)S(1)}, u32[]{:S(2)}, u32[]{:S(2)}) collective-permute-start(bf16[864,256]{1,0:T(8,128)(2,1)} %own.1), channel_id=1, source_target_pairs={{0,4},{1,5},{2,6},{3,7},{4,0},{5,1},{6,2},{7,3},{8,12},{9,13},{10,... | collective-permute-start | bytes 1327112 | tf_op jit(solution)/shard_map/ppermute | solution.py:372
  5.8 5.5 %collective-permute-start.2 = (f32[2,256]{1,0:T(2,128)S(1)}, f32[2,256]{1,0:T(2,128)S(1)}, u32[]{:S(2)}, u32[]{:S(2)}) collective-permute-start(f32[2,256]{1,0:T(2,128)S(1)} %get-tuple-element.34.order.own), channel_id=1, source_target_pairs={{0,16},{8,24},{16,0},{24,8},{32,48},{40,56},{48,32},{56,40},{64,80... | collective-permute-start | bytes 6152 | tf_op jit(solution)/shard_map/ppermute | solution.py:372
  9.7 4.4 %collective-permute-start.1 = (f32[2,256]{1,0:T(2,128)S(1)}, f32[2,256]{1,0:T(2,128)S(1)}, u32[]{:S(2)}, u32[]{:S(2)}) collective-permute-start(f32[2,256]{1,0:T(2,128)S(1)} %get-tuple-element.34.order.own), channel_id=1, source_target_pairs={{0,24},{8,0},{16,8},{24,16},{32,56},{40,32},{48,40},{56,48},{64,88... | collective-permute-start | bytes 6152 | tf_op jit(solution)/shard_map/ppermute | solution.py:372
  11.3 5.2 %collective-permute-start = (f32[2,256]{1,0:T(2,128)S(1)}, f32[2,256]{1,0:T(2,128)S(1)}, u32[]{:S(2)}, u32[]{:S(2)}) collective-permute-start(f32[2,256]{1,0:T(2,128)S(1)} %get-tuple-element.34.order.own), channel_id=1, source_target_pairs={{0,8},{8,16},{16,24},{24,0},{32,40},{40,48},{48,56},{56,32},{64,72... | collective-permute-start | bytes 6152 | tf_op jit(solution)/shard_map/ppermute | solution.py:372
  20.2 5.0 %collective-permute-start.4 = (f32[2,256]{1,0:T(2,128)S(1)}, f32[2,256]{1,0:T(2,128)S(1)}, u32[]{:S(2)}, u32[]{:S(2)}) collective-permute-start(f32[2,256]{1,0:T(2,128)S(1)} %add.6), channel_id=1, source_target_pairs={{0,96},{8,104},{16,112},{24,120},{32,64},{40,72},{48,80},{56,88},{... | collective-permute-start | bytes 6152 | tf_op jit(solution)/shard_map/ppermute | solution.py:382
  23.9 11.9 %collective-permute-start.5 = (bf16[1024,256]{1,0:T(8,128)(2,1)S(1)}, bf16[1024,256]{1,0:T(8,128)(2,1)S(1)}, u32[]{:S(2)}, u32[]{:S(2)}) collective-permute-start(bf16[1024,256]{1,0:T(8,128)(2,1)S(1)} %get-tuple-element.39), channel_id=1, source_target_pairs={{8,0},{16,8},{24,16},{32,24},{40,32},{48,40},{56,48},{64,56},{72,6... | collective-permute-start | bytes 1572872 | tf_op jit(solution)/shard_map/ppermute | solution.py:391
  25.2 13.5 %collective-permute-start.10 = (bf16[1024,256]{1,0:T(8,128)(2,1)S(1)}, bf16[1024,256]{1,0:T(8,128)(2,1)S(1)}, u32[]{:S(2)}, u32[]{:S(2)}) collective-permute-start(bf16[1024,256]{1,0:T(8,128)(2,1)S(1)} %get-tuple-element.44), channel_id=1, source_target_pairs={{0,8},{8,16},{16,24},{24,32},{32,40},{40,48},{48,56},{56,64},{64,7... | collective-permute-start | bytes 1572872 | tf_op jit(solution)/shard_map/ppermute | solution.py:391
  35.7 17.9 %collective-permute-start.15 = (bf16[4,864,256]{2,1,0:T(8,128)(2,1)S(1)}, bf16[4,864,256]{2,1,0:T(8,128)(2,1)S(1)}, u32[]{:S(2)}, u32[]{:S(2)}) collective-permute-start(bf16[4,864,256]{2,1,0:T(8,128)(2,1)S(1)} %shard_map.56.order.mine), channel_id=1, source_target_pairs={{0,1},{1,0},{2,3},{3,2},{4,5},{5,4},{6,7},{7,6},{8,9},{9,8},{10,11... | collective-permute-start | bytes 5308424 | tf_op jit(solution)/shard_map/ppermute | solution.py:386
  38.1 8.0 %collective-permute-start.9 = (bf16[1824,256]{1,0:T(8,128)(2,1)S(1)}, bf16[1824,256]{1,0:T(8,128)(2,1)S(1)}, u32[]{:S(2)}, u32[]{:S(2)}) collective-permute-start(bf16[1824,256]{1,0:T(8,128)(2,1)S(1)} %get-tuple-element.43.order), channel_id=1, source_target_pairs={{0,1},{1,0},{2,3},{3,2},{4,5},{5,4},{6,7},{7,6},{8,9},{9,8},{10,11... | collective-permute-start | bytes 2801672 | tf_op jit(solution)/shard_map/ppermute | solution.py:386
  44.9 16.2 %collective-permute-start.16 = (bf16[1024,256]{1,0:T(8,128)(2,1)S(1)}, bf16[1024,256]{1,0:T(8,128)(2,1)S(1)}, u32[]{:S(2)}, u32[]{:S(2)}) collective-permute-start(bf16[1024,256]{1,0:T(8,128)(2,1)S(1)} %copy-done.6), channel_id=1, source_target_pairs={{8,0},{16,8},{24,16},{32,24},{40,32},{48,40},{56,48},{64,56},{72,6... | collective-permute-start | bytes 1572872 | tf_op jit(solution)/shard_map/ppermute | solution.py:391
  48.2 22.1 %collective-permute-start.12 = (bf16[896,256]{1,0:T(8,128)(2,1)S(1)}, bf16[896,256]{1,0:T(8,128)(2,1)S(1)}, u32[]{:S(2)}, u32[]{:S(2)}) collective-permute-start(bf16[896,256]{1,0:T(8,128)(2,1)S(1)} %get-tuple-element.48), channel_id=1, source_target_pairs={{0,2},{1,3},{2,4},{3,5},{4,6},{5,7},{6,0},{7,1},{8,10},{9,11},{10,... | collective-permute-start | bytes 1376264 | tf_op jit(solution)/shard_map/ppermute | solution.py:372
  50.4 19.9 %collective-permute-start.13 = (bf16[896,256]{1,0:T(8,128)(2,1)S(1)}, bf16[896,256]{1,0:T(8,128)(2,1)S(1)}, u32[]{:S(2)}, u32[]{:S(2)}) collective-permute-start(bf16[896,256]{1,0:T(8,128)(2,1)S(1)} %get-tuple-element.49), channel_id=1, source_target_pairs={{0,6},{1,7},{2,0},{3,1},{4,2},{5,3},{6,4},{7,5},{8,14},{9,15},{10,... | collective-permute-start | bytes 1376264 | tf_op jit(solution)/shard_map/ppermute | solution.py:372
  50.4 23.3 %collective-permute-start.14 = (bf16[896,256]{1,0:T(8,128)(2,1)S(1)}, bf16[896,256]{1,0:T(8,128)(2,1)S(1)}, u32[]{:S(2)}, u32[]{:S(2)}) collective-permute-start(bf16[896,256]{1,0:T(8,128)(2,1)S(1)} %get-tuple-element.50), channel_id=1, source_target_pairs={{0,4},{1,5},{2,6},{3,7},{4,0},{5,1},{6,2},{7,3},{8,12},{9,13},{10,... | collective-permute-start | bytes 1376264 | tf_op jit(solution)/shard_map/ppermute | solution.py:372
  74.6 8.8 %collective-permute-start.17 = (bf16[240,256]{1,0:T(8,128)(2,1)S(1)}, bf16[240,256]{1,0:T(8,128)(2,1)S(1)}, u32[]{:S(2)}, u32[]{:S(2)}) collective-permute-start(bf16[240,256]{1,0:T(8,128)(2,1)S(1)} %get-tuple-element.57), channel_id=1, source_target_pairs={{0,32},{8,40},{16,48},{24,56},{32,64},{40,72},{48,80},{56,88},{64,... | collective-permute-start | bytes 368648 | tf_op jit(solution)/shard_map/ppermute | solution.py:372
  79.7 5.3 %collective-permute-start.18 = (bf16[240,256]{1,0:T(8,128)(2,1)S(1)}, bf16[240,256]{1,0:T(8,128)(2,1)S(1)}, u32[]{:S(2)}, u32[]{:S(2)}) collective-permute-start(bf16[240,256]{1,0:T(8,128)(2,1)S(1)} %get-tuple-element.58), channel_id=1, source_target_pairs={{0,96},{8,104},{16,112},{24,120},{32,0},{40,8},{48,16},{56,24},{64... | collective-permute-start | bytes 368648 | tf_op jit(solution)/shard_map/ppermute | solution.py:372
  79.7 6.4 %collective-permute-start.19 = (bf16[240,256]{1,0:T(8,128)(2,1)S(1)}, bf16[240,256]{1,0:T(8,128)(2,1)S(1)}, u32[]{:S(2)}, u32[]{:S(2)}) collective-permute-start(bf16[240,256]{1,0:T(8,128)(2,1)S(1)} %get-tuple-element.59), channel_id=1, source_target_pairs={{0,64},{8,72},{16,80},{24,88},{32,96},{40,104},{48,112},{56,120},{... | collective-permute-start | bytes 368648 | tf_op jit(solution)/shard_map/ppermute | solution.py:372
  86.2 6.6 %collective-permute-start.22 = (bf16[240,256]{1,0:T(8,128)(2,1)S(1)}, bf16[240,256]{1,0:T(8,128)(2,1)S(1)}, u32[]{:S(2)}, u32[]{:S(2)}) collective-permute-start(bf16[240,256]{1,0:T(8,128)(2,1)S(1)} %get-tuple-element.60.own), channel_id=1, source_target_pairs={{0,16},{8,24},{16,0},{24,8},{32,48},{40,56},{48,32},{56,40},{64,80... | collective-permute-start | bytes 368648 | tf_op jit(solution)/shard_map/ppermute | solution.py:372
  86.7 6.8 %collective-permute-start.21 = (bf16[240,256]{1,0:T(8,128)(2,1)S(1)}, bf16[240,256]{1,0:T(8,128)(2,1)S(1)}, u32[]{:S(2)}, u32[]{:S(2)}) collective-permute-start(bf16[240,256]{1,0:T(8,128)(2,1)S(1)} %get-tuple-element.60.own), channel_id=1, source_target_pairs={{0,24},{8,0},{16,8},{24,16},{32,56},{40,32},{48,40},{56,48},{64,88... | collective-permute-start | bytes 368648 | tf_op jit(solution)/shard_map/ppermute | solution.py:372
  89.4 6.1 %collective-permute-start.20 = (bf16[240,256]{1,0:T(8,128)(2,1)S(1)}, bf16[240,256]{1,0:T(8,128)(2,1)S(1)}, u32[]{:S(2)}, u32[]{:S(2)}) collective-permute-start(bf16[240,256]{1,0:T(8,128)(2,1)S(1)} %get-tuple-element.60.own), channel_id=1, source_target_pairs={{0,8},{8,16},{16,24},{24,0},{32,40},{40,48},{48,56},{56,32},{64,72... | collective-permute-start | bytes 368648 | tf_op jit(solution)/shard_map/ppermute | solution.py:372
  95.6 6.9 %collective-permute-start.25 = (bf16[224,256]{1,0:T(8,128)(2,1)S(1)}, bf16[224,256]{1,0:T(8,128)(2,1)S(1)}, u32[]{:S(2)}, u32[]{:S(2)}) collective-permute-start(bf16[224,256]{1,0:T(8,128)(2,1)S(1)} %get-tuple-element.65.own), channel_id=1, source_target_pairs={{0,64},{8,72},{16,80},{24,88},{32,96},{40,104},{48,112},{56,120},{... | collective-permute-start | bytes 344072 | tf_op jit(solution)/shard_map/ppermute | solution.py:372
  98.3 5.2 %collective-permute-start.24 = (bf16[224,256]{1,0:T(8,128)(2,1)S(1)}, bf16[224,256]{1,0:T(8,128)(2,1)S(1)}, u32[]{:S(2)}, u32[]{:S(2)}) collective-permute-start(bf16[224,256]{1,0:T(8,128)(2,1)S(1)} %get-tuple-element.65.own), channel_id=1, source_target_pairs={{0,96},{8,104},{16,112},{24,120},{32,0},{40,8},{48,16},{56,24},{64... | collective-permute-start | bytes 344072 | tf_op jit(solution)/shard_map/ppermute | solution.py:372
  100.4 6.0 %collective-permute-start.23 = (bf16[224,256]{1,0:T(8,128)(2,1)S(1)}, bf16[224,256]{1,0:T(8,128)(2,1)S(1)}, u32[]{:S(2)}, u32[]{:S(2)}) collective-permute-start(bf16[224,256]{1,0:T(8,128)(2,1)S(1)} %get-tuple-element.65.own), channel_id=1, source_target_pairs={{0,32},{8,40},{16,48},{24,56},{32,64},{40,72},{48,80},{56,88},{64,... | collective-permute-start | bytes 344072 | tf_op jit(solution)/shard_map/ppermute | solution.py:372
  (9 other events, 52.2 us)

commit v8 on v7

--- a/solution.py
+++ b/solution.py
@@ -71,8 +71,10 @@
 
     zero = jnp.zeros((8, C), f32)
     a, b = lax.fori_loop(0, 2 * ROWS // 128, step, (zero, zero))
-    out[0:1] = a.sum(0, keepdims=True)
-    out[1:2] = b.sum(0, keepdims=True)
+    row = lax.broadcasted_iota(jnp.int32, (8, C), 0)
+    both = jnp.where(row == 0, a.sum(0, keepdims=True), jnp.where(row == 1, b.sum(0, keepdims=True), 0.0))
+    for i in range(16):
+        out[i] = both
     last[...] = clip[1]
 
 
@@ -87,8 +89,11 @@
         widths(wide, lambda r, t=t: cot[t, pl.ds(r, W)], t)
 
 
-def ring_sum_kernel(own, before, after, far, held0, held1, out, pass0, pass1):
-    out[...] = (own[...] + far[...]) + (before[...] + after[...])
+def total_kernel(parts, held0, held1, out, pass0, pass1):
+    total = parts[0]
+    for i in range(1, 16):
+        total = total + parts[i]
+    out[...] = total[0:2]
 
 
 def tap_rows(kh):
@@ -373,15 +378,6 @@
     return got
 
 
-def swap(block, axis, partners):
-    name, size, stride = AXES[axis]
-    route = []
-    for i in range(size):
-        place = (i // stride) % 4
-        route.append((i, i + (partners[place] - place) * stride))
-    return lax.ppermute(block, name, route)
-
-
 def swap_core(block):
     return lax.ppermute(block, "fsdp", [(i, i ^ 1) for i in range(8)])
 
@@ -405,20 +401,18 @@
     where = jnp.stack([jnp.asarray(v, jnp.int32) for v in where])
     frame = S((ROWS, C), bf16)
 
-    sums, last = call(first_kernel, (S((2, C), f32), frame), (clip,))
-    got = ring("z", [sums] * 3)
+    sums, last = call(first_kernel, (S((16, 8, C), f32), frame), (clip,))
     first, second = call(copy_kernel, (frame, frame), (cot,), order=(sums,))
-    sums, first, last = call(
-        ring_sum_kernel,
+    parts = lax.all_to_all(sums, "tm", 0, 0, tiled=True)
+    stats, first, last = call(
+        total_kernel,
         (S((2, C), f32), frame, frame),
-        (sums, *got),
+        (parts,),
         order=(first, last),
-        aliases={4: 1, 5: 2},
+        aliases={1: 1, 2: 2},
         passed_out=2,
     )
-    near = call(widths_kernel, S((3, 2, PADDED, C), bf16), (cot,), order=(sums,))
-    half = sums + swap(sums, "y", (1, 0, 3, 2))
-    stats = half + swap(half, "y", (3, 2, 1, 0))
+    near = call(widths_kernel, S((3, 2, PADDED, C), bf16), (cot,), order=(stats,))
     after = call(widths_kernel, S((3, 1, PADDED, C), bf16), (passed(first, -1)[None],))
     before = passed(last, 1)
 

time: 108 us -> 108 us (level)
  starting transfers between devices: 43.1 us -> 39.9 us
  waiting for transfers between devices: 28.8 us -> 30 us
    all_to_all x0 -> x1, starting transfers between devices: none -> 8.05 us  [per_device(): parts = lax.all_to_all(sums, 'tm', 0, 0, tiled=True)]
    ppermute x18 -> x15, starting transfers between devices: 30.5 us -> 24 us  [ring(): got.append(lax.ppermute(block, name, route))]
    all_to_all x0 -> x1, waiting for transfers between devices: none -> 6.3 us  [per_device(): parts = lax.all_to_all(sums, 'tm', 0, 0, tiled=True)]
    ppermute x2 -> x0, starting transfers between devices: 4.66 us -> none  [swap(): return lax.ppermute(block, name, route)]
    ppermute x18 -> x15, waiting for transfers between devices: 24.3 us -> 21.2 us  [ring(): got.append(lax.ppermute(block, name, route))]
    ppermute x2 -> x0, waiting for transfers between devices: 2.01 us -> none  [swap(): return lax.ppermute(block, name, route)]
  transfers between devices with their start and end apart: 26 -> 22, of which waited for: 15 -> 13; matrix products, arithmetic and copies ran while one was open for 0% -> 1% of each run, Pallas kernels for 28% -> 29%
where the time goes in v8:
time: 108 us; the launch traced here: 107 us
  starting transfers between devices  39.9 us (37%)
  Pallas kernels  33.3 us (31%)
  waiting for transfers between devices  30 us (28%)
  local copies, waits for them, and re-layouts  2.67 us (2%)
    pallas_call x18, Pallas kernels, call(): pl.pallas_call(kernel, out_shape=out_shape, in_specs=specs, out_specs=out...  33.3 us
    ppermute x15, starting transfers between devices, ring(): got.append(lax.ppermute(block, name, route))  24 us
    ppermute x15, waiting for transfers between devices, ring(): got.append(lax.ppermute(block, name, route))  21.2 us
    all_to_all x1, starting transfers between devices, per_device(): parts = lax.all_to_all(sums, 'tm', 0, 0, tiled=True)  8.05 us
    ppermute x3, starting transfers between devices, passed(): return lax.ppermute(block, 'tm', route)  7.15 us
    all_to_all x1, waiting for transfers between devices, per_device(): parts = lax.all_to_all(sums, 'tm', 0, 0, tiled=True)  6.3 us
    unnamed x14, local copies, waits for them, and re-layouts  2.67 us
  transfers between devices with their start and end apart: 22, of which 13 were waited for; matrix products, arithmetic and copies ran while one was open for 1% of the time, Pallas kernels for 29%

profile of v8, /device:TPU:6, one launch (start us, length us, event | category | flops | bytes accessed | tf_op | source)
XLA Modules:
  0.0 107.4 jit_solution(16666497829409064369)
XLA Ops:
  1.5 2.4 %collective-permute-start.1 = (bf16[864,256]{1,0:T(8,128)(2,1)}, bf16[864,256]{1,0:T(8,128)(2,1)S(1)}, u32[]{:S(2)}, u32[]{:S(2)}) collective-permute-start(bf16[864,256]{1,0:T(8,128)(2,1)} %own.1), channel_id=1, source_target_pairs={{0,2},{1,3},{2,4},{3,5},{4,6},{5,7},{6,0},{7,1},{8,10},{9,11},{10,... | collective-permute-start | bytes 1327112 | tf_op jit(solution)/shard_map/ppermute | solution.py:377
  6.4 8.0 %all-to-all-start = ((f32[16,8,256]{2,1,0:T(8,128)}), f32[16,8,256]{2,1,0:T(8,128)S(1)}, u32[]{:S(2)}, u32[]{:S(2)}) async-start(f32[16,8,256]{2,1,0:T(8,128)} %get-tuple-element.34.order), calls=%async_computation | async-start | bytes 262144 | tf_op jit(solution)/shard_map/all_to_all | solution.py:406
  16.0 6.3 %all-to-all-done.parts = f32[16,8,256]{2,1,0:T(8,128)S(1)} async-done(((f32[16,8,256]{2,1,0:T(8,128)}), f32[16,8,256]{2,1,0:T(8,128)S(1)}, u32[]{:S(2)}, u32[]{:S(2)}) %all-to-all-start) | async-done | bytes 131104 | tf_op jit(solution)/shard_map/all_to_all | solution.py:406
  23.6 4.6 %collective-permute-start.5 = (bf16[1024,256]{1,0:T(8,128)(2,1)S(1)}, bf16[1024,256]{1,0:T(8,128)(2,1)S(1)}, u32[]{:S(2)}, u32[]{:S(2)}) collective-permute-start(bf16[1024,256]{1,0:T(8,128)(2,1)S(1)} %get-tuple-element.44), channel_id=1, source_target_pairs={{0,8},{8,16},{16,24},{24,32},{32,40},{40,48},{48,56},{56,64},{64,7... | collective-permute-start | bytes 1572872 | tf_op jit(solution)/shard_map/ppermute | solution.py:387
  29.5 5.2 %shard_map.54 = (bf16[2,1024,256]{2,1,0:T(8,128)(2,1)S(1)}, f32[1824,256]{1,0:T(8,128)S(1)}, bf16[1824,256]{1,0:T(8,128)(2,1)S(1)}) custom-call(s32[4]{0:T(128)S(1)} %copy-done.4, f32[2,256]{1,0:T(2,128)S(1)} %get-tuple-element.37.refs_0_.stats, bf16[2,1024,256]{2,1,0:T(8,128)(2,1)S(1)} %bitcast.13, bf16[3,2,1152,256]{3,2,1,0:T(8,128)(2,1)S(1)} %shard_map.53.near), custom_call_target="tpu_custom_call" | custom-call | flops 2415919104 | tf_op jit(solution)/shard_map/pallas_call | solution.py:354
  36.0 2.0 %shard_map.57 = (f32[1824,256]{1,0:T(8,128)S(1)}, bf16[1824,256]{1,0:T(8,128)(2,1)S(1)}) custom-call(s32[4]{0:T(128)S(1)} %copy-done.4, bf16[2,1024,256]{2,1,0:T(8,128)(2,1)S(1)} %get-tuple-element.38.order.act, bf16[3,2,1152,256]{3,2,1,0:T(8,128)(2,1)S(1)} %shard_map.53.near, ...), custom_call_target="tpu_custom_call", output_to_operand_aliasing={{0}: (4, {}), {1}: (5, {})} | custom-call | flops 1207959552 | tf_op jit(solution)/shard_map/pallas_call | solution.py:354
  38.3 6.1 %shard_map.58 = (f32[1824,256]{1,0:T(8,128)S(1)}, bf16[1824,256]{1,0:T(8,128)(2,1)S(1)}) custom-call(s32[4]{0:T(128)S(1)} %copy-done.4, f32[2,256]{1,0:T(2,128)S(1)} %get-tuple-element.37.refs_0_.stats, bf16[2,1024,256]{2,1,0:T(8,128)(2,1)S(1)} %get-tuple-element.38.order.act, bf16[1024,256]{1,0:T(8,128)(2,1)S(1)} %collective-permute-done.5.before, ...), custom_call_target="tpu_custom_call" | custom-call | flops 3623878656 | tf_op jit(solution)/shard_map/pallas_call | solution.py:354
  47.9 2.1 %collective-permute-start.7 = (bf16[896,256]{1,0:T(8,128)(2,1)S(1)}, bf16[896,256]{1,0:T(8,128)(2,1)S(1)}, u32[]{:S(2)}, u32[]{:S(2)}) collective-permute-start(bf16[896,256]{1,0:T(8,128)(2,1)S(1)} %get-tuple-element.48), channel_id=1, source_target_pairs={{0,2},{1,3},{2,4},{3,5},{4,6},{5,7},{6,0},{7,1},{8,10},{9,11},{10,... | collective-permute-start | bytes 1376264 | tf_op jit(solution)/shard_map/ppermute | solution.py:377
  50.0 3.3 %collective-permute-start.9 = (bf16[896,256]{1,0:T(8,128)(2,1)S(1)}, bf16[896,256]{1,0:T(8,128)(2,1)S(1)}, u32[]{:S(2)}, u32[]{:S(2)}) collective-permute-start(bf16[896,256]{1,0:T(8,128)(2,1)S(1)} %get-tuple-element.50), channel_id=1, source_target_pairs={{0,4},{1,5},{2,6},{3,7},{4,0},{5,1},{6,2},{7,3},{8,12},{9,13},{10,... | collective-permute-start | bytes 1376264 | tf_op jit(solution)/shard_map/ppermute | solution.py:377
  53.3 6.1 %shard_map.60 = (f32[1024,256]{1,0:T(8,128)S(1)}, f32[2,256]{1,0:T(2,128)S(1)}, bf16[6912,256]{1,0:T(8,128)(2,1)S(1)}) custom-call(s32[4]{0:T(128)S(1)} %copy-done.4, f32[2,256]{1,0:T(2,128)S(1)} %get-tuple-element.37.refs_0_.stats, bf16[2,1024,256]{2,1,0:T(8,128)(2,1)S(1)} %bitcast.14, bf16[3,2,1152,256]{3,2,1,0:T(8,128)(2,1)S(1)} %shard_map.53.near, ...), custom_call_target="tpu_custom_call" | custom-call | flops 3623878656 | tf_op jit(solution)/shard_map/pallas_call | solution.py:354
  61.0 5.4 %shard_map.62 = (f32[1024,256]{1,0:T(8,128)S(1)}, f32[2,256]{1,0:T(2,128)S(1)}) custom-call(f32[2,256]{1,0:T(2,128)S(1)} %get-tuple-element.37.refs_0_.stats, bf16[2,1024,256]{2,1,0:T(8,128)(2,1)S(1)} %bitcast.15, bf16[3,2,1152,256]{3,2,1,0:T(8,128)(2,1)S(1)} %shard_map.53.near, bf16[3,1,1152,256]{3,2,1,0:T(8,128)(2,1)S(1)} %shard_map.55.after, ...), custom_call_target="tpu_custom_call" | custom-call | flops 3623878656 | tf_op jit(solution)/shard_map/pallas_call | solution.py:354
  66.4 3.7 %collective-permute-done.7.a0 = bf16[896,256]{1,0:T(8,128)(2,1)S(1)} collective-permute-done((bf16[896,256]{1,0:T(8,128)(2,1)S(1)}, bf16[896,256]{1,0:T(8,128)(2,1)S(1)}, u32[]{:S(2)}, u32[]{:S(2)}) %collective-permute-start.7) | collective-permute-done | bytes 458784 | tf_op jit(solution)/shard_map/ppermute | solution.py:377
  70.1 3.4 %collective-permute-done.9.a2 = bf16[896,256]{1,0:T(8,128)(2,1)S(1)} collective-permute-done((bf16[896,256]{1,0:T(8,128)(2,1)S(1)}, bf16[896,256]{1,0:T(8,128)(2,1)S(1)}, u32[]{:S(2)}, u32[]{:S(2)}) %collective-permute-start.9) | collective-permute-done | bytes 458784 | tf_op jit(solution)/shard_map/ppermute | solution.py:377
  74.4 4.2 %collective-permute-start.12 = (bf16[240,256]{1,0:T(8,128)(2,1)S(1)}, bf16[240,256]{1,0:T(8,128)(2,1)S(1)}, u32[]{:S(2)}, u32[]{:S(2)}) collective-permute-start(bf16[240,256]{1,0:T(8,128)(2,1)S(1)} %get-tuple-element.57), channel_id=1, source_target_pairs={{0,32},{8,40},{16,48},{24,56},{32,64},{40,72},{48,80},{56,88},{64,... | collective-permute-start | bytes 368648 | tf_op jit(solution)/shard_map/ppermute | solution.py:377
  78.6 2.5 %collective-permute-start.14 = (bf16[240,256]{1,0:T(8,128)(2,1)S(1)}, bf16[240,256]{1,0:T(8,128)(2,1)S(1)}, u32[]{:S(2)}, u32[]{:S(2)}) collective-permute-start(bf16[240,256]{1,0:T(8,128)(2,1)S(1)} %get-tuple-element.59), channel_id=1, source_target_pairs={{0,64},{8,72},{16,80},{24,88},{32,96},{40,104},{48,112},{56,120},{... | collective-permute-start | bytes 368648 | tf_op jit(solution)/shard_map/ppermute | solution.py:377
  82.1 1.6 %collective-permute-done.13.a1 = bf16[240,256]{1,0:T(8,128)(2,1)S(1)} collective-permute-done((bf16[240,256]{1,0:T(8,128)(2,1)S(1)}, bf16[240,256]{1,0:T(8,128)(2,1)S(1)}, u32[]{:S(2)}, u32[]{:S(2)}) %collective-permute-start.13) | collective-permute-done | bytes 122912 | tf_op jit(solution)/shard_map/ppermute | solution.py:377
  86.7 2.4 %collective-permute-start.16 = (bf16[240,256]{1,0:T(8,128)(2,1)S(1)}, bf16[240,256]{1,0:T(8,128)(2,1)S(1)}, u32[]{:S(2)}, u32[]{:S(2)}) collective-permute-start(bf16[240,256]{1,0:T(8,128)(2,1)S(1)} %get-tuple-element.60.own), channel_id=1, source_target_pairs={{0,24},{8,0},{16,8},{24,16},{32,56},{40,32},{48,40},{56,48},{64,88... | collective-permute-start | bytes 368648 | tf_op jit(solution)/shard_map/ppermute | solution.py:377
  89.2 3.4 %collective-permute-done.17.a2 = bf16[240,256]{1,0:T(8,128)(2,1)S(1)} collective-permute-done((bf16[240,256]{1,0:T(8,128)(2,1)S(1)}, bf16[240,256]{1,0:T(8,128)(2,1)S(1)}, u32[]{:S(2)}, u32[]{:S(2)}) %collective-permute-start.17) | collective-permute-done | bytes 122912 | tf_op jit(solution)/shard_map/ppermute | solution.py:377
  92.6 2.7 %collective-permute-done.15.a0 = bf16[240,256]{1,0:T(8,128)(2,1)S(1)} collective-permute-done((bf16[240,256]{1,0:T(8,128)(2,1)S(1)}, bf16[240,256]{1,0:T(8,128)(2,1)S(1)}, u32[]{:S(2)}, u32[]{:S(2)}) %collective-permute-start.15) | collective-permute-done | bytes 122912 | tf_op jit(solution)/shard_map/ppermute | solution.py:377
  95.3 2.4 %collective-permute-start.20 = (bf16[224,256]{1,0:T(8,128)(2,1)S(1)}, bf16[224,256]{1,0:T(8,128)(2,1)S(1)}, u32[]{:S(2)}, u32[]{:S(2)}) collective-permute-start(bf16[224,256]{1,0:T(8,128)(2,1)S(1)} %get-tuple-element.65.own), channel_id=1, source_target_pairs={{0,64},{8,72},{16,80},{24,88},{32,96},{40,104},{48,112},{56,120},{... | collective-permute-start | bytes 344072 | tf_op jit(solution)/shard_map/ppermute | solution.py:377
  97.7 2.1 %collective-permute-start.19 = (bf16[224,256]{1,0:T(8,128)(2,1)S(1)}, bf16[224,256]{1,0:T(8,128)(2,1)S(1)}, u32[]{:S(2)}, u32[]{:S(2)}) collective-permute-start(bf16[224,256]{1,0:T(8,128)(2,1)S(1)} %get-tuple-element.65.own), channel_id=1, source_target_pairs={{0,96},{8,104},{16,112},{24,120},{32,0},{40,8},{48,16},{56,24},{64... | collective-permute-start | bytes 344072 | tf_op jit(solution)/shard_map/ppermute | solution.py:377
  99.8 2.1 %shard_map.66 = bf16[2,1024,256]{2,1,0:T(8,128)(2,1)} custom-call(f32[2,256]{1,0:T(2,128)S(1)} %get-tuple-element.37.refs_0_.stats, f32[2,256]{1,0:T(2,128)S(1)} %get-tuple-element.62.sums, bf16[2,1024,256]{2,1,0:T(8,128)(2,1)S(1)} %bitcast.16, bf16[2,1024,256]{2,1,0:T(8,128)(2,1)S(1)} %bitcast.11, f32[1024,256]{1,0:T(8,128)S(1)} %get-tuple-element.63.grad0, ...), custom_call_target="tpu_custom_call" | custom-call | bytes 8000000 | tf_op jit(solution)/shard_map/pallas_call | solution.py:354
  102.9 2.9 %collective-permute-done.18.a0 = bf16[224,256]{1,0:T(8,128)(2,1)S(1)} collective-permute-done((bf16[224,256]{1,0:T(8,128)(2,1)S(1)}, bf16[224,256]{1,0:T(8,128)(2,1)S(1)}, u32[]{:S(2)}, u32[]{:S(2)}) %collective-permute-start.18) | collective-permute-done | bytes 114720 | tf_op jit(solution)/shard_map/ppermute | solution.py:377
  105.8 1.6 %shard_map.67 = f32[864,256]{1,0:T(8,128)} custom-call(s32[4]{0:T(128)S(1)} %copy-done.4, bf16[224,256]{1,0:T(8,128)(2,1)S(1)} %get-tuple-element.65.own, bf16[224,256]{1,0:T(8,128)(2,1)S(1)} %collective-permute-done.18.a0, bf16[224,256]{1,0:T(8,128)(2,1)S(1)} %collective-permute-done.19.a1, bf16[224,256]{1,0:T(8,128)(2,1)S(1)} %collective-permute-done.20.a2), custom_call_target="tpu_custom_call" | custom-call | tf_op jit(solution)/shard_map/pallas_call | solution.py:354
  (53 shorter events, 20.0 us)
Async XLA Ops:
  0.6 13.9 %copy-start = (bf16[1,2,16,64,256]{4,3,2,1,0:T(8,128)(2,1)S(1)}, bf16[1,2,16,64,256]{4,3,2,1,0:T(8,128)(2,1)}, u32[]{:S(2)}) copy-start(bf16[1,2,16,64,256]{4,3,2,1,0:T(8,128)(2,1)} %param.4) | copy-start | bytes 3145732
  0.6 34.0 %collective-permute-start.2 = (bf16[864,256]{1,0:T(8,128)(2,1)}, bf16[864,256]{1,0:T(8,128)(2,1)S(1)}, u32[]{:S(2)}, u32[]{:S(2)}) collective-permute-start(bf16[864,256]{1,0:T(8,128)(2,1)} %own.1), channel_id=1, source_target_pairs={{0,6},{1,7},{2,0},{3,1},{4,2},{5,3},{6,4},{7,5},{8,14},{9,15},{10,... | collective-permute-start | bytes 1327112 | tf_op jit(solution)/shard_map/ppermute | solution.py:377
  1.5 33.1 %collective-permute-start.1 = (bf16[864,256]{1,0:T(8,128)(2,1)}, bf16[864,256]{1,0:T(8,128)(2,1)S(1)}, u32[]{:S(2)}, u32[]{:S(2)}) collective-permute-start(bf16[864,256]{1,0:T(8,128)(2,1)} %own.1), channel_id=1, source_target_pairs={{0,2},{1,3},{2,4},{3,5},{4,6},{5,7},{6,0},{7,1},{8,10},{9,11},{10,... | collective-permute-start | bytes 1327112 | tf_op jit(solution)/shard_map/ppermute | solution.py:377
  3.9 30.7 %collective-permute-start.3 = (bf16[864,256]{1,0:T(8,128)(2,1)}, bf16[864,256]{1,0:T(8,128)(2,1)S(1)}, u32[]{:S(2)}, u32[]{:S(2)}) collective-permute-start(bf16[864,256]{1,0:T(8,128)(2,1)} %own.1), channel_id=1, source_target_pairs={{0,4},{1,5},{2,6},{3,7},{4,0},{5,1},{6,2},{7,3},{8,12},{9,13},{10,... | collective-permute-start | bytes 1327112 | tf_op jit(solution)/shard_map/ppermute | solution.py:377
  6.4 15.9 %all-to-all-start = ((f32[16,8,256]{2,1,0:T(8,128)}), f32[16,8,256]{2,1,0:T(8,128)S(1)}, u32[]{:S(2)}, u32[]{:S(2)}) async-start(f32[16,8,256]{2,1,0:T(8,128)} %get-tuple-element.34.order), calls=%async_computation | async-start | bytes 262144 | tf_op jit(solution)/shard_map/all_to_all | solution.py:406
  22.3 13.4 %collective-permute-start = (bf16[1024,256]{1,0:T(8,128)(2,1)S(1)}, bf16[1024,256]{1,0:T(8,128)(2,1)S(1)}, u32[]{:S(2)}, u32[]{:S(2)}) collective-permute-start(bf16[1024,256]{1,0:T(8,128)(2,1)S(1)} %get-tuple-element.39), channel_id=1, source_target_pairs={{8,0},{16,8},{24,16},{32,24},{40,32},{48,40},{56,48},{64,56},{72,6... | collective-permute-start | bytes 1572872 | tf_op jit(solution)/shard_map/ppermute | solution.py:387
  23.6 14.7 %collective-permute-start.5 = (bf16[1024,256]{1,0:T(8,128)(2,1)S(1)}, bf16[1024,256]{1,0:T(8,128)(2,1)S(1)}, u32[]{:S(2)}, u32[]{:S(2)}) collective-permute-start(bf16[1024,256]{1,0:T(8,128)(2,1)S(1)} %get-tuple-element.44), channel_id=1, source_target_pairs={{0,8},{8,16},{16,24},{24,32},{32,40},{40,48},{48,56},{56,64},{64,7... | collective-permute-start | bytes 1572872 | tf_op jit(solution)/shard_map/ppermute | solution.py:387
  35.4 17.9 %collective-permute-start.10 = (bf16[4,864,256]{2,1,0:T(8,128)(2,1)S(1)}, bf16[4,864,256]{2,1,0:T(8,128)(2,1)S(1)}, u32[]{:S(2)}, u32[]{:S(2)}) collective-permute-start(bf16[4,864,256]{2,1,0:T(8,128)(2,1)S(1)} %shard_map.56.order.mine), channel_id=1, source_target_pairs={{0,1},{1,0},{2,3},{3,2},{4,5},{5,4},{6,7},{7,6},{8,9},{9,8},{10,11... | collective-permute-start | bytes 5308424 | tf_op jit(solution)/shard_map/ppermute | solution.py:382
  38.0 6.8 %copy-start.6 = (bf16[1024,256]{1,0:T(8,128)(2,1)S(1)}, bf16[1024,256]{1,0:T(8,128)(2,1)}, u32[]{:S(2)}) copy-start(bf16[1024,256]{1,0:T(8,128)(2,1)} %copy-done.5) | copy-start | bytes 1572868
  38.1 8.0 %collective-permute-start.4 = (bf16[1824,256]{1,0:T(8,128)(2,1)S(1)}, bf16[1824,256]{1,0:T(8,128)(2,1)S(1)}, u32[]{:S(2)}, u32[]{:S(2)}) collective-permute-start(bf16[1824,256]{1,0:T(8,128)(2,1)S(1)} %get-tuple-element.43.order), channel_id=1, source_target_pairs={{0,1},{1,0},{2,3},{3,2},{4,5},{5,4},{6,7},{7,6},{8,9},{9,8},{10,11... | collective-permute-start | bytes 2801672 | tf_op jit(solution)/shard_map/ppermute | solution.py:382
  44.4 2.6 %collective-permute-start.6 = (bf16[1824,256]{1,0:T(8,128)(2,1)S(1)}, bf16[1824,256]{1,0:T(8,128)(2,1)S(1)}, u32[]{:S(2)}, u32[]{:S(2)}) collective-permute-start(bf16[1824,256]{1,0:T(8,128)(2,1)S(1)} %get-tuple-element.46), channel_id=1, source_target_pairs={{0,1},{1,0},{2,3},{3,2},{4,5},{5,4},{6,7},{7,6},{8,9},{9,8},{10,11... | collective-permute-start | bytes 2801672 | tf_op jit(solution)/shard_map/ppermute | solution.py:382
  44.8 15.9 %collective-permute-start.11 = (bf16[1024,256]{1,0:T(8,128)(2,1)S(1)}, bf16[1024,256]{1,0:T(8,128)(2,1)S(1)}, u32[]{:S(2)}, u32[]{:S(2)}) collective-permute-start(bf16[1024,256]{1,0:T(8,128)(2,1)S(1)} %copy-done.6), channel_id=1, source_target_pairs={{8,0},{16,8},{24,16},{32,24},{40,32},{48,40},{56,48},{64,56},{72,6... | collective-permute-start | bytes 1572872 | tf_op jit(solution)/shard_map/ppermute | solution.py:387
  47.9 22.2 %collective-permute-start.7 = (bf16[896,256]{1,0:T(8,128)(2,1)S(1)}, bf16[896,256]{1,0:T(8,128)(2,1)S(1)}, u32[]{:S(2)}, u32[]{:S(2)}) collective-permute-start(bf16[896,256]{1,0:T(8,128)(2,1)S(1)} %get-tuple-element.48), channel_id=1, source_target_pairs={{0,2},{1,3},{2,4},{3,5},{4,6},{5,7},{6,0},{7,1},{8,10},{9,11},{10,... | collective-permute-start | bytes 1376264 | tf_op jit(solution)/shard_map/ppermute | solution.py:377
  50.0 20.1 %collective-permute-start.8 = (bf16[896,256]{1,0:T(8,128)(2,1)S(1)}, bf16[896,256]{1,0:T(8,128)(2,1)S(1)}, u32[]{:S(2)}, u32[]{:S(2)}) collective-permute-start(bf16[896,256]{1,0:T(8,128)(2,1)S(1)} %get-tuple-element.49), channel_id=1, source_target_pairs={{0,6},{1,7},{2,0},{3,1},{4,2},{5,3},{6,4},{7,5},{8,14},{9,15},{10,... | collective-permute-start | bytes 1376264 | tf_op jit(solution)/shard_map/ppermute | solution.py:377
  50.0 23.5 %collective-permute-start.9 = (bf16[896,256]{1,0:T(8,128)(2,1)S(1)}, bf16[896,256]{1,0:T(8,128)(2,1)S(1)}, u32[]{:S(2)}, u32[]{:S(2)}) collective-permute-start(bf16[896,256]{1,0:T(8,128)(2,1)S(1)} %get-tuple-element.50), channel_id=1, source_target_pairs={{0,4},{1,5},{2,6},{3,7},{4,0},{5,1},{6,2},{7,3},{8,12},{9,13},{10,... | collective-permute-start | bytes 1376264 | tf_op jit(solution)/shard_map/ppermute | solution.py:377
  74.4 7.7 %collective-permute-start.12 = (bf16[240,256]{1,0:T(8,128)(2,1)S(1)}, bf16[240,256]{1,0:T(8,128)(2,1)S(1)}, u32[]{:S(2)}, u32[]{:S(2)}) collective-permute-start(bf16[240,256]{1,0:T(8,128)(2,1)S(1)} %get-tuple-element.57), channel_id=1, source_target_pairs={{0,32},{8,40},{16,48},{24,56},{32,64},{40,72},{48,80},{56,88},{64,... | collective-permute-start | bytes 368648 | tf_op jit(solution)/shard_map/ppermute | solution.py:377
  78.6 5.1 %collective-permute-start.13 = (bf16[240,256]{1,0:T(8,128)(2,1)S(1)}, bf16[240,256]{1,0:T(8,128)(2,1)S(1)}, u32[]{:S(2)}, u32[]{:S(2)}) collective-permute-start(bf16[240,256]{1,0:T(8,128)(2,1)S(1)} %get-tuple-element.58), channel_id=1, source_target_pairs={{0,96},{8,104},{16,112},{24,120},{32,0},{40,8},{48,16},{56,24},{64... | collective-permute-start | bytes 368648 | tf_op jit(solution)/shard_map/ppermute | solution.py:377
  78.6 6.6 %collective-permute-start.14 = (bf16[240,256]{1,0:T(8,128)(2,1)S(1)}, bf16[240,256]{1,0:T(8,128)(2,1)S(1)}, u32[]{:S(2)}, u32[]{:S(2)}) collective-permute-start(bf16[240,256]{1,0:T(8,128)(2,1)S(1)} %get-tuple-element.59), channel_id=1, source_target_pairs={{0,64},{8,72},{16,80},{24,88},{32,96},{40,104},{48,112},{56,120},{... | collective-permute-start | bytes 368648 | tf_op jit(solution)/shard_map/ppermute | solution.py:377
  85.3 7.3 %collective-permute-start.17 = (bf16[240,256]{1,0:T(8,128)(2,1)S(1)}, bf16[240,256]{1,0:T(8,128)(2,1)S(1)}, u32[]{:S(2)}, u32[]{:S(2)}) collective-permute-start(bf16[240,256]{1,0:T(8,128)(2,1)S(1)} %get-tuple-element.60.own), channel_id=1, source_target_pairs={{0,16},{8,24},{16,0},{24,8},{32,48},{40,56},{48,32},{56,40},{64,80... | collective-permute-start | bytes 368648 | tf_op jit(solution)/shard_map/ppermute | solution.py:377
  86.7 5.9 %collective-permute-start.16 = (bf16[240,256]{1,0:T(8,128)(2,1)S(1)}, bf16[240,256]{1,0:T(8,128)(2,1)S(1)}, u32[]{:S(2)}, u32[]{:S(2)}) collective-permute-start(bf16[240,256]{1,0:T(8,128)(2,1)S(1)} %get-tuple-element.60.own), channel_id=1, source_target_pairs={{0,24},{8,0},{16,8},{24,16},{32,56},{40,32},{48,40},{56,48},{64,88... | collective-permute-start | bytes 368648 | tf_op jit(solution)/shard_map/ppermute | solution.py:377
  89.2 6.1 %collective-permute-start.15 = (bf16[240,256]{1,0:T(8,128)(2,1)S(1)}, bf16[240,256]{1,0:T(8,128)(2,1)S(1)}, u32[]{:S(2)}, u32[]{:S(2)}) collective-permute-start(bf16[240,256]{1,0:T(8,128)(2,1)S(1)} %get-tuple-element.60.own), channel_id=1, source_target_pairs={{0,8},{8,16},{16,24},{24,0},{32,40},{40,48},{48,56},{56,32},{64,72... | collective-permute-start | bytes 368648 | tf_op jit(solution)/shard_map/ppermute | solution.py:377
  95.3 6.6 %collective-permute-start.20 = (bf16[224,256]{1,0:T(8,128)(2,1)S(1)}, bf16[224,256]{1,0:T(8,128)(2,1)S(1)}, u32[]{:S(2)}, u32[]{:S(2)}) collective-permute-start(bf16[224,256]{1,0:T(8,128)(2,1)S(1)} %get-tuple-element.65.own), channel_id=1, source_target_pairs={{0,64},{8,72},{16,80},{24,88},{32,96},{40,104},{48,112},{56,120},{... | collective-permute-start | bytes 344072 | tf_op jit(solution)/shard_map/ppermute | solution.py:377
  97.7 5.2 %collective-permute-start.19 = (bf16[224,256]{1,0:T(8,128)(2,1)S(1)}, bf16[224,256]{1,0:T(8,128)(2,1)S(1)}, u32[]{:S(2)}, u32[]{:S(2)}) collective-permute-start(bf16[224,256]{1,0:T(8,128)(2,1)S(1)} %get-tuple-element.65.own), channel_id=1, source_target_pairs={{0,96},{8,104},{16,112},{24,120},{32,0},{40,8},{48,16},{56,24},{64... | collective-permute-start | bytes 344072 | tf_op jit(solution)/shard_map/ppermute | solution.py:377
  99.8 6.0 %collective-permute-start.18 = (bf16[224,256]{1,0:T(8,128)(2,1)S(1)}, bf16[224,256]{1,0:T(8,128)(2,1)S(1)}, u32[]{:S(2)}, u32[]{:S(2)}) collective-permute-start(bf16[224,256]{1,0:T(8,128)(2,1)S(1)} %get-tuple-element.65.own), channel_id=1, source_target_pairs={{0,32},{8,40},{16,48},{24,56},{32,64},{40,72},{48,80},{56,88},{64,... | collective-permute-start | bytes 344072 | tf_op jit(solution)/shard_map/ppermute | solution.py:377
  (5 other events, 9.7 us)

commit v9 on v8

--- a/solution.py
+++ b/solution.py
@@ -42,7 +42,7 @@
 
 
 def sigmoid(v):
-    return 1.0 / (1.0 + jnp.exp(-v))
+    return 0.5 * jnp.tanh(0.5 * v) + 0.5
 
 
 def widths(target, cot, slot):
@@ -71,10 +71,10 @@
 
     zero = jnp.zeros((8, C), f32)
     a, b = lax.fori_loop(0, 2 * ROWS // 128, step, (zero, zero))
-    row = lax.broadcasted_iota(jnp.int32, (8, C), 0)
-    both = jnp.where(row == 0, a.sum(0, keepdims=True), jnp.where(row == 1, b.sum(0, keepdims=True), 0.0))
+    a, b = a.sum(0, keepdims=True), b.sum(0, keepdims=True)
     for i in range(16):
-        out[i] = both
+        out[i, 0:1] = a
+        out[i, 1:2] = b
     last[...] = clip[1]
 
 
@@ -93,11 +93,11 @@
     total = parts[0]
     for i in range(1, 16):
         total = total + parts[i]
-    out[...] = total[0:2]
+    out[...] = total
 
 
 def tap_rows(kh):
-    return pl.ds(pl.multiple_of((2 - kh) * W, W), ROWS)
+    return slice((2 - kh) * W, (2 - kh) * W + ROWS)
 
 
 CONTRACT_ROWS = (((0,), (0,)), ((), ()))
@@ -157,8 +157,7 @@
     for t in range(2):
         activate(center, inverse, lambda at, t=t: clip[t, at], act.at[t])
 
-    @pl.loop(0, 3)
-    def _(kh):
+    for kh in range(3):
         rows = tap_rows(kh)
         for kw in range(3):
             total = tap_product((act[0], act[1]), (near[kw, 0, rows], near[kw, 1, rows]), slice(None))
@@ -178,8 +177,7 @@
     gain = jnp.where(where[0] == 1, 0.0, 1.0)
     activate(center, inverse, lambda at: before[at], act_before, gain)
 
-    @pl.loop(0, 3)
-    def _(kh):
+    for kh in range(3):
         rows = tap_rows(kh)
         for kw in range(3):
             total = tap_product((act_before, act[0]), (near[kw, 1, rows], after[kw, 0, rows]), slice(None))
@@ -336,12 +334,17 @@
     next_sums[...] = ring_sums(sums[...], (a0, a1, a2))
 
 
-def finish_kernel(where, own, a0, a1, a2, grad_weight, full):
+def finish_kernel(where, own, a0, a1, a2, grad_weight):
     y = where[3]
+    whole = SHARD - 3 * QUARTER
     for block, distance in ((own, 0), (a0, 3), (a1, 1), (a2, 2)):
-        at = pl.ds(pl.multiple_of(((y + distance) & 3) * QUARTER, UNIT), QUARTER)
-        full[at] = block[...].astype(f32)
-    grad_weight[...] = full[:SHARD]
+        quarter = (y + distance) & 3
+        start = pl.multiple_of(quarter * QUARTER, UNIT)
+        grad_weight[pl.ds(start, whole)] = block[:whole].astype(f32)
+
+        @pl.when(quarter < 3)
+        def _(block=block, start=start):
+            grad_weight[pl.ds(start + whole, QUARTER - whole)] = block[whole:].astype(f32)
 
 
 def call(kernel, out_shape, args, scratch=(), flops=0, bytes_accessed=0, scalars=0, order=(), aliases={}, passed_out=0):
@@ -401,7 +404,7 @@
     where = jnp.stack([jnp.asarray(v, jnp.int32) for v in where])
     frame = S((ROWS, C), bf16)
 
-    sums, last = call(first_kernel, (S((16, 8, C), f32), frame), (clip,))
+    sums, last = call(first_kernel, (S((16, 2, C), f32), frame), (clip,))
     first, second = call(copy_kernel, (frame, frame), (cot,), order=(sums,))
     parts = lax.all_to_all(sums, "tm", 0, 0, tiled=True)
     stats, first, last = call(
@@ -493,7 +496,6 @@
         finish_kernel,
         S((SHARD, C), f32),
         (where, own, *ring("y", [own] * 3)),
-        [pltpu.VMEM((SHARD_PAD, C), f32)],
         scalars=1,
     )
     return grad_input.reshape(shape), grad_weight

time: 108 us -> 106 us (0.981)
  Pallas kernels: 33.3 us -> 31.4 us
    pallas_call x18, Pallas kernels: 33.3 us -> 31.4 us  [call(): pl.pallas_call(kernel, out_shape=out_shape, in_specs=specs, out_specs=out...]
    unnamed x14 -> x12, local copies, waits for them, and re-layouts: 2.67 us -> 2.68 us
  transfers between devices with their start and end apart: 22 -> 22, of which waited for: 13 -> 13; matrix products, arithmetic and copies ran while one was open for 1% -> 0% of each run, Pallas kernels for 29% -> 27%
where the time goes in v9:
time: 106 us
  starting transfers between devices  40.2 us (38%)
  Pallas kernels  31.4 us (30%)
  waiting for transfers between devices  31 us (29%)
  local copies, waits for them, and re-layouts  2.68 us (3%)
    pallas_call x18, Pallas kernels, call(): pl.pallas_call(kernel, out_shape=out_shape, in_specs=specs, out_specs=out...  31.4 us
    ppermute x15, starting transfers between devices, ring(): got.append(lax.ppermute(block, name, route))  24.2 us
    ppermute x15, waiting for transfers between devices, ring(): got.append(lax.ppermute(block, name, route))  21.1 us
    all_to_all x1, starting transfers between devices, per_device(): parts = lax.all_to_all(sums, 'tm', 0, 0, tiled=True)  8.05 us
    ppermute x3, starting transfers between devices, passed(): return lax.ppermute(block, 'tm', route)  7.15 us
    all_to_all x1, waiting for transfers between devices, per_device(): parts = lax.all_to_all(sums, 'tm', 0, 0, tiled=True)  6.66 us
    unnamed x12, local copies, waits for them, and re-layouts  2.68 us
    ppermute x3, waiting for transfers between devices, passed(): return lax.ppermute(block, 'tm', route)  2.42 us
  transfers between devices with their start and end apart: 22, of which 13 were waited for; matrix products, arithmetic and copies ran while one was open for 0% of the time, Pallas kernels for 27%

profile of v9, /device:TPU:6, one launch (start us, length us, event | category | flops | bytes accessed | tf_op | source)
XLA Modules:
  0.0 106.2 jit_solution(11766174614857006196)
XLA Ops:
  1.5 2.4 %collective-permute-start.1 = (bf16[864,256]{1,0:T(8,128)(2,1)}, bf16[864,256]{1,0:T(8,128)(2,1)S(1)}, u32[]{:S(2)}, u32[]{:S(2)}) collective-permute-start(bf16[864,256]{1,0:T(8,128)(2,1)} %own.1), channel_id=1, source_target_pairs={{0,2},{1,3},{2,4},{3,5},{4,6},{5,7},{6,0},{7,1},{8,10},{9,11},{10,... | collective-permute-start | bytes 1327112 | tf_op jit(solution)/shard_map/ppermute | solution.py:380
  6.4 8.0 %all-to-all-start = ((f32[16,2,256]{2,1,0:T(2,128)}), f32[16,2,256]{2,1,0:T(2,128)S(1)}, u32[]{:S(2)}, u32[]{:S(2)}) async-start(f32[16,2,256]{2,1,0:T(2,128)} %get-tuple-element.34.order), calls=%async_computation | async-start | bytes 65536 | tf_op jit(solution)/shard_map/all_to_all | solution.py:409
  15.4 6.7 %all-to-all-done.parts = f32[16,2,256]{2,1,0:T(2,128)S(1)} async-done(((f32[16,2,256]{2,1,0:T(2,128)}), f32[16,2,256]{2,1,0:T(2,128)S(1)}, u32[]{:S(2)}, u32[]{:S(2)}) %all-to-all-start) | async-done | bytes 32800 | tf_op jit(solution)/shard_map/all_to_all | solution.py:409
  23.4 4.6 %collective-permute-start.5 = (bf16[1024,256]{1,0:T(8,128)(2,1)S(1)}, bf16[1024,256]{1,0:T(8,128)(2,1)S(1)}, u32[]{:S(2)}, u32[]{:S(2)}) collective-permute-start(bf16[1024,256]{1,0:T(8,128)(2,1)S(1)} %get-tuple-element.44), channel_id=1, source_target_pairs={{0,8},{8,16},{16,24},{24,32},{32,40},{40,48},{48,56},{56,64},{64,7... | collective-permute-start | bytes 1572872 | tf_op jit(solution)/shard_map/ppermute | solution.py:390
  29.2 4.3 %shard_map.54 = (bf16[2,1024,256]{2,1,0:T(8,128)(2,1)S(1)}, f32[1824,256]{1,0:T(8,128)S(1)}, bf16[1824,256]{1,0:T(8,128)(2,1)S(1)}) custom-call(s32[4]{0:T(128)S(1)} %pad_add_fusion.where, f32[2,256]{1,0:T(2,128)S(1)} %get-tuple-element.37.refs_0_.stats, bf16[2,1024,256]{2,1,0:T(8,128)(2,1)S(1)} %bitcast.13, bf16[3,2,1152,256]{3,2,1,0:T(8,128)(2,1)S(1)} %shard_map.53.near), custom_call_target="tpu_custom_call" | custom-call | flops 2415919104 | tf_op jit(solution)/shard_map/pallas_call | solution.py:357
  35.7 2.0 %shard_map.57 = (f32[1824,256]{1,0:T(8,128)S(1)}, bf16[1824,256]{1,0:T(8,128)(2,1)S(1)}) custom-call(s32[4]{0:T(128)S(1)} %pad_add_fusion.where, bf16[2,1024,256]{2,1,0:T(8,128)(2,1)S(1)} %get-tuple-element.38.order.act, bf16[3,2,1152,256]{3,2,1,0:T(8,128)(2,1)S(1)} %shard_map.53.near, ...), custom_call_target="tpu_custom_call", output_to_operand_aliasing={{0}: (4, {}), {1}: (5, {})} | custom-call | flops 1207959552 | tf_op jit(solution)/shard_map/pallas_call | solution.py:357
  37.9 5.2 %shard_map.58 = (f32[1824,256]{1,0:T(8,128)S(1)}, bf16[1824,256]{1,0:T(8,128)(2,1)S(1)}) custom-call(s32[4]{0:T(128)S(1)} %pad_add_fusion.where, f32[2,256]{1,0:T(2,128)S(1)} %get-tuple-element.37.refs_0_.stats, bf16[2,1024,256]{2,1,0:T(8,128)(2,1)S(1)} %get-tuple-element.38.order.act, bf16[1024,256]{1,0:T(8,128)(2,1)S(1)} %collective-permute-done.5.before, ...), custom_call_target="tpu_custom_call" | custom-call | flops 3623878656 | tf_op jit(solution)/shard_map/pallas_call | solution.py:357
  46.7 2.1 %collective-permute-start.7 = (bf16[896,256]{1,0:T(8,128)(2,1)S(1)}, bf16[896,256]{1,0:T(8,128)(2,1)S(1)}, u32[]{:S(2)}, u32[]{:S(2)}) collective-permute-start(bf16[896,256]{1,0:T(8,128)(2,1)S(1)} %get-tuple-element.48), channel_id=1, source_target_pairs={{0,2},{1,3},{2,4},{3,5},{4,6},{5,7},{6,0},{7,1},{8,10},{9,11},{10,... | collective-permute-start | bytes 1376264 | tf_op jit(solution)/shard_map/ppermute | solution.py:380
  48.8 3.2 %collective-permute-start.9 = (bf16[896,256]{1,0:T(8,128)(2,1)S(1)}, bf16[896,256]{1,0:T(8,128)(2,1)S(1)}, u32[]{:S(2)}, u32[]{:S(2)}) collective-permute-start(bf16[896,256]{1,0:T(8,128)(2,1)S(1)} %get-tuple-element.50), channel_id=1, source_target_pairs={{0,4},{1,5},{2,6},{3,7},{4,0},{5,1},{6,2},{7,3},{8,12},{9,13},{10,... | collective-permute-start | bytes 1376264 | tf_op jit(solution)/shard_map/ppermute | solution.py:380
  52.0 6.1 %shard_map.60 = (f32[1024,256]{1,0:T(8,128)S(1)}, f32[2,256]{1,0:T(2,128)S(1)}, bf16[6912,256]{1,0:T(8,128)(2,1)S(1)}) custom-call(s32[4]{0:T(128)S(1)} %pad_add_fusion.where, f32[2,256]{1,0:T(2,128)S(1)} %get-tuple-element.37.refs_0_.stats, bf16[2,1024,256]{2,1,0:T(8,128)(2,1)S(1)} %bitcast.14, bf16[3,2,1152,256]{3,2,1,0:T(8,128)(2,1)S(1)} %shard_map.53.near, ...), custom_call_target="tpu_custom_call" | custom-call | flops 3623878656 | tf_op jit(solution)/shard_map/pallas_call | solution.py:357
  59.7 5.4 %shard_map.62 = (f32[1024,256]{1,0:T(8,128)S(1)}, f32[2,256]{1,0:T(2,128)S(1)}) custom-call(f32[2,256]{1,0:T(2,128)S(1)} %get-tuple-element.37.refs_0_.stats, bf16[2,1024,256]{2,1,0:T(8,128)(2,1)S(1)} %bitcast.15, bf16[3,2,1152,256]{3,2,1,0:T(8,128)(2,1)S(1)} %shard_map.53.near, bf16[3,1,1152,256]{3,2,1,0:T(8,128)(2,1)S(1)} %shard_map.55.after, ...), custom_call_target="tpu_custom_call" | custom-call | flops 3623878656 | tf_op jit(solution)/shard_map/pallas_call | solution.py:357
  65.1 3.9 %collective-permute-done.7.a0 = bf16[896,256]{1,0:T(8,128)(2,1)S(1)} collective-permute-done((bf16[896,256]{1,0:T(8,128)(2,1)S(1)}, bf16[896,256]{1,0:T(8,128)(2,1)S(1)}, u32[]{:S(2)}, u32[]{:S(2)}) %collective-permute-start.7) | collective-permute-done | bytes 458784 | tf_op jit(solution)/shard_map/ppermute | solution.py:380
  68.9 3.4 %collective-permute-done.9.a2 = bf16[896,256]{1,0:T(8,128)(2,1)S(1)} collective-permute-done((bf16[896,256]{1,0:T(8,128)(2,1)S(1)}, bf16[896,256]{1,0:T(8,128)(2,1)S(1)}, u32[]{:S(2)}, u32[]{:S(2)}) %collective-permute-start.9) | collective-permute-done | bytes 458784 | tf_op jit(solution)/shard_map/ppermute | solution.py:380
  73.2 4.0 %collective-permute-start.12 = (bf16[240,256]{1,0:T(8,128)(2,1)S(1)}, bf16[240,256]{1,0:T(8,128)(2,1)S(1)}, u32[]{:S(2)}, u32[]{:S(2)}) collective-permute-start(bf16[240,256]{1,0:T(8,128)(2,1)S(1)} %get-tuple-element.57), channel_id=1, source_target_pairs={{0,32},{8,40},{16,48},{24,56},{32,64},{40,72},{48,80},{56,88},{64,... | collective-permute-start | bytes 368648 | tf_op jit(solution)/shard_map/ppermute | solution.py:380
  77.2 2.6 %collective-permute-start.14 = (bf16[240,256]{1,0:T(8,128)(2,1)S(1)}, bf16[240,256]{1,0:T(8,128)(2,1)S(1)}, u32[]{:S(2)}, u32[]{:S(2)}) collective-permute-start(bf16[240,256]{1,0:T(8,128)(2,1)S(1)} %get-tuple-element.59), channel_id=1, source_target_pairs={{0,64},{8,72},{16,80},{24,88},{32,96},{40,104},{48,112},{56,120},{... | collective-permute-start | bytes 368648 | tf_op jit(solution)/shard_map/ppermute | solution.py:380
  80.6 1.6 %collective-permute-done.13.a1 = bf16[240,256]{1,0:T(8,128)(2,1)S(1)} collective-permute-done((bf16[240,256]{1,0:T(8,128)(2,1)S(1)}, bf16[240,256]{1,0:T(8,128)(2,1)S(1)}, u32[]{:S(2)}, u32[]{:S(2)}) %collective-permute-start.13) | collective-permute-done | bytes 122912 | tf_op jit(solution)/shard_map/ppermute | solution.py:380
  83.7 1.8 %collective-permute-start.17 = (bf16[240,256]{1,0:T(8,128)(2,1)S(1)}, bf16[240,256]{1,0:T(8,128)(2,1)S(1)}, u32[]{:S(2)}, u32[]{:S(2)}) collective-permute-start(bf16[240,256]{1,0:T(8,128)(2,1)S(1)} %get-tuple-element.60.own), channel_id=1, source_target_pairs={{0,16},{8,24},{16,0},{24,8},{32,48},{40,56},{48,32},{56,40},{64,80... | collective-permute-start | bytes 368648 | tf_op jit(solution)/shard_map/ppermute | solution.py:380
  85.6 2.4 %collective-permute-start.16 = (bf16[240,256]{1,0:T(8,128)(2,1)S(1)}, bf16[240,256]{1,0:T(8,128)(2,1)S(1)}, u32[]{:S(2)}, u32[]{:S(2)}) collective-permute-start(bf16[240,256]{1,0:T(8,128)(2,1)S(1)} %get-tuple-element.60.own), channel_id=1, source_target_pairs={{0,24},{8,0},{16,8},{24,16},{32,56},{40,32},{48,40},{56,48},{64,88... | collective-permute-start | bytes 368648 | tf_op jit(solution)/shard_map/ppermute | solution.py:380
  88.0 3.5 %collective-permute-done.17.a2 = bf16[240,256]{1,0:T(8,128)(2,1)S(1)} collective-permute-done((bf16[240,256]{1,0:T(8,128)(2,1)S(1)}, bf16[240,256]{1,0:T(8,128)(2,1)S(1)}, u32[]{:S(2)}, u32[]{:S(2)}) %collective-permute-start.17) | collective-permute-done | bytes 122912 | tf_op jit(solution)/shard_map/ppermute | solution.py:380
  91.5 2.6 %collective-permute-done.15.a0 = bf16[240,256]{1,0:T(8,128)(2,1)S(1)} collective-permute-done((bf16[240,256]{1,0:T(8,128)(2,1)S(1)}, bf16[240,256]{1,0:T(8,128)(2,1)S(1)}, u32[]{:S(2)}, u32[]{:S(2)}) %collective-permute-start.15) | collective-permute-done | bytes 122912 | tf_op jit(solution)/shard_map/ppermute | solution.py:380
  94.2 2.4 %collective-permute-start.20 = (bf16[224,256]{1,0:T(8,128)(2,1)S(1)}, bf16[224,256]{1,0:T(8,128)(2,1)S(1)}, u32[]{:S(2)}, u32[]{:S(2)}) collective-permute-start(bf16[224,256]{1,0:T(8,128)(2,1)S(1)} %get-tuple-element.65.own), channel_id=1, source_target_pairs={{0,64},{8,72},{16,80},{24,88},{32,96},{40,104},{48,112},{56,120},{... | collective-permute-start | bytes 344072 | tf_op jit(solution)/shard_map/ppermute | solution.py:380
  96.6 2.1 %collective-permute-start.19 = (bf16[224,256]{1,0:T(8,128)(2,1)S(1)}, bf16[224,256]{1,0:T(8,128)(2,1)S(1)}, u32[]{:S(2)}, u32[]{:S(2)}) collective-permute-start(bf16[224,256]{1,0:T(8,128)(2,1)S(1)} %get-tuple-element.65.own), channel_id=1, source_target_pairs={{0,96},{8,104},{16,112},{24,120},{32,0},{40,8},{48,16},{56,24},{64... | collective-permute-start | bytes 344072 | tf_op jit(solution)/shard_map/ppermute | solution.py:380
  98.7 2.1 %shard_map.66 = bf16[2,1024,256]{2,1,0:T(8,128)(2,1)} custom-call(f32[2,256]{1,0:T(2,128)S(1)} %get-tuple-element.37.refs_0_.stats, f32[2,256]{1,0:T(2,128)S(1)} %get-tuple-element.62.sums, bf16[2,1024,256]{2,1,0:T(8,128)(2,1)S(1)} %bitcast.16, bf16[2,1024,256]{2,1,0:T(8,128)(2,1)S(1)} %bitcast.11, f32[1024,256]{1,0:T(8,128)S(1)} %get-tuple-element.63.grad0, ...), custom_call_target="tpu_custom_call" | custom-call | bytes 8000000 | tf_op jit(solution)/shard_map/pallas_call | solution.py:357
  101.8 2.9 %collective-permute-done.18.a0 = bf16[224,256]{1,0:T(8,128)(2,1)S(1)} collective-permute-done((bf16[224,256]{1,0:T(8,128)(2,1)S(1)}, bf16[224,256]{1,0:T(8,128)(2,1)S(1)}, u32[]{:S(2)}, u32[]{:S(2)}) %collective-permute-start.18) | collective-permute-done | bytes 114720 | tf_op jit(solution)/shard_map/ppermute | solution.py:380
  (51 shorter events, 20.0 us)
Async XLA Ops:
  0.6 13.9 %copy-start = (bf16[1,2,16,64,256]{4,3,2,1,0:T(8,128)(2,1)S(1)}, bf16[1,2,16,64,256]{4,3,2,1,0:T(8,128)(2,1)}, u32[]{:S(2)}) copy-start(bf16[1,2,16,64,256]{4,3,2,1,0:T(8,128)(2,1)} %param.4) | copy-start | bytes 3145732
  0.6 32.9 %collective-permute-start.2 = (bf16[864,256]{1,0:T(8,128)(2,1)}, bf16[864,256]{1,0:T(8,128)(2,1)S(1)}, u32[]{:S(2)}, u32[]{:S(2)}) collective-permute-start(bf16[864,256]{1,0:T(8,128)(2,1)} %own.1), channel_id=1, source_target_pairs={{0,6},{1,7},{2,0},{3,1},{4,2},{5,3},{6,4},{7,5},{8,14},{9,15},{10,... | collective-permute-start | bytes 1327112 | tf_op jit(solution)/shard_map/ppermute | solution.py:380
  1.5 32.0 %collective-permute-start.1 = (bf16[864,256]{1,0:T(8,128)(2,1)}, bf16[864,256]{1,0:T(8,128)(2,1)S(1)}, u32[]{:S(2)}, u32[]{:S(2)}) collective-permute-start(bf16[864,256]{1,0:T(8,128)(2,1)} %own.1), channel_id=1, source_target_pairs={{0,2},{1,3},{2,4},{3,5},{4,6},{5,7},{6,0},{7,1},{8,10},{9,11},{10,... | collective-permute-start | bytes 1327112 | tf_op jit(solution)/shard_map/ppermute | solution.py:380
  3.9 29.6 %collective-permute-start.3 = (bf16[864,256]{1,0:T(8,128)(2,1)}, bf16[864,256]{1,0:T(8,128)(2,1)S(1)}, u32[]{:S(2)}, u32[]{:S(2)}) collective-permute-start(bf16[864,256]{1,0:T(8,128)(2,1)} %own.1), channel_id=1, source_target_pairs={{0,4},{1,5},{2,6},{3,7},{4,0},{5,1},{6,2},{7,3},{8,12},{9,13},{10,... | collective-permute-start | bytes 1327112 | tf_op jit(solution)/shard_map/ppermute | solution.py:380
  6.4 15.7 %all-to-all-start = ((f32[16,2,256]{2,1,0:T(2,128)}), f32[16,2,256]{2,1,0:T(2,128)S(1)}, u32[]{:S(2)}, u32[]{:S(2)}) async-start(f32[16,2,256]{2,1,0:T(2,128)} %get-tuple-element.34.order), calls=%async_computation | async-start | bytes 65536 | tf_op jit(solution)/shard_map/all_to_all | solution.py:409
  22.1 13.4 %collective-permute-start = (bf16[1024,256]{1,0:T(8,128)(2,1)S(1)}, bf16[1024,256]{1,0:T(8,128)(2,1)S(1)}, u32[]{:S(2)}, u32[]{:S(2)}) collective-permute-start(bf16[1024,256]{1,0:T(8,128)(2,1)S(1)} %get-tuple-element.39), channel_id=1, source_target_pairs={{8,0},{16,8},{24,16},{32,24},{40,32},{48,40},{56,48},{64,56},{72,6... | collective-permute-start | bytes 1572872 | tf_op jit(solution)/shard_map/ppermute | solution.py:390
  23.4 14.5 %collective-permute-start.5 = (bf16[1024,256]{1,0:T(8,128)(2,1)S(1)}, bf16[1024,256]{1,0:T(8,128)(2,1)S(1)}, u32[]{:S(2)}, u32[]{:S(2)}) collective-permute-start(bf16[1024,256]{1,0:T(8,128)(2,1)S(1)} %get-tuple-element.44), channel_id=1, source_target_pairs={{0,8},{8,16},{16,24},{24,32},{32,40},{40,48},{48,56},{56,64},{64,7... | collective-permute-start | bytes 1572872 | tf_op jit(solution)/shard_map/ppermute | solution.py:390
  34.3 17.8 %collective-permute-start.10 = (bf16[4,864,256]{2,1,0:T(8,128)(2,1)S(1)}, bf16[4,864,256]{2,1,0:T(8,128)(2,1)S(1)}, u32[]{:S(2)}, u32[]{:S(2)}) collective-permute-start(bf16[4,864,256]{2,1,0:T(8,128)(2,1)S(1)} %shard_map.56.order.mine), channel_id=1, source_target_pairs={{0,1},{1,0},{2,3},{3,2},{4,5},{5,4},{6,7},{7,6},{8,9},{9,8},{10,11... | collective-permute-start | bytes 5308424 | tf_op jit(solution)/shard_map/ppermute | solution.py:385
  37.7 5.9 %copy-start.5 = (bf16[1024,256]{1,0:T(8,128)(2,1)S(1)}, bf16[1024,256]{1,0:T(8,128)(2,1)}, u32[]{:S(2)}) copy-start(bf16[1024,256]{1,0:T(8,128)(2,1)} %copy-done.4) | copy-start | bytes 1572868
  37.8 7.2 %collective-permute-start.4 = (bf16[1824,256]{1,0:T(8,128)(2,1)S(1)}, bf16[1824,256]{1,0:T(8,128)(2,1)S(1)}, u32[]{:S(2)}, u32[]{:S(2)}) collective-permute-start(bf16[1824,256]{1,0:T(8,128)(2,1)S(1)} %get-tuple-element.43.order), channel_id=1, source_target_pairs={{0,1},{1,0},{2,3},{3,2},{4,5},{5,4},{6,7},{7,6},{8,9},{9,8},{10,11... | collective-permute-start | bytes 2801672 | tf_op jit(solution)/shard_map/ppermute | solution.py:385
  43.1 2.7 %collective-permute-start.6 = (bf16[1824,256]{1,0:T(8,128)(2,1)S(1)}, bf16[1824,256]{1,0:T(8,128)(2,1)S(1)}, u32[]{:S(2)}, u32[]{:S(2)}) collective-permute-start(bf16[1824,256]{1,0:T(8,128)(2,1)S(1)} %get-tuple-element.46), channel_id=1, source_target_pairs={{0,1},{1,0},{2,3},{3,2},{4,5},{5,4},{6,7},{7,6},{8,9},{9,8},{10,11... | collective-permute-start | bytes 2801672 | tf_op jit(solution)/shard_map/ppermute | solution.py:385
  43.7 15.7 %collective-permute-start.11 = (bf16[1024,256]{1,0:T(8,128)(2,1)S(1)}, bf16[1024,256]{1,0:T(8,128)(2,1)S(1)}, u32[]{:S(2)}, u32[]{:S(2)}) collective-permute-start(bf16[1024,256]{1,0:T(8,128)(2,1)S(1)} %copy-done.5), channel_id=1, source_target_pairs={{8,0},{16,8},{24,16},{32,24},{40,32},{48,40},{56,48},{64,56},{72,6... | collective-permute-start | bytes 1572872 | tf_op jit(solution)/shard_map/ppermute | solution.py:390
  46.7 22.3 %collective-permute-start.7 = (bf16[896,256]{1,0:T(8,128)(2,1)S(1)}, bf16[896,256]{1,0:T(8,128)(2,1)S(1)}, u32[]{:S(2)}, u32[]{:S(2)}) collective-permute-start(bf16[896,256]{1,0:T(8,128)(2,1)S(1)} %get-tuple-element.48), channel_id=1, source_target_pairs={{0,2},{1,3},{2,4},{3,5},{4,6},{5,7},{6,0},{7,1},{8,10},{9,11},{10,... | collective-permute-start | bytes 1376264 | tf_op jit(solution)/shard_map/ppermute | solution.py:380
  48.8 20.2 %collective-permute-start.8 = (bf16[896,256]{1,0:T(8,128)(2,1)S(1)}, bf16[896,256]{1,0:T(8,128)(2,1)S(1)}, u32[]{:S(2)}, u32[]{:S(2)}) collective-permute-start(bf16[896,256]{1,0:T(8,128)(2,1)S(1)} %get-tuple-element.49), channel_id=1, source_target_pairs={{0,6},{1,7},{2,0},{3,1},{4,2},{5,3},{6,4},{7,5},{8,14},{9,15},{10,... | collective-permute-start | bytes 1376264 | tf_op jit(solution)/shard_map/ppermute | solution.py:380
  48.8 23.6 %collective-permute-start.9 = (bf16[896,256]{1,0:T(8,128)(2,1)S(1)}, bf16[896,256]{1,0:T(8,128)(2,1)S(1)}, u32[]{:S(2)}, u32[]{:S(2)}) collective-permute-start(bf16[896,256]{1,0:T(8,128)(2,1)S(1)} %get-tuple-element.50), channel_id=1, source_target_pairs={{0,4},{1,5},{2,6},{3,7},{4,0},{5,1},{6,2},{7,3},{8,12},{9,13},{10,... | collective-permute-start | bytes 1376264 | tf_op jit(solution)/shard_map/ppermute | solution.py:380
  73.2 7.4 %collective-permute-start.12 = (bf16[240,256]{1,0:T(8,128)(2,1)S(1)}, bf16[240,256]{1,0:T(8,128)(2,1)S(1)}, u32[]{:S(2)}, u32[]{:S(2)}) collective-permute-start(bf16[240,256]{1,0:T(8,128)(2,1)S(1)} %get-tuple-element.57), channel_id=1, source_target_pairs={{0,32},{8,40},{16,48},{24,56},{32,64},{40,72},{48,80},{56,88},{64,... | collective-permute-start | bytes 368648 | tf_op jit(solution)/shard_map/ppermute | solution.py:380
  77.2 4.9 %collective-permute-start.13 = (bf16[240,256]{1,0:T(8,128)(2,1)S(1)}, bf16[240,256]{1,0:T(8,128)(2,1)S(1)}, u32[]{:S(2)}, u32[]{:S(2)}) collective-permute-start(bf16[240,256]{1,0:T(8,128)(2,1)S(1)} %get-tuple-element.58), channel_id=1, source_target_pairs={{0,96},{8,104},{16,112},{24,120},{32,0},{40,8},{48,16},{56,24},{64... | collective-permute-start | bytes 368648 | tf_op jit(solution)/shard_map/ppermute | solution.py:380
  77.2 6.4 %collective-permute-start.14 = (bf16[240,256]{1,0:T(8,128)(2,1)S(1)}, bf16[240,256]{1,0:T(8,128)(2,1)S(1)}, u32[]{:S(2)}, u32[]{:S(2)}) collective-permute-start(bf16[240,256]{1,0:T(8,128)(2,1)S(1)} %get-tuple-element.59), channel_id=1, source_target_pairs={{0,64},{8,72},{16,80},{24,88},{32,96},{40,104},{48,112},{56,120},{... | collective-permute-start | bytes 368648 | tf_op jit(solution)/shard_map/ppermute | solution.py:380
  83.7 7.7 %collective-permute-start.17 = (bf16[240,256]{1,0:T(8,128)(2,1)S(1)}, bf16[240,256]{1,0:T(8,128)(2,1)S(1)}, u32[]{:S(2)}, u32[]{:S(2)}) collective-permute-start(bf16[240,256]{1,0:T(8,128)(2,1)S(1)} %get-tuple-element.60.own), channel_id=1, source_target_pairs={{0,16},{8,24},{16,0},{24,8},{32,48},{40,56},{48,32},{56,40},{64,80... | collective-permute-start | bytes 368648 | tf_op jit(solution)/shard_map/ppermute | solution.py:380
  85.6 5.9 %collective-permute-start.16 = (bf16[240,256]{1,0:T(8,128)(2,1)S(1)}, bf16[240,256]{1,0:T(8,128)(2,1)S(1)}, u32[]{:S(2)}, u32[]{:S(2)}) collective-permute-start(bf16[240,256]{1,0:T(8,128)(2,1)S(1)} %get-tuple-element.60.own), channel_id=1, source_target_pairs={{0,24},{8,0},{16,8},{24,16},{32,56},{40,32},{48,40},{56,48},{64,88... | collective-permute-start | bytes 368648 | tf_op jit(solution)/shard_map/ppermute | solution.py:380
  88.0 6.1 %collective-permute-start.15 = (bf16[240,256]{1,0:T(8,128)(2,1)S(1)}, bf16[240,256]{1,0:T(8,128)(2,1)S(1)}, u32[]{:S(2)}, u32[]{:S(2)}) collective-permute-start(bf16[240,256]{1,0:T(8,128)(2,1)S(1)} %get-tuple-element.60.own), channel_id=1, source_target_pairs={{0,8},{8,16},{16,24},{24,0},{32,40},{40,48},{48,56},{56,32},{64,72... | collective-permute-start | bytes 368648 | tf_op jit(solution)/shard_map/ppermute | solution.py:380
  94.2 6.6 %collective-permute-start.20 = (bf16[224,256]{1,0:T(8,128)(2,1)S(1)}, bf16[224,256]{1,0:T(8,128)(2,1)S(1)}, u32[]{:S(2)}, u32[]{:S(2)}) collective-permute-start(bf16[224,256]{1,0:T(8,128)(2,1)S(1)} %get-tuple-element.65.own), channel_id=1, source_target_pairs={{0,64},{8,72},{16,80},{24,88},{32,96},{40,104},{48,112},{56,120},{... | collective-permute-start | bytes 344072 | tf_op jit(solution)/shard_map/ppermute | solution.py:380
  96.6 5.2 %collective-permute-start.19 = (bf16[224,256]{1,0:T(8,128)(2,1)S(1)}, bf16[224,256]{1,0:T(8,128)(2,1)S(1)}, u32[]{:S(2)}, u32[]{:S(2)}) collective-permute-start(bf16[224,256]{1,0:T(8,128)(2,1)S(1)} %get-tuple-element.65.own), channel_id=1, source_target_pairs={{0,96},{8,104},{16,112},{24,120},{32,0},{40,8},{48,16},{56,24},{64... | collective-permute-start | bytes 344072 | tf_op jit(solution)/shard_map/ppermute | solution.py:380
  98.7 6.0 %collective-permute-start.18 = (bf16[224,256]{1,0:T(8,128)(2,1)S(1)}, bf16[224,256]{1,0:T(8,128)(2,1)S(1)}, u32[]{:S(2)}, u32[]{:S(2)}) collective-permute-start(bf16[224,256]{1,0:T(8,128)(2,1)S(1)} %get-tuple-element.65.own), channel_id=1, source_target_pairs={{0,32},{8,40},{16,48},{24,56},{32,64},{40,72},{48,80},{56,88},{64,... | collective-permute-start | bytes 344072 | tf_op jit(solution)/shard_map/ppermute | solution.py:380
  (4 other events, 7.6 us)

commit v10 on v9

--- a/solution.py
+++ b/solution.py
@@ -72,7 +72,7 @@
     zero = jnp.zeros((8, C), f32)
     a, b = lax.fori_loop(0, 2 * ROWS // 128, step, (zero, zero))
     a, b = a.sum(0, keepdims=True), b.sum(0, keepdims=True)
-    for i in range(16):
+    for i in range(4):
         out[i, 0:1] = a
         out[i, 1:2] = b
     last[...] = clip[1]
@@ -90,10 +90,13 @@
 
 
 def total_kernel(parts, held0, held1, out, pass0, pass1):
-    total = parts[0]
-    for i in range(1, 16):
-        total = total + parts[i]
-    out[...] = total
+    out[...] = (parts[0] + parts[1]) + (parts[2] + parts[3])
+
+
+def spread_total_kernel(parts, out):
+    total = (parts[0] + parts[1]) + (parts[2] + parts[3])
+    for i in range(4):
+        out[i] = total
 
 
 def tap_rows(kh):
@@ -404,9 +407,13 @@
     where = jnp.stack([jnp.asarray(v, jnp.int32) for v in where])
     frame = S((ROWS, C), bf16)
 
-    sums, last = call(first_kernel, (S((16, 2, C), f32), frame), (clip,))
+    sums, last = call(first_kernel, (S((4, 2, C), f32), frame), (clip,))
     first, second = call(copy_kernel, (frame, frame), (cot,), order=(sums,))
-    parts = lax.all_to_all(sums, "tm", 0, 0, tiled=True)
+    rows_of_z = [[4 * y + z for z in range(4)] for y in range(4)]
+    rows_of_y = [[4 * y + z for y in range(4)] for z in range(4)]
+    parts = lax.all_to_all(sums, "tm", 0, 0, axis_index_groups=rows_of_z, tiled=True)
+    parts = call(spread_total_kernel, S((4, 2, C), f32), (parts,))
+    parts = lax.all_to_all(parts, "tm", 0, 0, axis_index_groups=rows_of_y, tiled=True)
     stats, first, last = call(
         total_kernel,
         (S((2, C), f32), frame, frame),

time: 106 us -> 111 us (1.047)
  starting transfers between devices: 40.2 us -> 41.5 us
  local copies, waits for them, and re-layouts: 2.68 us -> 3.91 us
    all_to_all x1 -> x2, waiting for transfers between devices: 6.66 us -> 8.47 us  [the longest x1 5.32 us: per_device(): lax.all_to_all(sums, 'tm', 0, 0, axis_index_groups=rows_of_z, tiled=True)]
    all_to_all x1 -> x2, starting transfers between devices: 8.05 us -> 9.77 us  [the longest x1 5.31 us: per_device(): lax.all_to_all(sums, 'tm', 0, 0, axis_index_groups=rows_of_z, tiled=True)]
    unnamed x12 -> x14, local copies, waits for them, and re-layouts: 2.68 us -> 3.91 us
    pallas_call x18 -> x19, Pallas kernels: 31.4 us -> 32 us  [call(): pl.pallas_call(kernel, out_shape=out_shape, in_specs=specs, out_specs=out...]
  transfers between devices with their start and end apart: 22 -> 23, of which waited for: 13 -> 13; matrix products, arithmetic and copies ran while one was open for 0% -> 0% of each run, Pallas kernels for 27% -> 27%
where the time goes in v10:
time: 111 us; the launch traced here: 110 us
  starting transfers between devices  41.5 us (37%)
  Pallas kernels  32 us (29%)
  waiting for transfers between devices  32 us (29%)
  local copies, waits for them, and re-layouts  3.91 us (4%)
    pallas_call x19, Pallas kernels, call(): pl.pallas_call(kernel, out_shape=out_shape, in_specs=specs, out_specs=out...  32 us
    ppermute x15, starting transfers between devices, ring(): got.append(lax.ppermute(block, name, route))  23.8 us
    ppermute x15, waiting for transfers between devices, ring(): got.append(lax.ppermute(block, name, route))  21 us
    ppermute x3, starting transfers between devices, passed(): return lax.ppermute(block, 'tm', route)  7.15 us
    all_to_all x1, waiting for transfers between devices, per_device(): lax.all_to_all(sums, 'tm', 0, 0, axis_index_groups=rows_of_z, tiled=True)  5.32 us
    all_to_all x1, starting transfers between devices, per_device(): lax.all_to_all(sums, 'tm', 0, 0, axis_index_groups=rows_of_z, tiled=True)  5.31 us
    all_to_all x1, starting transfers between devices, per_device(): lax.all_to_all(parts, 'tm', 0, 0, axis_index_groups=rows_of_y, tiled=True)  4.46 us
    unnamed x14, local copies, waits for them, and re-layouts  3.91 us
  transfers between devices with their start and end apart: 23, of which 13 were waited for; matrix products, arithmetic and copies ran while one was open for 0% of the time, Pallas kernels for 27%

profile of v10, /device:TPU:6, one launch (start us, length us, event | category | flops | bytes accessed | tf_op | source)
XLA Modules:
  0.0 110.3 jit_solution(8987073779980065875)
XLA Ops:
  1.5 2.4 %collective-permute-start.1 = (bf16[864,256]{1,0:T(8,128)(2,1)}, bf16[864,256]{1,0:T(8,128)(2,1)S(1)}, u32[]{:S(2)}, u32[]{:S(2)}) collective-permute-start(bf16[864,256]{1,0:T(8,128)(2,1)} %own.1), channel_id=1, source_target_pairs={{0,2},{1,3},{2,4},{3,5},{4,6},{5,7},{6,0},{7,1},{8,10},{9,11},{10,... | collective-permute-start | bytes 1327112 | tf_op jit(solution)/shard_map/ppermute | solution.py:383
  6.4 5.3 %all-to-all-start = ((f32[4,2,256]{2,1,0:T(2,128)}), f32[4,2,256]{2,1,0:T(2,128)S(1)}, u32[]{:S(2)}, u32[]{:S(2)}) async-start(f32[4,2,256]{2,1,0:T(2,128)} %get-tuple-element.34.order), calls=%async_computation | async-start | bytes 16384 | tf_op jit(solution)/shard_map/all_to_all | solution.py:414
  11.7 5.3 %all-to-all-done.parts = f32[4,2,256]{2,1,0:T(2,128)S(1)} async-done(((f32[4,2,256]{2,1,0:T(2,128)}), f32[4,2,256]{2,1,0:T(2,128)S(1)}, u32[]{:S(2)}, u32[]{:S(2)}) %all-to-all-start) | async-done | bytes 8224 | tf_op jit(solution)/shard_map/all_to_all | solution.py:414
  17.6 4.5 %all-to-all-start.1 = ((f32[4,2,256]{2,1,0:T(2,128)}), f32[4,2,256]{2,1,0:T(2,128)S(1)}, u32[]{:S(2)}, u32[]{:S(2)}) async-start(f32[4,2,256]{2,1,0:T(2,128)} %shard_map.51), calls=%async_computation.1 | async-start | bytes 16384 | tf_op jit(solution)/shard_map/all_to_all | solution.py:416
  24.2 3.1 %all-to-all-done.1.parts = f32[4,2,256]{2,1,0:T(2,128)S(1)} async-done(((f32[4,2,256]{2,1,0:T(2,128)}), f32[4,2,256]{2,1,0:T(2,128)S(1)}, u32[]{:S(2)}, u32[]{:S(2)}) %all-to-all-start.1) | async-done | bytes 8224 | tf_op jit(solution)/shard_map/all_to_all | solution.py:416
  28.7 4.6 %collective-permute-start.5 = (bf16[1024,256]{1,0:T(8,128)(2,1)S(1)}, bf16[1024,256]{1,0:T(8,128)(2,1)S(1)}, u32[]{:S(2)}, u32[]{:S(2)}) collective-permute-start(bf16[1024,256]{1,0:T(8,128)(2,1)S(1)} %get-tuple-element.44), channel_id=1, source_target_pairs={{0,8},{8,16},{16,24},{24,32},{32,40},{40,48},{48,56},{56,64},{64,7... | collective-permute-start | bytes 1572872 | tf_op jit(solution)/shard_map/ppermute | solution.py:393
  34.5 4.3 %shard_map.55 = (bf16[2,1024,256]{2,1,0:T(8,128)(2,1)S(1)}, f32[1824,256]{1,0:T(8,128)S(1)}, bf16[1824,256]{1,0:T(8,128)(2,1)S(1)}) custom-call(s32[4]{0:T(128)S(1)} %pad_add_fusion.where, f32[2,256]{1,0:T(2,128)S(1)} %get-tuple-element.37.refs_0_.stats, bf16[2,1024,256]{2,1,0:T(8,128)(2,1)S(1)} %bitcast.13, bf16[3,2,1152,256]{3,2,1,0:T(8,128)(2,1)S(1)} %shard_map.54.near), custom_call_target="tpu_custom_call" | custom-call | flops 2415919104 | tf_op jit(solution)/shard_map/pallas_call | solution.py:360
  39.9 2.0 %shard_map.58 = (f32[1824,256]{1,0:T(8,128)S(1)}, bf16[1824,256]{1,0:T(8,128)(2,1)S(1)}) custom-call(s32[4]{0:T(128)S(1)} %pad_add_fusion.where, bf16[2,1024,256]{2,1,0:T(8,128)(2,1)S(1)} %get-tuple-element.38.order.act, bf16[3,2,1152,256]{3,2,1,0:T(8,128)(2,1)S(1)} %shard_map.54.near, ...), custom_call_target="tpu_custom_call", output_to_operand_aliasing={{0}: (4, {}), {1}: (5, {})} | custom-call | flops 1207959552 | tf_op jit(solution)/shard_map/pallas_call | solution.py:360
  42.5 5.2 %shard_map.59 = (f32[1824,256]{1,0:T(8,128)S(1)}, bf16[1824,256]{1,0:T(8,128)(2,1)S(1)}) custom-call(s32[4]{0:T(128)S(1)} %pad_add_fusion.where, f32[2,256]{1,0:T(2,128)S(1)} %get-tuple-element.37.refs_0_.stats, bf16[2,1024,256]{2,1,0:T(8,128)(2,1)S(1)} %get-tuple-element.38.order.act, bf16[1024,256]{1,0:T(8,128)(2,1)S(1)} %collective-permute-done.5.before, ...), custom_call_target="tpu_custom_call" | custom-call | flops 3623878656 | tf_op jit(solution)/shard_map/pallas_call | solution.py:360
  51.2 2.2 %collective-permute-start.7 = (bf16[896,256]{1,0:T(8,128)(2,1)S(1)}, bf16[896,256]{1,0:T(8,128)(2,1)S(1)}, u32[]{:S(2)}, u32[]{:S(2)}) collective-permute-start(bf16[896,256]{1,0:T(8,128)(2,1)S(1)} %get-tuple-element.48), channel_id=1, source_target_pairs={{0,2},{1,3},{2,4},{3,5},{4,6},{5,7},{6,0},{7,1},{8,10},{9,11},{10,... | collective-permute-start | bytes 1376264 | tf_op jit(solution)/shard_map/ppermute | solution.py:383
  53.4 3.3 %collective-permute-start.9 = (bf16[896,256]{1,0:T(8,128)(2,1)S(1)}, bf16[896,256]{1,0:T(8,128)(2,1)S(1)}, u32[]{:S(2)}, u32[]{:S(2)}) collective-permute-start(bf16[896,256]{1,0:T(8,128)(2,1)S(1)} %get-tuple-element.50), channel_id=1, source_target_pairs={{0,4},{1,5},{2,6},{3,7},{4,0},{5,1},{6,2},{7,3},{8,12},{9,13},{10,... | collective-permute-start | bytes 1376264 | tf_op jit(solution)/shard_map/ppermute | solution.py:383
  56.7 6.0 %shard_map.61 = (f32[1024,256]{1,0:T(8,128)S(1)}, f32[2,256]{1,0:T(2,128)S(1)}, bf16[6912,256]{1,0:T(8,128)(2,1)S(1)}) custom-call(s32[4]{0:T(128)S(1)} %pad_add_fusion.where, f32[2,256]{1,0:T(2,128)S(1)} %get-tuple-element.37.refs_0_.stats, bf16[2,1024,256]{2,1,0:T(8,128)(2,1)S(1)} %bitcast.14, bf16[3,2,1152,256]{3,2,1,0:T(8,128)(2,1)S(1)} %shard_map.54.near, ...), custom_call_target="tpu_custom_call" | custom-call | flops 3623878656 | tf_op jit(solution)/shard_map/pallas_call | solution.py:360
  64.4 5.4 %shard_map.63 = (f32[1024,256]{1,0:T(8,128)S(1)}, f32[2,256]{1,0:T(2,128)S(1)}) custom-call(f32[2,256]{1,0:T(2,128)S(1)} %get-tuple-element.37.refs_0_.stats, bf16[2,1024,256]{2,1,0:T(8,128)(2,1)S(1)} %bitcast.15, bf16[3,2,1152,256]{3,2,1,0:T(8,128)(2,1)S(1)} %shard_map.54.near, bf16[3,1,1152,256]{3,2,1,0:T(8,128)(2,1)S(1)} %shard_map.56.after, ...), custom_call_target="tpu_custom_call" | custom-call | flops 3623878656 | tf_op jit(solution)/shard_map/pallas_call | solution.py:360
  69.7 3.6 %collective-permute-done.7.a0 = bf16[896,256]{1,0:T(8,128)(2,1)S(1)} collective-permute-done((bf16[896,256]{1,0:T(8,128)(2,1)S(1)}, bf16[896,256]{1,0:T(8,128)(2,1)S(1)}, u32[]{:S(2)}, u32[]{:S(2)}) %collective-permute-start.7) | collective-permute-done | bytes 458784 | tf_op jit(solution)/shard_map/ppermute | solution.py:383
  73.4 3.4 %collective-permute-done.9.a2 = bf16[896,256]{1,0:T(8,128)(2,1)S(1)} collective-permute-done((bf16[896,256]{1,0:T(8,128)(2,1)S(1)}, bf16[896,256]{1,0:T(8,128)(2,1)S(1)}, u32[]{:S(2)}, u32[]{:S(2)}) %collective-permute-start.9) | collective-permute-done | bytes 458784 | tf_op jit(solution)/shard_map/ppermute | solution.py:383
  77.6 4.3 %collective-permute-start.12 = (bf16[240,256]{1,0:T(8,128)(2,1)S(1)}, bf16[240,256]{1,0:T(8,128)(2,1)S(1)}, u32[]{:S(2)}, u32[]{:S(2)}) collective-permute-start(bf16[240,256]{1,0:T(8,128)(2,1)S(1)} %get-tuple-element.57), channel_id=1, source_target_pairs={{0,32},{8,40},{16,48},{24,56},{32,64},{40,72},{48,80},{56,88},{64,... | collective-permute-start | bytes 368648 | tf_op jit(solution)/shard_map/ppermute | solution.py:383
  81.9 2.6 %collective-permute-start.14 = (bf16[240,256]{1,0:T(8,128)(2,1)S(1)}, bf16[240,256]{1,0:T(8,128)(2,1)S(1)}, u32[]{:S(2)}, u32[]{:S(2)}) collective-permute-start(bf16[240,256]{1,0:T(8,128)(2,1)S(1)} %get-tuple-element.59), channel_id=1, source_target_pairs={{0,64},{8,72},{16,80},{24,88},{32,96},{40,104},{48,112},{56,120},{... | collective-permute-start | bytes 368648 | tf_op jit(solution)/shard_map/ppermute | solution.py:383
  89.6 2.4 %collective-permute-start.16 = (bf16[240,256]{1,0:T(8,128)(2,1)S(1)}, bf16[240,256]{1,0:T(8,128)(2,1)S(1)}, u32[]{:S(2)}, u32[]{:S(2)}) collective-permute-start(bf16[240,256]{1,0:T(8,128)(2,1)S(1)} %get-tuple-element.60.own), channel_id=1, source_target_pairs={{0,24},{8,0},{16,8},{24,16},{32,56},{40,32},{48,40},{56,48},{64,88... | collective-permute-start | bytes 368648 | tf_op jit(solution)/shard_map/ppermute | solution.py:383
  92.0 3.9 %collective-permute-done.17.a2 = bf16[240,256]{1,0:T(8,128)(2,1)S(1)} collective-permute-done((bf16[240,256]{1,0:T(8,128)(2,1)S(1)}, bf16[240,256]{1,0:T(8,128)(2,1)S(1)}, u32[]{:S(2)}, u32[]{:S(2)}) %collective-permute-start.17) | collective-permute-done | bytes 122912 | tf_op jit(solution)/shard_map/ppermute | solution.py:383
  96.0 2.1 %collective-permute-done.15.a0 = bf16[240,256]{1,0:T(8,128)(2,1)S(1)} collective-permute-done((bf16[240,256]{1,0:T(8,128)(2,1)S(1)}, bf16[240,256]{1,0:T(8,128)(2,1)S(1)}, u32[]{:S(2)}, u32[]{:S(2)}) %collective-permute-start.15) | collective-permute-done | bytes 122912 | tf_op jit(solution)/shard_map/ppermute | solution.py:383
  98.2 2.5 %collective-permute-start.20 = (bf16[224,256]{1,0:T(8,128)(2,1)S(1)}, bf16[224,256]{1,0:T(8,128)(2,1)S(1)}, u32[]{:S(2)}, u32[]{:S(2)}) collective-permute-start(bf16[224,256]{1,0:T(8,128)(2,1)S(1)} %get-tuple-element.65.own), channel_id=1, source_target_pairs={{0,64},{8,72},{16,80},{24,88},{32,96},{40,104},{48,112},{56,120},{... | collective-permute-start | bytes 344072 | tf_op jit(solution)/shard_map/ppermute | solution.py:383
  100.7 2.0 %collective-permute-start.19 = (bf16[224,256]{1,0:T(8,128)(2,1)S(1)}, bf16[224,256]{1,0:T(8,128)(2,1)S(1)}, u32[]{:S(2)}, u32[]{:S(2)}) collective-permute-start(bf16[224,256]{1,0:T(8,128)(2,1)S(1)} %get-tuple-element.65.own), channel_id=1, source_target_pairs={{0,96},{8,104},{16,112},{24,120},{32,0},{40,8},{48,16},{56,24},{64... | collective-permute-start | bytes 344072 | tf_op jit(solution)/shard_map/ppermute | solution.py:383
  102.8 2.1 %shard_map.67 = bf16[2,1024,256]{2,1,0:T(8,128)(2,1)} custom-call(f32[2,256]{1,0:T(2,128)S(1)} %get-tuple-element.37.refs_0_.stats, f32[2,256]{1,0:T(2,128)S(1)} %get-tuple-element.62.sums, bf16[2,1024,256]{2,1,0:T(8,128)(2,1)S(1)} %bitcast.16, bf16[2,1024,256]{2,1,0:T(8,128)(2,1)S(1)} %bitcast.11, f32[1024,256]{1,0:T(8,128)S(1)} %get-tuple-element.63.grad0, ...), custom_call_target="tpu_custom_call" | custom-call | bytes 8000000 | tf_op jit(solution)/shard_map/pallas_call | solution.py:360
  105.7 3.1 %collective-permute-done.18.a0 = bf16[224,256]{1,0:T(8,128)(2,1)S(1)} collective-permute-done((bf16[224,256]{1,0:T(8,128)(2,1)S(1)}, bf16[224,256]{1,0:T(8,128)(2,1)S(1)}, u32[]{:S(2)}, u32[]{:S(2)}) %collective-permute-start.18) | collective-permute-done | bytes 114720 | tf_op jit(solution)/shard_map/ppermute | solution.py:383
  (56 shorter events, 23.6 us)
Async XLA Ops:
  0.6 32.6 %copy-start.1 = (bf16[1,2,16,64,256]{4,3,2,1,0:T(8,128)(2,1)S(1)}, bf16[1,2,16,64,256]{4,3,2,1,0:T(8,128)(2,1)}, u32[]{:S(2)}) copy-start(bf16[1,2,16,64,256]{4,3,2,1,0:T(8,128)(2,1)} %param.4) | copy-start | bytes 3145732
  0.6 38.2 %collective-permute-start.2 = (bf16[864,256]{1,0:T(8,128)(2,1)}, bf16[864,256]{1,0:T(8,128)(2,1)S(1)}, u32[]{:S(2)}, u32[]{:S(2)}) collective-permute-start(bf16[864,256]{1,0:T(8,128)(2,1)} %own.1), channel_id=1, source_target_pairs={{0,6},{1,7},{2,0},{3,1},{4,2},{5,3},{6,4},{7,5},{8,14},{9,15},{10,... | collective-permute-start | bytes 1327112 | tf_op jit(solution)/shard_map/ppermute | solution.py:383
  1.5 37.3 %collective-permute-start.1 = (bf16[864,256]{1,0:T(8,128)(2,1)}, bf16[864,256]{1,0:T(8,128)(2,1)S(1)}, u32[]{:S(2)}, u32[]{:S(2)}) collective-permute-start(bf16[864,256]{1,0:T(8,128)(2,1)} %own.1), channel_id=1, source_target_pairs={{0,2},{1,3},{2,4},{3,5},{4,6},{5,7},{6,0},{7,1},{8,10},{9,11},{10,... | collective-permute-start | bytes 1327112 | tf_op jit(solution)/shard_map/ppermute | solution.py:383
  3.9 34.9 %collective-permute-start.3 = (bf16[864,256]{1,0:T(8,128)(2,1)}, bf16[864,256]{1,0:T(8,128)(2,1)S(1)}, u32[]{:S(2)}, u32[]{:S(2)}) collective-permute-start(bf16[864,256]{1,0:T(8,128)(2,1)} %own.1), channel_id=1, source_target_pairs={{0,4},{1,5},{2,6},{3,7},{4,0},{5,1},{6,2},{7,3},{8,12},{9,13},{10,... | collective-permute-start | bytes 1327112 | tf_op jit(solution)/shard_map/ppermute | solution.py:383
  6.4 10.6 %all-to-all-start = ((f32[4,2,256]{2,1,0:T(2,128)}), f32[4,2,256]{2,1,0:T(2,128)S(1)}, u32[]{:S(2)}, u32[]{:S(2)}) async-start(f32[4,2,256]{2,1,0:T(2,128)} %get-tuple-element.34.order), calls=%async_computation | async-start | bytes 16384 | tf_op jit(solution)/shard_map/all_to_all | solution.py:414
  17.6 9.8 %all-to-all-start.1 = ((f32[4,2,256]{2,1,0:T(2,128)}), f32[4,2,256]{2,1,0:T(2,128)S(1)}, u32[]{:S(2)}, u32[]{:S(2)}) async-start(f32[4,2,256]{2,1,0:T(2,128)} %shard_map.51), calls=%async_computation.1 | async-start | bytes 16384 | tf_op jit(solution)/shard_map/all_to_all | solution.py:416
  27.4 12.3 %collective-permute-start = (bf16[1024,256]{1,0:T(8,128)(2,1)S(1)}, bf16[1024,256]{1,0:T(8,128)(2,1)S(1)}, u32[]{:S(2)}, u32[]{:S(2)}) collective-permute-start(bf16[1024,256]{1,0:T(8,128)(2,1)S(1)} %get-tuple-element.39), channel_id=1, source_target_pairs={{8,0},{16,8},{24,16},{32,24},{40,32},{48,40},{56,48},{64,56},{72,6... | collective-permute-start | bytes 1572872 | tf_op jit(solution)/shard_map/ppermute | solution.py:393
  28.7 13.9 %collective-permute-start.5 = (bf16[1024,256]{1,0:T(8,128)(2,1)S(1)}, bf16[1024,256]{1,0:T(8,128)(2,1)S(1)}, u32[]{:S(2)}, u32[]{:S(2)}) collective-permute-start(bf16[1024,256]{1,0:T(8,128)(2,1)S(1)} %get-tuple-element.44), channel_id=1, source_target_pairs={{0,8},{8,16},{16,24},{24,32},{32,40},{40,48},{48,56},{56,64},{64,7... | collective-permute-start | bytes 1572872 | tf_op jit(solution)/shard_map/ppermute | solution.py:393
  39.6 17.1 %collective-permute-start.10 = (bf16[4,864,256]{2,1,0:T(8,128)(2,1)S(1)}, bf16[4,864,256]{2,1,0:T(8,128)(2,1)S(1)}, u32[]{:S(2)}, u32[]{:S(2)}) collective-permute-start(bf16[4,864,256]{2,1,0:T(8,128)(2,1)S(1)} %shard_map.57.order.mine), channel_id=1, source_target_pairs={{0,1},{1,0},{2,3},{3,2},{4,5},{5,4},{6,7},{7,6},{8,9},{9,8},{10,11... | collective-permute-start | bytes 5308424 | tf_op jit(solution)/shard_map/ppermute | solution.py:388
  42.0 7.2 %collective-permute-start.4 = (bf16[1824,256]{1,0:T(8,128)(2,1)S(1)}, bf16[1824,256]{1,0:T(8,128)(2,1)S(1)}, u32[]{:S(2)}, u32[]{:S(2)}) collective-permute-start(bf16[1824,256]{1,0:T(8,128)(2,1)S(1)} %get-tuple-element.43.order), channel_id=1, source_target_pairs={{0,1},{1,0},{2,3},{3,2},{4,5},{5,4},{6,7},{7,6},{8,9},{9,8},{10,11... | collective-permute-start | bytes 2801672 | tf_op jit(solution)/shard_map/ppermute | solution.py:388
  47.8 2.6 %collective-permute-start.6 = (bf16[1824,256]{1,0:T(8,128)(2,1)S(1)}, bf16[1824,256]{1,0:T(8,128)(2,1)S(1)}, u32[]{:S(2)}, u32[]{:S(2)}) collective-permute-start(bf16[1824,256]{1,0:T(8,128)(2,1)S(1)} %get-tuple-element.46), channel_id=1, source_target_pairs={{0,1},{1,0},{2,3},{3,2},{4,5},{5,4},{6,7},{7,6},{8,9},{9,8},{10,11... | collective-permute-start | bytes 2801672 | tf_op jit(solution)/shard_map/ppermute | solution.py:388
  47.9 16.2 %collective-permute-start.11 = (bf16[1024,256]{1,0:T(8,128)(2,1)S(1)}, bf16[1024,256]{1,0:T(8,128)(2,1)S(1)}, u32[]{:S(2)}, u32[]{:S(2)}) collective-permute-start(bf16[1024,256]{1,0:T(8,128)(2,1)S(1)} %copy-done.6), channel_id=1, source_target_pairs={{8,0},{16,8},{24,16},{32,24},{40,32},{48,40},{56,48},{64,56},{72,6... | collective-permute-start | bytes 1572872 | tf_op jit(solution)/shard_map/ppermute | solution.py:393
  51.2 22.1 %collective-permute-start.7 = (bf16[896,256]{1,0:T(8,128)(2,1)S(1)}, bf16[896,256]{1,0:T(8,128)(2,1)S(1)}, u32[]{:S(2)}, u32[]{:S(2)}) collective-permute-start(bf16[896,256]{1,0:T(8,128)(2,1)S(1)} %get-tuple-element.48), channel_id=1, source_target_pairs={{0,2},{1,3},{2,4},{3,5},{4,6},{5,7},{6,0},{7,1},{8,10},{9,11},{10,... | collective-permute-start | bytes 1376264 | tf_op jit(solution)/shard_map/ppermute | solution.py:383
  53.4 19.9 %collective-permute-start.8 = (bf16[896,256]{1,0:T(8,128)(2,1)S(1)}, bf16[896,256]{1,0:T(8,128)(2,1)S(1)}, u32[]{:S(2)}, u32[]{:S(2)}) collective-permute-start(bf16[896,256]{1,0:T(8,128)(2,1)S(1)} %get-tuple-element.49), channel_id=1, source_target_pairs={{0,6},{1,7},{2,0},{3,1},{4,2},{5,3},{6,4},{7,5},{8,14},{9,15},{10,... | collective-permute-start | bytes 1376264 | tf_op jit(solution)/shard_map/ppermute | solution.py:383
  53.4 23.3 %collective-permute-start.9 = (bf16[896,256]{1,0:T(8,128)(2,1)S(1)}, bf16[896,256]{1,0:T(8,128)(2,1)S(1)}, u32[]{:S(2)}, u32[]{:S(2)}) collective-permute-start(bf16[896,256]{1,0:T(8,128)(2,1)S(1)} %get-tuple-element.50), channel_id=1, source_target_pairs={{0,4},{1,5},{2,6},{3,7},{4,0},{5,1},{6,2},{7,3},{8,12},{9,13},{10,... | collective-permute-start | bytes 1376264 | tf_op jit(solution)/shard_map/ppermute | solution.py:383
  77.6 7.9 %collective-permute-start.12 = (bf16[240,256]{1,0:T(8,128)(2,1)S(1)}, bf16[240,256]{1,0:T(8,128)(2,1)S(1)}, u32[]{:S(2)}, u32[]{:S(2)}) collective-permute-start(bf16[240,256]{1,0:T(8,128)(2,1)S(1)} %get-tuple-element.57), channel_id=1, source_target_pairs={{0,32},{8,40},{16,48},{24,56},{32,64},{40,72},{48,80},{56,88},{64,... | collective-permute-start | bytes 368648 | tf_op jit(solution)/shard_map/ppermute | solution.py:383
  81.9 5.3 %collective-permute-start.13 = (bf16[240,256]{1,0:T(8,128)(2,1)S(1)}, bf16[240,256]{1,0:T(8,128)(2,1)S(1)}, u32[]{:S(2)}, u32[]{:S(2)}) collective-permute-start(bf16[240,256]{1,0:T(8,128)(2,1)S(1)} %get-tuple-element.58), channel_id=1, source_target_pairs={{0,96},{8,104},{16,112},{24,120},{32,0},{40,8},{48,16},{56,24},{64... | collective-permute-start | bytes 368648 | tf_op jit(solution)/shard_map/ppermute | solution.py:383
  81.9 6.6 %collective-permute-start.14 = (bf16[240,256]{1,0:T(8,128)(2,1)S(1)}, bf16[240,256]{1,0:T(8,128)(2,1)S(1)}, u32[]{:S(2)}, u32[]{:S(2)}) collective-permute-start(bf16[240,256]{1,0:T(8,128)(2,1)S(1)} %get-tuple-element.59), channel_id=1, source_target_pairs={{0,64},{8,72},{16,80},{24,88},{32,96},{40,104},{48,112},{56,120},{... | collective-permute-start | bytes 368648 | tf_op jit(solution)/shard_map/ppermute | solution.py:383
  88.7 7.3 %collective-permute-start.17 = (bf16[240,256]{1,0:T(8,128)(2,1)S(1)}, bf16[240,256]{1,0:T(8,128)(2,1)S(1)}, u32[]{:S(2)}, u32[]{:S(2)}) collective-permute-start(bf16[240,256]{1,0:T(8,128)(2,1)S(1)} %get-tuple-element.60.own), channel_id=1, source_target_pairs={{0,16},{8,24},{16,0},{24,8},{32,48},{40,56},{48,32},{56,40},{64,80... | collective-permute-start | bytes 368648 | tf_op jit(solution)/shard_map/ppermute | solution.py:383
  89.6 6.4 %collective-permute-start.16 = (bf16[240,256]{1,0:T(8,128)(2,1)S(1)}, bf16[240,256]{1,0:T(8,128)(2,1)S(1)}, u32[]{:S(2)}, u32[]{:S(2)}) collective-permute-start(bf16[240,256]{1,0:T(8,128)(2,1)S(1)} %get-tuple-element.60.own), channel_id=1, source_target_pairs={{0,24},{8,0},{16,8},{24,16},{32,56},{40,32},{48,40},{56,48},{64,88... | collective-permute-start | bytes 368648 | tf_op jit(solution)/shard_map/ppermute | solution.py:383
  92.0 6.1 %collective-permute-start.15 = (bf16[240,256]{1,0:T(8,128)(2,1)S(1)}, bf16[240,256]{1,0:T(8,128)(2,1)S(1)}, u32[]{:S(2)}, u32[]{:S(2)}) collective-permute-start(bf16[240,256]{1,0:T(8,128)(2,1)S(1)} %get-tuple-element.60.own), channel_id=1, source_target_pairs={{0,8},{8,16},{16,24},{24,0},{32,40},{40,48},{48,56},{56,32},{64,72... | collective-permute-start | bytes 368648 | tf_op jit(solution)/shard_map/ppermute | solution.py:383
  98.2 6.7 %collective-permute-start.20 = (bf16[224,256]{1,0:T(8,128)(2,1)S(1)}, bf16[224,256]{1,0:T(8,128)(2,1)S(1)}, u32[]{:S(2)}, u32[]{:S(2)}) collective-permute-start(bf16[224,256]{1,0:T(8,128)(2,1)S(1)} %get-tuple-element.65.own), channel_id=1, source_target_pairs={{0,64},{8,72},{16,80},{24,88},{32,96},{40,104},{48,112},{56,120},{... | collective-permute-start | bytes 344072 | tf_op jit(solution)/shard_map/ppermute | solution.py:383
  100.7 4.9 %collective-permute-start.19 = (bf16[224,256]{1,0:T(8,128)(2,1)S(1)}, bf16[224,256]{1,0:T(8,128)(2,1)S(1)}, u32[]{:S(2)}, u32[]{:S(2)}) collective-permute-start(bf16[224,256]{1,0:T(8,128)(2,1)S(1)} %get-tuple-element.65.own), channel_id=1, source_target_pairs={{0,96},{8,104},{16,112},{24,120},{32,0},{40,8},{48,16},{56,24},{64... | collective-permute-start | bytes 344072 | tf_op jit(solution)/shard_map/ppermute | solution.py:383
  102.8 6.0 %collective-permute-start.18 = (bf16[224,256]{1,0:T(8,128)(2,1)S(1)}, bf16[224,256]{1,0:T(8,128)(2,1)S(1)}, u32[]{:S(2)}, u32[]{:S(2)}) collective-permute-start(bf16[224,256]{1,0:T(8,128)(2,1)S(1)} %get-tuple-element.65.own), channel_id=1, source_target_pairs={{0,32},{8,40},{16,48},{24,56},{32,64},{40,72},{48,80},{56,88},{64,... | collective-permute-start | bytes 344072 | tf_op jit(solution)/shard_map/ppermute | solution.py:383
  (6 other events, 14.8 us)

commit v11 on v9

--- a/solution.py
+++ b/solution.py
@@ -89,7 +89,7 @@
         widths(wide, lambda r, t=t: cot[t, pl.ds(r, W)], t)
 
 
-def total_kernel(parts, held0, held1, out, pass0, pass1):
+def total_kernel(parts, held, out, passed_on):
     total = parts[0]
     for i in range(1, 16):
         total = total + parts[i]
@@ -407,13 +407,8 @@
     sums, last = call(first_kernel, (S((16, 2, C), f32), frame), (clip,))
     first, second = call(copy_kernel, (frame, frame), (cot,), order=(sums,))
     parts = lax.all_to_all(sums, "tm", 0, 0, tiled=True)
-    stats, first, last = call(
-        total_kernel,
-        (S((2, C), f32), frame, frame),
-        (parts,),
-        order=(first, last),
-        aliases={1: 1, 2: 2},
-        passed_out=2,
+    stats, last = call(
+        total_kernel, (S((2, C), f32), frame), (parts,), order=(last,), aliases={1: 1}, passed_out=1
     )
     near = call(widths_kernel, S((3, 2, PADDED, C), bf16), (cot,), order=(stats,))
     after = call(widths_kernel, S((3, 1, PADDED, C), bf16), (passed(first, -1)[None],))

time: 106 us -> 105 us (level)
  waiting for transfers between devices: 31 us -> 27.9 us
  local copies, waits for them, and re-layouts: 2.68 us -> 3.91 us
    all_to_all x1, waiting for transfers between devices: 6.66 us -> 3.37 us  [per_device(): parts = lax.all_to_all(sums, 'tm', 0, 0, tiled=True)]
    ppermute x3, starting transfers between devices: 7.15 us -> 5.16 us  [passed(): return lax.ppermute(block, 'tm', route)]
    ppermute x15, starting transfers between devices: 24.2 us -> 26 us  [ring(): got.append(lax.ppermute(block, name, route))]
    unnamed x12 -> x14, local copies, waits for them, and re-layouts: 2.68 us -> 3.91 us
  transfers between devices with their start and end apart: 22 -> 22, of which waited for: 13 -> 14; matrix products, arithmetic and copies ran while one was open for 0% -> 0% of each run, Pallas kernels for 27% -> 28%
where the time goes in v11:
time: 105 us
  starting transfers between devices  39.9 us (38%)
  Pallas kernels  32.2 us (31%)
  waiting for transfers between devices  27.9 us (27%)
  local copies, waits for them, and re-layouts  3.91 us (4%)
    pallas_call x18, Pallas kernels, call(): pl.pallas_call(kernel, out_shape=out_shape, in_specs=specs, out_specs=out...  32.2 us
    ppermute x15, starting transfers between devices, ring(): got.append(lax.ppermute(block, name, route))  26 us
    ppermute x15, waiting for transfers between devices, ring(): got.append(lax.ppermute(block, name, route))  21.5 us
    all_to_all x1, starting transfers between devices, per_device(): parts = lax.all_to_all(sums, 'tm', 0, 0, tiled=True)  8.05 us
    ppermute x3, starting transfers between devices, passed(): return lax.ppermute(block, 'tm', route)  5.16 us
    unnamed x14, local copies, waits for them, and re-layouts  3.91 us
    all_to_all x1, waiting for transfers between devices, per_device(): parts = lax.all_to_all(sums, 'tm', 0, 0, tiled=True)  3.37 us
    ppermute x3, waiting for transfers between devices, passed(): return lax.ppermute(block, 'tm', route)  2.29 us
  transfers between devices with their start and end apart: 22, of which 14 were waited for; matrix products, arithmetic and copies ran while one was open for 0% of the time, Pallas kernels for 28%

profile of v11, /device:TPU:6, one launch (start us, length us, event | category | flops | bytes accessed | tf_op | source)
XLA Modules:
  0.0 104.9 jit_solution(11585074264571796227)
XLA Ops:
  1.5 2.4 %collective-permute-start.1 = (bf16[864,256]{1,0:T(8,128)(2,1)}, bf16[864,256]{1,0:T(8,128)(2,1)S(1)}, u32[]{:S(2)}, u32[]{:S(2)}) collective-permute-start(bf16[864,256]{1,0:T(8,128)(2,1)} %own.1), channel_id=1, source_target_pairs={{0,2},{1,3},{2,4},{3,5},{4,6},{5,7},{6,0},{7,1},{8,10},{9,11},{10,... | collective-permute-start | bytes 1327112 | tf_op jit(solution)/shard_map/ppermute | solution.py:380
  6.4 8.0 %all-to-all-start = ((f32[16,2,256]{2,1,0:T(2,128)}), f32[16,2,256]{2,1,0:T(2,128)S(1)}, u32[]{:S(2)}, u32[]{:S(2)}) async-start(f32[16,2,256]{2,1,0:T(2,128)} %get-tuple-element.33.order), calls=%async_computation | async-start | bytes 65536 | tf_op jit(solution)/shard_map/all_to_all | solution.py:409
  18.7 3.4 %all-to-all-done.parts = f32[16,2,256]{2,1,0:T(2,128)S(1)} async-done(((f32[16,2,256]{2,1,0:T(2,128)}), f32[16,2,256]{2,1,0:T(2,128)S(1)}, u32[]{:S(2)}, u32[]{:S(2)}) %all-to-all-start) | async-done | bytes 32800 | tf_op jit(solution)/shard_map/all_to_all | solution.py:409
  22.1 2.6 %collective-permute-start.5 = (bf16[1024,256]{1,0:T(8,128)(2,1)S(1)}, bf16[1024,256]{1,0:T(8,128)(2,1)S(1)}, u32[]{:S(2)}, u32[]{:S(2)}) collective-permute-start(bf16[1024,256]{1,0:T(8,128)(2,1)S(1)} %get-tuple-element.42), channel_id=1, source_target_pairs={{0,8},{8,16},{16,24},{24,32},{32,40},{40,48},{48,56},{56,64},{64,7... | collective-permute-start | bytes 1572872 | tf_op jit(solution)/shard_map/ppermute | solution.py:390
  25.9 4.3 %shard_map.53 = (bf16[2,1024,256]{2,1,0:T(8,128)(2,1)S(1)}, f32[1824,256]{1,0:T(8,128)S(1)}, bf16[1824,256]{1,0:T(8,128)(2,1)S(1)}) custom-call(s32[4]{0:T(128)S(1)} %pad_add_fusion.where, f32[2,256]{1,0:T(2,128)S(1)} %get-tuple-element.35.refs_0_.stats, bf16[2,1024,256]{2,1,0:T(8,128)(2,1)S(1)} %bitcast.13, bf16[3,2,1152,256]{3,2,1,0:T(8,128)(2,1)S(1)} %shard_map.52.near), custom_call_target="tpu_custom_call" | custom-call | flops 2415919104 | tf_op jit(solution)/shard_map/pallas_call | solution.py:357
  32.3 2.0 %shard_map.57 = (f32[1824,256]{1,0:T(8,128)S(1)}, bf16[1824,256]{1,0:T(8,128)(2,1)S(1)}) custom-call(s32[4]{0:T(128)S(1)} %pad_add_fusion.where, bf16[2,1024,256]{2,1,0:T(8,128)(2,1)S(1)} %get-tuple-element.36.order.act, bf16[3,2,1152,256]{3,2,1,0:T(8,128)(2,1)S(1)} %shard_map.52.near, ...), custom_call_target="tpu_custom_call", output_to_operand_aliasing={{0}: (4, {}), {1}: (5, {})} | custom-call | flops 1207959552 | tf_op jit(solution)/shard_map/pallas_call | solution.py:357
  34.5 5.2 %shard_map.58 = (f32[1824,256]{1,0:T(8,128)S(1)}, bf16[1824,256]{1,0:T(8,128)(2,1)S(1)}) custom-call(s32[4]{0:T(128)S(1)} %pad_add_fusion.where, f32[2,256]{1,0:T(2,128)S(1)} %get-tuple-element.35.refs_0_.stats, bf16[2,1024,256]{2,1,0:T(8,128)(2,1)S(1)} %get-tuple-element.36.order.act, bf16[1024,256]{1,0:T(8,128)(2,1)S(1)} %collective-permute-done.5.before, ...), custom_call_target="tpu_custom_call" | custom-call | flops 3623878656 | tf_op jit(solution)/shard_map/pallas_call | solution.py:357
  43.3 2.1 %collective-permute-start.7 = (bf16[896,256]{1,0:T(8,128)(2,1)S(1)}, bf16[896,256]{1,0:T(8,128)(2,1)S(1)}, u32[]{:S(2)}, u32[]{:S(2)}) collective-permute-start(bf16[896,256]{1,0:T(8,128)(2,1)S(1)} %get-tuple-element.46), channel_id=1, source_target_pairs={{0,2},{1,3},{2,4},{3,5},{4,6},{5,7},{6,0},{7,1},{8,10},{9,11},{10,... | collective-permute-start | bytes 1376264 | tf_op jit(solution)/shard_map/ppermute | solution.py:380
  45.4 3.2 %collective-permute-start.9 = (bf16[896,256]{1,0:T(8,128)(2,1)S(1)}, bf16[896,256]{1,0:T(8,128)(2,1)S(1)}, u32[]{:S(2)}, u32[]{:S(2)}) collective-permute-start(bf16[896,256]{1,0:T(8,128)(2,1)S(1)} %get-tuple-element.48), channel_id=1, source_target_pairs={{0,4},{1,5},{2,6},{3,7},{4,0},{5,1},{6,2},{7,3},{8,12},{9,13},{10,... | collective-permute-start | bytes 1376264 | tf_op jit(solution)/shard_map/ppermute | solution.py:380
  48.6 6.1 %shard_map.60 = (f32[1024,256]{1,0:T(8,128)S(1)}, f32[2,256]{1,0:T(2,128)S(1)}, bf16[6912,256]{1,0:T(8,128)(2,1)S(1)}) custom-call(s32[4]{0:T(128)S(1)} %pad_add_fusion.where, f32[2,256]{1,0:T(2,128)S(1)} %get-tuple-element.35.refs_0_.stats, bf16[2,1024,256]{2,1,0:T(8,128)(2,1)S(1)} %bitcast.14, bf16[3,2,1152,256]{3,2,1,0:T(8,128)(2,1)S(1)} %shard_map.52.near, ...), custom_call_target="tpu_custom_call" | custom-call | flops 3623878656 | tf_op jit(solution)/shard_map/pallas_call | solution.py:357
  56.3 5.4 %shard_map.62 = (f32[1024,256]{1,0:T(8,128)S(1)}, f32[2,256]{1,0:T(2,128)S(1)}) custom-call(f32[2,256]{1,0:T(2,128)S(1)} %get-tuple-element.35.refs_0_.stats, bf16[2,1024,256]{2,1,0:T(8,128)(2,1)S(1)} %bitcast.15, bf16[3,2,1152,256]{3,2,1,0:T(8,128)(2,1)S(1)} %shard_map.52.near, bf16[3,1,1152,256]{3,2,1,0:T(8,128)(2,1)S(1)} %shard_map.55.after, ...), custom_call_target="tpu_custom_call" | custom-call | flops 3623878656 | tf_op jit(solution)/shard_map/pallas_call | solution.py:357
  61.6 3.9 %collective-permute-done.7.a0 = bf16[896,256]{1,0:T(8,128)(2,1)S(1)} collective-permute-done((bf16[896,256]{1,0:T(8,128)(2,1)S(1)}, bf16[896,256]{1,0:T(8,128)(2,1)S(1)}, u32[]{:S(2)}, u32[]{:S(2)}) %collective-permute-start.7) | collective-permute-done | bytes 458784 | tf_op jit(solution)/shard_map/ppermute | solution.py:380
  65.5 3.4 %collective-permute-done.9.a2 = bf16[896,256]{1,0:T(8,128)(2,1)S(1)} collective-permute-done((bf16[896,256]{1,0:T(8,128)(2,1)S(1)}, bf16[896,256]{1,0:T(8,128)(2,1)S(1)}, u32[]{:S(2)}, u32[]{:S(2)}) %collective-permute-start.9) | collective-permute-done | bytes 458784 | tf_op jit(solution)/shard_map/ppermute | solution.py:380
  69.8 5.7 %collective-permute-start.12 = (bf16[240,256]{1,0:T(8,128)(2,1)S(1)}, bf16[240,256]{1,0:T(8,128)(2,1)S(1)}, u32[]{:S(2)}, u32[]{:S(2)}) collective-permute-start(bf16[240,256]{1,0:T(8,128)(2,1)S(1)} %get-tuple-element.55), channel_id=1, source_target_pairs={{0,32},{8,40},{16,48},{24,56},{32,64},{40,72},{48,80},{56,88},{64,... | collective-permute-start | bytes 368648 | tf_op jit(solution)/shard_map/ppermute | solution.py:380
  75.5 1.6 %collective-permute-start.13 = (bf16[240,256]{1,0:T(8,128)(2,1)S(1)}, bf16[240,256]{1,0:T(8,128)(2,1)S(1)}, u32[]{:S(2)}, u32[]{:S(2)}) collective-permute-start(bf16[240,256]{1,0:T(8,128)(2,1)S(1)} %get-tuple-element.56), channel_id=1, source_target_pairs={{0,96},{8,104},{16,112},{24,120},{32,0},{40,8},{48,16},{56,24},{64... | collective-permute-start | bytes 368648 | tf_op jit(solution)/shard_map/ppermute | solution.py:380
  77.1 1.9 %collective-permute-start.14 = (bf16[240,256]{1,0:T(8,128)(2,1)S(1)}, bf16[240,256]{1,0:T(8,128)(2,1)S(1)}, u32[]{:S(2)}, u32[]{:S(2)}) collective-permute-start(bf16[240,256]{1,0:T(8,128)(2,1)S(1)} %get-tuple-element.57), channel_id=1, source_target_pairs={{0,64},{8,72},{16,80},{24,88},{32,96},{40,104},{48,112},{56,120},{... | collective-permute-start | bytes 368648 | tf_op jit(solution)/shard_map/ppermute | solution.py:380
  79.0 1.7 %collective-permute-done.12.a0 = bf16[240,256]{1,0:T(8,128)(2,1)S(1)} collective-permute-done((bf16[240,256]{1,0:T(8,128)(2,1)S(1)}, bf16[240,256]{1,0:T(8,128)(2,1)S(1)}, u32[]{:S(2)}, u32[]{:S(2)}) %collective-permute-start.12) | collective-permute-done | bytes 122912 | tf_op jit(solution)/shard_map/ppermute | solution.py:380
  81.1 2.4 %collective-permute-done.14.a2 = bf16[240,256]{1,0:T(8,128)(2,1)S(1)} collective-permute-done((bf16[240,256]{1,0:T(8,128)(2,1)S(1)}, bf16[240,256]{1,0:T(8,128)(2,1)S(1)}, u32[]{:S(2)}, u32[]{:S(2)}) %collective-permute-start.14) | collective-permute-done | bytes 122912 | tf_op jit(solution)/shard_map/ppermute | solution.py:380
  83.7 4.2 %collective-permute-start.16 = (bf16[240,256]{1,0:T(8,128)(2,1)S(1)}, bf16[240,256]{1,0:T(8,128)(2,1)S(1)}, u32[]{:S(2)}, u32[]{:S(2)}) collective-permute-start(bf16[240,256]{1,0:T(8,128)(2,1)S(1)} %get-tuple-element.58.own), channel_id=1, source_target_pairs={{0,24},{8,0},{16,8},{24,16},{32,56},{40,32},{48,40},{56,48},{64,88... | collective-permute-start | bytes 368648 | tf_op jit(solution)/shard_map/ppermute | solution.py:380
  87.9 3.0 %collective-permute-done.17.a2 = bf16[240,256]{1,0:T(8,128)(2,1)S(1)} collective-permute-done((bf16[240,256]{1,0:T(8,128)(2,1)S(1)}, bf16[240,256]{1,0:T(8,128)(2,1)S(1)}, u32[]{:S(2)}, u32[]{:S(2)}) %collective-permute-start.17) | collective-permute-done | bytes 122912 | tf_op jit(solution)/shard_map/ppermute | solution.py:380
  90.8 3.1 %collective-permute-done.15.a0 = bf16[240,256]{1,0:T(8,128)(2,1)S(1)} collective-permute-done((bf16[240,256]{1,0:T(8,128)(2,1)S(1)}, bf16[240,256]{1,0:T(8,128)(2,1)S(1)}, u32[]{:S(2)}, u32[]{:S(2)}) %collective-permute-start.15) | collective-permute-done | bytes 122912 | tf_op jit(solution)/shard_map/ppermute | solution.py:380
  95.6 1.8 %collective-permute-start.19 = (bf16[224,256]{1,0:T(8,128)(2,1)S(1)}, bf16[224,256]{1,0:T(8,128)(2,1)S(1)}, u32[]{:S(2)}, u32[]{:S(2)}) collective-permute-start(bf16[224,256]{1,0:T(8,128)(2,1)S(1)} %get-tuple-element.63.own), channel_id=1, source_target_pairs={{0,96},{8,104},{16,112},{24,120},{32,0},{40,8},{48,16},{56,24},{64... | collective-permute-start | bytes 344072 | tf_op jit(solution)/shard_map/ppermute | solution.py:380
  97.7 2.1 %shard_map.66 = bf16[2,1024,256]{2,1,0:T(8,128)(2,1)} custom-call(f32[2,256]{1,0:T(2,128)S(1)} %get-tuple-element.35.refs_0_.stats, f32[2,256]{1,0:T(2,128)S(1)} %get-tuple-element.60.sums, bf16[2,1024,256]{2,1,0:T(8,128)(2,1)S(1)} %bitcast.16, bf16[2,1024,256]{2,1,0:T(8,128)(2,1)S(1)} %bitcast.11, f32[1024,256]{1,0:T(8,128)S(1)} %get-tuple-element.61.grad0, ...), custom_call_target="tpu_custom_call" | custom-call | bytes 8000000 | tf_op jit(solution)/shard_map/pallas_call | solution.py:357
  100.7 2.7 %collective-permute-done.18.a0 = bf16[224,256]{1,0:T(8,128)(2,1)S(1)} collective-permute-done((bf16[224,256]{1,0:T(8,128)(2,1)S(1)}, bf16[224,256]{1,0:T(8,128)(2,1)S(1)}, u32[]{:S(2)}, u32[]{:S(2)}) %collective-permute-start.18) | collective-permute-done | bytes 114720 | tf_op jit(solution)/shard_map/ppermute | solution.py:380
  (53 shorter events, 21.8 us)
Async XLA Ops:
  0.6 24.1 %copy-start.1 = (bf16[1,2,16,64,256]{4,3,2,1,0:T(8,128)(2,1)S(1)}, bf16[1,2,16,64,256]{4,3,2,1,0:T(8,128)(2,1)}, u32[]{:S(2)}) copy-start(bf16[1,2,16,64,256]{4,3,2,1,0:T(8,128)(2,1)} %param.4) | copy-start | bytes 3145732
  0.6 29.6 %collective-permute-start.2 = (bf16[864,256]{1,0:T(8,128)(2,1)}, bf16[864,256]{1,0:T(8,128)(2,1)S(1)}, u32[]{:S(2)}, u32[]{:S(2)}) collective-permute-start(bf16[864,256]{1,0:T(8,128)(2,1)} %own.1), channel_id=1, source_target_pairs={{0,6},{1,7},{2,0},{3,1},{4,2},{5,3},{6,4},{7,5},{8,14},{9,15},{10,... | collective-permute-start | bytes 1327112 | tf_op jit(solution)/shard_map/ppermute | solution.py:380
  1.5 28.7 %collective-permute-start.1 = (bf16[864,256]{1,0:T(8,128)(2,1)}, bf16[864,256]{1,0:T(8,128)(2,1)S(1)}, u32[]{:S(2)}, u32[]{:S(2)}) collective-permute-start(bf16[864,256]{1,0:T(8,128)(2,1)} %own.1), channel_id=1, source_target_pairs={{0,2},{1,3},{2,4},{3,5},{4,6},{5,7},{6,0},{7,1},{8,10},{9,11},{10,... | collective-permute-start | bytes 1327112 | tf_op jit(solution)/shard_map/ppermute | solution.py:380
  3.9 26.3 %collective-permute-start.3 = (bf16[864,256]{1,0:T(8,128)(2,1)}, bf16[864,256]{1,0:T(8,128)(2,1)S(1)}, u32[]{:S(2)}, u32[]{:S(2)}) collective-permute-start(bf16[864,256]{1,0:T(8,128)(2,1)} %own.1), channel_id=1, source_target_pairs={{0,4},{1,5},{2,6},{3,7},{4,0},{5,1},{6,2},{7,3},{8,12},{9,13},{10,... | collective-permute-start | bytes 1327112 | tf_op jit(solution)/shard_map/ppermute | solution.py:380
  6.4 15.7 %all-to-all-start = ((f32[16,2,256]{2,1,0:T(2,128)}), f32[16,2,256]{2,1,0:T(2,128)S(1)}, u32[]{:S(2)}, u32[]{:S(2)}) async-start(f32[16,2,256]{2,1,0:T(2,128)} %get-tuple-element.33.order), calls=%async_computation | async-start | bytes 65536 | tf_op jit(solution)/shard_map/all_to_all | solution.py:409
  17.3 14.7 %collective-permute-start = (bf16[1024,256]{1,0:T(8,128)(2,1)}, bf16[1024,256]{1,0:T(8,128)(2,1)S(1)}, u32[]{:S(2)}, u32[]{:S(2)}) collective-permute-start(bf16[1024,256]{1,0:T(8,128)(2,1)} %get-tuple-element.37), channel_id=1, source_target_pairs={{8,0},{16,8},{24,16},{32,24},{40,32},{48,40},{56,48},{64,56},{72,6... | collective-permute-start | bytes 1572872 | tf_op jit(solution)/shard_map/ppermute | solution.py:390
  22.1 12.4 %collective-permute-start.5 = (bf16[1024,256]{1,0:T(8,128)(2,1)S(1)}, bf16[1024,256]{1,0:T(8,128)(2,1)S(1)}, u32[]{:S(2)}, u32[]{:S(2)}) collective-permute-start(bf16[1024,256]{1,0:T(8,128)(2,1)S(1)} %get-tuple-element.42), channel_id=1, source_target_pairs={{0,8},{8,16},{16,24},{24,32},{32,40},{40,48},{48,56},{56,64},{64,7... | collective-permute-start | bytes 1572872 | tf_op jit(solution)/shard_map/ppermute | solution.py:390
  31.0 17.7 %collective-permute-start.10 = (bf16[4,864,256]{2,1,0:T(8,128)(2,1)S(1)}, bf16[4,864,256]{2,1,0:T(8,128)(2,1)S(1)}, u32[]{:S(2)}, u32[]{:S(2)}) collective-permute-start(bf16[4,864,256]{2,1,0:T(8,128)(2,1)S(1)} %shard_map.56.order.mine), channel_id=1, source_target_pairs={{0,1},{1,0},{2,3},{3,2},{4,5},{5,4},{6,7},{7,6},{8,9},{9,8},{10,11... | collective-permute-start | bytes 5308424 | tf_op jit(solution)/shard_map/ppermute | solution.py:385
  34.3 5.9 %copy-start.6 = (bf16[1024,256]{1,0:T(8,128)(2,1)S(1)}, bf16[1024,256]{1,0:T(8,128)(2,1)}, u32[]{:S(2)}) copy-start(bf16[1024,256]{1,0:T(8,128)(2,1)} %copy-done.5) | copy-start | bytes 1572868
  34.4 7.2 %collective-permute-start.4 = (bf16[1824,256]{1,0:T(8,128)(2,1)S(1)}, bf16[1824,256]{1,0:T(8,128)(2,1)S(1)}, u32[]{:S(2)}, u32[]{:S(2)}) collective-permute-start(bf16[1824,256]{1,0:T(8,128)(2,1)S(1)} %get-tuple-element.41.order), channel_id=1, source_target_pairs={{0,1},{1,0},{2,3},{3,2},{4,5},{5,4},{6,7},{7,6},{8,9},{9,8},{10,11... | collective-permute-start | bytes 2801672 | tf_op jit(solution)/shard_map/ppermute | solution.py:385
  39.7 2.7 %collective-permute-start.6 = (bf16[1824,256]{1,0:T(8,128)(2,1)S(1)}, bf16[1824,256]{1,0:T(8,128)(2,1)S(1)}, u32[]{:S(2)}, u32[]{:S(2)}) collective-permute-start(bf16[1824,256]{1,0:T(8,128)(2,1)S(1)} %get-tuple-element.44), channel_id=1, source_target_pairs={{0,1},{1,0},{2,3},{3,2},{4,5},{5,4},{6,7},{7,6},{8,9},{9,8},{10,11... | collective-permute-start | bytes 2801672 | tf_op jit(solution)/shard_map/ppermute | solution.py:385
  40.3 15.7 %collective-permute-start.11 = (bf16[1024,256]{1,0:T(8,128)(2,1)S(1)}, bf16[1024,256]{1,0:T(8,128)(2,1)S(1)}, u32[]{:S(2)}, u32[]{:S(2)}) collective-permute-start(bf16[1024,256]{1,0:T(8,128)(2,1)S(1)} %copy-done.6), channel_id=1, source_target_pairs={{8,0},{16,8},{24,16},{32,24},{40,32},{48,40},{56,48},{64,56},{72,6... | collective-permute-start | bytes 1572872 | tf_op jit(solution)/shard_map/ppermute | solution.py:390
  43.3 22.3 %collective-permute-start.7 = (bf16[896,256]{1,0:T(8,128)(2,1)S(1)}, bf16[896,256]{1,0:T(8,128)(2,1)S(1)}, u32[]{:S(2)}, u32[]{:S(2)}) collective-permute-start(bf16[896,256]{1,0:T(8,128)(2,1)S(1)} %get-tuple-element.46), channel_id=1, source_target_pairs={{0,2},{1,3},{2,4},{3,5},{4,6},{5,7},{6,0},{7,1},{8,10},{9,11},{10,... | collective-permute-start | bytes 1376264 | tf_op jit(solution)/shard_map/ppermute | solution.py:380
  45.4 20.2 %collective-permute-start.8 = (bf16[896,256]{1,0:T(8,128)(2,1)S(1)}, bf16[896,256]{1,0:T(8,128)(2,1)S(1)}, u32[]{:S(2)}, u32[]{:S(2)}) collective-permute-start(bf16[896,256]{1,0:T(8,128)(2,1)S(1)} %get-tuple-element.47), channel_id=1, source_target_pairs={{0,6},{1,7},{2,0},{3,1},{4,2},{5,3},{6,4},{7,5},{8,14},{9,15},{10,... | collective-permute-start | bytes 1376264 | tf_op jit(solution)/shard_map/ppermute | solution.py:380
  45.4 23.6 %collective-permute-start.9 = (bf16[896,256]{1,0:T(8,128)(2,1)S(1)}, bf16[896,256]{1,0:T(8,128)(2,1)S(1)}, u32[]{:S(2)}, u32[]{:S(2)}) collective-permute-start(bf16[896,256]{1,0:T(8,128)(2,1)S(1)} %get-tuple-element.48), channel_id=1, source_target_pairs={{0,4},{1,5},{2,6},{3,7},{4,0},{5,1},{6,2},{7,3},{8,12},{9,13},{10,... | collective-permute-start | bytes 1376264 | tf_op jit(solution)/shard_map/ppermute | solution.py:380
  69.8 10.9 %collective-permute-start.12 = (bf16[240,256]{1,0:T(8,128)(2,1)S(1)}, bf16[240,256]{1,0:T(8,128)(2,1)S(1)}, u32[]{:S(2)}, u32[]{:S(2)}) collective-permute-start(bf16[240,256]{1,0:T(8,128)(2,1)S(1)} %get-tuple-element.55), channel_id=1, source_target_pairs={{0,32},{8,40},{16,48},{24,56},{32,64},{40,72},{48,80},{56,88},{64,... | collective-permute-start | bytes 368648 | tf_op jit(solution)/shard_map/ppermute | solution.py:380
  75.5 5.6 %collective-permute-start.13 = (bf16[240,256]{1,0:T(8,128)(2,1)S(1)}, bf16[240,256]{1,0:T(8,128)(2,1)S(1)}, u32[]{:S(2)}, u32[]{:S(2)}) collective-permute-start(bf16[240,256]{1,0:T(8,128)(2,1)S(1)} %get-tuple-element.56), channel_id=1, source_target_pairs={{0,96},{8,104},{16,112},{24,120},{32,0},{40,8},{48,16},{56,24},{64... | collective-permute-start | bytes 368648 | tf_op jit(solution)/shard_map/ppermute | solution.py:380
  77.1 6.4 %collective-permute-start.14 = (bf16[240,256]{1,0:T(8,128)(2,1)S(1)}, bf16[240,256]{1,0:T(8,128)(2,1)S(1)}, u32[]{:S(2)}, u32[]{:S(2)}) collective-permute-start(bf16[240,256]{1,0:T(8,128)(2,1)S(1)} %get-tuple-element.57), channel_id=1, source_target_pairs={{0,64},{8,72},{16,80},{24,88},{32,96},{40,104},{48,112},{56,120},{... | collective-permute-start | bytes 368648 | tf_op jit(solution)/shard_map/ppermute | solution.py:380
  83.6 7.3 %collective-permute-start.17 = (bf16[240,256]{1,0:T(8,128)(2,1)S(1)}, bf16[240,256]{1,0:T(8,128)(2,1)S(1)}, u32[]{:S(2)}, u32[]{:S(2)}) collective-permute-start(bf16[240,256]{1,0:T(8,128)(2,1)S(1)} %get-tuple-element.58.own), channel_id=1, source_target_pairs={{0,16},{8,24},{16,0},{24,8},{32,48},{40,56},{48,32},{56,40},{64,80... | collective-permute-start | bytes 368648 | tf_op jit(solution)/shard_map/ppermute | solution.py:380
  83.7 7.2 %collective-permute-start.16 = (bf16[240,256]{1,0:T(8,128)(2,1)S(1)}, bf16[240,256]{1,0:T(8,128)(2,1)S(1)}, u32[]{:S(2)}, u32[]{:S(2)}) collective-permute-start(bf16[240,256]{1,0:T(8,128)(2,1)S(1)} %get-tuple-element.58.own), channel_id=1, source_target_pairs={{0,24},{8,0},{16,8},{24,16},{32,56},{40,32},{48,40},{56,48},{64,88... | collective-permute-start | bytes 368648 | tf_op jit(solution)/shard_map/ppermute | solution.py:380
  87.9 6.1 %collective-permute-start.15 = (bf16[240,256]{1,0:T(8,128)(2,1)S(1)}, bf16[240,256]{1,0:T(8,128)(2,1)S(1)}, u32[]{:S(2)}, u32[]{:S(2)}) collective-permute-start(bf16[240,256]{1,0:T(8,128)(2,1)S(1)} %get-tuple-element.58.own), channel_id=1, source_target_pairs={{0,8},{8,16},{16,24},{24,0},{32,40},{40,48},{48,56},{56,32},{64,72... | collective-permute-start | bytes 368648 | tf_op jit(solution)/shard_map/ppermute | solution.py:380
  94.0 6.4 %collective-permute-start.20 = (bf16[224,256]{1,0:T(8,128)(2,1)S(1)}, bf16[224,256]{1,0:T(8,128)(2,1)S(1)}, u32[]{:S(2)}, u32[]{:S(2)}) collective-permute-start(bf16[224,256]{1,0:T(8,128)(2,1)S(1)} %get-tuple-element.63.own), channel_id=1, source_target_pairs={{0,64},{8,72},{16,80},{24,88},{32,96},{40,104},{48,112},{56,120},{... | collective-permute-start | bytes 344072 | tf_op jit(solution)/shard_map/ppermute | solution.py:380
  95.6 5.1 %collective-permute-start.19 = (bf16[224,256]{1,0:T(8,128)(2,1)S(1)}, bf16[224,256]{1,0:T(8,128)(2,1)S(1)}, u32[]{:S(2)}, u32[]{:S(2)}) collective-permute-start(bf16[224,256]{1,0:T(8,128)(2,1)S(1)} %get-tuple-element.63.own), channel_id=1, source_target_pairs={{0,96},{8,104},{16,112},{24,120},{32,0},{40,8},{48,16},{56,24},{64... | collective-permute-start | bytes 344072 | tf_op jit(solution)/shard_map/ppermute | solution.py:380
  97.4 6.0 %collective-permute-start.18 = (bf16[224,256]{1,0:T(8,128)(2,1)S(1)}, bf16[224,256]{1,0:T(8,128)(2,1)S(1)}, u32[]{:S(2)}, u32[]{:S(2)}) collective-permute-start(bf16[224,256]{1,0:T(8,128)(2,1)S(1)} %get-tuple-element.63.own), channel_id=1, source_target_pairs={{0,32},{8,40},{16,48},{24,56},{32,64},{40,72},{48,80},{56,88},{64,... | collective-permute-start | bytes 344072 | tf_op jit(solution)/shard_map/ppermute | solution.py:380
  (5 other events, 8.9 us)

commit v12 on v11

--- a/solution.py
+++ b/solution.py
@@ -78,8 +78,11 @@
     last[...] = clip[1]
 
 
-def copy_kernel(cot, order, first, second):
+def copy_kernel(cot, order, first):
     first[...] = cot[0]
+
+
+def second_frame_kernel(cot, order, second):
     second[...] = cot[1]
 
 
@@ -405,7 +408,7 @@
     frame = S((ROWS, C), bf16)
 
     sums, last = call(first_kernel, (S((16, 2, C), f32), frame), (clip,))
-    first, second = call(copy_kernel, (frame, frame), (cot,), order=(sums,))
+    first = call(copy_kernel, frame, (cot,), order=(sums,))
     parts = lax.all_to_all(sums, "tm", 0, 0, tiled=True)
     stats, last = call(
         total_kernel, (S((2, C), f32), frame), (parts,), order=(last,), aliases={1: 1}, passed_out=1
@@ -451,6 +454,7 @@
     held, *out = call(
         split_core_kernel, block(SHARD_PAD), (where, keep_up, got_up, keep_low, got_low), scalars=1
     )
+    second = call(second_frame_kernel, frame, (cot,), order=(keep_low,))
     later = passed(second, -1)[None]
     grad0, sums0, full = call(
         partial(first_grad_kernel, count),

time: 105 us -> 104 us (level)
  starting transfers between devices: 39.9 us -> 38.7 us
    all_to_all x1, waiting for transfers between devices: 3.37 us -> 4.97 us  [per_device(): parts = lax.all_to_all(sums, 'tm', 0, 0, tiled=True)]
    ppermute x15, starting transfers between devices: 26 us -> 24.9 us  [ring(): got.append(lax.ppermute(block, name, route))]
    unnamed x14 -> x10, local copies, waits for them, and re-layouts: 3.91 us -> 3.11 us
    pallas_call x18 -> x19, Pallas kernels: 32.2 us -> 32 us  [call(): pl.pallas_call(kernel, out_shape=out_shape, in_specs=specs, out_specs=out...]
  transfers between devices with their start and end apart: 22 -> 22, of which waited for: 14 -> 13; matrix products, arithmetic and copies ran while one was open for 0% -> 0% of each run, Pallas kernels for 28% -> 28%
where the time goes in v12:
time: 104 us; the launch traced here: 103 us
  starting transfers between devices  38.7 us (37%)
  Pallas kernels  32 us (31%)
  waiting for transfers between devices  28.7 us (28%)
  local copies, waits for them, and re-layouts  3.11 us (3%)
    pallas_call x19, Pallas kernels, call(): pl.pallas_call(kernel, out_shape=out_shape, in_specs=specs, out_specs=out...  32 us
    ppermute x15, starting transfers between devices, ring(): got.append(lax.ppermute(block, name, route))  24.9 us
    ppermute x15, waiting for transfers between devices, ring(): got.append(lax.ppermute(block, name, route))  21.2 us
    all_to_all x1, starting transfers between devices, per_device(): parts = lax.all_to_all(sums, 'tm', 0, 0, tiled=True)  8.05 us
    ppermute x3, starting transfers between devices, passed(): return lax.ppermute(block, 'tm', route)  5.09 us
    all_to_all x1, waiting for transfers between devices, per_device(): parts = lax.all_to_all(sums, 'tm', 0, 0, tiled=True)  4.97 us
    unnamed x10, local copies, waits for them, and re-layouts  3.11 us
  transfers between devices with their start and end apart: 22, of which 13 were waited for; matrix products, arithmetic and copies ran while one was open for 0% of the time, Pallas kernels for 28%

profile of v12, /device:TPU:6, one launch (start us, length us, event | category | flops | bytes accessed | tf_op | source)
XLA Modules:
  0.0 103.4 jit_solution(1479723357558040898)
XLA Ops:
  1.5 2.4 %collective-permute-start.1 = (bf16[864,256]{1,0:T(8,128)(2,1)}, bf16[864,256]{1,0:T(8,128)(2,1)S(1)}, u32[]{:S(2)}, u32[]{:S(2)}) collective-permute-start(bf16[864,256]{1,0:T(8,128)(2,1)} %own.1), channel_id=1, source_target_pairs={{0,2},{1,3},{2,4},{3,5},{4,6},{5,7},{6,0},{7,1},{8,10},{9,11},{10,... | collective-permute-start | bytes 1327112 | tf_op jit(solution)/shard_map/ppermute | solution.py:383
  6.4 8.0 %all-to-all-start = ((f32[16,2,256]{2,1,0:T(2,128)}), f32[16,2,256]{2,1,0:T(2,128)S(1)}, u32[]{:S(2)}, u32[]{:S(2)}) async-start(f32[16,2,256]{2,1,0:T(2,128)} %get-tuple-element.31.order), calls=%async_computation | async-start | bytes 65536 | tf_op jit(solution)/shard_map/all_to_all | solution.py:412
  17.1 5.0 %all-to-all-done.parts = f32[16,2,256]{2,1,0:T(2,128)S(1)} async-done(((f32[16,2,256]{2,1,0:T(2,128)}), f32[16,2,256]{2,1,0:T(2,128)S(1)}, u32[]{:S(2)}, u32[]{:S(2)}) %all-to-all-start) | async-done | bytes 32800 | tf_op jit(solution)/shard_map/all_to_all | solution.py:412
  22.1 2.5 %collective-permute-start.5 = (bf16[1024,256]{1,0:T(8,128)(2,1)S(1)}, bf16[1024,256]{1,0:T(8,128)(2,1)S(1)}, u32[]{:S(2)}, u32[]{:S(2)}) collective-permute-start(bf16[1024,256]{1,0:T(8,128)(2,1)S(1)} %get-tuple-element.39), channel_id=1, source_target_pairs={{0,8},{8,16},{16,24},{24,32},{32,40},{40,48},{48,56},{56,64},{64,7... | collective-permute-start | bytes 1572872 | tf_op jit(solution)/shard_map/ppermute | solution.py:393
  25.8 4.4 %shard_map.53 = (bf16[2,1024,256]{2,1,0:T(8,128)(2,1)S(1)}, f32[1824,256]{1,0:T(8,128)S(1)}, bf16[1824,256]{1,0:T(8,128)(2,1)S(1)}) custom-call(s32[4]{0:T(128)S(1)} %pad_add_fusion.where, f32[2,256]{1,0:T(2,128)S(1)} %get-tuple-element.33.refs_0_.stats, bf16[2,1024,256]{2,1,0:T(8,128)(2,1)S(1)} %bitcast.14, bf16[3,2,1152,256]{3,2,1,0:T(8,128)(2,1)S(1)} %shard_map.52.near), custom_call_target="tpu_custom_call" | custom-call | flops 2415919104 | tf_op jit(solution)/shard_map/pallas_call | solution.py:360
  31.8 2.0 %shard_map.57 = (f32[1824,256]{1,0:T(8,128)S(1)}, bf16[1824,256]{1,0:T(8,128)(2,1)S(1)}) custom-call(s32[4]{0:T(128)S(1)} %pad_add_fusion.where, bf16[2,1024,256]{2,1,0:T(8,128)(2,1)S(1)} %get-tuple-element.34.order.act, bf16[3,2,1152,256]{3,2,1,0:T(8,128)(2,1)S(1)} %shard_map.52.near, ...), custom_call_target="tpu_custom_call", output_to_operand_aliasing={{0}: (4, {}), {1}: (5, {})} | custom-call | flops 1207959552 | tf_op jit(solution)/shard_map/pallas_call | solution.py:360
  34.4 5.2 %shard_map.58 = (f32[1824,256]{1,0:T(8,128)S(1)}, bf16[1824,256]{1,0:T(8,128)(2,1)S(1)}) custom-call(s32[4]{0:T(128)S(1)} %pad_add_fusion.where, f32[2,256]{1,0:T(2,128)S(1)} %get-tuple-element.33.refs_0_.stats, bf16[2,1024,256]{2,1,0:T(8,128)(2,1)S(1)} %get-tuple-element.34.order.act, bf16[1024,256]{1,0:T(8,128)(2,1)S(1)} %collective-permute-done.5.before, ...), custom_call_target="tpu_custom_call" | custom-call | flops 3623878656 | tf_op jit(solution)/shard_map/pallas_call | solution.py:360
  43.1 2.2 %collective-permute-start.7 = (bf16[896,256]{1,0:T(8,128)(2,1)S(1)}, bf16[896,256]{1,0:T(8,128)(2,1)S(1)}, u32[]{:S(2)}, u32[]{:S(2)}) collective-permute-start(bf16[896,256]{1,0:T(8,128)(2,1)S(1)} %get-tuple-element.43), channel_id=1, source_target_pairs={{0,2},{1,3},{2,4},{3,5},{4,6},{5,7},{6,0},{7,1},{8,10},{9,11},{10,... | collective-permute-start | bytes 1376264 | tf_op jit(solution)/shard_map/ppermute | solution.py:383
  45.3 3.3 %collective-permute-start.9 = (bf16[896,256]{1,0:T(8,128)(2,1)S(1)}, bf16[896,256]{1,0:T(8,128)(2,1)S(1)}, u32[]{:S(2)}, u32[]{:S(2)}) collective-permute-start(bf16[896,256]{1,0:T(8,128)(2,1)S(1)} %get-tuple-element.45), channel_id=1, source_target_pairs={{0,4},{1,5},{2,6},{3,7},{4,0},{5,1},{6,2},{7,3},{8,12},{9,13},{10,... | collective-permute-start | bytes 1376264 | tf_op jit(solution)/shard_map/ppermute | solution.py:383
  48.5 6.1 %shard_map.60 = (f32[1024,256]{1,0:T(8,128)S(1)}, f32[2,256]{1,0:T(2,128)S(1)}, bf16[6912,256]{1,0:T(8,128)(2,1)S(1)}) custom-call(s32[4]{0:T(128)S(1)} %pad_add_fusion.where, f32[2,256]{1,0:T(2,128)S(1)} %get-tuple-element.33.refs_0_.stats, bf16[2,1024,256]{2,1,0:T(8,128)(2,1)S(1)} %bitcast.15, bf16[3,2,1152,256]{3,2,1,0:T(8,128)(2,1)S(1)} %shard_map.52.near, ...), custom_call_target="tpu_custom_call" | custom-call | flops 3623878656 | tf_op jit(solution)/shard_map/pallas_call | solution.py:360
  56.2 5.4 %shard_map.63 = (f32[1024,256]{1,0:T(8,128)S(1)}, f32[2,256]{1,0:T(2,128)S(1)}) custom-call(f32[2,256]{1,0:T(2,128)S(1)} %get-tuple-element.33.refs_0_.stats, bf16[2,1024,256]{2,1,0:T(8,128)(2,1)S(1)} %bitcast.16, bf16[3,2,1152,256]{3,2,1,0:T(8,128)(2,1)S(1)} %shard_map.52.near, bf16[3,1,1152,256]{3,2,1,0:T(8,128)(2,1)S(1)} %shard_map.55.after, ...), custom_call_target="tpu_custom_call" | custom-call | flops 3623878656 | tf_op jit(solution)/shard_map/pallas_call | solution.py:360
  61.6 3.6 %collective-permute-done.7.a0 = bf16[896,256]{1,0:T(8,128)(2,1)S(1)} collective-permute-done((bf16[896,256]{1,0:T(8,128)(2,1)S(1)}, bf16[896,256]{1,0:T(8,128)(2,1)S(1)}, u32[]{:S(2)}, u32[]{:S(2)}) %collective-permute-start.7) | collective-permute-done | bytes 458784 | tf_op jit(solution)/shard_map/ppermute | solution.py:383
  65.2 3.4 %collective-permute-done.9.a2 = bf16[896,256]{1,0:T(8,128)(2,1)S(1)} collective-permute-done((bf16[896,256]{1,0:T(8,128)(2,1)S(1)}, bf16[896,256]{1,0:T(8,128)(2,1)S(1)}, u32[]{:S(2)}, u32[]{:S(2)}) %collective-permute-start.9) | collective-permute-done | bytes 458784 | tf_op jit(solution)/shard_map/ppermute | solution.py:383
  69.5 4.3 %collective-permute-start.12 = (bf16[240,256]{1,0:T(8,128)(2,1)S(1)}, bf16[240,256]{1,0:T(8,128)(2,1)S(1)}, u32[]{:S(2)}, u32[]{:S(2)}) collective-permute-start(bf16[240,256]{1,0:T(8,128)(2,1)S(1)} %get-tuple-element.51), channel_id=1, source_target_pairs={{0,32},{8,40},{16,48},{24,56},{32,64},{40,72},{48,80},{56,88},{64,... | collective-permute-start | bytes 368648 | tf_op jit(solution)/shard_map/ppermute | solution.py:383
  73.7 1.6 %collective-permute-start.13 = (bf16[240,256]{1,0:T(8,128)(2,1)S(1)}, bf16[240,256]{1,0:T(8,128)(2,1)S(1)}, u32[]{:S(2)}, u32[]{:S(2)}) collective-permute-start(bf16[240,256]{1,0:T(8,128)(2,1)S(1)} %get-tuple-element.52), channel_id=1, source_target_pairs={{0,96},{8,104},{16,112},{24,120},{32,0},{40,8},{48,16},{56,24},{64... | collective-permute-start | bytes 368648 | tf_op jit(solution)/shard_map/ppermute | solution.py:383
  75.3 1.9 %collective-permute-start.14 = (bf16[240,256]{1,0:T(8,128)(2,1)S(1)}, bf16[240,256]{1,0:T(8,128)(2,1)S(1)}, u32[]{:S(2)}, u32[]{:S(2)}) collective-permute-start(bf16[240,256]{1,0:T(8,128)(2,1)S(1)} %get-tuple-element.53), channel_id=1, source_target_pairs={{0,64},{8,72},{16,80},{24,88},{32,96},{40,104},{48,112},{56,120},{... | collective-permute-start | bytes 368648 | tf_op jit(solution)/shard_map/ppermute | solution.py:383
  77.3 1.7 %collective-permute-done.12.a0 = bf16[240,256]{1,0:T(8,128)(2,1)S(1)} collective-permute-done((bf16[240,256]{1,0:T(8,128)(2,1)S(1)}, bf16[240,256]{1,0:T(8,128)(2,1)S(1)}, u32[]{:S(2)}, u32[]{:S(2)}) %collective-permute-start.12) | collective-permute-done | bytes 122912 | tf_op jit(solution)/shard_map/ppermute | solution.py:383
  79.3 2.4 %collective-permute-done.14.a2 = bf16[240,256]{1,0:T(8,128)(2,1)S(1)} collective-permute-done((bf16[240,256]{1,0:T(8,128)(2,1)S(1)}, bf16[240,256]{1,0:T(8,128)(2,1)S(1)}, u32[]{:S(2)}, u32[]{:S(2)}) %collective-permute-start.14) | collective-permute-done | bytes 122912 | tf_op jit(solution)/shard_map/ppermute | solution.py:383
  82.5 3.8 %collective-permute-start.16 = (bf16[240,256]{1,0:T(8,128)(2,1)S(1)}, bf16[240,256]{1,0:T(8,128)(2,1)S(1)}, u32[]{:S(2)}, u32[]{:S(2)}) collective-permute-start(bf16[240,256]{1,0:T(8,128)(2,1)S(1)} %get-tuple-element.54.own), channel_id=1, source_target_pairs={{0,24},{8,0},{16,8},{24,16},{32,56},{40,32},{48,40},{56,48},{64,88... | collective-permute-start | bytes 368648 | tf_op jit(solution)/shard_map/ppermute | solution.py:383
  86.4 3.0 %collective-permute-done.17.a2 = bf16[240,256]{1,0:T(8,128)(2,1)S(1)} collective-permute-done((bf16[240,256]{1,0:T(8,128)(2,1)S(1)}, bf16[240,256]{1,0:T(8,128)(2,1)S(1)}, u32[]{:S(2)}, u32[]{:S(2)}) %collective-permute-start.17) | collective-permute-done | bytes 122912 | tf_op jit(solution)/shard_map/ppermute | solution.py:383
  89.3 3.1 %collective-permute-done.15.a0 = bf16[240,256]{1,0:T(8,128)(2,1)S(1)} collective-permute-done((bf16[240,256]{1,0:T(8,128)(2,1)S(1)}, bf16[240,256]{1,0:T(8,128)(2,1)S(1)}, u32[]{:S(2)}, u32[]{:S(2)}) %collective-permute-start.15) | collective-permute-done | bytes 122912 | tf_op jit(solution)/shard_map/ppermute | solution.py:383
  94.1 1.8 %collective-permute-start.19 = (bf16[224,256]{1,0:T(8,128)(2,1)S(1)}, bf16[224,256]{1,0:T(8,128)(2,1)S(1)}, u32[]{:S(2)}, u32[]{:S(2)}) collective-permute-start(bf16[224,256]{1,0:T(8,128)(2,1)S(1)} %get-tuple-element.59.own), channel_id=1, source_target_pairs={{0,96},{8,104},{16,112},{24,120},{32,0},{40,8},{48,16},{56,24},{64... | collective-permute-start | bytes 344072 | tf_op jit(solution)/shard_map/ppermute | solution.py:383
  96.1 2.1 %shard_map.67 = bf16[2,1024,256]{2,1,0:T(8,128)(2,1)} custom-call(f32[2,256]{1,0:T(2,128)S(1)} %get-tuple-element.33.refs_0_.stats, f32[2,256]{1,0:T(2,128)S(1)} %get-tuple-element.56.sums, bf16[2,1024,256]{2,1,0:T(8,128)(2,1)S(1)} %bitcast.17, bf16[2,1024,256]{2,1,0:T(8,128)(2,1)S(1)} %bitcast.12, f32[1024,256]{1,0:T(8,128)S(1)} %get-tuple-element.57.grad0, ...), custom_call_target="tpu_custom_call" | custom-call | bytes 8000000 | tf_op jit(solution)/shard_map/pallas_call | solution.py:360
  99.2 2.7 %collective-permute-done.18.a0 = bf16[224,256]{1,0:T(8,128)(2,1)S(1)} collective-permute-done((bf16[224,256]{1,0:T(8,128)(2,1)S(1)}, bf16[224,256]{1,0:T(8,128)(2,1)S(1)}, u32[]{:S(2)}, u32[]{:S(2)}) %collective-permute-start.18) | collective-permute-done | bytes 114720 | tf_op jit(solution)/shard_map/ppermute | solution.py:383
  (50 shorter events, 20.8 us)
Async XLA Ops:
  0.6 24.0 %copy-start.1 = (bf16[1,2,16,64,256]{4,3,2,1,0:T(8,128)(2,1)S(1)}, bf16[1,2,16,64,256]{4,3,2,1,0:T(8,128)(2,1)}, u32[]{:S(2)}) copy-start(bf16[1,2,16,64,256]{4,3,2,1,0:T(8,128)(2,1)} %param.4) | copy-start | bytes 3145732
  0.6 29.6 %collective-permute-start.2 = (bf16[864,256]{1,0:T(8,128)(2,1)}, bf16[864,256]{1,0:T(8,128)(2,1)S(1)}, u32[]{:S(2)}, u32[]{:S(2)}) collective-permute-start(bf16[864,256]{1,0:T(8,128)(2,1)} %own.1), channel_id=1, source_target_pairs={{0,6},{1,7},{2,0},{3,1},{4,2},{5,3},{6,4},{7,5},{8,14},{9,15},{10,... | collective-permute-start | bytes 1327112 | tf_op jit(solution)/shard_map/ppermute | solution.py:383
  1.5 28.7 %collective-permute-start.1 = (bf16[864,256]{1,0:T(8,128)(2,1)}, bf16[864,256]{1,0:T(8,128)(2,1)S(1)}, u32[]{:S(2)}, u32[]{:S(2)}) collective-permute-start(bf16[864,256]{1,0:T(8,128)(2,1)} %own.1), channel_id=1, source_target_pairs={{0,2},{1,3},{2,4},{3,5},{4,6},{5,7},{6,0},{7,1},{8,10},{9,11},{10,... | collective-permute-start | bytes 1327112 | tf_op jit(solution)/shard_map/ppermute | solution.py:383
  3.9 26.3 %collective-permute-start.3 = (bf16[864,256]{1,0:T(8,128)(2,1)}, bf16[864,256]{1,0:T(8,128)(2,1)}, u32[]{:S(2)}, u32[]{:S(2)}) collective-permute-start(bf16[864,256]{1,0:T(8,128)(2,1)} %own.1), channel_id=1, source_target_pairs={{0,4},{1,5},{2,6},{3,7},{4,0},{5,1},{6,2},{7,3},{8,12},{9,13},{10,... | collective-permute-start | bytes 1327112 | tf_op jit(solution)/shard_map/ppermute | solution.py:383
  6.4 15.7 %all-to-all-start = ((f32[16,2,256]{2,1,0:T(2,128)}), f32[16,2,256]{2,1,0:T(2,128)S(1)}, u32[]{:S(2)}, u32[]{:S(2)}) async-start(f32[16,2,256]{2,1,0:T(2,128)} %get-tuple-element.31.order), calls=%async_computation | async-start | bytes 65536 | tf_op jit(solution)/shard_map/all_to_all | solution.py:412
  15.7 15.8 %collective-permute-start = (bf16[1024,256]{1,0:T(8,128)(2,1)S(1)}, bf16[1024,256]{1,0:T(8,128)(2,1)S(1)}, u32[]{:S(2)}, u32[]{:S(2)}) collective-permute-start(bf16[1024,256]{1,0:T(8,128)(2,1)S(1)} %shard_map.54), channel_id=1, source_target_pairs={{8,0},{16,8},{24,16},{32,24},{40,32},{48,40},{56,48},{64,56},{72,6... | collective-permute-start | bytes 1572872 | tf_op jit(solution)/shard_map/ppermute | solution.py:393
  22.1 12.3 %collective-permute-start.5 = (bf16[1024,256]{1,0:T(8,128)(2,1)S(1)}, bf16[1024,256]{1,0:T(8,128)(2,1)S(1)}, u32[]{:S(2)}, u32[]{:S(2)}) collective-permute-start(bf16[1024,256]{1,0:T(8,128)(2,1)S(1)} %get-tuple-element.39), channel_id=1, source_target_pairs={{0,8},{8,16},{16,24},{24,32},{32,40},{40,48},{48,56},{56,64},{64,7... | collective-permute-start | bytes 1572872 | tf_op jit(solution)/shard_map/ppermute | solution.py:393
  25.8 4.4 %copy-start.4 = (bf16[864,256]{1,0:T(8,128)(2,1)S(1)}, bf16[864,256]{1,0:T(8,128)(2,1)}, u32[]{:S(2)}) copy-start(bf16[864,256]{1,0:T(8,128)(2,1)} %own.1) | copy-start | bytes 1327108
  31.4 17.1 %collective-permute-start.10 = (bf16[4,864,256]{2,1,0:T(8,128)(2,1)S(1)}, bf16[4,864,256]{2,1,0:T(8,128)(2,1)S(1)}, u32[]{:S(2)}, u32[]{:S(2)}) collective-permute-start(bf16[4,864,256]{2,1,0:T(8,128)(2,1)S(1)} %shard_map.56.order.mine), channel_id=1, source_target_pairs={{0,1},{1,0},{2,3},{3,2},{4,5},{5,4},{6,7},{7,6},{8,9},{9,8},{10,11... | collective-permute-start | bytes 5308424 | tf_op jit(solution)/shard_map/ppermute | solution.py:388
  33.8 7.2 %collective-permute-start.4 = (bf16[1824,256]{1,0:T(8,128)(2,1)S(1)}, bf16[1824,256]{1,0:T(8,128)(2,1)S(1)}, u32[]{:S(2)}, u32[]{:S(2)}) collective-permute-start(bf16[1824,256]{1,0:T(8,128)(2,1)S(1)} %get-tuple-element.38.order), channel_id=1, source_target_pairs={{0,1},{1,0},{2,3},{3,2},{4,5},{5,4},{6,7},{7,6},{8,9},{9,8},{10,11... | collective-permute-start | bytes 2801672 | tf_op jit(solution)/shard_map/ppermute | solution.py:388
  39.6 2.6 %collective-permute-start.6 = (bf16[1824,256]{1,0:T(8,128)(2,1)S(1)}, bf16[1824,256]{1,0:T(8,128)(2,1)S(1)}, u32[]{:S(2)}, u32[]{:S(2)}) collective-permute-start(bf16[1824,256]{1,0:T(8,128)(2,1)S(1)} %get-tuple-element.41), channel_id=1, source_target_pairs={{0,1},{1,0},{2,3},{3,2},{4,5},{5,4},{6,7},{7,6},{8,9},{9,8},{10,11... | collective-permute-start | bytes 2801672 | tf_op jit(solution)/shard_map/ppermute | solution.py:388
  39.7 16.2 %collective-permute-start.11 = (bf16[1024,256]{1,0:T(8,128)(2,1)S(1)}, bf16[1024,256]{1,0:T(8,128)(2,1)S(1)}, u32[]{:S(2)}, u32[]{:S(2)}) collective-permute-start(bf16[1024,256]{1,0:T(8,128)(2,1)S(1)} %shard_map.61), channel_id=1, source_target_pairs={{8,0},{16,8},{24,16},{32,24},{40,32},{48,40},{56,48},{64,56},{72,6... | collective-permute-start | bytes 1572872 | tf_op jit(solution)/shard_map/ppermute | solution.py:393
  43.1 22.1 %collective-permute-start.7 = (bf16[896,256]{1,0:T(8,128)(2,1)S(1)}, bf16[896,256]{1,0:T(8,128)(2,1)S(1)}, u32[]{:S(2)}, u32[]{:S(2)}) collective-permute-start(bf16[896,256]{1,0:T(8,128)(2,1)S(1)} %get-tuple-element.43), channel_id=1, source_target_pairs={{0,2},{1,3},{2,4},{3,5},{4,6},{5,7},{6,0},{7,1},{8,10},{9,11},{10,... | collective-permute-start | bytes 1376264 | tf_op jit(solution)/shard_map/ppermute | solution.py:383
  45.3 19.9 %collective-permute-start.8 = (bf16[896,256]{1,0:T(8,128)(2,1)S(1)}, bf16[896,256]{1,0:T(8,128)(2,1)S(1)}, u32[]{:S(2)}, u32[]{:S(2)}) collective-permute-start(bf16[896,256]{1,0:T(8,128)(2,1)S(1)} %get-tuple-element.44), channel_id=1, source_target_pairs={{0,6},{1,7},{2,0},{3,1},{4,2},{5,3},{6,4},{7,5},{8,14},{9,15},{10,... | collective-permute-start | bytes 1376264 | tf_op jit(solution)/shard_map/ppermute | solution.py:383
  45.3 23.3 %collective-permute-start.9 = (bf16[896,256]{1,0:T(8,128)(2,1)S(1)}, bf16[896,256]{1,0:T(8,128)(2,1)S(1)}, u32[]{:S(2)}, u32[]{:S(2)}) collective-permute-start(bf16[896,256]{1,0:T(8,128)(2,1)S(1)} %get-tuple-element.45), channel_id=1, source_target_pairs={{0,4},{1,5},{2,6},{3,7},{4,0},{5,1},{6,2},{7,3},{8,12},{9,13},{10,... | collective-permute-start | bytes 1376264 | tf_op jit(solution)/shard_map/ppermute | solution.py:383
  69.5 9.5 %collective-permute-start.12 = (bf16[240,256]{1,0:T(8,128)(2,1)S(1)}, bf16[240,256]{1,0:T(8,128)(2,1)S(1)}, u32[]{:S(2)}, u32[]{:S(2)}) collective-permute-start(bf16[240,256]{1,0:T(8,128)(2,1)S(1)} %get-tuple-element.51), channel_id=1, source_target_pairs={{0,32},{8,40},{16,48},{24,56},{32,64},{40,72},{48,80},{56,88},{64,... | collective-permute-start | bytes 368648 | tf_op jit(solution)/shard_map/ppermute | solution.py:383
  73.7 5.6 %collective-permute-start.13 = (bf16[240,256]{1,0:T(8,128)(2,1)S(1)}, bf16[240,256]{1,0:T(8,128)(2,1)S(1)}, u32[]{:S(2)}, u32[]{:S(2)}) collective-permute-start(bf16[240,256]{1,0:T(8,128)(2,1)S(1)} %get-tuple-element.52), channel_id=1, source_target_pairs={{0,96},{8,104},{16,112},{24,120},{32,0},{40,8},{48,16},{56,24},{64... | collective-permute-start | bytes 368648 | tf_op jit(solution)/shard_map/ppermute | solution.py:383
  75.3 6.4 %collective-permute-start.14 = (bf16[240,256]{1,0:T(8,128)(2,1)S(1)}, bf16[240,256]{1,0:T(8,128)(2,1)S(1)}, u32[]{:S(2)}, u32[]{:S(2)}) collective-permute-start(bf16[240,256]{1,0:T(8,128)(2,1)S(1)} %get-tuple-element.53), channel_id=1, source_target_pairs={{0,64},{8,72},{16,80},{24,88},{32,96},{40,104},{48,112},{56,120},{... | collective-permute-start | bytes 368648 | tf_op jit(solution)/shard_map/ppermute | solution.py:383
  81.8 7.5 %collective-permute-start.17 = (bf16[240,256]{1,0:T(8,128)(2,1)S(1)}, bf16[240,256]{1,0:T(8,128)(2,1)S(1)}, u32[]{:S(2)}, u32[]{:S(2)}) collective-permute-start(bf16[240,256]{1,0:T(8,128)(2,1)S(1)} %get-tuple-element.54.own), channel_id=1, source_target_pairs={{0,16},{8,24},{16,0},{24,8},{32,48},{40,56},{48,32},{56,40},{64,80... | collective-permute-start | bytes 368648 | tf_op jit(solution)/shard_map/ppermute | solution.py:383
  82.5 6.8 %collective-permute-start.16 = (bf16[240,256]{1,0:T(8,128)(2,1)S(1)}, bf16[240,256]{1,0:T(8,128)(2,1)S(1)}, u32[]{:S(2)}, u32[]{:S(2)}) collective-permute-start(bf16[240,256]{1,0:T(8,128)(2,1)S(1)} %get-tuple-element.54.own), channel_id=1, source_target_pairs={{0,24},{8,0},{16,8},{24,16},{32,56},{40,32},{48,40},{56,48},{64,88... | collective-permute-start | bytes 368648 | tf_op jit(solution)/shard_map/ppermute | solution.py:383
  86.4 6.1 %collective-permute-start.15 = (bf16[240,256]{1,0:T(8,128)(2,1)S(1)}, bf16[240,256]{1,0:T(8,128)(2,1)S(1)}, u32[]{:S(2)}, u32[]{:S(2)}) collective-permute-start(bf16[240,256]{1,0:T(8,128)(2,1)S(1)} %get-tuple-element.54.own), channel_id=1, source_target_pairs={{0,8},{8,16},{16,24},{24,0},{32,40},{40,48},{48,56},{56,32},{64,72... | collective-permute-start | bytes 368648 | tf_op jit(solution)/shard_map/ppermute | solution.py:383
  92.5 6.4 %collective-permute-start.20 = (bf16[224,256]{1,0:T(8,128)(2,1)S(1)}, bf16[224,256]{1,0:T(8,128)(2,1)S(1)}, u32[]{:S(2)}, u32[]{:S(2)}) collective-permute-start(bf16[224,256]{1,0:T(8,128)(2,1)S(1)} %get-tuple-element.59.own), channel_id=1, source_target_pairs={{0,64},{8,72},{16,80},{24,88},{32,96},{40,104},{48,112},{56,120},{... | collective-permute-start | bytes 344072 | tf_op jit(solution)/shard_map/ppermute | solution.py:383
  94.1 5.1 %collective-permute-start.19 = (bf16[224,256]{1,0:T(8,128)(2,1)S(1)}, bf16[224,256]{1,0:T(8,128)(2,1)S(1)}, u32[]{:S(2)}, u32[]{:S(2)}) collective-permute-start(bf16[224,256]{1,0:T(8,128)(2,1)S(1)} %get-tuple-element.59.own), channel_id=1, source_target_pairs={{0,96},{8,104},{16,112},{24,120},{32,0},{40,8},{48,16},{56,24},{64... | collective-permute-start | bytes 344072 | tf_op jit(solution)/shard_map/ppermute | solution.py:383
  95.9 6.0 %collective-permute-start.18 = (bf16[224,256]{1,0:T(8,128)(2,1)S(1)}, bf16[224,256]{1,0:T(8,128)(2,1)S(1)}, u32[]{:S(2)}, u32[]{:S(2)}) collective-permute-start(bf16[224,256]{1,0:T(8,128)(2,1)S(1)} %get-tuple-element.59.own), channel_id=1, source_target_pairs={{0,32},{8,40},{16,48},{24,56},{32,64},{40,72},{48,80},{56,88},{64,... | collective-permute-start | bytes 344072 | tf_op jit(solution)/shard_map/ppermute | solution.py:383
  (3 other events, 3.7 us)

commit v13 on v12

--- a/solution.py
+++ b/solution.py
@@ -337,17 +337,31 @@
     next_sums[...] = ring_sums(sums[...], (a0, a1, a2))
 
 
-def finish_kernel(where, own, a0, a1, a2, grad_weight):
+def finish_kernel(where, own, a0, a1, a2, grad_weight, wide, sems):
     y = where[3]
     whole = SHARD - 3 * QUARTER
-    for block, distance in ((own, 0), (a0, 3), (a1, 1), (a2, 2)):
+    for k, (block, distance) in enumerate(((own, 0), (a0, 3), (a1, 1), (a2, 2))):
+        quarter = (y + distance) & 3
+        wide[k] = block[...].astype(f32)
+        start = pl.multiple_of(quarter * QUARTER, UNIT)
+        pltpu.make_async_copy(wide.at[k, :whole], grad_weight.at[pl.ds(start, whole)], sems.at[0, k]).start()
+
+        @pl.when(quarter < 3)
+        def _(k=k, start=start):
+            pltpu.make_async_copy(
+                wide.at[k, whole:], grad_weight.at[pl.ds(start + whole, QUARTER - whole)], sems.at[1, k]
+            ).start()
+
+    for k, distance in enumerate((0, 3, 1, 2)):
         quarter = (y + distance) & 3
         start = pl.multiple_of(quarter * QUARTER, UNIT)
-        grad_weight[pl.ds(start, whole)] = block[:whole].astype(f32)
+        pltpu.make_async_copy(wide.at[k, :whole], grad_weight.at[pl.ds(start, whole)], sems.at[0, k]).wait()
 
         @pl.when(quarter < 3)
-        def _(block=block, start=start):
-            grad_weight[pl.ds(start + whole, QUARTER - whole)] = block[whole:].astype(f32)
+        def _(k=k, start=start):
+            pltpu.make_async_copy(
+                wide.at[k, whole:], grad_weight.at[pl.ds(start + whole, QUARTER - whole)], sems.at[1, k]
+            ).wait()
 
 
 def call(kernel, out_shape, args, scratch=(), flops=0, bytes_accessed=0, scalars=0, order=(), aliases={}, passed_out=0):
@@ -491,12 +505,14 @@
         (stats, sums, clip, cot, grad0, grad1),
         bytes_accessed=8_000_000,
     )
-    grad_weight = call(
+    grad_weight = pl.pallas_call(
         finish_kernel,
-        S((SHARD, C), f32),
-        (where, own, *ring("y", [own] * 3)),
-        scalars=1,
-    )
+        out_shape=S((SHARD, C), f32),
+        in_specs=[pl.BlockSpec(memory_space=pltpu.SMEM)] + [pl.BlockSpec(memory_space=pltpu.VMEM)] * 4,
+        out_specs=pl.BlockSpec(memory_space=pl.ANY),
+        scratch_shapes=[pltpu.VMEM((4, QUARTER, C), f32), pltpu.SemaphoreType.DMA((2, 4))],
+        compiler_params=pltpu.CompilerParams(vmem_limit_bytes=VMEM),
+    )(where, own, *ring("y", [own] * 3))
     return grad_input.reshape(shape), grad_weight
 
 

time: 104 us -> 104 us (level)
    pallas_call x19 -> x18, Pallas kernels: 32 us -> 30.4 us  [call(): pl.pallas_call(kernel, out_shape=out_shape, in_specs=specs, out_specs=out...]
    pallas_call x0 -> x1, Pallas kernels: none -> 1.52 us  [per_device(): pl.pallas_call(finish_kernel, out_shape=S((SHARD, C), f32), in_specs=[pl....]
where the time goes in v13:
time: 104 us
  starting transfers between devices  38.7 us (37%)
  Pallas kernels  32 us (31%)
  waiting for transfers between devices  28.7 us (28%)
  local copies, waits for them, and re-layouts  3.11 us (3%)
    pallas_call x18, Pallas kernels, call(): pl.pallas_call(kernel, out_shape=out_shape, in_specs=specs, out_specs=out...  30.4 us
    ppermute x15, starting transfers between devices, ring(): got.append(lax.ppermute(block, name, route))  24.9 us
    ppermute x15, waiting for transfers between devices, ring(): got.append(lax.ppermute(block, name, route))  21.2 us
    all_to_all x1, starting transfers between devices, per_device(): parts = lax.all_to_all(sums, 'tm', 0, 0, tiled=True)  8.05 us
    ppermute x3, starting transfers between devices, passed(): return lax.ppermute(block, 'tm', route)  5.09 us
    all_to_all x1, waiting for transfers between devices, per_device(): parts = lax.all_to_all(sums, 'tm', 0, 0, tiled=True)  4.97 us
    unnamed x10, local copies, waits for them, and re-layouts  3.11 us
  transfers between devices with their start and end apart: 22, of which 13 were waited for; matrix products, arithmetic and copies ran while one was open for 0% of the time, Pallas kernels for 28%

profile of v13, /device:TPU:6, one launch (start us, length us, event | category | flops | bytes accessed | tf_op | source)
XLA Modules:
  0.0 103.6 jit_solution(8694561147063257456)
XLA Ops:
  1.5 2.4 %collective-permute-start.1 = (bf16[864,256]{1,0:T(8,128)(2,1)}, bf16[864,256]{1,0:T(8,128)(2,1)S(1)}, u32[]{:S(2)}, u32[]{:S(2)}) collective-permute-start(bf16[864,256]{1,0:T(8,128)(2,1)} %own.1), channel_id=1, source_target_pairs={{0,2},{1,3},{2,4},{3,5},{4,6},{5,7},{6,0},{7,1},{8,10},{9,11},{10,... | collective-permute-start | bytes 1327112 | tf_op jit(solution)/shard_map/ppermute | solution.py:397
  6.4 8.0 %all-to-all-start = ((f32[16,2,256]{2,1,0:T(2,128)}), f32[16,2,256]{2,1,0:T(2,128)S(1)}, u32[]{:S(2)}, u32[]{:S(2)}) async-start(f32[16,2,256]{2,1,0:T(2,128)} %get-tuple-element.31.order), calls=%async_computation | async-start | bytes 65536 | tf_op jit(solution)/shard_map/all_to_all | solution.py:426
  17.1 5.0 %all-to-all-done.parts = f32[16,2,256]{2,1,0:T(2,128)S(1)} async-done(((f32[16,2,256]{2,1,0:T(2,128)}), f32[16,2,256]{2,1,0:T(2,128)S(1)}, u32[]{:S(2)}, u32[]{:S(2)}) %all-to-all-start) | async-done | bytes 32800 | tf_op jit(solution)/shard_map/all_to_all | solution.py:426
  22.1 2.5 %collective-permute-start.5 = (bf16[1024,256]{1,0:T(8,128)(2,1)S(1)}, bf16[1024,256]{1,0:T(8,128)(2,1)S(1)}, u32[]{:S(2)}, u32[]{:S(2)}) collective-permute-start(bf16[1024,256]{1,0:T(8,128)(2,1)S(1)} %get-tuple-element.39), channel_id=1, source_target_pairs={{0,8},{8,16},{16,24},{24,32},{32,40},{40,48},{48,56},{56,64},{64,7... | collective-permute-start | bytes 1572872 | tf_op jit(solution)/shard_map/ppermute | solution.py:407
  25.8 4.4 %shard_map.53 = (bf16[2,1024,256]{2,1,0:T(8,128)(2,1)S(1)}, f32[1824,256]{1,0:T(8,128)S(1)}, bf16[1824,256]{1,0:T(8,128)(2,1)S(1)}) custom-call(s32[4]{0:T(128)S(1)} %pad_add_fusion.where, f32[2,256]{1,0:T(2,128)S(1)} %get-tuple-element.33.refs_0_.stats, bf16[2,1024,256]{2,1,0:T(8,128)(2,1)S(1)} %bitcast.14, bf16[3,2,1152,256]{3,2,1,0:T(8,128)(2,1)S(1)} %shard_map.52.near), custom_call_target="tpu_custom_call" | custom-call | flops 2415919104 | tf_op jit(solution)/shard_map/pallas_call | solution.py:374
  31.8 2.0 %shard_map.57 = (f32[1824,256]{1,0:T(8,128)S(1)}, bf16[1824,256]{1,0:T(8,128)(2,1)S(1)}) custom-call(s32[4]{0:T(128)S(1)} %pad_add_fusion.where, bf16[2,1024,256]{2,1,0:T(8,128)(2,1)S(1)} %get-tuple-element.34.order.act, bf16[3,2,1152,256]{3,2,1,0:T(8,128)(2,1)S(1)} %shard_map.52.near, ...), custom_call_target="tpu_custom_call", output_to_operand_aliasing={{0}: (4, {}), {1}: (5, {})} | custom-call | flops 1207959552 | tf_op jit(solution)/shard_map/pallas_call | solution.py:374
  34.4 5.2 %shard_map.58 = (f32[1824,256]{1,0:T(8,128)S(1)}, bf16[1824,256]{1,0:T(8,128)(2,1)S(1)}) custom-call(s32[4]{0:T(128)S(1)} %pad_add_fusion.where, f32[2,256]{1,0:T(2,128)S(1)} %get-tuple-element.33.refs_0_.stats, bf16[2,1024,256]{2,1,0:T(8,128)(2,1)S(1)} %get-tuple-element.34.order.act, bf16[1024,256]{1,0:T(8,128)(2,1)S(1)} %collective-permute-done.5.before, ...), custom_call_target="tpu_custom_call" | custom-call | flops 3623878656 | tf_op jit(solution)/shard_map/pallas_call | solution.py:374
  43.1 2.2 %collective-permute-start.7 = (bf16[896,256]{1,0:T(8,128)(2,1)S(1)}, bf16[896,256]{1,0:T(8,128)(2,1)S(1)}, u32[]{:S(2)}, u32[]{:S(2)}) collective-permute-start(bf16[896,256]{1,0:T(8,128)(2,1)S(1)} %get-tuple-element.43), channel_id=1, source_target_pairs={{0,2},{1,3},{2,4},{3,5},{4,6},{5,7},{6,0},{7,1},{8,10},{9,11},{10,... | collective-permute-start | bytes 1376264 | tf_op jit(solution)/shard_map/ppermute | solution.py:397
  45.3 3.3 %collective-permute-start.9 = (bf16[896,256]{1,0:T(8,128)(2,1)S(1)}, bf16[896,256]{1,0:T(8,128)(2,1)S(1)}, u32[]{:S(2)}, u32[]{:S(2)}) collective-permute-start(bf16[896,256]{1,0:T(8,128)(2,1)S(1)} %get-tuple-element.45), channel_id=1, source_target_pairs={{0,4},{1,5},{2,6},{3,7},{4,0},{5,1},{6,2},{7,3},{8,12},{9,13},{10,... | collective-permute-start | bytes 1376264 | tf_op jit(solution)/shard_map/ppermute | solution.py:397
  48.5 6.1 %shard_map.60 = (f32[1024,256]{1,0:T(8,128)S(1)}, f32[2,256]{1,0:T(2,128)S(1)}, bf16[6912,256]{1,0:T(8,128)(2,1)S(1)}) custom-call(s32[4]{0:T(128)S(1)} %pad_add_fusion.where, f32[2,256]{1,0:T(2,128)S(1)} %get-tuple-element.33.refs_0_.stats, bf16[2,1024,256]{2,1,0:T(8,128)(2,1)S(1)} %bitcast.15, bf16[3,2,1152,256]{3,2,1,0:T(8,128)(2,1)S(1)} %shard_map.52.near, ...), custom_call_target="tpu_custom_call" | custom-call | flops 3623878656 | tf_op jit(solution)/shard_map/pallas_call | solution.py:374
  56.2 5.4 %shard_map.63 = (f32[1024,256]{1,0:T(8,128)S(1)}, f32[2,256]{1,0:T(2,128)S(1)}) custom-call(f32[2,256]{1,0:T(2,128)S(1)} %get-tuple-element.33.refs_0_.stats, bf16[2,1024,256]{2,1,0:T(8,128)(2,1)S(1)} %bitcast.16, bf16[3,2,1152,256]{3,2,1,0:T(8,128)(2,1)S(1)} %shard_map.52.near, bf16[3,1,1152,256]{3,2,1,0:T(8,128)(2,1)S(1)} %shard_map.55.after, ...), custom_call_target="tpu_custom_call" | custom-call | flops 3623878656 | tf_op jit(solution)/shard_map/pallas_call | solution.py:374
  61.6 3.6 %collective-permute-done.7.a0 = bf16[896,256]{1,0:T(8,128)(2,1)S(1)} collective-permute-done((bf16[896,256]{1,0:T(8,128)(2,1)S(1)}, bf16[896,256]{1,0:T(8,128)(2,1)S(1)}, u32[]{:S(2)}, u32[]{:S(2)}) %collective-permute-start.7) | collective-permute-done | bytes 458784 | tf_op jit(solution)/shard_map/ppermute | solution.py:397
  65.2 3.4 %collective-permute-done.9.a2 = bf16[896,256]{1,0:T(8,128)(2,1)S(1)} collective-permute-done((bf16[896,256]{1,0:T(8,128)(2,1)S(1)}, bf16[896,256]{1,0:T(8,128)(2,1)S(1)}, u32[]{:S(2)}, u32[]{:S(2)}) %collective-permute-start.9) | collective-permute-done | bytes 458784 | tf_op jit(solution)/shard_map/ppermute | solution.py:397
  69.5 4.3 %collective-permute-start.12 = (bf16[240,256]{1,0:T(8,128)(2,1)S(1)}, bf16[240,256]{1,0:T(8,128)(2,1)S(1)}, u32[]{:S(2)}, u32[]{:S(2)}) collective-permute-start(bf16[240,256]{1,0:T(8,128)(2,1)S(1)} %get-tuple-element.51), channel_id=1, source_target_pairs={{0,32},{8,40},{16,48},{24,56},{32,64},{40,72},{48,80},{56,88},{64,... | collective-permute-start | bytes 368648 | tf_op jit(solution)/shard_map/ppermute | solution.py:397
  73.7 1.6 %collective-permute-start.13 = (bf16[240,256]{1,0:T(8,128)(2,1)S(1)}, bf16[240,256]{1,0:T(8,128)(2,1)S(1)}, u32[]{:S(2)}, u32[]{:S(2)}) collective-permute-start(bf16[240,256]{1,0:T(8,128)(2,1)S(1)} %get-tuple-element.52), channel_id=1, source_target_pairs={{0,96},{8,104},{16,112},{24,120},{32,0},{40,8},{48,16},{56,24},{64... | collective-permute-start | bytes 368648 | tf_op jit(solution)/shard_map/ppermute | solution.py:397
  75.3 1.9 %collective-permute-start.14 = (bf16[240,256]{1,0:T(8,128)(2,1)S(1)}, bf16[240,256]{1,0:T(8,128)(2,1)S(1)}, u32[]{:S(2)}, u32[]{:S(2)}) collective-permute-start(bf16[240,256]{1,0:T(8,128)(2,1)S(1)} %get-tuple-element.53), channel_id=1, source_target_pairs={{0,64},{8,72},{16,80},{24,88},{32,96},{40,104},{48,112},{56,120},{... | collective-permute-start | bytes 368648 | tf_op jit(solution)/shard_map/ppermute | solution.py:397
  77.3 1.7 %collective-permute-done.12.a0 = bf16[240,256]{1,0:T(8,128)(2,1)S(1)} collective-permute-done((bf16[240,256]{1,0:T(8,128)(2,1)S(1)}, bf16[240,256]{1,0:T(8,128)(2,1)S(1)}, u32[]{:S(2)}, u32[]{:S(2)}) %collective-permute-start.12) | collective-permute-done | bytes 122912 | tf_op jit(solution)/shard_map/ppermute | solution.py:397
  79.3 2.4 %collective-permute-done.14.a2 = bf16[240,256]{1,0:T(8,128)(2,1)S(1)} collective-permute-done((bf16[240,256]{1,0:T(8,128)(2,1)S(1)}, bf16[240,256]{1,0:T(8,128)(2,1)S(1)}, u32[]{:S(2)}, u32[]{:S(2)}) %collective-permute-start.14) | collective-permute-done | bytes 122912 | tf_op jit(solution)/shard_map/ppermute | solution.py:397
  82.5 3.8 %collective-permute-start.16 = (bf16[240,256]{1,0:T(8,128)(2,1)S(1)}, bf16[240,256]{1,0:T(8,128)(2,1)S(1)}, u32[]{:S(2)}, u32[]{:S(2)}) collective-permute-start(bf16[240,256]{1,0:T(8,128)(2,1)S(1)} %get-tuple-element.54.own), channel_id=1, source_target_pairs={{0,24},{8,0},{16,8},{24,16},{32,56},{40,32},{48,40},{56,48},{64,88... | collective-permute-start | bytes 368648 | tf_op jit(solution)/shard_map/ppermute | solution.py:397
  86.4 3.0 %collective-permute-done.17.a2 = bf16[240,256]{1,0:T(8,128)(2,1)S(1)} collective-permute-done((bf16[240,256]{1,0:T(8,128)(2,1)S(1)}, bf16[240,256]{1,0:T(8,128)(2,1)S(1)}, u32[]{:S(2)}, u32[]{:S(2)}) %collective-permute-start.17) | collective-permute-done | bytes 122912 | tf_op jit(solution)/shard_map/ppermute | solution.py:397
  89.3 3.1 %collective-permute-done.15.a0 = bf16[240,256]{1,0:T(8,128)(2,1)S(1)} collective-permute-done((bf16[240,256]{1,0:T(8,128)(2,1)S(1)}, bf16[240,256]{1,0:T(8,128)(2,1)S(1)}, u32[]{:S(2)}, u32[]{:S(2)}) %collective-permute-start.15) | collective-permute-done | bytes 122912 | tf_op jit(solution)/shard_map/ppermute | solution.py:397
  94.1 1.8 %collective-permute-start.19 = (bf16[224,256]{1,0:T(8,128)(2,1)S(1)}, bf16[224,256]{1,0:T(8,128)(2,1)S(1)}, u32[]{:S(2)}, u32[]{:S(2)}) collective-permute-start(bf16[224,256]{1,0:T(8,128)(2,1)S(1)} %get-tuple-element.59.own), channel_id=1, source_target_pairs={{0,96},{8,104},{16,112},{24,120},{32,0},{40,8},{48,16},{56,24},{64... | collective-permute-start | bytes 344072 | tf_op jit(solution)/shard_map/ppermute | solution.py:397
  96.1 2.1 %shard_map.67 = bf16[2,1024,256]{2,1,0:T(8,128)(2,1)} custom-call(f32[2,256]{1,0:T(2,128)S(1)} %get-tuple-element.33.refs_0_.stats, f32[2,256]{1,0:T(2,128)S(1)} %get-tuple-element.56.sums, bf16[2,1024,256]{2,1,0:T(8,128)(2,1)S(1)} %bitcast.17, bf16[2,1024,256]{2,1,0:T(8,128)(2,1)S(1)} %bitcast.12, f32[1024,256]{1,0:T(8,128)S(1)} %get-tuple-element.57.grad0, ...), custom_call_target="tpu_custom_call" | custom-call | bytes 8000000 | tf_op jit(solution)/shard_map/pallas_call | solution.py:374
  99.2 2.7 %collective-permute-done.18.a0 = bf16[224,256]{1,0:T(8,128)(2,1)S(1)} collective-permute-done((bf16[224,256]{1,0:T(8,128)(2,1)S(1)}, bf16[224,256]{1,0:T(8,128)(2,1)S(1)}, u32[]{:S(2)}, u32[]{:S(2)}) %collective-permute-start.18) | collective-permute-done | bytes 114720 | tf_op jit(solution)/shard_map/ppermute | solution.py:397
  (50 shorter events, 20.8 us)
Async XLA Ops:
  0.6 24.0 %copy-start.1 = (bf16[1,2,16,64,256]{4,3,2,1,0:T(8,128)(2,1)S(1)}, bf16[1,2,16,64,256]{4,3,2,1,0:T(8,128)(2,1)}, u32[]{:S(2)}) copy-start(bf16[1,2,16,64,256]{4,3,2,1,0:T(8,128)(2,1)} %param.4) | copy-start | bytes 3145732
  0.6 29.6 %collective-permute-start.2 = (bf16[864,256]{1,0:T(8,128)(2,1)}, bf16[864,256]{1,0:T(8,128)(2,1)S(1)}, u32[]{:S(2)}, u32[]{:S(2)}) collective-permute-start(bf16[864,256]{1,0:T(8,128)(2,1)} %own.1), channel_id=1, source_target_pairs={{0,6},{1,7},{2,0},{3,1},{4,2},{5,3},{6,4},{7,5},{8,14},{9,15},{10,... | collective-permute-start | bytes 1327112 | tf_op jit(solution)/shard_map/ppermute | solution.py:397
  1.5 28.7 %collective-permute-start.1 = (bf16[864,256]{1,0:T(8,128)(2,1)}, bf16[864,256]{1,0:T(8,128)(2,1)S(1)}, u32[]{:S(2)}, u32[]{:S(2)}) collective-permute-start(bf16[864,256]{1,0:T(8,128)(2,1)} %own.1), channel_id=1, source_target_pairs={{0,2},{1,3},{2,4},{3,5},{4,6},{5,7},{6,0},{7,1},{8,10},{9,11},{10,... | collective-permute-start | bytes 1327112 | tf_op jit(solution)/shard_map/ppermute | solution.py:397
  3.9 26.3 %collective-permute-start.3 = (bf16[864,256]{1,0:T(8,128)(2,1)}, bf16[864,256]{1,0:T(8,128)(2,1)}, u32[]{:S(2)}, u32[]{:S(2)}) collective-permute-start(bf16[864,256]{1,0:T(8,128)(2,1)} %own.1), channel_id=1, source_target_pairs={{0,4},{1,5},{2,6},{3,7},{4,0},{5,1},{6,2},{7,3},{8,12},{9,13},{10,... | collective-permute-start | bytes 1327112 | tf_op jit(solution)/shard_map/ppermute | solution.py:397
  6.4 15.7 %all-to-all-start = ((f32[16,2,256]{2,1,0:T(2,128)}), f32[16,2,256]{2,1,0:T(2,128)S(1)}, u32[]{:S(2)}, u32[]{:S(2)}) async-start(f32[16,2,256]{2,1,0:T(2,128)} %get-tuple-element.31.order), calls=%async_computation | async-start | bytes 65536 | tf_op jit(solution)/shard_map/all_to_all | solution.py:426
  15.7 15.8 %collective-permute-start = (bf16[1024,256]{1,0:T(8,128)(2,1)S(1)}, bf16[1024,256]{1,0:T(8,128)(2,1)S(1)}, u32[]{:S(2)}, u32[]{:S(2)}) collective-permute-start(bf16[1024,256]{1,0:T(8,128)(2,1)S(1)} %shard_map.54), channel_id=1, source_target_pairs={{8,0},{16,8},{24,16},{32,24},{40,32},{48,40},{56,48},{64,56},{72,6... | collective-permute-start | bytes 1572872 | tf_op jit(solution)/shard_map/ppermute | solution.py:407
  22.1 12.3 %collective-permute-start.5 = (bf16[1024,256]{1,0:T(8,128)(2,1)S(1)}, bf16[1024,256]{1,0:T(8,128)(2,1)S(1)}, u32[]{:S(2)}, u32[]{:S(2)}) collective-permute-start(bf16[1024,256]{1,0:T(8,128)(2,1)S(1)} %get-tuple-element.39), channel_id=1, source_target_pairs={{0,8},{8,16},{16,24},{24,32},{32,40},{40,48},{48,56},{56,64},{64,7... | collective-permute-start | bytes 1572872 | tf_op jit(solution)/shard_map/ppermute | solution.py:407
  25.8 4.4 %copy-start.4 = (bf16[864,256]{1,0:T(8,128)(2,1)S(1)}, bf16[864,256]{1,0:T(8,128)(2,1)}, u32[]{:S(2)}) copy-start(bf16[864,256]{1,0:T(8,128)(2,1)} %own.1) | copy-start | bytes 1327108
  31.4 17.1 %collective-permute-start.10 = (bf16[4,864,256]{2,1,0:T(8,128)(2,1)S(1)}, bf16[4,864,256]{2,1,0:T(8,128)(2,1)S(1)}, u32[]{:S(2)}, u32[]{:S(2)}) collective-permute-start(bf16[4,864,256]{2,1,0:T(8,128)(2,1)S(1)} %shard_map.56.order.mine), channel_id=1, source_target_pairs={{0,1},{1,0},{2,3},{3,2},{4,5},{5,4},{6,7},{7,6},{8,9},{9,8},{10,11... | collective-permute-start | bytes 5308424 | tf_op jit(solution)/shard_map/ppermute | solution.py:402
  33.8 7.2 %collective-permute-start.4 = (bf16[1824,256]{1,0:T(8,128)(2,1)S(1)}, bf16[1824,256]{1,0:T(8,128)(2,1)S(1)}, u32[]{:S(2)}, u32[]{:S(2)}) collective-permute-start(bf16[1824,256]{1,0:T(8,128)(2,1)S(1)} %get-tuple-element.38.order), channel_id=1, source_target_pairs={{0,1},{1,0},{2,3},{3,2},{4,5},{5,4},{6,7},{7,6},{8,9},{9,8},{10,11... | collective-permute-start | bytes 2801672 | tf_op jit(solution)/shard_map/ppermute | solution.py:402
  39.6 2.6 %collective-permute-start.6 = (bf16[1824,256]{1,0:T(8,128)(2,1)S(1)}, bf16[1824,256]{1,0:T(8,128)(2,1)S(1)}, u32[]{:S(2)}, u32[]{:S(2)}) collective-permute-start(bf16[1824,256]{1,0:T(8,128)(2,1)S(1)} %get-tuple-element.41), channel_id=1, source_target_pairs={{0,1},{1,0},{2,3},{3,2},{4,5},{5,4},{6,7},{7,6},{8,9},{9,8},{10,11... | collective-permute-start | bytes 2801672 | tf_op jit(solution)/shard_map/ppermute | solution.py:402
  39.7 16.2 %collective-permute-start.11 = (bf16[1024,256]{1,0:T(8,128)(2,1)S(1)}, bf16[1024,256]{1,0:T(8,128)(2,1)S(1)}, u32[]{:S(2)}, u32[]{:S(2)}) collective-permute-start(bf16[1024,256]{1,0:T(8,128)(2,1)S(1)} %shard_map.61), channel_id=1, source_target_pairs={{8,0},{16,8},{24,16},{32,24},{40,32},{48,40},{56,48},{64,56},{72,6... | collective-permute-start | bytes 1572872 | tf_op jit(solution)/shard_map/ppermute | solution.py:407
  43.1 22.1 %collective-permute-start.7 = (bf16[896,256]{1,0:T(8,128)(2,1)S(1)}, bf16[896,256]{1,0:T(8,128)(2,1)S(1)}, u32[]{:S(2)}, u32[]{:S(2)}) collective-permute-start(bf16[896,256]{1,0:T(8,128)(2,1)S(1)} %get-tuple-element.43), channel_id=1, source_target_pairs={{0,2},{1,3},{2,4},{3,5},{4,6},{5,7},{6,0},{7,1},{8,10},{9,11},{10,... | collective-permute-start | bytes 1376264 | tf_op jit(solution)/shard_map/ppermute | solution.py:397
  45.3 19.9 %collective-permute-start.8 = (bf16[896,256]{1,0:T(8,128)(2,1)S(1)}, bf16[896,256]{1,0:T(8,128)(2,1)S(1)}, u32[]{:S(2)}, u32[]{:S(2)}) collective-permute-start(bf16[896,256]{1,0:T(8,128)(2,1)S(1)} %get-tuple-element.44), channel_id=1, source_target_pairs={{0,6},{1,7},{2,0},{3,1},{4,2},{5,3},{6,4},{7,5},{8,14},{9,15},{10,... | collective-permute-start | bytes 1376264 | tf_op jit(solution)/shard_map/ppermute | solution.py:397
  45.3 23.3 %collective-permute-start.9 = (bf16[896,256]{1,0:T(8,128)(2,1)S(1)}, bf16[896,256]{1,0:T(8,128)(2,1)S(1)}, u32[]{:S(2)}, u32[]{:S(2)}) collective-permute-start(bf16[896,256]{1,0:T(8,128)(2,1)S(1)} %get-tuple-element.45), channel_id=1, source_target_pairs={{0,4},{1,5},{2,6},{3,7},{4,0},{5,1},{6,2},{7,3},{8,12},{9,13},{10,... | collective-permute-start | bytes 1376264 | tf_op jit(solution)/shard_map/ppermute | solution.py:397
  69.5 9.5 %collective-permute-start.12 = (bf16[240,256]{1,0:T(8,128)(2,1)S(1)}, bf16[240,256]{1,0:T(8,128)(2,1)S(1)}, u32[]{:S(2)}, u32[]{:S(2)}) collective-permute-start(bf16[240,256]{1,0:T(8,128)(2,1)S(1)} %get-tuple-element.51), channel_id=1, source_target_pairs={{0,32},{8,40},{16,48},{24,56},{32,64},{40,72},{48,80},{56,88},{64,... | collective-permute-start | bytes 368648 | tf_op jit(solution)/shard_map/ppermute | solution.py:397
  73.7 5.6 %collective-permute-start.13 = (bf16[240,256]{1,0:T(8,128)(2,1)S(1)}, bf16[240,256]{1,0:T(8,128)(2,1)S(1)}, u32[]{:S(2)}, u32[]{:S(2)}) collective-permute-start(bf16[240,256]{1,0:T(8,128)(2,1)S(1)} %get-tuple-element.52), channel_id=1, source_target_pairs={{0,96},{8,104},{16,112},{24,120},{32,0},{40,8},{48,16},{56,24},{64... | collective-permute-start | bytes 368648 | tf_op jit(solution)/shard_map/ppermute | solution.py:397
  75.3 6.4 %collective-permute-start.14 = (bf16[240,256]{1,0:T(8,128)(2,1)S(1)}, bf16[240,256]{1,0:T(8,128)(2,1)S(1)}, u32[]{:S(2)}, u32[]{:S(2)}) collective-permute-start(bf16[240,256]{1,0:T(8,128)(2,1)S(1)} %get-tuple-element.53), channel_id=1, source_target_pairs={{0,64},{8,72},{16,80},{24,88},{32,96},{40,104},{48,112},{56,120},{... | collective-permute-start | bytes 368648 | tf_op jit(solution)/shard_map/ppermute | solution.py:397
  81.8 7.5 %collective-permute-start.17 = (bf16[240,256]{1,0:T(8,128)(2,1)S(1)}, bf16[240,256]{1,0:T(8,128)(2,1)S(1)}, u32[]{:S(2)}, u32[]{:S(2)}) collective-permute-start(bf16[240,256]{1,0:T(8,128)(2,1)S(1)} %get-tuple-element.54.own), channel_id=1, source_target_pairs={{0,16},{8,24},{16,0},{24,8},{32,48},{40,56},{48,32},{56,40},{64,80... | collective-permute-start | bytes 368648 | tf_op jit(solution)/shard_map/ppermute | solution.py:397
  82.5 6.8 %collective-permute-start.16 = (bf16[240,256]{1,0:T(8,128)(2,1)S(1)}, bf16[240,256]{1,0:T(8,128)(2,1)S(1)}, u32[]{:S(2)}, u32[]{:S(2)}) collective-permute-start(bf16[240,256]{1,0:T(8,128)(2,1)S(1)} %get-tuple-element.54.own), channel_id=1, source_target_pairs={{0,24},{8,0},{16,8},{24,16},{32,56},{40,32},{48,40},{56,48},{64,88... | collective-permute-start | bytes 368648 | tf_op jit(solution)/shard_map/ppermute | solution.py:397
  86.4 6.1 %collective-permute-start.15 = (bf16[240,256]{1,0:T(8,128)(2,1)S(1)}, bf16[240,256]{1,0:T(8,128)(2,1)S(1)}, u32[]{:S(2)}, u32[]{:S(2)}) collective-permute-start(bf16[240,256]{1,0:T(8,128)(2,1)S(1)} %get-tuple-element.54.own), channel_id=1, source_target_pairs={{0,8},{8,16},{16,24},{24,0},{32,40},{40,48},{48,56},{56,32},{64,72... | collective-permute-start | bytes 368648 | tf_op jit(solution)/shard_map/ppermute | solution.py:397
  92.5 6.4 %collective-permute-start.20 = (bf16[224,256]{1,0:T(8,128)(2,1)S(1)}, bf16[224,256]{1,0:T(8,128)(2,1)S(1)}, u32[]{:S(2)}, u32[]{:S(2)}) collective-permute-start(bf16[224,256]{1,0:T(8,128)(2,1)S(1)} %get-tuple-element.59.own), channel_id=1, source_target_pairs={{0,64},{8,72},{16,80},{24,88},{32,96},{40,104},{48,112},{56,120},{... | collective-permute-start | bytes 344072 | tf_op jit(solution)/shard_map/ppermute | solution.py:397
  94.1 5.1 %collective-permute-start.19 = (bf16[224,256]{1,0:T(8,128)(2,1)S(1)}, bf16[224,256]{1,0:T(8,128)(2,1)S(1)}, u32[]{:S(2)}, u32[]{:S(2)}) collective-permute-start(bf16[224,256]{1,0:T(8,128)(2,1)S(1)} %get-tuple-element.59.own), channel_id=1, source_target_pairs={{0,96},{8,104},{16,112},{24,120},{32,0},{40,8},{48,16},{56,24},{64... | collective-permute-start | bytes 344072 | tf_op jit(solution)/shard_map/ppermute | solution.py:397
  95.9 6.0 %collective-permute-start.18 = (bf16[224,256]{1,0:T(8,128)(2,1)S(1)}, bf16[224,256]{1,0:T(8,128)(2,1)S(1)}, u32[]{:S(2)}, u32[]{:S(2)}) collective-permute-start(bf16[224,256]{1,0:T(8,128)(2,1)S(1)} %get-tuple-element.59.own), channel_id=1, source_target_pairs={{0,32},{8,40},{16,48},{24,56},{32,64},{40,72},{48,80},{56,88},{64,... | collective-permute-start | bytes 344072 | tf_op jit(solution)/shard_map/ppermute | solution.py:397
  (3 other events, 3.7 us)

commit v14 on v12

--- a/solution.py
+++ b/solution.py
@@ -435,7 +435,7 @@
         (where, act, near, after, keep_up, send_up),
         flops=9 * tap_flops // 2,
         scalars=1,
-        order=(mine,),
+        order=(act,),
         aliases={4: 0, 5: 1},
     )
     got_up = swap_core(send_up)

time: 104 us -> 104 us (level)
  no operation moved by 1% of the time
where the time goes in v14:
time: 104 us; the launch traced here: 103 us
  starting transfers between devices  38.7 us (37%)
  Pallas kernels  32.1 us (31%)
  waiting for transfers between devices  28.7 us (28%)
  local copies, waits for them, and re-layouts  3.11 us (3%)
    pallas_call x19, Pallas kernels, call(): pl.pallas_call(kernel, out_shape=out_shape, in_specs=specs, out_specs=out...  32.1 us
    ppermute x15, starting transfers between devices, ring(): got.append(lax.ppermute(block, name, route))  24.8 us
    ppermute x15, waiting for transfers between devices, ring(): got.append(lax.ppermute(block, name, route))  21.2 us
    all_to_all x1, starting transfers between devices, per_device(): parts = lax.all_to_all(sums, 'tm', 0, 0, tiled=True)  8.05 us
    ppermute x3, starting transfers between devices, passed(): return lax.ppermute(block, 'tm', route)  5.09 us
    all_to_all x1, waiting for transfers between devices, per_device(): parts = lax.all_to_all(sums, 'tm', 0, 0, tiled=True)  4.97 us
    unnamed x10, local copies, waits for them, and re-layouts  3.11 us
  transfers between devices with their start and end apart: 22, of which 13 were waited for; matrix products, arithmetic and copies ran while one was open for 0% of the time, Pallas kernels for 28%

profile of v14, /device:TPU:6, one launch (start us, length us, event | category | flops | bytes accessed | tf_op | source)
XLA Modules:
  0.0 103.5 jit_solution(14994406761021101278)
XLA Ops:
  1.5 2.4 %collective-permute-start.7 = (bf16[864,256]{1,0:T(8,128)(2,1)}, bf16[864,256]{1,0:T(8,128)(2,1)S(1)}, u32[]{:S(2)}, u32[]{:S(2)}) collective-permute-start(bf16[864,256]{1,0:T(8,128)(2,1)} %own.1), channel_id=1, source_target_pairs={{0,2},{1,3},{2,4},{3,5},{4,6},{5,7},{6,0},{7,1},{8,10},{9,11},{10,... | collective-permute-start | bytes 1327112 | tf_op jit(solution)/shard_map/ppermute | solution.py:383
  6.4 8.0 %all-to-all-start = ((f32[16,2,256]{2,1,0:T(2,128)}), f32[16,2,256]{2,1,0:T(2,128)S(1)}, u32[]{:S(2)}, u32[]{:S(2)}) async-start(f32[16,2,256]{2,1,0:T(2,128)} %get-tuple-element.31.order), calls=%async_computation | async-start | bytes 65536 | tf_op jit(solution)/shard_map/all_to_all | solution.py:412
  17.1 5.0 %all-to-all-done.parts = f32[16,2,256]{2,1,0:T(2,128)S(1)} async-done(((f32[16,2,256]{2,1,0:T(2,128)}), f32[16,2,256]{2,1,0:T(2,128)S(1)}, u32[]{:S(2)}, u32[]{:S(2)}) %all-to-all-start) | async-done | bytes 32800 | tf_op jit(solution)/shard_map/all_to_all | solution.py:412
  22.1 2.5 %collective-permute-start.2 = (bf16[1024,256]{1,0:T(8,128)(2,1)S(1)}, bf16[1024,256]{1,0:T(8,128)(2,1)S(1)}, u32[]{:S(2)}, u32[]{:S(2)}) collective-permute-start(bf16[1024,256]{1,0:T(8,128)(2,1)S(1)} %get-tuple-element.39), channel_id=1, source_target_pairs={{0,8},{8,16},{16,24},{24,32},{32,40},{40,48},{48,56},{56,64},{64,7... | collective-permute-start | bytes 1572872 | tf_op jit(solution)/shard_map/ppermute | solution.py:393
  25.8 4.4 %shard_map.53 = (bf16[2,1024,256]{2,1,0:T(8,128)(2,1)S(1)}, f32[1824,256]{1,0:T(8,128)S(1)}, bf16[1824,256]{1,0:T(8,128)(2,1)S(1)}) custom-call(s32[4]{0:T(128)S(1)} %pad_add_fusion.where, f32[2,256]{1,0:T(2,128)S(1)} %get-tuple-element.33.refs_0_.stats, bf16[2,1024,256]{2,1,0:T(8,128)(2,1)S(1)} %bitcast.14, bf16[3,2,1152,256]{3,2,1,0:T(8,128)(2,1)S(1)} %shard_map.52.near), custom_call_target="tpu_custom_call" | custom-call | flops 2415919104 | tf_op jit(solution)/shard_map/pallas_call | solution.py:360
  31.8 2.0 %shard_map.56 = (f32[1824,256]{1,0:T(8,128)S(1)}, bf16[1824,256]{1,0:T(8,128)(2,1)S(1)}) custom-call(s32[4]{0:T(128)S(1)} %pad_add_fusion.where, bf16[2,1024,256]{2,1,0:T(8,128)(2,1)S(1)} %get-tuple-element.34.act.order, bf16[3,2,1152,256]{3,2,1,0:T(8,128)(2,1)S(1)} %shard_map.52.near, ...), custom_call_target="tpu_custom_call", output_to_operand_aliasing={{0}: (4, {}), {1}: (5, {})} | custom-call | flops 1207959552 | tf_op jit(solution)/shard_map/pallas_call | solution.py:360
  34.4 5.2 %shard_map.57 = (f32[1824,256]{1,0:T(8,128)S(1)}, bf16[1824,256]{1,0:T(8,128)(2,1)S(1)}) custom-call(s32[4]{0:T(128)S(1)} %pad_add_fusion.where, f32[2,256]{1,0:T(2,128)S(1)} %get-tuple-element.33.refs_0_.stats, bf16[2,1024,256]{2,1,0:T(8,128)(2,1)S(1)} %get-tuple-element.34.act.order, bf16[1024,256]{1,0:T(8,128)(2,1)S(1)} %collective-permute-done.2.before, ...), custom_call_target="tpu_custom_call" | custom-call | flops 3623878656 | tf_op jit(solution)/shard_map/pallas_call | solution.py:360
  43.2 2.1 %collective-permute-start.4 = (bf16[896,256]{1,0:T(8,128)(2,1)S(1)}, bf16[896,256]{1,0:T(8,128)(2,1)S(1)}, u32[]{:S(2)}, u32[]{:S(2)}) collective-permute-start(bf16[896,256]{1,0:T(8,128)(2,1)S(1)} %get-tuple-element.43), channel_id=1, source_target_pairs={{0,2},{1,3},{2,4},{3,5},{4,6},{5,7},{6,0},{7,1},{8,10},{9,11},{10,... | collective-permute-start | bytes 1376264 | tf_op jit(solution)/shard_map/ppermute | solution.py:383
  45.3 3.3 %collective-permute-start.6 = (bf16[896,256]{1,0:T(8,128)(2,1)S(1)}, bf16[896,256]{1,0:T(8,128)(2,1)S(1)}, u32[]{:S(2)}, u32[]{:S(2)}) collective-permute-start(bf16[896,256]{1,0:T(8,128)(2,1)S(1)} %get-tuple-element.45), channel_id=1, source_target_pairs={{0,4},{1,5},{2,6},{3,7},{4,0},{5,1},{6,2},{7,3},{8,12},{9,13},{10,... | collective-permute-start | bytes 1376264 | tf_op jit(solution)/shard_map/ppermute | solution.py:383
  48.6 6.0 %shard_map.60 = (f32[1024,256]{1,0:T(8,128)S(1)}, f32[2,256]{1,0:T(2,128)S(1)}, bf16[6912,256]{1,0:T(8,128)(2,1)S(1)}) custom-call(s32[4]{0:T(128)S(1)} %pad_add_fusion.where, f32[2,256]{1,0:T(2,128)S(1)} %get-tuple-element.33.refs_0_.stats, bf16[2,1024,256]{2,1,0:T(8,128)(2,1)S(1)} %bitcast.15, bf16[3,2,1152,256]{3,2,1,0:T(8,128)(2,1)S(1)} %shard_map.52.near, ...), custom_call_target="tpu_custom_call" | custom-call | flops 3623878656 | tf_op jit(solution)/shard_map/pallas_call | solution.py:360
  56.2 5.4 %shard_map.63 = (f32[1024,256]{1,0:T(8,128)S(1)}, f32[2,256]{1,0:T(2,128)S(1)}) custom-call(f32[2,256]{1,0:T(2,128)S(1)} %get-tuple-element.33.refs_0_.stats, bf16[2,1024,256]{2,1,0:T(8,128)(2,1)S(1)} %bitcast.16, bf16[3,2,1152,256]{3,2,1,0:T(8,128)(2,1)S(1)} %shard_map.52.near, bf16[3,1,1152,256]{3,2,1,0:T(8,128)(2,1)S(1)} %shard_map.55.after, ...), custom_call_target="tpu_custom_call" | custom-call | flops 3623878656 | tf_op jit(solution)/shard_map/pallas_call | solution.py:360
  61.6 3.6 %collective-permute-done.4.a0 = bf16[896,256]{1,0:T(8,128)(2,1)S(1)} collective-permute-done((bf16[896,256]{1,0:T(8,128)(2,1)S(1)}, bf16[896,256]{1,0:T(8,128)(2,1)S(1)}, u32[]{:S(2)}, u32[]{:S(2)}) %collective-permute-start.4) | collective-permute-done | bytes 458784 | tf_op jit(solution)/shard_map/ppermute | solution.py:383
  65.2 3.4 %collective-permute-done.6.a2 = bf16[896,256]{1,0:T(8,128)(2,1)S(1)} collective-permute-done((bf16[896,256]{1,0:T(8,128)(2,1)S(1)}, bf16[896,256]{1,0:T(8,128)(2,1)S(1)}, u32[]{:S(2)}, u32[]{:S(2)}) %collective-permute-start.6) | collective-permute-done | bytes 458784 | tf_op jit(solution)/shard_map/ppermute | solution.py:383
  69.5 4.3 %collective-permute-start.12 = (bf16[240,256]{1,0:T(8,128)(2,1)S(1)}, bf16[240,256]{1,0:T(8,128)(2,1)S(1)}, u32[]{:S(2)}, u32[]{:S(2)}) collective-permute-start(bf16[240,256]{1,0:T(8,128)(2,1)S(1)} %get-tuple-element.51), channel_id=1, source_target_pairs={{0,32},{8,40},{16,48},{24,56},{32,64},{40,72},{48,80},{56,88},{64,... | collective-permute-start | bytes 368648 | tf_op jit(solution)/shard_map/ppermute | solution.py:383
  73.8 1.6 %collective-permute-start.13 = (bf16[240,256]{1,0:T(8,128)(2,1)S(1)}, bf16[240,256]{1,0:T(8,128)(2,1)S(1)}, u32[]{:S(2)}, u32[]{:S(2)}) collective-permute-start(bf16[240,256]{1,0:T(8,128)(2,1)S(1)} %get-tuple-element.52), channel_id=1, source_target_pairs={{0,96},{8,104},{16,112},{24,120},{32,0},{40,8},{48,16},{56,24},{64... | collective-permute-start | bytes 368648 | tf_op jit(solution)/shard_map/ppermute | solution.py:383
  75.4 1.9 %collective-permute-start.14 = (bf16[240,256]{1,0:T(8,128)(2,1)S(1)}, bf16[240,256]{1,0:T(8,128)(2,1)S(1)}, u32[]{:S(2)}, u32[]{:S(2)}) collective-permute-start(bf16[240,256]{1,0:T(8,128)(2,1)S(1)} %get-tuple-element.53), channel_id=1, source_target_pairs={{0,64},{8,72},{16,80},{24,88},{32,96},{40,104},{48,112},{56,120},{... | collective-permute-start | bytes 368648 | tf_op jit(solution)/shard_map/ppermute | solution.py:383
  77.3 1.7 %collective-permute-done.12.a0 = bf16[240,256]{1,0:T(8,128)(2,1)S(1)} collective-permute-done((bf16[240,256]{1,0:T(8,128)(2,1)S(1)}, bf16[240,256]{1,0:T(8,128)(2,1)S(1)}, u32[]{:S(2)}, u32[]{:S(2)}) %collective-permute-start.12) | collective-permute-done | bytes 122912 | tf_op jit(solution)/shard_map/ppermute | solution.py:383
  79.3 2.4 %collective-permute-done.14.a2 = bf16[240,256]{1,0:T(8,128)(2,1)S(1)} collective-permute-done((bf16[240,256]{1,0:T(8,128)(2,1)S(1)}, bf16[240,256]{1,0:T(8,128)(2,1)S(1)}, u32[]{:S(2)}, u32[]{:S(2)}) %collective-permute-start.14) | collective-permute-done | bytes 122912 | tf_op jit(solution)/shard_map/ppermute | solution.py:383
  82.6 3.8 %collective-permute-start.16 = (bf16[240,256]{1,0:T(8,128)(2,1)S(1)}, bf16[240,256]{1,0:T(8,128)(2,1)S(1)}, u32[]{:S(2)}, u32[]{:S(2)}) collective-permute-start(bf16[240,256]{1,0:T(8,128)(2,1)S(1)} %get-tuple-element.54.own), channel_id=1, source_target_pairs={{0,24},{8,0},{16,8},{24,16},{32,56},{40,32},{48,40},{56,48},{64,88... | collective-permute-start | bytes 368648 | tf_op jit(solution)/shard_map/ppermute | solution.py:383
  86.4 3.0 %collective-permute-done.17.a2 = bf16[240,256]{1,0:T(8,128)(2,1)S(1)} collective-permute-done((bf16[240,256]{1,0:T(8,128)(2,1)S(1)}, bf16[240,256]{1,0:T(8,128)(2,1)S(1)}, u32[]{:S(2)}, u32[]{:S(2)}) %collective-permute-start.17) | collective-permute-done | bytes 122912 | tf_op jit(solution)/shard_map/ppermute | solution.py:383
  89.4 3.1 %collective-permute-done.15.a0 = bf16[240,256]{1,0:T(8,128)(2,1)S(1)} collective-permute-done((bf16[240,256]{1,0:T(8,128)(2,1)S(1)}, bf16[240,256]{1,0:T(8,128)(2,1)S(1)}, u32[]{:S(2)}, u32[]{:S(2)}) %collective-permute-start.15) | collective-permute-done | bytes 122912 | tf_op jit(solution)/shard_map/ppermute | solution.py:383
  94.1 1.8 %collective-permute-start.19 = (bf16[224,256]{1,0:T(8,128)(2,1)S(1)}, bf16[224,256]{1,0:T(8,128)(2,1)S(1)}, u32[]{:S(2)}, u32[]{:S(2)}) collective-permute-start(bf16[224,256]{1,0:T(8,128)(2,1)S(1)} %get-tuple-element.59.own), channel_id=1, source_target_pairs={{0,96},{8,104},{16,112},{24,120},{32,0},{40,8},{48,16},{56,24},{64... | collective-permute-start | bytes 344072 | tf_op jit(solution)/shard_map/ppermute | solution.py:383
  96.2 2.1 %shard_map.67 = bf16[2,1024,256]{2,1,0:T(8,128)(2,1)} custom-call(f32[2,256]{1,0:T(2,128)S(1)} %get-tuple-element.33.refs_0_.stats, f32[2,256]{1,0:T(2,128)S(1)} %get-tuple-element.56.sums, bf16[2,1024,256]{2,1,0:T(8,128)(2,1)S(1)} %bitcast.17, bf16[2,1024,256]{2,1,0:T(8,128)(2,1)S(1)} %bitcast.12, f32[1024,256]{1,0:T(8,128)S(1)} %get-tuple-element.57.grad0, ...), custom_call_target="tpu_custom_call" | custom-call | bytes 8000000 | tf_op jit(solution)/shard_map/pallas_call | solution.py:360
  99.2 2.7 %collective-permute-done.18.a0 = bf16[224,256]{1,0:T(8,128)(2,1)S(1)} collective-permute-done((bf16[224,256]{1,0:T(8,128)(2,1)S(1)}, bf16[224,256]{1,0:T(8,128)(2,1)S(1)}, u32[]{:S(2)}, u32[]{:S(2)}) %collective-permute-start.18) | collective-permute-done | bytes 114720 | tf_op jit(solution)/shard_map/ppermute | solution.py:383
  (50 shorter events, 20.8 us)
Async XLA Ops:
  0.6 24.0 %copy-start.1 = (bf16[1,2,16,64,256]{4,3,2,1,0:T(8,128)(2,1)S(1)}, bf16[1,2,16,64,256]{4,3,2,1,0:T(8,128)(2,1)}, u32[]{:S(2)}) copy-start(bf16[1,2,16,64,256]{4,3,2,1,0:T(8,128)(2,1)} %param.4) | copy-start | bytes 3145732
  0.6 29.6 %collective-permute-start.8 = (bf16[864,256]{1,0:T(8,128)(2,1)}, bf16[864,256]{1,0:T(8,128)(2,1)S(1)}, u32[]{:S(2)}, u32[]{:S(2)}) collective-permute-start(bf16[864,256]{1,0:T(8,128)(2,1)} %own.1), channel_id=1, source_target_pairs={{0,6},{1,7},{2,0},{3,1},{4,2},{5,3},{6,4},{7,5},{8,14},{9,15},{10,... | collective-permute-start | bytes 1327112 | tf_op jit(solution)/shard_map/ppermute | solution.py:383
  1.5 28.7 %collective-permute-start.7 = (bf16[864,256]{1,0:T(8,128)(2,1)}, bf16[864,256]{1,0:T(8,128)(2,1)S(1)}, u32[]{:S(2)}, u32[]{:S(2)}) collective-permute-start(bf16[864,256]{1,0:T(8,128)(2,1)} %own.1), channel_id=1, source_target_pairs={{0,2},{1,3},{2,4},{3,5},{4,6},{5,7},{6,0},{7,1},{8,10},{9,11},{10,... | collective-permute-start | bytes 1327112 | tf_op jit(solution)/shard_map/ppermute | solution.py:383
  3.9 26.3 %collective-permute-start.9 = (bf16[864,256]{1,0:T(8,128)(2,1)}, bf16[864,256]{1,0:T(8,128)(2,1)}, u32[]{:S(2)}, u32[]{:S(2)}) collective-permute-start(bf16[864,256]{1,0:T(8,128)(2,1)} %own.1), channel_id=1, source_target_pairs={{0,4},{1,5},{2,6},{3,7},{4,0},{5,1},{6,2},{7,3},{8,12},{9,13},{10,... | collective-permute-start | bytes 1327112 | tf_op jit(solution)/shard_map/ppermute | solution.py:383
  6.4 15.7 %all-to-all-start = ((f32[16,2,256]{2,1,0:T(2,128)}), f32[16,2,256]{2,1,0:T(2,128)S(1)}, u32[]{:S(2)}, u32[]{:S(2)}) async-start(f32[16,2,256]{2,1,0:T(2,128)} %get-tuple-element.31.order), calls=%async_computation | async-start | bytes 65536 | tf_op jit(solution)/shard_map/all_to_all | solution.py:412
  15.7 15.8 %collective-permute-start = (bf16[1024,256]{1,0:T(8,128)(2,1)S(1)}, bf16[1024,256]{1,0:T(8,128)(2,1)S(1)}, u32[]{:S(2)}, u32[]{:S(2)}) collective-permute-start(bf16[1024,256]{1,0:T(8,128)(2,1)S(1)} %shard_map.54), channel_id=1, source_target_pairs={{8,0},{16,8},{24,16},{32,24},{40,32},{48,40},{56,48},{64,56},{72,6... | collective-permute-start | bytes 1572872 | tf_op jit(solution)/shard_map/ppermute | solution.py:393
  22.1 12.3 %collective-permute-start.2 = (bf16[1024,256]{1,0:T(8,128)(2,1)S(1)}, bf16[1024,256]{1,0:T(8,128)(2,1)S(1)}, u32[]{:S(2)}, u32[]{:S(2)}) collective-permute-start(bf16[1024,256]{1,0:T(8,128)(2,1)S(1)} %get-tuple-element.39), channel_id=1, source_target_pairs={{0,8},{8,16},{16,24},{24,32},{32,40},{40,48},{48,56},{56,64},{64,7... | collective-permute-start | bytes 1572872 | tf_op jit(solution)/shard_map/ppermute | solution.py:393
  25.8 4.4 %copy-start.4 = (bf16[864,256]{1,0:T(8,128)(2,1)S(1)}, bf16[864,256]{1,0:T(8,128)(2,1)}, u32[]{:S(2)}) copy-start(bf16[864,256]{1,0:T(8,128)(2,1)} %own.1) | copy-start | bytes 1327108
  31.4 17.2 %collective-permute-start.10 = (bf16[4,864,256]{2,1,0:T(8,128)(2,1)S(1)}, bf16[4,864,256]{2,1,0:T(8,128)(2,1)S(1)}, u32[]{:S(2)}, u32[]{:S(2)}) collective-permute-start(bf16[4,864,256]{2,1,0:T(8,128)(2,1)S(1)} %shard_map.59.mine), channel_id=1, source_target_pairs={{0,1},{1,0},{2,3},{3,2},{4,5},{5,4},{6,7},{7,6},{8,9},{9,8},{10,11... | collective-permute-start | bytes 5308424 | tf_op jit(solution)/shard_map/ppermute | solution.py:388
  33.8 7.2 %collective-permute-start.1 = (bf16[1824,256]{1,0:T(8,128)(2,1)S(1)}, bf16[1824,256]{1,0:T(8,128)(2,1)S(1)}, u32[]{:S(2)}, u32[]{:S(2)}) collective-permute-start(bf16[1824,256]{1,0:T(8,128)(2,1)S(1)} %get-tuple-element.38.order), channel_id=1, source_target_pairs={{0,1},{1,0},{2,3},{3,2},{4,5},{5,4},{6,7},{7,6},{8,9},{9,8},{10,11... | collective-permute-start | bytes 2801672 | tf_op jit(solution)/shard_map/ppermute | solution.py:388
  39.6 2.6 %collective-permute-start.3 = (bf16[1824,256]{1,0:T(8,128)(2,1)S(1)}, bf16[1824,256]{1,0:T(8,128)(2,1)S(1)}, u32[]{:S(2)}, u32[]{:S(2)}) collective-permute-start(bf16[1824,256]{1,0:T(8,128)(2,1)S(1)} %get-tuple-element.41), channel_id=1, source_target_pairs={{0,1},{1,0},{2,3},{3,2},{4,5},{5,4},{6,7},{7,6},{8,9},{9,8},{10,11... | collective-permute-start | bytes 2801672 | tf_op jit(solution)/shard_map/ppermute | solution.py:388
  39.7 16.2 %collective-permute-start.11 = (bf16[1024,256]{1,0:T(8,128)(2,1)S(1)}, bf16[1024,256]{1,0:T(8,128)(2,1)S(1)}, u32[]{:S(2)}, u32[]{:S(2)}) collective-permute-start(bf16[1024,256]{1,0:T(8,128)(2,1)S(1)} %shard_map.61), channel_id=1, source_target_pairs={{8,0},{16,8},{24,16},{32,24},{40,32},{48,40},{56,48},{64,56},{72,6... | collective-permute-start | bytes 1572872 | tf_op jit(solution)/shard_map/ppermute | solution.py:393
  43.2 22.1 %collective-permute-start.4 = (bf16[896,256]{1,0:T(8,128)(2,1)S(1)}, bf16[896,256]{1,0:T(8,128)(2,1)S(1)}, u32[]{:S(2)}, u32[]{:S(2)}) collective-permute-start(bf16[896,256]{1,0:T(8,128)(2,1)S(1)} %get-tuple-element.43), channel_id=1, source_target_pairs={{0,2},{1,3},{2,4},{3,5},{4,6},{5,7},{6,0},{7,1},{8,10},{9,11},{10,... | collective-permute-start | bytes 1376264 | tf_op jit(solution)/shard_map/ppermute | solution.py:383
  45.3 19.9 %collective-permute-start.5 = (bf16[896,256]{1,0:T(8,128)(2,1)S(1)}, bf16[896,256]{1,0:T(8,128)(2,1)S(1)}, u32[]{:S(2)}, u32[]{:S(2)}) collective-permute-start(bf16[896,256]{1,0:T(8,128)(2,1)S(1)} %get-tuple-element.44), channel_id=1, source_target_pairs={{0,6},{1,7},{2,0},{3,1},{4,2},{5,3},{6,4},{7,5},{8,14},{9,15},{10,... | collective-permute-start | bytes 1376264 | tf_op jit(solution)/shard_map/ppermute | solution.py:383
  45.3 23.3 %collective-permute-start.6 = (bf16[896,256]{1,0:T(8,128)(2,1)S(1)}, bf16[896,256]{1,0:T(8,128)(2,1)S(1)}, u32[]{:S(2)}, u32[]{:S(2)}) collective-permute-start(bf16[896,256]{1,0:T(8,128)(2,1)S(1)} %get-tuple-element.45), channel_id=1, source_target_pairs={{0,4},{1,5},{2,6},{3,7},{4,0},{5,1},{6,2},{7,3},{8,12},{9,13},{10,... | collective-permute-start | bytes 1376264 | tf_op jit(solution)/shard_map/ppermute | solution.py:383
  69.5 9.5 %collective-permute-start.12 = (bf16[240,256]{1,0:T(8,128)(2,1)S(1)}, bf16[240,256]{1,0:T(8,128)(2,1)S(1)}, u32[]{:S(2)}, u32[]{:S(2)}) collective-permute-start(bf16[240,256]{1,0:T(8,128)(2,1)S(1)} %get-tuple-element.51), channel_id=1, source_target_pairs={{0,32},{8,40},{16,48},{24,56},{32,64},{40,72},{48,80},{56,88},{64,... | collective-permute-start | bytes 368648 | tf_op jit(solution)/shard_map/ppermute | solution.py:383
  73.8 5.6 %collective-permute-start.13 = (bf16[240,256]{1,0:T(8,128)(2,1)S(1)}, bf16[240,256]{1,0:T(8,128)(2,1)S(1)}, u32[]{:S(2)}, u32[]{:S(2)}) collective-permute-start(bf16[240,256]{1,0:T(8,128)(2,1)S(1)} %get-tuple-element.52), channel_id=1, source_target_pairs={{0,96},{8,104},{16,112},{24,120},{32,0},{40,8},{48,16},{56,24},{64... | collective-permute-start | bytes 368648 | tf_op jit(solution)/shard_map/ppermute | solution.py:383
  75.4 6.4 %collective-permute-start.14 = (bf16[240,256]{1,0:T(8,128)(2,1)S(1)}, bf16[240,256]{1,0:T(8,128)(2,1)S(1)}, u32[]{:S(2)}, u32[]{:S(2)}) collective-permute-start(bf16[240,256]{1,0:T(8,128)(2,1)S(1)} %get-tuple-element.53), channel_id=1, source_target_pairs={{0,64},{8,72},{16,80},{24,88},{32,96},{40,104},{48,112},{56,120},{... | collective-permute-start | bytes 368648 | tf_op jit(solution)/shard_map/ppermute | solution.py:383
  81.9 7.5 %collective-permute-start.17 = (bf16[240,256]{1,0:T(8,128)(2,1)S(1)}, bf16[240,256]{1,0:T(8,128)(2,1)S(1)}, u32[]{:S(2)}, u32[]{:S(2)}) collective-permute-start(bf16[240,256]{1,0:T(8,128)(2,1)S(1)} %get-tuple-element.54.own), channel_id=1, source_target_pairs={{0,16},{8,24},{16,0},{24,8},{32,48},{40,56},{48,32},{56,40},{64,80... | collective-permute-start | bytes 368648 | tf_op jit(solution)/shard_map/ppermute | solution.py:383
  82.6 6.8 %collective-permute-start.16 = (bf16[240,256]{1,0:T(8,128)(2,1)S(1)}, bf16[240,256]{1,0:T(8,128)(2,1)S(1)}, u32[]{:S(2)}, u32[]{:S(2)}) collective-permute-start(bf16[240,256]{1,0:T(8,128)(2,1)S(1)} %get-tuple-element.54.own), channel_id=1, source_target_pairs={{0,24},{8,0},{16,8},{24,16},{32,56},{40,32},{48,40},{56,48},{64,88... | collective-permute-start | bytes 368648 | tf_op jit(solution)/shard_map/ppermute | solution.py:383
  86.4 6.1 %collective-permute-start.15 = (bf16[240,256]{1,0:T(8,128)(2,1)S(1)}, bf16[240,256]{1,0:T(8,128)(2,1)S(1)}, u32[]{:S(2)}, u32[]{:S(2)}) collective-permute-start(bf16[240,256]{1,0:T(8,128)(2,1)S(1)} %get-tuple-element.54.own), channel_id=1, source_target_pairs={{0,8},{8,16},{16,24},{24,0},{32,40},{40,48},{48,56},{56,32},{64,72... | collective-permute-start | bytes 368648 | tf_op jit(solution)/shard_map/ppermute | solution.py:383
  92.6 6.4 %collective-permute-start.20 = (bf16[224,256]{1,0:T(8,128)(2,1)S(1)}, bf16[224,256]{1,0:T(8,128)(2,1)S(1)}, u32[]{:S(2)}, u32[]{:S(2)}) collective-permute-start(bf16[224,256]{1,0:T(8,128)(2,1)S(1)} %get-tuple-element.59.own), channel_id=1, source_target_pairs={{0,64},{8,72},{16,80},{24,88},{32,96},{40,104},{48,112},{56,120},{... | collective-permute-start | bytes 344072 | tf_op jit(solution)/shard_map/ppermute | solution.py:383
  94.1 5.1 %collective-permute-start.19 = (bf16[224,256]{1,0:T(8,128)(2,1)S(1)}, bf16[224,256]{1,0:T(8,128)(2,1)S(1)}, u32[]{:S(2)}, u32[]{:S(2)}) collective-permute-start(bf16[224,256]{1,0:T(8,128)(2,1)S(1)} %get-tuple-element.59.own), channel_id=1, source_target_pairs={{0,96},{8,104},{16,112},{24,120},{32,0},{40,8},{48,16},{56,24},{64... | collective-permute-start | bytes 344072 | tf_op jit(solution)/shard_map/ppermute | solution.py:383
  95.9 6.0 %collective-permute-start.18 = (bf16[224,256]{1,0:T(8,128)(2,1)S(1)}, bf16[224,256]{1,0:T(8,128)(2,1)S(1)}, u32[]{:S(2)}, u32[]{:S(2)}) collective-permute-start(bf16[224,256]{1,0:T(8,128)(2,1)S(1)} %get-tuple-element.59.own), channel_id=1, source_target_pairs={{0,32},{8,40},{16,48},{24,56},{32,64},{40,72},{48,80},{56,88},{64,... | collective-permute-start | bytes 344072 | tf_op jit(solution)/shard_map/ppermute | solution.py:383
  (3 other events, 3.7 us)
